TPU v7x, 32 devices: a whole 2x2x4 slice. The times are simulated.
32 devices in a mesh: ctx: 16 (over z, x, core), head: 2 (over y).
Axes of the slice: x: 2, y: 2, z: 4, core: 2. Of those that a mesh axis runs over, the one named last changes fastest.
Arguments:
- queries: bfloat16 [2048, 512], P('ctx', 'head'), may hold values from -6 to 6
- key_rows: bfloat16 [2048, 128], P('ctx'), may hold values from -6 to 6
- value_rows: bfloat16 [2048, 128], P('ctx'), may hold values from -6 to 6
- out_grad: bfloat16 [2048, 512], P('ctx', 'head'), may hold values from -6 to 6
- doc_lengths: int32 [8], replicated, may hold values from 1 to 1024, 2048 in all
- span_order: int32 [16, 2], replicated, may hold values from 0 to 31, as said below
Outputs:
- query_grad: bfloat16 [2048, 512], P('ctx', 'head')
- key_grad: bfloat16 [2048, 128], P(('ctx', 'head'))
- value_grad: bfloat16 [2048, 128], P(('ctx', 'head'))
Inputs may be any that keep to these rules, and one draw needn't show every extreme that they name: `doc_lengths`: the lengths sum to 2048; the longest is exactly 1024. `span_order`: row i holds a span number c and its mirror 32 - 1 - c, in that order; the first entries of all rows are distinct.
All inputs are finite; a program needn't handle non-finite values.
Results may differ from a plain program's by a relative error of at most 0.025.
Values may be sent and summed in bfloat16 or wider, within the bound.
No kernel may reach another device: no remote copies, remote signals or barrier semaphores. Data moves between devices by JAX's collectives and lax.ppermute only.
A program may use at most 64 MiB of HBM per device.

v0:
```python
import jax
import jax.numpy as jnp
from jax import lax
from jax.sharding import PartitionSpec as P

masked_value = -1e30


def local(queries, key_rows, value_rows, out_grad, doc_lengths, span_order):
    local_rows = queries.shape[0]
    head_dim = key_rows.shape[1]
    local_heads = queries.shape[1] // head_dim
    ctx_size = lax.axis_size("ctx")
    total_rows = local_rows * ctx_size
    span_rows = local_rows // 2
    positions = (
        span_order.reshape(-1)[:, None] * span_rows
        + jnp.arange(span_rows, dtype=jnp.int32)[None, :]
    ).reshape(-1)
    starts = jnp.cumsum(doc_lengths) - doc_lengths
    documents = jnp.sum((starts[None, :] <= positions[:, None]).astype(jnp.int32), axis=1) - 1
    ctx_index = lax.axis_index("ctx")
    own_pos = lax.dynamic_slice_in_dim(positions, ctx_index * local_rows, local_rows)
    own_doc = lax.dynamic_slice_in_dim(documents, ctx_index * local_rows, local_rows)
    all_keys, all_values = (
        lax.all_gather(key_rows, "ctx", axis=0, tiled=True),
        lax.all_gather(value_rows, "ctx", axis=0, tiled=True),
    )
    scaling = head_dim ** (-0.5)
    query_heads = queries.reshape(local_rows, local_heads, head_dim)
    grad_heads = out_grad.reshape(local_rows, local_heads, head_dim)
    width = min(512, total_rows)
    blocks = total_rows // width

    def block_data(index):
        start = index * width
        key_block = lax.dynamic_slice_in_dim(all_keys, start, width)
        value_block = lax.dynamic_slice_in_dim(all_values, start, width)
        key_pos = lax.dynamic_slice_in_dim(positions, start, width)
        key_doc = lax.dynamic_slice_in_dim(documents, start, width)
        allowed = (own_doc[:, None] == key_doc[None, :]) & (key_pos[None, :] <= own_pos[:, None])
        return (key_block, value_block, allowed)

    def products(key_block, value_block):
        scores = (
            jnp.einsum("qhd,kd->hqk", query_heads, key_block, preferred_element_type=jnp.float32)
            * scaling
        )
        dprobs = jnp.einsum(
            "qhd,kd->hqk", grad_heads, value_block, preferred_element_type=jnp.float32
        )
        return (scores, dprobs)

    def gather_stats(index, carry):
        key_block, value_block, allowed = block_data(index)
        run_max, run_sum, run_dot = carry
        scores, dprobs = products(key_block, value_block)
        masked = jnp.where(allowed[None], scores, masked_value)
        new_max = jnp.maximum(run_max, jnp.max(masked, axis=-1))
        expo = jnp.where(allowed[None], jnp.exp(masked - new_max[..., None]), 0.0)
        rescale = jnp.exp(run_max - new_max)
        return (
            new_max,
            run_sum * rescale + jnp.sum(expo, axis=-1),
            run_dot * rescale + jnp.sum(expo * dprobs, axis=-1),
        )

    start_stats = (
        jnp.full((local_heads, local_rows), masked_value, jnp.float32),
        jnp.zeros((local_heads, local_rows), jnp.float32),
        jnp.zeros((local_heads, local_rows), jnp.float32),
    )
    run_max, run_sum, run_dot = lax.fori_loop(0, blocks, gather_stats, start_stats)
    log_total = run_max + jnp.log(run_sum)
    row_delta = run_dot / run_sum

    def backward(dq_total, index):
        key_block, value_block, allowed = block_data(index)
        total = dq_total
        scores, dprobs = products(key_block, value_block)
        masked = jnp.where(allowed[None], scores, masked_value)
        weights = jnp.where(allowed[None], jnp.exp(masked - log_total[..., None]), 0.0)
        weights_low = weights.astype(jnp.bfloat16)
        dscores = (weights * (dprobs - row_delta[..., None])).astype(jnp.bfloat16)
        value_part = jnp.einsum(
            "hqk,qhd->kd", weights_low, grad_heads, preferred_element_type=jnp.float32
        )
        key_part = (
            jnp.einsum("hqk,qhd->kd", dscores, query_heads, preferred_element_type=jnp.float32)
            * scaling
        )
        total = total + jnp.einsum(
            "hqk,kd->qhd", dscores, key_block, preferred_element_type=jnp.float32
        )
        return (total, jnp.concatenate([key_part, value_part], axis=1))

    dq_total, pieces = lax.scan(
        backward, jnp.zeros((local_rows, local_heads, head_dim), jnp.float32), jnp.arange(blocks)
    )
    query_grad = (
        (dq_total * scaling).reshape(local_rows, local_heads * head_dim).astype(jnp.bfloat16)
    )
    partial_value = pieces.reshape(total_rows, 2 * head_dim)
    terms = partial_value.reshape(ctx_size, local_rows, 2 * head_dim)
    terms = lax.all_to_all(
        terms.astype(jnp.bfloat16), "ctx", split_axis=0, concat_axis=0, tiled=True
    ).astype(terms.dtype)
    owned = jnp.sum(terms, axis=0)
    summed = lax.psum_scatter(
        owned.astype(jnp.bfloat16), "head", scatter_dimension=0, tiled=True
    ).astype(jnp.float32)
    key_grad = summed[:, :head_dim].astype(jnp.bfloat16)
    value_grad = summed[:, head_dim:].astype(jnp.bfloat16)
    return (query_grad, key_grad, value_grad)


def solution(mesh):
    in_specs = (P("ctx", "head"), P("ctx", None), P("ctx", None), P("ctx", "head"), P(), P())
    out_specs = (P("ctx", "head"), P(("ctx", "head"), None), P(("ctx", "head"), None))
    return jax.shard_map(local, mesh=mesh, in_specs=in_specs, out_specs=out_specs, check_vma=False)
```

profile of v0, /device:TPU:0, one launch (start us, length us, event | category | flops | bytes accessed | tf_op | source)
XLA Modules:
  0.0 117.9 jit_solution(777267238021749976)
XLA Ops:
  7.3 0.6 copy-done.5
  7.9 0.2 reduce-window.9
  8.7 0.1 copy.41
  8.8 0.1 copy.43
  8.9 0.7 copy-done.1
  9.7 0.1 copy.44
  9.9 0.6 copy-done.2
  10.5 24.7 %all_gather.6 = bf16[2048,128]{1,0:T(8,128)(2,1)S(1)} all-gather(bf16[128,128]{1,0:T(8,128)(2,1)S(1)} %copy-done.2), channel_id=1, replica_groups=mesh['ctx'=16,'head'=2] {'ctx'}, dimensions={0}, use_global_device_ids=true | all-gather | bytes 557056 | tf_op jit(solution)/shard_map/all_gather | solution.py:26
  35.2 18.9 %all_gather.7 = bf16[2048,128]{1,0:T(8,128)(2,1)S(1)} all-gather(bf16[128,128]{1,0:T(8,128)(2,1)S(1)} %copy-done.3), channel_id=1, replica_groups=mesh['ctx'=16,'head'=2] {'ctx'}, dimensions={0}, use_global_device_ids=true | all-gather | bytes 557056 | tf_op jit(solution)/shard_map/all_gather | solution.py:27
  54.1 4.4 %while.31 = (s32[]{:T(128)}, f32[2,128]{1,0:T(2,128)S(1)}, f32[2,128]{1,0:T(2,128)S(1)}, f32[2,128]{1,0:T(2,128)S(1)}, s32[128]{0:T(128)S(1)}, /*index=5*/s32[20...) while((s32[]{:T(128)}, f32[2,128]{1,0:T(2,128)S(1)}, ...), condition=%wide.region_6.7_spmd.clone, body=%wide.region_2.6_spmd.clone.sunk | while | flops 68617984 | bytes 2260198 | solution.py:73
  54.2 0.2 compare_and_fusion.4
  54.4 0.3 fusion.70
  54.7 0.3 fusion.72
  55.0 0.1 fusion.73
  55.3 0.2 compare_and_fusion.4
  55.5 0.3 fusion.70
  55.8 0.3 fusion.72
  56.1 0.1 fusion.73
  56.4 0.2 compare_and_fusion.4
  56.6 0.3 fusion.70
  56.9 0.3 fusion.72
  57.2 0.1 fusion.73
  57.5 0.2 compare_and_fusion.4
  57.8 0.3 fusion.70
  58.0 0.3 fusion.72
  58.3 0.1 fusion.73
  58.5 12.2 %while.32 = (s32[]{:T(128)}, f32[128,2,128]{0,2,1:T(8,128)S(1)}, bf16[4,512,256]{2,1,0:T(8,128)(2,1)S(1)}, s32[4]{0:T(128)S(1)}, bf16[2048,128]{1,0:T(8,128)(2,1...) while((s32[]{:T(128)}, f32[128,2,128]{0,2,1:T(8,128)S(1)}, ...), condition=%wide.region_8.9_spmd.clone, body=%wide.region_7.8_spmd.clone.sunk | while | flops 169738240 | bytes 5258505 | solution.py:97
  58.5 0.6 dynamic_slice.100
  59.9 0.2 compare_and_fusion.5
  60.1 0.3 fusion.85
  60.4 0.2 convolution_bitcast_fusion.6
  60.7 0.2 fusion.86
  60.9 0.3 fusion.87
  61.1 0.2 fusion.88
  61.4 0.1 copy.58
  61.6 0.6 dynamic_slice.100
  63.0 0.2 compare_and_fusion.5
  63.2 0.3 fusion.85
  63.5 0.2 convolution_bitcast_fusion.6
  63.7 0.2 fusion.86
  63.9 0.3 fusion.87
  64.2 0.2 fusion.88
  64.5 0.1 copy.58
  64.6 0.6 dynamic_slice.100
  66.0 0.2 compare_and_fusion.5
  66.3 0.3 fusion.85
  66.5 0.2 convolution_bitcast_fusion.6
  66.8 0.2 fusion.86
  67.0 0.3 fusion.87
  67.3 0.2 fusion.88
  67.5 0.1 copy.58
  67.7 0.6 dynamic_slice.100
  69.1 0.2 compare_and_fusion.5
  69.3 0.3 fusion.85
  69.6 0.2 convolution_bitcast_fusion.6
  69.8 0.2 fusion.86
  70.0 0.3 fusion.87
  70.3 0.2 fusion.88
  70.6 0.1 copy.58
  70.8 27.8 %all_to_all.5 = bf16[16,128,256]{2,1,0:T(8,128)(2,1)S(1)} all-to-all(bf16[16,128,256]{2,1,0:T(8,128)(2,1)S(1)} %bitcast.119), channel_id=1, replica_groups=mesh['ctx'=16,'head'=2] {'ctx'}, dimensions={0} | all-to-all | bytes 2097152 | tf_op jit(solution)/shard_map/all_to_all | solution.py:105
  98.5 0.8 reduce_sum.48
  99.3 0.7 copy.53
  100.1 9.6 %reduce-scatter.2.cloned.1.call-done = bf16[64,256]{1,0:T(8,128)(2,1)} async-done(((bf16[128,256]{1,0:T(8,128)(2,1)}), bf16[64,256]{1,0:T(8,128)(2,1)}) %reduce-scatter.2.cloned.1.call-update) | async-done | bytes 32784 | tf_op jit(solution)/shard_map/reduce_scatter | solution.py:109
  109.7 1.3 %fusion.35 = (bf16[64,128]{1,0:T(8,128)(2,1)}, bf16[64,128]{1,0:T(8,128)(2,1)}) fusion(bf16[64,256]{1,0:T(8,128)(2,1)} %reduce-scatter.2.cloned.1.call-done), kind=kLoop, calls=%fused_computation.58 | loop fusion | bytes 65536 | tf_op jit(solution)/shard_map/slice | solution.py:113
  (66 shorter events, 2.3 us)
Async XLA Ops:
  7.2 102.5 %reduce-scatter.2.cloned.1.call-start = ((), (), s32[]{:S(2)}) async-start(), calls=%async_computation.2 | async-start | bytes 98304 | tf_op jit(solution)/shard_map/reduce_scatter | solution.py:109
  7.2 0.7 copy-start.5
  7.2 0.8 copy-start.4
  7.2 1.4 %copy-start = (bf16[128,256]{1,0:T(8,128)(2,1)S(1)}, bf16[128,256]{1,0:T(8,128)(2,1)}, u32[]{:S(2)}) copy-start(bf16[128,256]{1,0:T(8,128)(2,1)} %param.10) | copy-start | bytes 196612
  8.8 0.8 copy-start.1
  9.7 0.8 copy-start.2
  10.5 24.7 %copy-start.3 = (bf16[128,128]{1,0:T(8,128)(2,1)S(1)}, bf16[128,128]{1,0:T(8,128)(2,1)}, u32[]{:S(2)}) copy-start(bf16[128,128]{1,0:T(8,128)(2,1)} %param.12) | copy-start | bytes 98308
Sparse Core Ops, SparseCore 0:
  99.4 10.2 reduce-scatter.1
where the time goes:
time: 118 us
  blocking collectives  71.3 us (60%)
  between operations  14.2 us (12%)
  waiting for transfers between devices  9.63 us (8%)
  local copies, waits for them, and re-layouts  9.08 us (8%)
  matrix products  7 us (6%)
  other arithmetic  3.45 us (3%)
  loops' own time  3.17 us (3%)
    all_to_all x1, blocking collectives, local(): lax.all_to_all(terms.astype(jnp.bfloat16), 'ctx', split_axis=0, concat_ax...  27.8 us
    all_gather x1, blocking collectives, local(): lax.all_gather(key_rows, 'ctx', axis=0, tiled=True)  24.7 us
    all_gather x1, blocking collectives, local(): lax.all_gather(value_rows, 'ctx', axis=0, tiled=True)  18.9 us
    reduce_scatter x1, waiting for transfers between devices, local(): lax.psum_scatter(owned.astype(jnp.bfloat16), 'head', scatter_dimension=0,...  9.61 us
    another operation x1, loops' own time, local(): lax.scan(backward, jnp.zeros((local_rows, local_heads, head_dim), jnp.flo...  2.97 us
    unnamed x16, local copies, waits for them, and re-layouts  2.39 us
  transfers between devices with their start and end apart: 1, of which 1 were waited for; matrix products, arithmetic and copies ran while one was open for 1% of the time, Pallas kernels for 0%

commit v1 on v0

v1 whole, which is shorter than its diff:
```python
import functools

import jax
import jax.numpy as jnp
from jax import lax
from jax.experimental import pallas as pl
from jax.experimental.pallas import tpu as pltpu
from jax.sharding import PartitionSpec as P

masked_value = -1e30
log2_e = 1.4426950408889634
GROUP = 4

NT = (((1,), (1,)), ((), ()))
NN = (((1,), (0,)), ((), ()))
TN = (((0,), (0,)), ((), ()))


def dot(a, b, dims):
    return lax.dot_general(a, b, dims, preferred_element_type=jnp.float32)


def span_positions(order_ref, index, shape, dim):
    rows = shape[dim]
    half = rows // 2
    at = lax.broadcasted_iota(jnp.int32, shape, dim)
    first = order_ref[index, 0] * half
    second = order_ref[index, 1] * half - half
    return at + jnp.where(at < half, first, second)


def document_start(lengths_ref, pos):
    start = jnp.int32(0)
    result = jnp.zeros_like(pos)
    for d in range(lengths_ref.shape[0]):
        result = jnp.where(pos >= start, start, result)
        start = start + lengths_ref[d]
    return result


def key_positions(order_ref, index, chunks, rows):
    base, member = index // GROUP, index % GROUP
    return [
        span_positions(order_ref, (base ^ b) * GROUP + member, (rows, 1), 0) for b in range(chunks)
    ]


def allowed_keys(lengths_ref, order_ref, index, j, key_pos, rows):
    owner = (index // GROUP) * GROUP + ((index % GROUP) ^ j)
    pos = span_positions(order_ref, owner, (1, rows), 1)
    first = document_start(lengths_ref, pos)
    return (key_pos <= pos) & (key_pos >= first)


def stats_kernel(chunks, heads, index_ref, lengths_ref, order_ref, *refs):
    group, chunk, out_ref = refs[:GROUP], refs[GROUP : GROUP + chunks], refs[-1]
    rows, width = chunk[0].shape
    hd = width // 2
    index = index_ref[0]
    factor = hd ** (-0.5) * log2_e
    keys = jnp.concatenate([c[:, :hd] for c in chunk], axis=0)
    values = jnp.concatenate([c[:, hd:] for c in chunk], axis=0)
    key_pos = jnp.concatenate(key_positions(order_ref, index, chunks, rows), axis=0)
    for j in range(GROUP):
        allowed = allowed_keys(lengths_ref, order_ref, index, j, key_pos, rows)
        for h in range(heads):
            query = group[j][:, h * hd : (h + 1) * hd]
            grad = group[j][:, (heads + h) * hd : (heads + h + 1) * hd]
            scores = jnp.where(allowed, dot(keys, query, NT) * factor, masked_value)
            dprobs = dot(values, grad, NT)
            top = jnp.max(scores, axis=0, keepdims=True)
            expo = jnp.exp2(scores - top)
            at = pl.ds((j * heads + h) * rows, rows)
            out_ref[0:1, at] = top
            out_ref[1:2, at] = jnp.sum(expo, axis=0, keepdims=True)
            out_ref[2:3, at] = jnp.sum(expo * dprobs, axis=0, keepdims=True)


def backward_kernel(chunks, heads, shards, index_ref, lengths_ref, order_ref, *refs):
    group, chunk = refs[:GROUP], refs[GROUP : GROUP + chunks]
    stats = refs[GROUP + chunks : 2 * GROUP + chunks]
    dq_ref, dkv_ref, dv_total, dk_total = refs[2 * GROUP + chunks :]
    rows, width = chunk[0].shape
    hd = width // 2
    index, shard = index_ref[0], index_ref[1]
    scaling = hd ** (-0.5)
    factor = scaling * log2_e
    keys = jnp.concatenate([c[:, :hd] for c in chunk], axis=0)
    values = jnp.concatenate([c[:, hd:] for c in chunk], axis=0)
    key_pos = jnp.concatenate(key_positions(order_ref, index, chunks, rows), axis=0)
    for j in range(GROUP):
        allowed = allowed_keys(lengths_ref, order_ref, index, j, key_pos, rows)
        for h in range(heads):
            query = group[j][:, h * hd : (h + 1) * hd]
            grad = group[j][:, (heads + h) * hd : (heads + h + 1) * hd]
            parts = [
                s[0:3, pl.ds(((j ^ t) * heads + h) * rows, rows)] for t, s in enumerate(stats)
            ]
            top = functools.reduce(jnp.maximum, [p[0:1] for p in parts])
            weight = [jnp.exp2(p[0:1] - top) for p in parts]
            total = sum(w * p[1:2] for w, p in zip(weight, parts))
            delta = sum(w * p[2:3] for w, p in zip(weight, parts)) / total
            log_total = top + jnp.log2(total)
            scores = jnp.where(allowed, dot(keys, query, NT) * factor, masked_value)
            weights = jnp.exp2(scores - log_total)
            dprobs = dot(values, grad, NT)
            weights_low = weights.astype(jnp.bfloat16)
            dscores = (weights * (dprobs - delta)).astype(jnp.bfloat16)
            dv = dot(weights_low, grad, NN)
            dk = dot(dscores, query, NN)
            if j == 0 and h == 0:
                dv_total[...] = dv
                dk_total[...] = dk
            else:
                dv_total[...] += dv
                dk_total[...] += dk
            dq = dot(dscores, keys, TN) * scaling
            dq_ref[pl.ds(j * rows, rows), h * hd : (h + 1) * hd] = dq.astype(jnp.bfloat16)
    part = rows // shards
    for t in range(shards):
        owner = lax.rem(shard + t, shards)
        for b in range(chunks):
            at = pl.ds(pl.multiple_of(b * rows + owner * part, part), part)
            to = pl.ds(b * part, part)
            dkv_ref[t, to, :hd] = (dk_total[at, :] * scaling).astype(jnp.bfloat16)
            dkv_ref[t, to, hd:] = dv_total[at, :].astype(jnp.bfloat16)


def local(queries, key_rows, value_rows, out_grad, doc_lengths, span_order):
    rows = queries.shape[0]
    hd = key_rows.shape[1]
    heads = queries.shape[1] // hd
    ctx_size, shards = lax.axis_size("ctx"), lax.axis_size("head")
    chunks = ctx_size // GROUP
    part = rows // shards
    index = jnp.stack([lax.axis_index("ctx"), lax.axis_index("head")]).astype(jnp.int32)

    def swap(x, bits):
        return lax.ppermute(x, "ctx", [(i, i ^ bits) for i in range(ctx_size)])

    def turn(x, by):
        return lax.ppermute(x, "head", [(i, (i + by) % shards) for i in range(shards)])

    packed_kv = jnp.concatenate([key_rows, value_rows], axis=1)
    packed_qg = jnp.concatenate([queries, out_grad], axis=1)
    chunk = [packed_kv] + [swap(packed_kv, b * GROUP) for b in range(1, chunks)]
    across = swap(packed_qg, 2)
    group = [packed_qg, swap(packed_qg, 1), across, swap(across, 1)]

    smem = pl.BlockSpec(memory_space=pltpu.SMEM)
    vmem = pl.BlockSpec(memory_space=pltpu.VMEM)
    params = pltpu.CompilerParams(vmem_limit_bytes=48 * 1024 * 1024)
    stats = pl.pallas_call(
        functools.partial(stats_kernel, chunks, heads),
        out_shape=jax.ShapeDtypeStruct((4, GROUP * heads * rows), jnp.float32),
        in_specs=[smem] * 3 + [vmem] * (GROUP + chunks),
        out_specs=vmem,
        compiler_params=params,
        name="stats",
    )(index, doc_lengths, span_order, *group, *chunk)
    all_stats = [stats] + [swap(stats, t) for t in range(1, GROUP)]

    dq, dkv = pl.pallas_call(
        functools.partial(backward_kernel, chunks, heads, shards),
        out_shape=(
            jax.ShapeDtypeStruct((GROUP * rows, heads * hd), jnp.bfloat16),
            jax.ShapeDtypeStruct((shards, chunks * part, 2 * hd), jnp.bfloat16),
        ),
        in_specs=[smem] * 3 + [vmem] * (2 * GROUP + chunks),
        out_specs=(vmem, vmem),
        scratch_shapes=[pltpu.VMEM((chunks * rows, hd), jnp.float32)] * 2,
        compiler_params=params,
        name="backward",
    )(index, doc_lengths, span_order, *group, *chunk, *all_stats)

    owned = dkv[0].astype(jnp.float32)
    for t in range(1, shards):
        owned = owned + turn(dkv[t], t).astype(jnp.float32)
    owned = owned.astype(jnp.bfloat16)
    total = owned[:part].astype(jnp.float32)
    for b in range(1, chunks):
        total = total + swap(owned[b * part : (b + 1) * part], b * GROUP).astype(jnp.float32)
    key_grad = total[:, :hd].astype(jnp.bfloat16)
    value_grad = total[:, hd:].astype(jnp.bfloat16)

    pair = dq[: 2 * rows].astype(jnp.float32) + swap(dq[2 * rows :], 2).astype(jnp.float32)
    pair = pair.astype(jnp.bfloat16)
    query_grad = pair[:rows].astype(jnp.float32) + swap(pair[rows:], 1).astype(jnp.float32)
    return (query_grad.astype(jnp.bfloat16), key_grad, value_grad)


def solution(mesh):
    in_specs = (P("ctx", "head"), P("ctx", None), P("ctx", None), P("ctx", "head"), P(), P())
    out_specs = (P("ctx", "head"), P(("ctx", "head"), None), P(("ctx", "head"), None))
    return jax.shard_map(local, mesh=mesh, in_specs=in_specs, out_specs=out_specs, check_vma=False)
```

time: 118 us -> 41.9 us (0.36)
  blocking collectives: 71.3 us -> 0 us
  starting transfers between devices: 0.04 us -> 15.5 us
  between operations: 14.2 us -> 0.75 us
  waiting for transfers between devices: 9.63 us -> 17.4 us
  matrix products: 7 us -> 0 us
  local copies, waits for them, and re-layouts: 9.08 us -> 2.33 us
  Pallas kernels: 0 us -> 4.86 us
  loops' own time: 3.17 us -> 0 us
  other arithmetic: 3.45 us -> 0.81 us
    all_gather x2 -> x0, blocking collectives: 43.6 us -> none  [the longest x1 24.7 us: local(): lax.all_gather(key_rows, 'ctx', axis=0, tiled=True)]
    all_to_all x1 -> x0, blocking collectives: 27.8 us -> none  [local(): lax.all_to_all(terms.astype(jnp.bfloat16), 'ctx', split_axis=0, concat_ax...]
    ppermute x0 -> x15, waiting for transfers between devices: none -> 17.4 us  [the longest x14 14.7 us: swap(): return lax.ppermute(x, 'ctx', [(i, i ^ bits) for i in range(ctx_size)])]
    ppermute x0 -> x15, starting transfers between devices: none -> 15.5 us  [the longest x14 13.9 us: swap(): return lax.ppermute(x, 'ctx', [(i, i ^ bits) for i in range(ctx_size)])]
    reduce_scatter x1 -> x0, waiting for transfers between devices: 9.61 us -> none  [local(): lax.psum_scatter(owned.astype(jnp.bfloat16), 'head', scatter_dimension=0,...]
    dot_general x28 -> x0, matrix products: 7 us -> none  [the longest x8 2.13 us: products(): jnp.einsum('qhd,kd->hqk', query_heads, key_block, preferred_element_type=...]
    pallas_call x0 -> x2, Pallas kernels: none -> 4.86 us  [the longest x1 3.1 us: local(): pl.pallas_call(functools.partial(backward_kernel, chunks, heads, shards),...]
    dynamic_slice x22 -> x0, local copies, waits for them, and re-layouts: 3.71 us -> none  [the longest x4 2.35 us: local(): lax.scan(backward, jnp.zeros((local_rows, local_heads, head_dim), jnp.flo...]
  transfers between devices with their start and end apart: 1 -> 15, of which waited for: 1 -> 9; matrix products, arithmetic and copies ran while one was open for 1% -> 2% of each run, Pallas kernels for 0% -> 0%
where the time goes in v1:
time: 41.9 us; the launch traced here: 41.7 us
  waiting for transfers between devices  17.4 us (42%)
  starting transfers between devices  15.5 us (37%)
  Pallas kernels  4.86 us (12%)
  local copies, waits for them, and re-layouts  2.33 us (6%)
  other arithmetic  0.81 us (2%)
  between operations  0.75 us (2%)
    ppermute x14, waiting for transfers between devices, swap(): return lax.ppermute(x, 'ctx', [(i, i ^ bits) for i in range(ctx_size)])  14.7 us
    ppermute x14, starting transfers between devices, swap(): return lax.ppermute(x, 'ctx', [(i, i ^ bits) for i in range(ctx_size)])  13.9 us
    pallas_call x1, Pallas kernels, local(): pl.pallas_call(functools.partial(backward_kernel, chunks, heads, shards),...  3.1 us
    ppermute x1, waiting for transfers between devices, turn(): lax.ppermute(x, 'head', [(i, (i + by) % shards) for i in range(shards)])  2.68 us
    pallas_call x1, Pallas kernels, local(): pl.pallas_call(functools.partial(stats_kernel, chunks, heads), out_shape=...  1.76 us
    unnamed x13, local copies, waits for them, and re-layouts  1.66 us
    ppermute x1, starting transfers between devices, turn(): lax.ppermute(x, 'head', [(i, (i + by) % shards) for i in range(shards)])  1.58 us
  transfers between devices with their start and end apart: 15, of which 9 were waited for; matrix products, arithmetic and copies ran while one was open for 2% of the time, Pallas kernels for 0%

profile of v1, /device:TPU:0, one launch (start us, length us, event | category | flops | bytes accessed | tf_op | source)
XLA Modules:
  0.0 41.7 jit_solution(16347212445612282731)
XLA Ops:
  0.6 0.0 copy-start.1
  0.6 0.9 %constant_dynamic-update-slice_fusion.1 = bf16[128,512]{1,0:T(8,128)(2,1)S(1)} fusion(bf16[128,256]{1,0:T(8,128)(2,1)} %param.6), kind=kLoop, calls=%fused_computation.7 | loop fusion | bytes 131072
  1.5 0.0 copy-done.1
  1.5 0.0 copy-start.2
  1.5 0.0 copy-start.3
  1.6 3.0 %collective-permute-start.1 = (bf16[128,512]{1,0:T(8,128)(2,1)S(1)}, bf16[128,512]{1,0:T(8,128)(2,1)S(1)}, u32[]{:S(2)}, u32[]{:S(2)}) collective-permute-start(bf16[128,512]{1,0:T(8,128)(2,1)S(1)} %constant_dynamic-update-slice_fusion.refs_0_), channel_id=1, source_target_pairs={{0,4},{2,6},{4,0},{6,2},{8,12},{10,14},{12,8},{14,10},{16,20},{18,... | collective-permute-start | bytes 393224 | tf_op jit(solution)/shard_map/ppermute | solution.py:139
  4.6 0.0 collective-permute-start
  4.6 0.0 copy-done.2
  4.6 3.5 %collective-permute-done.1.refs_2_ = bf16[128,512]{1,0:T(8,128)(2,1)S(1)} collective-permute-done((bf16[128,512]{1,0:T(8,128)(2,1)S(1)}, bf16[128,512]{1,0:T(8,128)(2,1)S(1)}, u32[]{:S(2)}, u32[]{:S(2)}) %collective-permute-start.1) | collective-permute-done | bytes 131104 | tf_op jit(solution)/shard_map/ppermute | solution.py:139
  8.1 0.0 collective-permute-start.2
  8.1 0.0 copy-done.3
  8.1 3.9 %collective-permute-start.5 = (bf16[128,256]{1,0:T(8,128)(2,1)S(1)}, bf16[128,256]{1,0:T(8,128)(2,1)S(1)}, u32[]{:S(2)}, u32[]{:S(2)}) collective-permute-start(bf16[128,256]{1,0:T(8,128)(2,1)S(1)} %constant_dynamic-update-slice_fusion.2.refs_4_), channel_id=1, source_target_pairs={{0,24},{2,26},{4,28},{6,30},{8,16},{10,18},{12,20},{14,22},{16,8},... | collective-permute-start | bytes 196616 | tf_op jit(solution)/shard_map/ppermute | solution.py:139
  12.0 0.0 collective-permute-start.4
  12.0 0.6 %collective-permute-start.3 = (bf16[128,256]{1,0:T(8,128)(2,1)S(1)}, bf16[128,256]{1,0:T(8,128)(2,1)S(1)}, u32[]{:S(2)}, u32[]{:S(2)}) collective-permute-start(bf16[128,256]{1,0:T(8,128)(2,1)S(1)} %constant_dynamic-update-slice_fusion.2.refs_4_), channel_id=1, source_target_pairs={{0,8},{2,10},{4,12},{6,14},{8,0},{10,2},{12,4},{14,6},{16,24},{18,... | collective-permute-start | bytes 196616 | tf_op jit(solution)/shard_map/ppermute | solution.py:139
  12.6 0.0 copy-start.4
  12.6 0.7 %copy-done.4 = s32[16,2]{0,1:T(2,128)S(1)} copy-done((s32[16,2]{0,1:T(2,128)S(1)}, s32[16,2]{0,1:T(2,128)}, u32[]{:S(2)}) %copy-start.4) | copy-done | bytes 152
  13.3 0.1 copy.10.order_ref
  13.4 0.0 copy-start
  13.4 0.1 pad_add_fusion.index_ref
  13.5 1.5 %collective-permute-done.5.refs_7_ = bf16[128,256]{1,0:T(8,128)(2,1)S(1)} collective-permute-done((bf16[128,256]{1,0:T(8,128)(2,1)S(1)}, bf16[128,256]{1,0:T(8,128)(2,1)S(1)}, u32[]{:S(2)}, u32[]{:S(2)}) %collective-permute-start.5) | collective-permute-done | bytes 65568 | tf_op jit(solution)/shard_map/ppermute | solution.py:139
  14.9 3.2 %collective-permute-done.4.refs_6_ = bf16[128,256]{1,0:T(8,128)(2,1)S(1)} collective-permute-done((bf16[128,256]{1,0:T(8,128)(2,1)S(1)}, bf16[128,256]{1,0:T(8,128)(2,1)S(1)}, u32[]{:S(2)}, u32[]{:S(2)}) %collective-permute-start.4) | collective-permute-done | bytes 65568 | tf_op jit(solution)/shard_map/ppermute | solution.py:139
  18.1 0.0 collective-permute-done.3.refs_5_
  18.1 0.0 collective-permute-done.refs_1_
  18.1 0.0 collective-permute-done.2.refs_3_
  18.1 0.0 copy-done
  18.1 1.8 %stats.1.refs_8_ = f32[4,1024]{1,0:T(4,128)S(1)} custom-call(s32[2]{0:T(128)S(1)} %pad_add_fusion.index_ref, s32[8]{0:T(128)S(1)} %copy-done, s32[16,2]{1,0:T(8,128)S(1)} %copy.10.order_ref, bf16[128,512]{1,0:T(8,128)(2,1)S(1)} %constant_dynamic-update-slice_fusion.refs_0_, bf16[128,512]{1,0:T(8,128)(2,1)S(1)} %collective-permute-done.refs_1_, ...), custom_call_target="tpu_custom_call" | custom-call | tf_op jit(solution)/shard_map/stats/pallas_call | solution.py:153
  19.9 0.9 %collective-permute-start.8 = (f32[4,1024]{1,0:T(4,128)S(1)}, f32[4,1024]{1,0:T(4,128)S(1)}, u32[]{:S(2)}, u32[]{:S(2)}) collective-permute-start(f32[4,1024]{1,0:T(4,128)S(1)} %stats.1.refs_8_), channel_id=1, source_target_pairs={{0,6},{2,4},{4,2},{6,0},{8,14},{10,12},{12,10},{14,8},{16,22},{18,... | collective-permute-start | bytes 49160 | tf_op jit(solution)/shard_map/ppermute | solution.py:139
  20.8 0.7 %collective-permute-start.7 = (f32[4,1024]{1,0:T(4,128)S(1)}, f32[4,1024]{1,0:T(4,128)S(1)}, u32[]{:S(2)}, u32[]{:S(2)}) collective-permute-start(f32[4,1024]{1,0:T(4,128)S(1)} %stats.1.refs_8_), channel_id=1, source_target_pairs={{0,4},{2,6},{4,0},{6,2},{8,12},{10,14},{12,8},{14,10},{16,20},{18,... | collective-permute-start | bytes 49160 | tf_op jit(solution)/shard_map/ppermute | solution.py:139
  21.5 0.3 collective-permute-start.6
  21.8 1.4 %collective-permute-done.8.refs_11_ = f32[4,1024]{1,0:T(4,128)S(1)} collective-permute-done((f32[4,1024]{1,0:T(4,128)S(1)}, f32[4,1024]{1,0:T(4,128)S(1)}, u32[]{:S(2)}, u32[]{:S(2)}) %collective-permute-start.8) | collective-permute-done | bytes 16416 | tf_op jit(solution)/shard_map/ppermute | solution.py:139
  23.3 1.3 %collective-permute-done.7.refs_10_ = f32[4,1024]{1,0:T(4,128)S(1)} collective-permute-done((f32[4,1024]{1,0:T(4,128)S(1)}, f32[4,1024]{1,0:T(4,128)S(1)}, u32[]{:S(2)}, u32[]{:S(2)}) %collective-permute-start.7) | collective-permute-done | bytes 16416 | tf_op jit(solution)/shard_map/ppermute | solution.py:139
  24.5 0.0 collective-permute-done.6.refs_9_
  24.5 3.1 %backward.1 = (bf16[512,256]{1,0:T(8,128)(2,1)S(1)}, bf16[2,256,256]{2,1,0:T(8,128)(2,1)S(1)}) custom-call(s32[2]{0:T(128)S(1)} %pad_add_fusion.index_ref, s32[8]{0:T(128)S(1)} %copy-done, s32[16,2]{1,0:T(8,128)S(1)} %copy.10.order_ref, bf16[128,512]{1,0:T(8,128)(2,1)S(1)} %constant_dynamic-update-slice_fusion.refs_0_, ...), custom_call_target="tpu_custom_call" | custom-call | tf_op jit(solution)/shard_map/backward/pallas_call | solution.py:163
  27.7 1.6 %collective-permute-start.11 = (bf16[256,256]{1,0:T(8,128)(2,1)S(1)}, bf16[256,256]{1,0:T(8,128)(2,1)S(1)}, u32[]{:S(2)}, u32[]{:S(2)}) collective-permute-start(bf16[256,256]{1,0:T(8,128)(2,1)S(1)} %slice_bitcast_fusion), channel_id=1, source_target_pairs={{0,1},{1,0},{2,3},{3,2},{4,5},{5,4},{6,7},{7,6},{8,9},{9,8},{10,11... | collective-permute-start | bytes 393224 | tf_op jit(solution)/shard_map/ppermute | solution.py:142
  29.2 0.8 %collective-permute-start.9 = (bf16[256,256]{1,0:T(8,128)(2,1)S(1)}, bf16[256,256]{1,0:T(8,128)(2,1)S(1)}, u32[]{:S(2)}, u32[]{:S(2)}) collective-permute-start(bf16[256,256]{1,0:T(8,128)(2,1)S(1)} %slice.39), channel_id=1, source_target_pairs={{0,4},{2,6},{4,0},{6,2},{8,12},{10,14},{12,8},{14,10},{16,20},{18,... | collective-permute-start | bytes 393224 | tf_op jit(solution)/shard_map/ppermute | solution.py:139
  30.1 2.7 %collective-permute-done.11 = bf16[256,256]{1,0:T(8,128)(2,1)S(1)} collective-permute-done((bf16[256,256]{1,0:T(8,128)(2,1)S(1)}, bf16[256,256]{1,0:T(8,128)(2,1)S(1)}, u32[]{:S(2)}, u32[]{:S(2)}) %collective-permute-start.11) | collective-permute-done | bytes 131104 | tf_op jit(solution)/shard_map/ppermute | solution.py:142
  32.8 1.3 %collective-permute-start.12 = (bf16[64,256]{1,0:T(8,128)(2,1)S(1)}, bf16[64,256]{1,0:T(8,128)(2,1)S(1)}, u32[]{:S(2)}, u32[]{:S(2)}) collective-permute-start(bf16[64,256]{1,0:T(8,128)(2,1)S(1)} %get-tuple-element.7), channel_id=1, source_target_pairs={{0,8},{2,10},{4,12},{6,14},{8,0},{10,2},{12,4},{14,6},{16,24},{18,... | collective-permute-start | bytes 98312 | tf_op jit(solution)/shard_map/ppermute | solution.py:139
  34.1 1.4 %collective-permute-start.14 = (bf16[64,256]{1,0:T(8,128)(2,1)S(1)}, bf16[64,256]{1,0:T(8,128)(2,1)S(1)}, u32[]{:S(2)}, u32[]{:S(2)}) collective-permute-start(bf16[64,256]{1,0:T(8,128)(2,1)S(1)} %get-tuple-element.8), channel_id=1, source_target_pairs={{0,24},{2,26},{4,28},{6,30},{8,16},{10,18},{12,20},{14,22},{16,8},... | collective-permute-start | bytes 98312 | tf_op jit(solution)/shard_map/ppermute | solution.py:139
  35.6 0.8 %collective-permute-start.13 = (bf16[64,256]{1,0:T(8,128)(2,1)S(1)}, bf16[64,256]{1,0:T(8,128)(2,1)S(1)}, u32[]{:S(2)}, u32[]{:S(2)}) collective-permute-start(bf16[64,256]{1,0:T(8,128)(2,1)S(1)} %get-tuple-element.9), channel_id=1, source_target_pairs={{0,16},{2,18},{4,20},{6,22},{8,24},{10,26},{12,28},{14,30},{16,0},... | collective-permute-start | bytes 98312 | tf_op jit(solution)/shard_map/ppermute | solution.py:139
  36.4 0.0 collective-permute-done.9
  36.4 0.1 collective-permute-start.10
  36.5 0.3 collective-permute-done.12
  36.8 3.0 %collective-permute-done.14 = bf16[64,256]{1,0:T(8,128)(2,1)S(1)} collective-permute-done((bf16[64,256]{1,0:T(8,128)(2,1)S(1)}, bf16[64,256]{1,0:T(8,128)(2,1)S(1)}, u32[]{:S(2)}, u32[]{:S(2)}) %collective-permute-start.14) | collective-permute-done | bytes 32800 | tf_op jit(solution)/shard_map/ppermute | solution.py:139
  39.8 0.5 %collective-permute-done.13 = bf16[64,256]{1,0:T(8,128)(2,1)S(1)} collective-permute-done((bf16[64,256]{1,0:T(8,128)(2,1)S(1)}, bf16[64,256]{1,0:T(8,128)(2,1)S(1)}, u32[]{:S(2)}, u32[]{:S(2)}) %collective-permute-start.13) | collective-permute-done | bytes 32800 | tf_op jit(solution)/shard_map/ppermute | solution.py:139
  40.4 0.6 %fusion.2 = (bf16[64,128]{1,0:T(8,128)(2,1)}, bf16[64,128]{1,0:T(8,128)(2,1)}) fusion(bf16[64,256]{1,0:T(8,128)(2,1)S(1)} %add_convert_fusion.2), kind=kLoop, calls=%fused_computation.12 | loop fusion | bytes 65536 | tf_op jit(solution)/shard_map/slice | solution.py:184
  41.0 0.0 collective-permute-done.10
  41.0 0.6 %add_convert_fusion.1 = bf16[128,256]{1,0:T(8,128)(2,1)} fusion(bf16[128,256]{1,0:T(8,128)(2,1)S(1)} %collective-permute-done.10, bf16[256,256]{1,0:T(8,128)(2,1)S(1)} %add_convert_fusion), kind=kLoop, calls=%fused_computation.4 | loop fusion | flops 131072 | bytes 196608 | tf_op jit(solution)/shard_map/convert_element_type | solution.py:189
  (10 shorter events, 0.2 us)
Async XLA Ops:
  0.6 0.9 %copy-start.1 = (bf16[128,256]{1,0:T(8,128)(2,1)S(1)}, bf16[128,256]{1,0:T(8,128)(2,1)}, u32[]{:S(2)}) copy-start(bf16[128,256]{1,0:T(8,128)(2,1)} %param.9) | copy-start | bytes 196612
  1.5 3.0 %copy-start.2 = (bf16[128,128]{1,0:T(8,128)(2,1)S(1)}, bf16[128,128]{1,0:T(8,128)(2,1)}, u32[]{:S(2)}) copy-start(bf16[128,128]{1,0:T(8,128)(2,1)} %param.7) | copy-start | bytes 98308
  1.5 6.5 %copy-start.3 = (bf16[128,128]{1,0:T(8,128)(2,1)S(1)}, bf16[128,128]{1,0:T(8,128)(2,1)}, u32[]{:S(2)}) copy-start(bf16[128,128]{1,0:T(8,128)(2,1)} %param.8) | copy-start | bytes 98308
  1.6 6.5 %collective-permute-start.1 = (bf16[128,512]{1,0:T(8,128)(2,1)S(1)}, bf16[128,512]{1,0:T(8,128)(2,1)S(1)}, u32[]{:S(2)}, u32[]{:S(2)}) collective-permute-start(bf16[128,512]{1,0:T(8,128)(2,1)S(1)} %constant_dynamic-update-slice_fusion.refs_0_), channel_id=1, source_target_pairs={{0,4},{2,6},{4,0},{6,2},{8,12},{10,14},{12,8},{14,10},{16,20},{18,... | collective-permute-start | bytes 393224 | tf_op jit(solution)/shard_map/ppermute | solution.py:139
  4.6 13.6 %collective-permute-start = (bf16[128,512]{1,0:T(8,128)(2,1)S(1)}, bf16[128,512]{1,0:T(8,128)(2,1)S(1)}, u32[]{:S(2)}, u32[]{:S(2)}) collective-permute-start(bf16[128,512]{1,0:T(8,128)(2,1)S(1)} %constant_dynamic-update-slice_fusion.refs_0_), channel_id=1, source_target_pairs={{0,2},{2,0},{4,6},{6,4},{8,10},{10,8},{12,14},{14,12},{16,18},{18,... | collective-permute-start | bytes 393224 | tf_op jit(solution)/shard_map/ppermute | solution.py:139
  8.1 10.1 %collective-permute-start.2 = (bf16[128,512]{1,0:T(8,128)(2,1)S(1)}, bf16[128,512]{1,0:T(8,128)(2,1)S(1)}, u32[]{:S(2)}, u32[]{:S(2)}) collective-permute-start(bf16[128,512]{1,0:T(8,128)(2,1)S(1)} %collective-permute-done.1.refs_2_), channel_id=1, source_target_pairs={{0,2},{2,0},{4,6},{6,4},{8,10},{10,8},{12,14},{14,12},{16,18},{18,... | collective-permute-start | bytes 393224 | tf_op jit(solution)/shard_map/ppermute | solution.py:139
  8.1 6.9 %collective-permute-start.5 = (bf16[128,256]{1,0:T(8,128)(2,1)S(1)}, bf16[128,256]{1,0:T(8,128)(2,1)S(1)}, u32[]{:S(2)}, u32[]{:S(2)}) collective-permute-start(bf16[128,256]{1,0:T(8,128)(2,1)S(1)} %constant_dynamic-update-slice_fusion.2.refs_4_), channel_id=1, source_target_pairs={{0,24},{2,26},{4,28},{6,30},{8,16},{10,18},{12,20},{14,22},{16,8},... | collective-permute-start | bytes 196616 | tf_op jit(solution)/shard_map/ppermute | solution.py:139
  12.0 6.1 %collective-permute-start.4 = (bf16[128,256]{1,0:T(8,128)(2,1)S(1)}, bf16[128,256]{1,0:T(8,128)(2,1)S(1)}, u32[]{:S(2)}, u32[]{:S(2)}) collective-permute-start(bf16[128,256]{1,0:T(8,128)(2,1)S(1)} %constant_dynamic-update-slice_fusion.2.refs_4_), channel_id=1, source_target_pairs={{0,16},{2,18},{4,20},{6,22},{8,24},{10,26},{12,28},{14,30},{16,0},... | collective-permute-start | bytes 196616 | tf_op jit(solution)/shard_map/ppermute | solution.py:139
  12.0 6.1 %collective-permute-start.3 = (bf16[128,256]{1,0:T(8,128)(2,1)S(1)}, bf16[128,256]{1,0:T(8,128)(2,1)S(1)}, u32[]{:S(2)}, u32[]{:S(2)}) collective-permute-start(bf16[128,256]{1,0:T(8,128)(2,1)S(1)} %constant_dynamic-update-slice_fusion.2.refs_4_), channel_id=1, source_target_pairs={{0,8},{2,10},{4,12},{6,14},{8,0},{10,2},{12,4},{14,6},{16,24},{18,... | collective-permute-start | bytes 196616 | tf_op jit(solution)/shard_map/ppermute | solution.py:139
  12.6 0.7 %copy-start.4 = (s32[16,2]{0,1:T(2,128)S(1)}, s32[16,2]{0,1:T(2,128)}, u32[]{:S(2)}) copy-start(s32[16,2]{0,1:T(2,128)} %param.11) | copy-start | bytes 388
  13.4 4.7 %copy-start = (s32[8]{0:T(128)S(1)}, s32[8]{0:T(128)}, u32[]{:S(2)}) copy-start(s32[8]{0:T(128)} %lengths_ref.3) | copy-start | bytes 100
  19.9 3.4 %collective-permute-start.8 = (f32[4,1024]{1,0:T(4,128)S(1)}, f32[4,1024]{1,0:T(4,128)S(1)}, u32[]{:S(2)}, u32[]{:S(2)}) collective-permute-start(f32[4,1024]{1,0:T(4,128)S(1)} %stats.1.refs_8_), channel_id=1, source_target_pairs={{0,6},{2,4},{4,2},{6,0},{8,14},{10,12},{12,10},{14,8},{16,22},{18,... | collective-permute-start | bytes 49160 | tf_op jit(solution)/shard_map/ppermute | solution.py:139
  20.8 3.7 %collective-permute-start.7 = (f32[4,1024]{1,0:T(4,128)S(1)}, f32[4,1024]{1,0:T(4,128)S(1)}, u32[]{:S(2)}, u32[]{:S(2)}) collective-permute-start(f32[4,1024]{1,0:T(4,128)S(1)} %stats.1.refs_8_), channel_id=1, source_target_pairs={{0,4},{2,6},{4,0},{6,2},{8,12},{10,14},{12,8},{14,10},{16,20},{18,... | collective-permute-start | bytes 49160 | tf_op jit(solution)/shard_map/ppermute | solution.py:139
  21.5 3.0 %collective-permute-start.6 = (f32[4,1024]{1,0:T(4,128)S(1)}, f32[4,1024]{1,0:T(4,128)S(1)}, u32[]{:S(2)}, u32[]{:S(2)}) collective-permute-start(f32[4,1024]{1,0:T(4,128)S(1)} %stats.1.refs_8_), channel_id=1, source_target_pairs={{0,2},{2,0},{4,6},{6,4},{8,10},{10,8},{12,14},{14,12},{16,18},{18,... | collective-permute-start | bytes 49160 | tf_op jit(solution)/shard_map/ppermute | solution.py:139
  27.7 5.1 %collective-permute-start.11 = (bf16[256,256]{1,0:T(8,128)(2,1)S(1)}, bf16[256,256]{1,0:T(8,128)(2,1)S(1)}, u32[]{:S(2)}, u32[]{:S(2)}) collective-permute-start(bf16[256,256]{1,0:T(8,128)(2,1)S(1)} %slice_bitcast_fusion), channel_id=1, source_target_pairs={{0,1},{1,0},{2,3},{3,2},{4,5},{5,4},{6,7},{7,6},{8,9},{9,8},{10,11... | collective-permute-start | bytes 393224 | tf_op jit(solution)/shard_map/ppermute | solution.py:142
  29.2 7.1 %collective-permute-start.9 = (bf16[256,256]{1,0:T(8,128)(2,1)S(1)}, bf16[256,256]{1,0:T(8,128)(2,1)S(1)}, u32[]{:S(2)}, u32[]{:S(2)}) collective-permute-start(bf16[256,256]{1,0:T(8,128)(2,1)S(1)} %slice.39), channel_id=1, source_target_pairs={{0,4},{2,6},{4,0},{6,2},{8,12},{10,14},{12,8},{14,10},{16,20},{18,... | collective-permute-start | bytes 393224 | tf_op jit(solution)/shard_map/ppermute | solution.py:139
  32.8 4.0 %collective-permute-start.12 = (bf16[64,256]{1,0:T(8,128)(2,1)S(1)}, bf16[64,256]{1,0:T(8,128)(2,1)S(1)}, u32[]{:S(2)}, u32[]{:S(2)}) collective-permute-start(bf16[64,256]{1,0:T(8,128)(2,1)S(1)} %get-tuple-element.7), channel_id=1, source_target_pairs={{0,8},{2,10},{4,12},{6,14},{8,0},{10,2},{12,4},{14,6},{16,24},{18,... | collective-permute-start | bytes 98312 | tf_op jit(solution)/shard_map/ppermute | solution.py:139
  34.1 5.7 %collective-permute-start.14 = (bf16[64,256]{1,0:T(8,128)(2,1)S(1)}, bf16[64,256]{1,0:T(8,128)(2,1)S(1)}, u32[]{:S(2)}, u32[]{:S(2)}) collective-permute-start(bf16[64,256]{1,0:T(8,128)(2,1)S(1)} %get-tuple-element.8), channel_id=1, source_target_pairs={{0,24},{2,26},{4,28},{6,30},{8,16},{10,18},{12,20},{14,22},{16,8},... | collective-permute-start | bytes 98312 | tf_op jit(solution)/shard_map/ppermute | solution.py:139
  35.6 4.8 %collective-permute-start.13 = (bf16[64,256]{1,0:T(8,128)(2,1)S(1)}, bf16[64,256]{1,0:T(8,128)(2,1)S(1)}, u32[]{:S(2)}, u32[]{:S(2)}) collective-permute-start(bf16[64,256]{1,0:T(8,128)(2,1)S(1)} %get-tuple-element.9), channel_id=1, source_target_pairs={{0,16},{2,18},{4,20},{6,22},{8,24},{10,26},{12,28},{14,30},{16,0},... | collective-permute-start | bytes 98312 | tf_op jit(solution)/shard_map/ppermute | solution.py:139
  36.4 4.6 %collective-permute-start.10 = (bf16[128,256]{1,0:T(8,128)(2,1)S(1)}, bf16[128,256]{1,0:T(8,128)(2,1)S(1)}, u32[]{:S(2)}, u32[]{:S(2)}) collective-permute-start(bf16[128,256]{1,0:T(8,128)(2,1)S(1)} %slice.51), channel_id=1, source_target_pairs={{0,2},{2,0},{4,6},{6,4},{8,10},{10,8},{12,14},{14,12},{16,18},{18,... | collective-permute-start | bytes 196616 | tf_op jit(solution)/shard_map/ppermute | solution.py:139

commit v2 on v1

--- a/solution.py
+++ b/solution.py
@@ -144,8 +144,7 @@
     packed_kv = jnp.concatenate([key_rows, value_rows], axis=1)
     packed_qg = jnp.concatenate([queries, out_grad], axis=1)
     chunk = [packed_kv] + [swap(packed_kv, b * GROUP) for b in range(1, chunks)]
-    across = swap(packed_qg, 2)
-    group = [packed_qg, swap(packed_qg, 1), across, swap(across, 1)]
+    group = [packed_qg] + [swap(packed_qg, t) for t in range(1, GROUP)]
 
     smem = pl.BlockSpec(memory_space=pltpu.SMEM)
     vmem = pl.BlockSpec(memory_space=pltpu.VMEM)

time: 41.9 us -> 39 us (0.931)
  waiting for transfers between devices: 17.4 us -> 13.7 us
  starting transfers between devices: 15.5 us -> 16.4 us
    ppermute x14, waiting for transfers between devices: 14.7 us -> 11.3 us  [swap(): return lax.ppermute(x, 'ctx', [(i, i ^ bits) for i in range(ctx_size)])]
    ppermute x14, starting transfers between devices: 13.9 us -> 14.9 us  [swap(): return lax.ppermute(x, 'ctx', [(i, i ^ bits) for i in range(ctx_size)])]
where the time goes in v2:
time: 39 us; the launch traced here: 38.9 us
  starting transfers between devices  16.4 us (42%)
  waiting for transfers between devices  13.7 us (35%)
  Pallas kernels  4.86 us (12%)
  local copies, waits for them, and re-layouts  2.26 us (6%)
  other arithmetic  0.81 us (2%)
  between operations  0.76 us (2%)
    ppermute x14, starting transfers between devices, swap(): return lax.ppermute(x, 'ctx', [(i, i ^ bits) for i in range(ctx_size)])  14.9 us
    ppermute x14, waiting for transfers between devices, swap(): return lax.ppermute(x, 'ctx', [(i, i ^ bits) for i in range(ctx_size)])  11.3 us
    pallas_call x1, Pallas kernels, local(): pl.pallas_call(functools.partial(backward_kernel, chunks, heads, shards),...  3.11 us
    ppermute x1, waiting for transfers between devices, turn(): lax.ppermute(x, 'head', [(i, (i + by) % shards) for i in range(shards)])  2.4 us
    pallas_call x1, Pallas kernels, local(): pl.pallas_call(functools.partial(stats_kernel, chunks, heads), out_shape=...  1.75 us
    ppermute x1, starting transfers between devices, turn(): lax.ppermute(x, 'head', [(i, (i + by) % shards) for i in range(shards)])  1.58 us
    unnamed x13, local copies, waits for them, and re-layouts  1.58 us
  transfers between devices with their start and end apart: 15, of which 9 were waited for; matrix products, arithmetic and copies ran while one was open for 2% of the time, Pallas kernels for 0%

profile of v2, /device:TPU:0, one launch (start us, length us, event | category | flops | bytes accessed | tf_op | source)
XLA Modules:
  0.0 38.9 jit_solution(7139559154657694592)
XLA Ops:
  0.6 0.0 copy-start.3
  0.6 0.0 copy-start.1
  0.7 0.8 %constant_dynamic-update-slice_fusion.3 = bf16[128,256]{1,0:T(8,128)(2,1)S(1)} fusion(bf16[128,128]{1,0:T(8,128)(2,1)} %param.7), kind=kLoop, calls=%fused_computation.9 | loop fusion | bytes 65536
  1.4 0.0 copy-done.3
  1.5 0.0 copy-start.2
  1.5 5.1 %collective-permute-start.5 = (bf16[128,256]{1,0:T(8,128)(2,1)S(1)}, bf16[128,256]{1,0:T(8,128)(2,1)S(1)}, u32[]{:S(2)}, u32[]{:S(2)}) collective-permute-start(bf16[128,256]{1,0:T(8,128)(2,1)S(1)} %constant_dynamic-update-slice_fusion.2.refs_4_), channel_id=1, source_target_pairs={{0,24},{2,26},{4,28},{6,30},{8,16},{10,18},{12,20},{14,22},{16,8},... | collective-permute-start | bytes 196616 | tf_op jit(solution)/shard_map/ppermute | solution.py:139
  6.6 0.0 copy-done.1
  6.6 0.0 copy-done.2
  6.6 0.7 %collective-permute-start.2 = (bf16[128,512]{1,0:T(8,128)(2,1)S(1)}, bf16[128,512]{1,0:T(8,128)(2,1)S(1)}, u32[]{:S(2)}, u32[]{:S(2)}) collective-permute-start(bf16[128,512]{1,0:T(8,128)(2,1)S(1)} %constant_dynamic-update-slice_fusion.refs_0_), channel_id=1, source_target_pairs={{0,6},{2,4},{4,2},{6,0},{8,14},{10,12},{12,10},{14,8},{16,22},{18,... | collective-permute-start | bytes 393224 | tf_op jit(solution)/shard_map/ppermute | solution.py:139
  7.4 0.9 %collective-permute-start.1 = (bf16[128,512]{1,0:T(8,128)(2,1)S(1)}, bf16[128,512]{1,0:T(8,128)(2,1)S(1)}, u32[]{:S(2)}, u32[]{:S(2)}) collective-permute-start(bf16[128,512]{1,0:T(8,128)(2,1)S(1)} %constant_dynamic-update-slice_fusion.refs_0_), channel_id=1, source_target_pairs={{0,4},{2,6},{4,0},{6,2},{8,12},{10,14},{12,8},{14,10},{16,20},{18,... | collective-permute-start | bytes 393224 | tf_op jit(solution)/shard_map/ppermute | solution.py:139
  8.3 0.3 collective-permute-start
  8.6 0.0 collective-permute-start.4
  8.6 0.0 copy-start.4
  8.6 0.7 %copy-done.4 = s32[16,2]{0,1:T(2,128)S(1)} copy-done((s32[16,2]{0,1:T(2,128)S(1)}, s32[16,2]{0,1:T(2,128)}, u32[]{:S(2)}) %copy-start.4) | copy-done | bytes 152
  9.2 0.1 copy.10.order_ref
  9.3 0.0 collective-permute-done.5.refs_7_
  9.3 1.2 %collective-permute-start.3 = (bf16[128,256]{1,0:T(8,128)(2,1)S(1)}, bf16[128,256]{1,0:T(8,128)(2,1)S(1)}, u32[]{:S(2)}, u32[]{:S(2)}) collective-permute-start(bf16[128,256]{1,0:T(8,128)(2,1)S(1)} %constant_dynamic-update-slice_fusion.2.refs_4_), channel_id=1, source_target_pairs={{0,8},{2,10},{4,12},{6,14},{8,0},{10,2},{12,4},{14,6},{16,24},{18,... | collective-permute-start | bytes 196616 | tf_op jit(solution)/shard_map/ppermute | solution.py:139
  10.6 0.0 copy-start
  10.6 0.1 pad_add_fusion.index_ref
  10.6 3.6 %collective-permute-done.4.refs_6_ = bf16[128,256]{1,0:T(8,128)(2,1)S(1)} collective-permute-done((bf16[128,256]{1,0:T(8,128)(2,1)S(1)}, bf16[128,256]{1,0:T(8,128)(2,1)S(1)}, u32[]{:S(2)}, u32[]{:S(2)}) %collective-permute-start.4) | collective-permute-done | bytes 65568 | tf_op jit(solution)/shard_map/ppermute | solution.py:139
  14.2 0.7 %collective-permute-done.3.refs_5_ = bf16[128,256]{1,0:T(8,128)(2,1)S(1)} collective-permute-done((bf16[128,256]{1,0:T(8,128)(2,1)S(1)}, bf16[128,256]{1,0:T(8,128)(2,1)S(1)}, u32[]{:S(2)}, u32[]{:S(2)}) %collective-permute-start.3) | collective-permute-done | bytes 65568 | tf_op jit(solution)/shard_map/ppermute | solution.py:139
  15.0 0.0 collective-permute-done.2.refs_3_
  15.0 0.3 collective-permute-done.1.refs_2_
  15.3 0.0 collective-permute-done.refs_1_
  15.3 0.0 copy-done
  15.3 1.7 %stats.1.refs_8_ = f32[4,1024]{1,0:T(4,128)S(1)} custom-call(s32[2]{0:T(128)S(1)} %pad_add_fusion.index_ref, s32[8]{0:T(128)S(1)} %copy-done, s32[16,2]{1,0:T(8,128)S(1)} %copy.10.order_ref, bf16[128,512]{1,0:T(8,128)(2,1)S(1)} %constant_dynamic-update-slice_fusion.refs_0_, bf16[128,512]{1,0:T(8,128)(2,1)S(1)} %collective-permute-done.refs_1_, ...), custom_call_target="tpu_custom_call" | custom-call | tf_op jit(solution)/shard_map/stats/pallas_call | solution.py:152
  17.1 0.8 %collective-permute-start.8 = (f32[4,1024]{1,0:T(4,128)S(1)}, f32[4,1024]{1,0:T(4,128)S(1)}, u32[]{:S(2)}, u32[]{:S(2)}) collective-permute-start(f32[4,1024]{1,0:T(4,128)S(1)} %stats.1.refs_8_), channel_id=1, source_target_pairs={{0,6},{2,4},{4,2},{6,0},{8,14},{10,12},{12,10},{14,8},{16,22},{18,... | collective-permute-start | bytes 49160 | tf_op jit(solution)/shard_map/ppermute | solution.py:139
  17.9 1.0 %collective-permute-start.7 = (f32[4,1024]{1,0:T(4,128)S(1)}, f32[4,1024]{1,0:T(4,128)S(1)}, u32[]{:S(2)}, u32[]{:S(2)}) collective-permute-start(f32[4,1024]{1,0:T(4,128)S(1)} %stats.1.refs_8_), channel_id=1, source_target_pairs={{0,4},{2,6},{4,0},{6,2},{8,12},{10,14},{12,8},{14,10},{16,20},{18,... | collective-permute-start | bytes 49160 | tf_op jit(solution)/shard_map/ppermute | solution.py:139
  18.8 0.2 collective-permute-start.6
  19.0 1.3 %collective-permute-done.8.refs_11_ = f32[4,1024]{1,0:T(4,128)S(1)} collective-permute-done((f32[4,1024]{1,0:T(4,128)S(1)}, f32[4,1024]{1,0:T(4,128)S(1)}, u32[]{:S(2)}, u32[]{:S(2)}) %collective-permute-start.8) | collective-permute-done | bytes 16416 | tf_op jit(solution)/shard_map/ppermute | solution.py:139
  20.3 1.3 %collective-permute-done.7.refs_10_ = f32[4,1024]{1,0:T(4,128)S(1)} collective-permute-done((f32[4,1024]{1,0:T(4,128)S(1)}, f32[4,1024]{1,0:T(4,128)S(1)}, u32[]{:S(2)}, u32[]{:S(2)}) %collective-permute-start.7) | collective-permute-done | bytes 16416 | tf_op jit(solution)/shard_map/ppermute | solution.py:139
  21.6 0.0 collective-permute-done.6.refs_9_
  21.6 3.1 %backward.1 = (bf16[512,256]{1,0:T(8,128)(2,1)S(1)}, bf16[2,256,256]{2,1,0:T(8,128)(2,1)S(1)}) custom-call(s32[2]{0:T(128)S(1)} %pad_add_fusion.index_ref, s32[8]{0:T(128)S(1)} %copy-done, s32[16,2]{1,0:T(8,128)S(1)} %copy.10.order_ref, bf16[128,512]{1,0:T(8,128)(2,1)S(1)} %constant_dynamic-update-slice_fusion.refs_0_, ...), custom_call_target="tpu_custom_call" | custom-call | tf_op jit(solution)/shard_map/backward/pallas_call | solution.py:162
  24.7 1.6 %collective-permute-start.11 = (bf16[256,256]{1,0:T(8,128)(2,1)S(1)}, bf16[256,256]{1,0:T(8,128)(2,1)S(1)}, u32[]{:S(2)}, u32[]{:S(2)}) collective-permute-start(bf16[256,256]{1,0:T(8,128)(2,1)S(1)} %slice_bitcast_fusion), channel_id=1, source_target_pairs={{0,1},{1,0},{2,3},{3,2},{4,5},{5,4},{6,7},{7,6},{8,9},{9,8},{10,11... | collective-permute-start | bytes 393224 | tf_op jit(solution)/shard_map/ppermute | solution.py:142
  26.3 1.0 %collective-permute-start.9 = (bf16[256,256]{1,0:T(8,128)(2,1)S(1)}, bf16[256,256]{1,0:T(8,128)(2,1)S(1)}, u32[]{:S(2)}, u32[]{:S(2)}) collective-permute-start(bf16[256,256]{1,0:T(8,128)(2,1)S(1)} %slice.39), channel_id=1, source_target_pairs={{0,4},{2,6},{4,0},{6,2},{8,12},{10,14},{12,8},{14,10},{16,20},{18,... | collective-permute-start | bytes 393224 | tf_op jit(solution)/shard_map/ppermute | solution.py:139
  27.4 2.4 %collective-permute-done.11 = bf16[256,256]{1,0:T(8,128)(2,1)S(1)} collective-permute-done((bf16[256,256]{1,0:T(8,128)(2,1)S(1)}, bf16[256,256]{1,0:T(8,128)(2,1)S(1)}, u32[]{:S(2)}, u32[]{:S(2)}) %collective-permute-start.11) | collective-permute-done | bytes 131104 | tf_op jit(solution)/shard_map/ppermute | solution.py:142
  29.8 0.1 collective-permute-start.12
  29.9 2.8 %collective-permute-start.14 = (bf16[64,256]{1,0:T(8,128)(2,1)S(1)}, bf16[64,256]{1,0:T(8,128)(2,1)S(1)}, u32[]{:S(2)}, u32[]{:S(2)}) collective-permute-start(bf16[64,256]{1,0:T(8,128)(2,1)S(1)} %get-tuple-element.8), channel_id=1, source_target_pairs={{0,24},{2,26},{4,28},{6,30},{8,16},{10,18},{12,20},{14,22},{16,8},... | collective-permute-start | bytes 98312 | tf_op jit(solution)/shard_map/ppermute | solution.py:139
  32.7 0.6 %collective-permute-start.13 = (bf16[64,256]{1,0:T(8,128)(2,1)S(1)}, bf16[64,256]{1,0:T(8,128)(2,1)S(1)}, u32[]{:S(2)}, u32[]{:S(2)}) collective-permute-start(bf16[64,256]{1,0:T(8,128)(2,1)S(1)} %get-tuple-element.9), channel_id=1, source_target_pairs={{0,16},{2,18},{4,20},{6,22},{8,24},{10,26},{12,28},{14,30},{16,0},... | collective-permute-start | bytes 98312 | tf_op jit(solution)/shard_map/ppermute | solution.py:139
  33.4 0.0 collective-permute-done.9
  33.4 0.1 collective-permute-start.10
  33.5 0.4 %collective-permute-done.12 = bf16[64,256]{1,0:T(8,128)(2,1)S(1)} collective-permute-done((bf16[64,256]{1,0:T(8,128)(2,1)S(1)}, bf16[64,256]{1,0:T(8,128)(2,1)S(1)}, u32[]{:S(2)}, u32[]{:S(2)}) %collective-permute-start.12) | collective-permute-done | bytes 32800 | tf_op jit(solution)/shard_map/ppermute | solution.py:139
  33.9 1.8 %collective-permute-done.14 = bf16[64,256]{1,0:T(8,128)(2,1)S(1)} collective-permute-done((bf16[64,256]{1,0:T(8,128)(2,1)S(1)}, bf16[64,256]{1,0:T(8,128)(2,1)S(1)}, u32[]{:S(2)}, u32[]{:S(2)}) %collective-permute-start.14) | collective-permute-done | bytes 32800 | tf_op jit(solution)/shard_map/ppermute | solution.py:139
  35.7 1.9 %collective-permute-done.13 = bf16[64,256]{1,0:T(8,128)(2,1)S(1)} collective-permute-done((bf16[64,256]{1,0:T(8,128)(2,1)S(1)}, bf16[64,256]{1,0:T(8,128)(2,1)S(1)}, u32[]{:S(2)}, u32[]{:S(2)}) %collective-permute-start.13) | collective-permute-done | bytes 32800 | tf_op jit(solution)/shard_map/ppermute | solution.py:139
  37.6 0.6 %fusion.2 = (bf16[64,128]{1,0:T(8,128)(2,1)}, bf16[64,128]{1,0:T(8,128)(2,1)}) fusion(bf16[64,256]{1,0:T(8,128)(2,1)S(1)} %add_convert_fusion.2), kind=kLoop, calls=%fused_computation.12 | loop fusion | bytes 65536 | tf_op jit(solution)/shard_map/slice | solution.py:183
  38.2 0.0 collective-permute-done.10
  38.2 0.6 %add_convert_fusion.1 = bf16[128,256]{1,0:T(8,128)(2,1)} fusion(bf16[128,256]{1,0:T(8,128)(2,1)S(1)} %collective-permute-done.10, bf16[256,256]{1,0:T(8,128)(2,1)S(1)} %add_convert_fusion), kind=kLoop, calls=%fused_computation.4 | loop fusion | flops 131072 | bytes 196608 | tf_op jit(solution)/shard_map/convert_element_type | solution.py:188
  (10 shorter events, 0.2 us)
Async XLA Ops:
  0.6 0.8 %copy-start.3 = (bf16[128,128]{1,0:T(8,128)(2,1)S(1)}, bf16[128,128]{1,0:T(8,128)(2,1)}, u32[]{:S(2)}) copy-start(bf16[128,128]{1,0:T(8,128)(2,1)} %param.8) | copy-start | bytes 98308
  0.6 6.0 %copy-start.1 = (bf16[128,256]{1,0:T(8,128)(2,1)S(1)}, bf16[128,256]{1,0:T(8,128)(2,1)}, u32[]{:S(2)}) copy-start(bf16[128,256]{1,0:T(8,128)(2,1)} %param.6) | copy-start | bytes 196612
  1.5 5.1 %copy-start.2 = (bf16[128,256]{1,0:T(8,128)(2,1)S(1)}, bf16[128,256]{1,0:T(8,128)(2,1)}, u32[]{:S(2)}) copy-start(bf16[128,256]{1,0:T(8,128)(2,1)} %param.9) | copy-start | bytes 196612
  1.5 7.8 %collective-permute-start.5 = (bf16[128,256]{1,0:T(8,128)(2,1)S(1)}, bf16[128,256]{1,0:T(8,128)(2,1)S(1)}, u32[]{:S(2)}, u32[]{:S(2)}) collective-permute-start(bf16[128,256]{1,0:T(8,128)(2,1)S(1)} %constant_dynamic-update-slice_fusion.2.refs_4_), channel_id=1, source_target_pairs={{0,24},{2,26},{4,28},{6,30},{8,16},{10,18},{12,20},{14,22},{16,8},... | collective-permute-start | bytes 196616 | tf_op jit(solution)/shard_map/ppermute | solution.py:139
  6.6 8.3 %collective-permute-start.2 = (bf16[128,512]{1,0:T(8,128)(2,1)S(1)}, bf16[128,512]{1,0:T(8,128)(2,1)S(1)}, u32[]{:S(2)}, u32[]{:S(2)}) collective-permute-start(bf16[128,512]{1,0:T(8,128)(2,1)S(1)} %constant_dynamic-update-slice_fusion.refs_0_), channel_id=1, source_target_pairs={{0,6},{2,4},{4,2},{6,0},{8,14},{10,12},{12,10},{14,8},{16,22},{18,... | collective-permute-start | bytes 393224 | tf_op jit(solution)/shard_map/ppermute | solution.py:139
  7.4 8.0 %collective-permute-start.1 = (bf16[128,512]{1,0:T(8,128)(2,1)S(1)}, bf16[128,512]{1,0:T(8,128)(2,1)S(1)}, u32[]{:S(2)}, u32[]{:S(2)}) collective-permute-start(bf16[128,512]{1,0:T(8,128)(2,1)S(1)} %constant_dynamic-update-slice_fusion.refs_0_), channel_id=1, source_target_pairs={{0,4},{2,6},{4,0},{6,2},{8,12},{10,14},{12,8},{14,10},{16,20},{18,... | collective-permute-start | bytes 393224 | tf_op jit(solution)/shard_map/ppermute | solution.py:139
  8.3 7.0 %collective-permute-start = (bf16[128,512]{1,0:T(8,128)(2,1)S(1)}, bf16[128,512]{1,0:T(8,128)(2,1)S(1)}, u32[]{:S(2)}, u32[]{:S(2)}) collective-permute-start(bf16[128,512]{1,0:T(8,128)(2,1)S(1)} %constant_dynamic-update-slice_fusion.refs_0_), channel_id=1, source_target_pairs={{0,2},{2,0},{4,6},{6,4},{8,10},{10,8},{12,14},{14,12},{16,18},{18,... | collective-permute-start | bytes 393224 | tf_op jit(solution)/shard_map/ppermute | solution.py:139
  8.6 5.7 %collective-permute-start.4 = (bf16[128,256]{1,0:T(8,128)(2,1)S(1)}, bf16[128,256]{1,0:T(8,128)(2,1)S(1)}, u32[]{:S(2)}, u32[]{:S(2)}) collective-permute-start(bf16[128,256]{1,0:T(8,128)(2,1)S(1)} %constant_dynamic-update-slice_fusion.2.refs_4_), channel_id=1, source_target_pairs={{0,16},{2,18},{4,20},{6,22},{8,24},{10,26},{12,28},{14,30},{16,0},... | collective-permute-start | bytes 196616 | tf_op jit(solution)/shard_map/ppermute | solution.py:139
  8.6 0.7 %copy-start.4 = (s32[16,2]{0,1:T(2,128)S(1)}, s32[16,2]{0,1:T(2,128)}, u32[]{:S(2)}) copy-start(s32[16,2]{0,1:T(2,128)} %param.11) | copy-start | bytes 388
  9.3 5.6 %collective-permute-start.3 = (bf16[128,256]{1,0:T(8,128)(2,1)S(1)}, bf16[128,256]{1,0:T(8,128)(2,1)S(1)}, u32[]{:S(2)}, u32[]{:S(2)}) collective-permute-start(bf16[128,256]{1,0:T(8,128)(2,1)S(1)} %constant_dynamic-update-slice_fusion.2.refs_4_), channel_id=1, source_target_pairs={{0,8},{2,10},{4,12},{6,14},{8,0},{10,2},{12,4},{14,6},{16,24},{18,... | collective-permute-start | bytes 196616 | tf_op jit(solution)/shard_map/ppermute | solution.py:139
  10.6 4.7 %copy-start = (s32[8]{0:T(128)S(1)}, s32[8]{0:T(128)}, u32[]{:S(2)}) copy-start(s32[8]{0:T(128)} %lengths_ref.3) | copy-start | bytes 100
  17.1 3.2 %collective-permute-start.8 = (f32[4,1024]{1,0:T(4,128)S(1)}, f32[4,1024]{1,0:T(4,128)S(1)}, u32[]{:S(2)}, u32[]{:S(2)}) collective-permute-start(f32[4,1024]{1,0:T(4,128)S(1)} %stats.1.refs_8_), channel_id=1, source_target_pairs={{0,6},{2,4},{4,2},{6,0},{8,14},{10,12},{12,10},{14,8},{16,22},{18,... | collective-permute-start | bytes 49160 | tf_op jit(solution)/shard_map/ppermute | solution.py:139
  17.9 3.7 %collective-permute-start.7 = (f32[4,1024]{1,0:T(4,128)S(1)}, f32[4,1024]{1,0:T(4,128)S(1)}, u32[]{:S(2)}, u32[]{:S(2)}) collective-permute-start(f32[4,1024]{1,0:T(4,128)S(1)} %stats.1.refs_8_), channel_id=1, source_target_pairs={{0,4},{2,6},{4,0},{6,2},{8,12},{10,14},{12,8},{14,10},{16,20},{18,... | collective-permute-start | bytes 49160 | tf_op jit(solution)/shard_map/ppermute | solution.py:139
  18.8 2.8 %collective-permute-start.6 = (f32[4,1024]{1,0:T(4,128)S(1)}, f32[4,1024]{1,0:T(4,128)S(1)}, u32[]{:S(2)}, u32[]{:S(2)}) collective-permute-start(f32[4,1024]{1,0:T(4,128)S(1)} %stats.1.refs_8_), channel_id=1, source_target_pairs={{0,2},{2,0},{4,6},{6,4},{8,10},{10,8},{12,14},{14,12},{16,18},{18,... | collective-permute-start | bytes 49160 | tf_op jit(solution)/shard_map/ppermute | solution.py:139
  24.7 5.0 %collective-permute-start.11 = (bf16[256,256]{1,0:T(8,128)(2,1)S(1)}, bf16[256,256]{1,0:T(8,128)(2,1)S(1)}, u32[]{:S(2)}, u32[]{:S(2)}) collective-permute-start(bf16[256,256]{1,0:T(8,128)(2,1)S(1)} %slice_bitcast_fusion), channel_id=1, source_target_pairs={{0,1},{1,0},{2,3},{3,2},{4,5},{5,4},{6,7},{7,6},{8,9},{9,8},{10,11... | collective-permute-start | bytes 393224 | tf_op jit(solution)/shard_map/ppermute | solution.py:142
  26.3 7.0 %collective-permute-start.9 = (bf16[256,256]{1,0:T(8,128)(2,1)S(1)}, bf16[256,256]{1,0:T(8,128)(2,1)S(1)}, u32[]{:S(2)}, u32[]{:S(2)}) collective-permute-start(bf16[256,256]{1,0:T(8,128)(2,1)S(1)} %slice.39), channel_id=1, source_target_pairs={{0,4},{2,6},{4,0},{6,2},{8,12},{10,14},{12,8},{14,10},{16,20},{18,... | collective-permute-start | bytes 393224 | tf_op jit(solution)/shard_map/ppermute | solution.py:139
  29.8 4.1 %collective-permute-start.12 = (bf16[64,256]{1,0:T(8,128)(2,1)S(1)}, bf16[64,256]{1,0:T(8,128)(2,1)S(1)}, u32[]{:S(2)}, u32[]{:S(2)}) collective-permute-start(bf16[64,256]{1,0:T(8,128)(2,1)S(1)} %get-tuple-element.7), channel_id=1, source_target_pairs={{0,8},{2,10},{4,12},{6,14},{8,0},{10,2},{12,4},{14,6},{16,24},{18,... | collective-permute-start | bytes 98312 | tf_op jit(solution)/shard_map/ppermute | solution.py:139
  29.9 5.8 %collective-permute-start.14 = (bf16[64,256]{1,0:T(8,128)(2,1)S(1)}, bf16[64,256]{1,0:T(8,128)(2,1)S(1)}, u32[]{:S(2)}, u32[]{:S(2)}) collective-permute-start(bf16[64,256]{1,0:T(8,128)(2,1)S(1)} %get-tuple-element.8), channel_id=1, source_target_pairs={{0,24},{2,26},{4,28},{6,30},{8,16},{10,18},{12,20},{14,22},{16,8},... | collective-permute-start | bytes 98312 | tf_op jit(solution)/shard_map/ppermute | solution.py:139
  32.7 4.8 %collective-permute-start.13 = (bf16[64,256]{1,0:T(8,128)(2,1)S(1)}, bf16[64,256]{1,0:T(8,128)(2,1)S(1)}, u32[]{:S(2)}, u32[]{:S(2)}) collective-permute-start(bf16[64,256]{1,0:T(8,128)(2,1)S(1)} %get-tuple-element.9), channel_id=1, source_target_pairs={{0,16},{2,18},{4,20},{6,22},{8,24},{10,26},{12,28},{14,30},{16,0},... | collective-permute-start | bytes 98312 | tf_op jit(solution)/shard_map/ppermute | solution.py:139
  33.4 4.8 %collective-permute-start.10 = (bf16[128,256]{1,0:T(8,128)(2,1)S(1)}, bf16[128,256]{1,0:T(8,128)(2,1)S(1)}, u32[]{:S(2)}, u32[]{:S(2)}) collective-permute-start(bf16[128,256]{1,0:T(8,128)(2,1)S(1)} %slice.51), channel_id=1, source_target_pairs={{0,2},{2,0},{4,6},{6,4},{8,10},{10,8},{12,14},{14,12},{16,18},{18,... | collective-permute-start | bytes 196616 | tf_op jit(solution)/shard_map/ppermute | solution.py:139

commit v3 on v2

v3 whole, which is shorter than its diff:
```python
import functools

import jax
import jax.numpy as jnp
from jax import lax
from jax.experimental import pallas as pl
from jax.experimental.pallas import tpu as pltpu
from jax.sharding import PartitionSpec as P

masked_value = -1e30
log2_e = 1.4426950408889634
GROUP = 4

NT = (((1,), (1,)), ((), ()))
NN = (((1,), (0,)), ((), ()))


def dot(a, b, dims):
    return lax.dot_general(a, b, dims, preferred_element_type=jnp.float32)


def offsets(size):
    group = (0, 1, 2, 3)
    return group, tuple(range(0, size, 4))


def place_kernel(group, chunk, lengths, order, place_ref):
    rows = place_ref.shape[1]
    index = lax.axis_index("ctx")
    half = rows // 2
    at = lax.broadcasted_iota(jnp.int32, (1, rows), 1)
    for j, bits in enumerate(group):
        first = order[0, index ^ bits] * half
        second = order[1, index ^ bits] * half - half
        pos = at + jnp.where(at < half, first, second)
        start = jnp.int32(0)
        opens = jnp.zeros_like(pos)
        for d in range(lengths.shape[0]):
            opens = jnp.where(pos >= start, start, opens)
            start = start + lengths[d]
        place_ref[j : j + 1, :] = pos
        place_ref[GROUP + j : GROUP + j + 1, :] = opens
    for b, bits in enumerate(chunk):
        for h in range(2):
            to = 2 * GROUP + 2 * b + h
            place_ref[to : to + 1, :] = jnp.full((1, rows), order[h, index ^ bits] * half)


def both_heads(ref, heads, at):
    hd = ref.shape[1] // (2 * heads)
    return jnp.concatenate(
        [ref[:, (at + h) * hd : (at + h + 1) * hd] for h in range(heads)], axis=0
    )


def stats_kernel(chunks, heads, place_ref, *refs):
    group, chunk = refs[:GROUP], refs[GROUP : GROUP + chunks]
    out_ref, expo_ref, dprobs_ref = refs[GROUP + chunks :]
    rows, width = chunk[0].shape
    hd = width // 2
    factor = hd ** (-0.5) * log2_e
    keys = jnp.concatenate([c[:, :hd] for c in chunk], axis=0)
    values = jnp.concatenate([c[:, hd:] for c in chunk], axis=0)
    at = lax.broadcasted_iota(jnp.int32, (rows // 2, rows), 0)
    key_pos = jnp.concatenate(
        [at + place_ref[2 * GROUP + s : 2 * GROUP + s + 1, :] for s in range(2 * chunks)], axis=0
    )
    for j in range(GROUP):
        pos, opens = place_ref[j : j + 1, :], place_ref[GROUP + j : GROUP + j + 1, :]
        allowed = (key_pos <= pos) & (key_pos >= opens)
        bias = jnp.where(allowed, 0.0, masked_value)
        bias = jnp.concatenate([bias] * heads, axis=1)
        scores = dot(keys, both_heads(group[j], heads, 0), NT) * factor + bias
        dprobs = dot(values, both_heads(group[j], heads, heads), NT)
        top = jnp.max(scores, axis=0, keepdims=True)
        expo = jnp.exp2(scores - top)
        at = pl.ds(j * heads * rows, heads * rows)
        out_ref[0:1, at] = top
        out_ref[1:2, at] = jnp.sum(expo, axis=0, keepdims=True)
        out_ref[2:3, at] = jnp.sum(expo * dprobs, axis=0, keepdims=True)
        expo_ref[:, at] = expo
        dprobs_ref[:, at] = dprobs


def backward_kernel(chunks, heads, shards, *refs):
    group, chunk = refs[:GROUP], refs[GROUP : GROUP + chunks]
    stats = refs[GROUP + chunks : 2 * GROUP + chunks]
    expo_ref, dprobs_ref, near_ref, far_ref = refs[2 * GROUP + chunks : 2 * GROUP + chunks + 4]
    outs = refs[2 * GROUP + chunks + 4 : -2]
    dv_total, dk_total = refs[-2:]
    rows, width = chunk[0].shape
    hd = width // 2
    shard = lax.axis_index("head")
    scaling = hd ** (-0.5)
    keys = jnp.concatenate([c[:, :hd] for c in chunk], axis=0)
    keys_across = keys.T
    for j in range(GROUP):
        parts = [
            s[0:3, pl.ds((j ^ t) * heads * rows, heads * rows)] for t, s in enumerate(stats)
        ]
        top = functools.reduce(jnp.maximum, [p[0:1] for p in parts])
        weight = [jnp.exp2(p[0:1] - top) for p in parts]
        total = sum(w * p[1:2] for w, p in zip(weight, parts))
        delta = sum(w * p[2:3] for w, p in zip(weight, parts)) / total
        own = weight[0] / total
        at = pl.ds(j * heads * rows, heads * rows)
        weights = expo_ref[:, at] * own
        weights_low = weights.astype(jnp.bfloat16)
        dscores = (weights * (dprobs_ref[:, at] - delta)).astype(jnp.bfloat16)
        dv = dot(weights_low, both_heads(group[j], heads, heads), NN)
        dk = dot(dscores, both_heads(group[j], heads, 0), NN)
        if j == 0:
            dv_total[...] = dv
            dk_total[...] = dk
        else:
            dv_total[...] += dv
            dk_total[...] += dk
        dq = ((dot(keys_across, dscores, NN) * scaling).T).astype(jnp.bfloat16)
        half = GROUP // 2
        to = (near_ref, far_ref)[j // half]
        for h in range(heads):
            to[pl.ds(j % half * rows, rows), h * hd : (h + 1) * hd] = dq[h * rows : (h + 1) * rows]
    part = rows // shards
    for t in range(shards):
        owner = lax.rem(shard + t, shards)
        for b in range(chunks):
            at = pl.ds(pl.multiple_of(b * rows + owner * part, part), part)
            to = pl.ds(b * part, part)
            outs[t][to, :hd] = (dk_total[at, :] * scaling).astype(jnp.bfloat16)
            outs[t][to, hd:] = dv_total[at, :].astype(jnp.bfloat16)


def finish_kernel(chunks, owned_ref, *refs):
    came, (pair_ref, other_ref) = refs[: chunks - 1], refs[chunks - 1 : chunks + 1]
    query_ref, key_ref, value_ref = refs[chunks + 1 :]
    part, hd = key_ref.shape
    rows = query_ref.shape[0]
    total = owned_ref[:part].astype(jnp.float32)
    for ref in came:
        total = total + ref[...].astype(jnp.float32)
    key_ref[...] = total[:, :hd].astype(jnp.bfloat16)
    value_ref[...] = total[:, hd:].astype(jnp.bfloat16)
    query = pair_ref[:rows].astype(jnp.float32) + other_ref[...].astype(jnp.float32)
    query_ref[...] = query.astype(jnp.bfloat16)


def local(queries, key_rows, value_rows, out_grad, doc_lengths, span_order):
    rows, width = queries.shape
    hd = key_rows.shape[1]
    heads = width // hd
    ctx_size, shards = lax.axis_size("ctx"), lax.axis_size("head")
    chunks = ctx_size // GROUP
    part = rows // shards
    group_bits, chunk_bits = offsets(ctx_size)

    def swap(x, bits):
        return lax.ppermute(x, "ctx", [(i, i ^ bits) for i in range(ctx_size)])

    def turn(x, by):
        return lax.ppermute(x, "head", [(i, (i + by) % shards) for i in range(shards)])

    vmem = pl.BlockSpec(memory_space=pltpu.VMEM)
    params = pltpu.CompilerParams(vmem_limit_bytes=40 * 1024 * 1024)
    small = pltpu.CompilerParams(vmem_limit_bytes=4 * 1024 * 1024)

    def array(shape, dtype=jnp.bfloat16):
        return jax.ShapeDtypeStruct(shape, dtype)

    place = pl.pallas_call(
        functools.partial(place_kernel, group_bits, chunk_bits),
        out_shape=array((2 * (GROUP + chunks), rows), jnp.int32),
        in_specs=[pl.BlockSpec(memory_space=pltpu.SMEM)] * 2,
        out_specs=vmem,
        compiler_params=small,
        name="place",
    )(doc_lengths, span_order.T)

    packed_kv = jnp.concatenate([key_rows, value_rows], axis=1)
    packed_qg = jnp.concatenate([queries, out_grad], axis=1)
    chunk = [packed_kv] + [swap(packed_kv, bits) for bits in chunk_bits[1:]]
    group = [packed_qg] + [swap(packed_qg, bits) for bits in group_bits[1:]]

    square = array((chunks * rows, GROUP * heads * rows), jnp.float32)
    stats, expo, dprobs = pl.pallas_call(
        functools.partial(stats_kernel, chunks, heads),
        out_shape=(array((4, GROUP * heads * rows), jnp.float32), square, square),
        in_specs=[vmem] * (1 + GROUP + chunks),
        out_specs=(vmem, vmem, vmem),
        compiler_params=params,
        name="stats",
    )(place, *group, *chunk)
    all_stats = [stats] + [swap(stats, bits) for bits in group_bits[1:]]

    half = array((GROUP // 2 * rows, width))
    piece = array((chunks * part, 2 * hd))
    near, far, *dkv = pl.pallas_call(
        functools.partial(backward_kernel, chunks, heads, shards),
        out_shape=(half, half) + (piece,) * shards,
        in_specs=[vmem] * (2 * GROUP + chunks + 2),
        out_specs=(vmem,) * (2 + shards),
        scratch_shapes=[pltpu.VMEM((chunks * rows, hd), jnp.float32)] * 2,
        compiler_params=params,
        name="backward",
    )(*group, *chunk, *all_stats, expo, dprobs)

    owned = dkv[0].astype(jnp.float32)
    for t in range(1, shards):
        owned = owned + turn(dkv[t], t).astype(jnp.float32)
    owned = owned.astype(jnp.bfloat16)
    came = [
        swap(owned[b * part : (b + 1) * part], chunk_bits[b]) for b in range(1, chunks)
    ]
    pair = (near.astype(jnp.float32) + swap(far, group_bits[2]).astype(jnp.float32)).astype(jnp.bfloat16)
    other = swap(pair[rows:], group_bits[1])
    return tuple(
        pl.pallas_call(
            functools.partial(finish_kernel, chunks),
            out_shape=(array((rows, width)), array((part, hd)), array((part, hd))),
            in_specs=[vmem] * (chunks + 2),
            out_specs=(vmem, vmem, vmem),
            compiler_params=small,
            name="finish",
        )(owned, *came, pair, other)
    )


def solution(mesh):
    in_specs = (P("ctx", "head"), P("ctx", None), P("ctx", None), P("ctx", "head"), P(), P())
    out_specs = (P("ctx", "head"), P(("ctx", "head"), None), P(("ctx", "head"), None))
    return jax.shard_map(local, mesh=mesh, in_specs=in_specs, out_specs=out_specs, check_vma=False)
```

time: 39 us -> 37.7 us (0.967)
  local copies, waits for them, and re-layouts: 2.26 us -> 4.57 us
  waiting for transfers between devices: 13.7 us -> 12 us
  Pallas kernels: 4.86 us -> 3.35 us
  other arithmetic: 0.81 us -> 0.07 us
    pallas_call x1, Pallas kernels: 3.11 us -> 0.98 us  [local(): pl.pallas_call(functools.partial(backward_kernel, chunks, heads, shards),...]
    ppermute x1, waiting for transfers between devices: 2.4 us -> 0.9 us  [turn(): lax.ppermute(x, 'head', [(i, (i + by) % shards) for i in range(shards)])]
    unnamed x13 -> x6, local copies, waits for them, and re-layouts: 1.58 us -> 2.94 us
    pallas_call x0 -> x2, Pallas kernels: none -> 1.25 us  [the longest x1 0.67 us: local(): pl.pallas_call(functools.partial(finish_kernel, chunks), out_shape=(array...]
    concatenate x1, local copies, waits for them, and re-layouts: 0.01 us -> 0.84 us  [local(): packed_qg = jnp.concatenate([queries, out_grad], axis=1)]
    concatenate x1, local copies, waits for them, and re-layouts: 0.01 us -> 0.77 us  [local(): packed_kv = jnp.concatenate([key_rows, value_rows], axis=1)]
    convert_element_type x2 -> x1, other arithmetic: 0.68 us -> 0.03 us  [local(): (near.astype(jnp.float32) + swap(far, group_bits[2]).astype(jnp.float32))...]
    pallas_call x1, Pallas kernels: 1.75 us -> 1.11 us  [local(): pl.pallas_call(functools.partial(stats_kernel, chunks, heads), out_shape=...]
  transfers between devices with their start and end apart: 15 -> 15, of which waited for: 9 -> 8; matrix products, arithmetic and copies ran while one was open for 2% -> 5% of each run, Pallas kernels for 0% -> 2%
where the time goes in v3:
time: 37.7 us; the launch traced here: 37.3 us
  starting transfers between devices  16.6 us (44%)
  waiting for transfers between devices  12 us (32%)
  local copies, waits for them, and re-layouts  4.57 us (12%)
  Pallas kernels  3.35 us (9%)
  between operations  0.7 us (2%)
    ppermute x14, starting transfers between devices, swap(): return lax.ppermute(x, 'ctx', [(i, i ^ bits) for i in range(ctx_size)])  15.1 us
    ppermute x14, waiting for transfers between devices, swap(): return lax.ppermute(x, 'ctx', [(i, i ^ bits) for i in range(ctx_size)])  11.1 us
    unnamed x6, local copies, waits for them, and re-layouts  2.94 us
    ppermute x1, starting transfers between devices, turn(): lax.ppermute(x, 'head', [(i, (i + by) % shards) for i in range(shards)])  1.52 us
    pallas_call x1, Pallas kernels, local(): pl.pallas_call(functools.partial(stats_kernel, chunks, heads), out_shape=...  1.11 us
    pallas_call x1, Pallas kernels, local(): pl.pallas_call(functools.partial(backward_kernel, chunks, heads, shards),...  0.98 us
    ppermute x1, waiting for transfers between devices, turn(): lax.ppermute(x, 'head', [(i, (i + by) % shards) for i in range(shards)])  0.9 us
    concatenate x1, local copies, waits for them, and re-layouts, local(): packed_qg = jnp.concatenate([queries, out_grad], axis=1)  0.84 us
  transfers between devices with their start and end apart: 15, of which 8 were waited for; matrix products, arithmetic and copies ran while one was open for 5% of the time, Pallas kernels for 2%

profile of v3, /device:TPU:0, one launch (start us, length us, event | category | flops | bytes accessed | tf_op | source)
XLA Modules:
  0.0 37.3 jit_solution(15570423579828791393)
XLA Ops:
  0.6 0.8 %constant_dynamic-update-slice_fusion.3 = bf16[128,256]{1,0:T(8,128)(2,1)S(1)} fusion(bf16[128,128]{1,0:T(8,128)(2,1)} %param.7), kind=kLoop, calls=%fused_computation.5 | loop fusion | bytes 65536
  1.4 0.8 %constant_dynamic-update-slice_fusion.2.refs_4_ = bf16[128,256]{1,0:T(8,128)(2,1)S(1)} fusion(bf16[128,256]{1,0:T(8,128)(2,1)S(1)} %constant_dynamic-update-slice_fusion.3, bf16[128,128]{1,0:T(8,128)(2,1)} %param.8), kind=kLoop, calls=%fused_computation.4 | loop fusion | bytes 65536 | tf_op jit(solution)/shard_map/concatenate | solution.py:178
  2.2 5.1 %collective-permute-start.5 = (bf16[128,256]{1,0:T(8,128)(2,1)S(1)}, bf16[128,256]{1,0:T(8,128)(2,1)S(1)}, u32[]{:S(2)}, u32[]{:S(2)}) collective-permute-start(bf16[128,256]{1,0:T(8,128)(2,1)S(1)} %constant_dynamic-update-slice_fusion.2.refs_4_), channel_id=1, source_target_pairs={{0,24},{2,26},{4,28},{6,30},{8,16},{10,18},{12,20},{14,22},{16,8},... | collective-permute-start | bytes 196616 | tf_op jit(solution)/shard_map/ppermute | solution.py:157
  7.3 0.8 %constant_dynamic-update-slice_fusion.1 = bf16[128,512]{1,0:T(8,128)(2,1)S(1)} fusion(bf16[128,256]{1,0:T(8,128)(2,1)} %param.6), kind=kLoop, calls=%fused_computation.3 | loop fusion | bytes 131072
  8.1 0.8 %constant_dynamic-update-slice_fusion.refs_0_ = bf16[128,512]{1,0:T(8,128)(2,1)S(1)} fusion(bf16[128,512]{1,0:T(8,128)(2,1)S(1)} %constant_dynamic-update-slice_fusion.1, bf16[128,256]{1,0:T(8,128)(2,1)} %param.9), kind=kLoop, calls=%fused_computation.2 | loop fusion | bytes 131072 | tf_op jit(solution)/shard_map/concatenate | solution.py:179
  9.0 0.7 %collective-permute-start.2 = (bf16[128,512]{1,0:T(8,128)(2,1)S(1)}, bf16[128,512]{1,0:T(8,128)(2,1)S(1)}, u32[]{:S(2)}, u32[]{:S(2)}) collective-permute-start(bf16[128,512]{1,0:T(8,128)(2,1)S(1)} %constant_dynamic-update-slice_fusion.refs_0_), channel_id=1, source_target_pairs={{0,6},{2,4},{4,2},{6,0},{8,14},{10,12},{12,10},{14,8},{16,22},{18,... | collective-permute-start | bytes 393224 | tf_op jit(solution)/shard_map/ppermute | solution.py:157
  9.6 0.9 %collective-permute-start.1 = (bf16[128,512]{1,0:T(8,128)(2,1)S(1)}, bf16[128,512]{1,0:T(8,128)(2,1)S(1)}, u32[]{:S(2)}, u32[]{:S(2)}) collective-permute-start(bf16[128,512]{1,0:T(8,128)(2,1)S(1)} %constant_dynamic-update-slice_fusion.refs_0_), channel_id=1, source_target_pairs={{0,4},{2,6},{4,0},{6,2},{8,12},{10,14},{12,8},{14,10},{16,20},{18,... | collective-permute-start | bytes 393224 | tf_op jit(solution)/shard_map/ppermute | solution.py:157
  10.5 0.3 collective-permute-start
  10.8 0.0 collective-permute-start.4
  10.8 0.0 collective-permute-done.5.refs_7_
  10.8 0.6 %collective-permute-start.3 = (bf16[128,256]{1,0:T(8,128)(2,1)S(1)}, bf16[128,256]{1,0:T(8,128)(2,1)S(1)}, u32[]{:S(2)}, u32[]{:S(2)}) collective-permute-start(bf16[128,256]{1,0:T(8,128)(2,1)S(1)} %constant_dynamic-update-slice_fusion.2.refs_4_), channel_id=1, source_target_pairs={{0,8},{2,10},{4,12},{6,14},{8,0},{10,2},{12,4},{14,6},{16,24},{18,... | collective-permute-start | bytes 196616 | tf_op jit(solution)/shard_map/ppermute | solution.py:157
  11.4 0.0 copy-start
  11.4 0.7 %copy-done = s32[16,2]{0,1:T(2,128)S(1)} copy-done((s32[16,2]{0,1:T(2,128)S(1)}, s32[16,2]{0,1:T(2,128)}, u32[]{:S(2)}) %copy-start) | copy-done | bytes 152
  12.1 0.0 copy-start.1
  12.1 0.7 %copy-done.1 = s32[8]{0:T(128)S(1)} copy-done((s32[8]{0:T(128)S(1)}, s32[8]{0:T(128)}, u32[]{:S(2)}) %copy-start.1) | copy-done | bytes 56
  12.8 0.6 %place.1.place_ref = s32[16,128]{1,0:T(8,128)S(1)} custom-call(s32[8]{0:T(128)S(1)} %copy-done.1, s32[2,16]{1,0:T(2,128)S(1)} %bitcast.1), custom_call_target="tpu_custom_call" | custom-call | tf_op jit(solution)/shard_map/place/pallas_call | solution.py:169
  13.4 3.1 %collective-permute-done.4.refs_6_ = bf16[128,256]{1,0:T(8,128)(2,1)S(1)} collective-permute-done((bf16[128,256]{1,0:T(8,128)(2,1)S(1)}, bf16[128,256]{1,0:T(8,128)(2,1)S(1)}, u32[]{:S(2)}, u32[]{:S(2)}) %collective-permute-start.4) | collective-permute-done | bytes 65568 | tf_op jit(solution)/shard_map/ppermute | solution.py:157
  16.5 0.0 collective-permute-done.3.refs_5_
  16.5 0.0 collective-permute-done.2.refs_3_
  16.5 1.1 %collective-permute-done.1.refs_2_ = bf16[128,512]{1,0:T(8,128)(2,1)S(1)} collective-permute-done((bf16[128,512]{1,0:T(8,128)(2,1)S(1)}, bf16[128,512]{1,0:T(8,128)(2,1)S(1)}, u32[]{:S(2)}, u32[]{:S(2)}) %collective-permute-start.1) | collective-permute-done | bytes 131104 | tf_op jit(solution)/shard_map/ppermute | solution.py:157
  17.6 0.0 collective-permute-done.refs_1_
  17.6 1.1 %stats.1 = (f32[4,1024]{1,0:T(4,128)S(1)}, f32[512,1024]{1,0:T(8,128)S(1)}, f32[512,1024]{1,0:T(8,128)S(1)}) custom-call(s32[16,128]{1,0:T(8,128)S(1)} %place.1.place_ref, bf16[128,512]{1,0:T(8,128)(2,1)S(1)} %constant_dynamic-update-slice_fusion.refs_0_, bf16[128,512]{1,0:T(8,128)(2,1)S(1)} %collective-permute-done.refs_1_, ...), custom_call_target="tpu_custom_call" | custom-call | tf_op jit(solution)/shard_map/stats/pallas_call | solution.py:184
  18.7 0.7 %collective-permute-start.8 = (f32[4,1024]{1,0:T(4,128)S(1)}, f32[4,1024]{1,0:T(4,128)S(1)}, u32[]{:S(2)}, u32[]{:S(2)}) collective-permute-start(f32[4,1024]{1,0:T(4,128)S(1)} %get-tuple-element.10.refs_8_), channel_id=1, source_target_pairs={{0,6},{2,4},{4,2},{6,0},{8,14},{10,12},{12,10},{14,8},{16,22},{18,... | collective-permute-start | bytes 49160 | tf_op jit(solution)/shard_map/ppermute | solution.py:157
  19.4 1.0 %collective-permute-start.7 = (f32[4,1024]{1,0:T(4,128)S(1)}, f32[4,1024]{1,0:T(4,128)S(1)}, u32[]{:S(2)}, u32[]{:S(2)}) collective-permute-start(f32[4,1024]{1,0:T(4,128)S(1)} %get-tuple-element.10.refs_8_), channel_id=1, source_target_pairs={{0,4},{2,6},{4,0},{6,2},{8,12},{10,14},{12,8},{14,10},{16,20},{18,... | collective-permute-start | bytes 49160 | tf_op jit(solution)/shard_map/ppermute | solution.py:157
  20.5 0.2 collective-permute-start.6
  20.6 1.3 %collective-permute-done.8.refs_11_ = f32[4,1024]{1,0:T(4,128)S(1)} collective-permute-done((f32[4,1024]{1,0:T(4,128)S(1)}, f32[4,1024]{1,0:T(4,128)S(1)}, u32[]{:S(2)}, u32[]{:S(2)}) %collective-permute-start.8) | collective-permute-done | bytes 16416 | tf_op jit(solution)/shard_map/ppermute | solution.py:157
  21.9 1.3 %collective-permute-done.7.refs_10_ = f32[4,1024]{1,0:T(4,128)S(1)} collective-permute-done((f32[4,1024]{1,0:T(4,128)S(1)}, f32[4,1024]{1,0:T(4,128)S(1)}, u32[]{:S(2)}, u32[]{:S(2)}) %collective-permute-start.7) | collective-permute-done | bytes 16416 | tf_op jit(solution)/shard_map/ppermute | solution.py:157
  23.2 0.0 collective-permute-done.6.refs_9_
  23.2 1.0 %backward.1 = (bf16[256,256]{1,0:T(8,128)(2,1)S(1)}, bf16[256,256]{1,0:T(8,128)(2,1)S(1)}, bf16[256,256]{1,0:T(8,128)(2,1)S(1)}, bf16[256,256]{1,0:T(8,128)(2,1)S(1)}) custom-call(bf16[128,512]{1,0:T(8,128)(2,1)S(1)} %constant_dynamic-update-slice_fusion.refs_0_, bf16[128,512]{1,0:T(8,128)(2,1)S(1)} %collective-permute-done.refs_1_, ...), custom_call_target="tpu_custom_call" | custom-call | tf_op jit(solution)/shard_map/backward/pallas_call | solution.py:196
  24.2 1.1 %collective-permute-start.13 = (bf16[256,256]{1,0:T(8,128)(2,1)S(1)}, bf16[256,256]{1,0:T(8,128)(2,1)S(1)}, u32[]{:S(2)}, u32[]{:S(2)}) collective-permute-start(bf16[256,256]{1,0:T(8,128)(2,1)S(1)} %get-tuple-element.16), channel_id=1, source_target_pairs={{0,4},{2,6},{4,0},{6,2},{8,12},{10,14},{12,8},{14,10},{16,20},{18,... | collective-permute-start | bytes 393224 | tf_op jit(solution)/shard_map/ppermute | solution.py:157
  25.3 1.5 %collective-permute-start.9 = (bf16[256,256]{1,0:T(8,128)(2,1)S(1)}, bf16[256,256]{1,0:T(8,128)(2,1)S(1)}, u32[]{:S(2)}, u32[]{:S(2)}) collective-permute-start(bf16[256,256]{1,0:T(8,128)(2,1)S(1)} %get-tuple-element.14), channel_id=1, source_target_pairs={{0,1},{1,0},{2,3},{3,2},{4,5},{5,4},{6,7},{7,6},{8,9},{9,8},{10,11... | collective-permute-start | bytes 393224 | tf_op jit(solution)/shard_map/ppermute | solution.py:160
  26.8 2.4 %collective-permute-done.13 = bf16[256,256]{1,0:T(8,128)(2,1)S(1)} collective-permute-done((bf16[256,256]{1,0:T(8,128)(2,1)S(1)}, bf16[256,256]{1,0:T(8,128)(2,1)S(1)}, u32[]{:S(2)}, u32[]{:S(2)}) %collective-permute-start.13) | collective-permute-done | bytes 131104 | tf_op jit(solution)/shard_map/ppermute | solution.py:157
  29.2 0.1 collective-permute-start.14
  29.3 0.9 %collective-permute-done.9 = bf16[256,256]{1,0:T(8,128)(2,1)S(1)} collective-permute-done((bf16[256,256]{1,0:T(8,128)(2,1)S(1)}, bf16[256,256]{1,0:T(8,128)(2,1)S(1)}, u32[]{:S(2)}, u32[]{:S(2)}) %collective-permute-start.9) | collective-permute-done | bytes 131104 | tf_op jit(solution)/shard_map/ppermute | solution.py:160
  30.3 0.4 collective-permute-start.12
  30.6 0.7 %collective-permute-start.11 = (bf16[64,256]{1,0:T(8,128)(2,1)S(1)}, bf16[64,256]{1,0:T(8,128)(2,1)S(1)}, u32[]{:S(2)}, u32[]{:S(2)}) collective-permute-start(bf16[64,256]{1,0:T(8,128)(2,1)S(1)} %get-tuple-element.18), channel_id=1, source_target_pairs={{0,16},{2,18},{4,20},{6,22},{8,24},{10,26},{12,28},{14,30},{16,0},... | collective-permute-start | bytes 98312 | tf_op jit(solution)/shard_map/ppermute | solution.py:157
  31.4 3.4 %collective-permute-start.10 = (bf16[64,256]{1,0:T(8,128)(2,1)S(1)}, bf16[64,256]{1,0:T(8,128)(2,1)S(1)}, u32[]{:S(2)}, u32[]{:S(2)}) collective-permute-start(bf16[64,256]{1,0:T(8,128)(2,1)S(1)} %get-tuple-element.19), channel_id=1, source_target_pairs={{0,8},{2,10},{4,12},{6,14},{8,0},{10,2},{12,4},{14,6},{16,24},{18,... | collective-permute-start | bytes 98312 | tf_op jit(solution)/shard_map/ppermute | solution.py:157
  34.7 1.3 %collective-permute-done.12.refs_2_ = bf16[64,256]{1,0:T(8,128)(2,1)S(1)} collective-permute-done((bf16[64,256]{1,0:T(8,128)(2,1)S(1)}, bf16[64,256]{1,0:T(8,128)(2,1)S(1)}, u32[]{:S(2)}, u32[]{:S(2)}) %collective-permute-start.12) | collective-permute-done | bytes 32800 | tf_op jit(solution)/shard_map/ppermute | solution.py:157
  36.1 0.0 collective-permute-done.11.refs_1_
  36.1 0.6 %collective-permute-done.10.refs_0_ = bf16[64,256]{1,0:T(8,128)(2,1)S(1)} collective-permute-done((bf16[64,256]{1,0:T(8,128)(2,1)S(1)}, bf16[64,256]{1,0:T(8,128)(2,1)S(1)}, u32[]{:S(2)}, u32[]{:S(2)}) %collective-permute-start.10) | collective-permute-done | bytes 32800 | tf_op jit(solution)/shard_map/ppermute | solution.py:157
  36.6 0.0 collective-permute-done.14.refs_4_
  36.6 0.7 %finish.1 = (bf16[128,256]{1,0:T(8,128)(2,1)}, bf16[64,128]{1,0:T(8,128)(2,1)}, bf16[64,128]{1,0:T(8,128)(2,1)}) custom-call(bf16[256,256]{1,0:T(8,128)(2,1)S(1)} %add_convert_fusion.1.owned_ref, bf16[64,256]{1,0:T(8,128)(2,1)S(1)} %collective-permute-done.10.refs_0_, bf16[64,256]{1,0:T(8,128)(2,1)S(1)} %collective-permute-done.11.refs_1_, ...), custom_call_target="tpu_custom_call" | custom-call | tf_op jit(solution)/shard_map/finish/pallas_call | solution.py:216
  (4 shorter events, 0.1 us)
Async XLA Ops:
  2.2 8.7 %collective-permute-start.5 = (bf16[128,256]{1,0:T(8,128)(2,1)S(1)}, bf16[128,256]{1,0:T(8,128)(2,1)S(1)}, u32[]{:S(2)}, u32[]{:S(2)}) collective-permute-start(bf16[128,256]{1,0:T(8,128)(2,1)S(1)} %constant_dynamic-update-slice_fusion.2.refs_4_), channel_id=1, source_target_pairs={{0,24},{2,26},{4,28},{6,30},{8,16},{10,18},{12,20},{14,22},{16,8},... | collective-permute-start | bytes 196616 | tf_op jit(solution)/shard_map/ppermute | solution.py:157
  9.0 7.5 %collective-permute-start.2 = (bf16[128,512]{1,0:T(8,128)(2,1)S(1)}, bf16[128,512]{1,0:T(8,128)(2,1)S(1)}, u32[]{:S(2)}, u32[]{:S(2)}) collective-permute-start(bf16[128,512]{1,0:T(8,128)(2,1)S(1)} %constant_dynamic-update-slice_fusion.refs_0_), channel_id=1, source_target_pairs={{0,6},{2,4},{4,2},{6,0},{8,14},{10,12},{12,10},{14,8},{16,22},{18,... | collective-permute-start | bytes 393224 | tf_op jit(solution)/shard_map/ppermute | solution.py:157
  9.6 8.0 %collective-permute-start.1 = (bf16[128,512]{1,0:T(8,128)(2,1)S(1)}, bf16[128,512]{1,0:T(8,128)(2,1)S(1)}, u32[]{:S(2)}, u32[]{:S(2)}) collective-permute-start(bf16[128,512]{1,0:T(8,128)(2,1)S(1)} %constant_dynamic-update-slice_fusion.refs_0_), channel_id=1, source_target_pairs={{0,4},{2,6},{4,0},{6,2},{8,12},{10,14},{12,8},{14,10},{16,20},{18,... | collective-permute-start | bytes 393224 | tf_op jit(solution)/shard_map/ppermute | solution.py:157
  10.5 7.1 %collective-permute-start = (bf16[128,512]{1,0:T(8,128)(2,1)S(1)}, bf16[128,512]{1,0:T(8,128)(2,1)S(1)}, u32[]{:S(2)}, u32[]{:S(2)}) collective-permute-start(bf16[128,512]{1,0:T(8,128)(2,1)S(1)} %constant_dynamic-update-slice_fusion.refs_0_), channel_id=1, source_target_pairs={{0,2},{2,0},{4,6},{6,4},{8,10},{10,8},{12,14},{14,12},{16,18},{18,... | collective-permute-start | bytes 393224 | tf_op jit(solution)/shard_map/ppermute | solution.py:157
  10.8 5.7 %collective-permute-start.4 = (bf16[128,256]{1,0:T(8,128)(2,1)S(1)}, bf16[128,256]{1,0:T(8,128)(2,1)S(1)}, u32[]{:S(2)}, u32[]{:S(2)}) collective-permute-start(bf16[128,256]{1,0:T(8,128)(2,1)S(1)} %constant_dynamic-update-slice_fusion.2.refs_4_), channel_id=1, source_target_pairs={{0,16},{2,18},{4,20},{6,22},{8,24},{10,26},{12,28},{14,30},{16,0},... | collective-permute-start | bytes 196616 | tf_op jit(solution)/shard_map/ppermute | solution.py:157
  10.8 5.7 %collective-permute-start.3 = (bf16[128,256]{1,0:T(8,128)(2,1)S(1)}, bf16[128,256]{1,0:T(8,128)(2,1)S(1)}, u32[]{:S(2)}, u32[]{:S(2)}) collective-permute-start(bf16[128,256]{1,0:T(8,128)(2,1)S(1)} %constant_dynamic-update-slice_fusion.2.refs_4_), channel_id=1, source_target_pairs={{0,8},{2,10},{4,12},{6,14},{8,0},{10,2},{12,4},{14,6},{16,24},{18,... | collective-permute-start | bytes 196616 | tf_op jit(solution)/shard_map/ppermute | solution.py:157
  11.4 0.7 %copy-start = (s32[16,2]{0,1:T(2,128)S(1)}, s32[16,2]{0,1:T(2,128)}, u32[]{:S(2)}) copy-start(s32[16,2]{0,1:T(2,128)} %param.11) | copy-start | bytes 388
  12.1 0.7 %copy-start.1 = (s32[8]{0:T(128)S(1)}, s32[8]{0:T(128)}, u32[]{:S(2)}) copy-start(s32[8]{0:T(128)} %lengths.1) | copy-start | bytes 100
  18.7 3.2 %collective-permute-start.8 = (f32[4,1024]{1,0:T(4,128)S(1)}, f32[4,1024]{1,0:T(4,128)S(1)}, u32[]{:S(2)}, u32[]{:S(2)}) collective-permute-start(f32[4,1024]{1,0:T(4,128)S(1)} %get-tuple-element.10.refs_8_), channel_id=1, source_target_pairs={{0,6},{2,4},{4,2},{6,0},{8,14},{10,12},{12,10},{14,8},{16,22},{18,... | collective-permute-start | bytes 49160 | tf_op jit(solution)/shard_map/ppermute | solution.py:157
  19.4 3.7 %collective-permute-start.7 = (f32[4,1024]{1,0:T(4,128)S(1)}, f32[4,1024]{1,0:T(4,128)S(1)}, u32[]{:S(2)}, u32[]{:S(2)}) collective-permute-start(f32[4,1024]{1,0:T(4,128)S(1)} %get-tuple-element.10.refs_8_), channel_id=1, source_target_pairs={{0,4},{2,6},{4,0},{6,2},{8,12},{10,14},{12,8},{14,10},{16,20},{18,... | collective-permute-start | bytes 49160 | tf_op jit(solution)/shard_map/ppermute | solution.py:157
  20.5 2.7 %collective-permute-start.6 = (f32[4,1024]{1,0:T(4,128)S(1)}, f32[4,1024]{1,0:T(4,128)S(1)}, u32[]{:S(2)}, u32[]{:S(2)}) collective-permute-start(f32[4,1024]{1,0:T(4,128)S(1)} %get-tuple-element.10.refs_8_), channel_id=1, source_target_pairs={{0,2},{2,0},{4,6},{6,4},{8,10},{10,8},{12,14},{14,12},{16,18},{18,... | collective-permute-start | bytes 49160 | tf_op jit(solution)/shard_map/ppermute | solution.py:157
  24.2 5.0 %collective-permute-start.13 = (bf16[256,256]{1,0:T(8,128)(2,1)S(1)}, bf16[256,256]{1,0:T(8,128)(2,1)S(1)}, u32[]{:S(2)}, u32[]{:S(2)}) collective-permute-start(bf16[256,256]{1,0:T(8,128)(2,1)S(1)} %get-tuple-element.16), channel_id=1, source_target_pairs={{0,4},{2,6},{4,0},{6,2},{8,12},{10,14},{12,8},{14,10},{16,20},{18,... | collective-permute-start | bytes 393224 | tf_op jit(solution)/shard_map/ppermute | solution.py:157
  25.3 5.0 %collective-permute-start.9 = (bf16[256,256]{1,0:T(8,128)(2,1)S(1)}, bf16[256,256]{1,0:T(8,128)(2,1)S(1)}, u32[]{:S(2)}, u32[]{:S(2)}) collective-permute-start(bf16[256,256]{1,0:T(8,128)(2,1)S(1)} %get-tuple-element.14), channel_id=1, source_target_pairs={{0,1},{1,0},{2,3},{3,2},{4,5},{5,4},{6,7},{7,6},{8,9},{9,8},{10,11... | collective-permute-start | bytes 393224 | tf_op jit(solution)/shard_map/ppermute | solution.py:160
  29.2 7.4 %collective-permute-start.14 = (bf16[128,256]{1,0:T(8,128)(2,1)S(1)}, bf16[128,256]{1,0:T(8,128)(2,1)S(1)}, u32[]{:S(2)}, u32[]{:S(2)}) collective-permute-start(bf16[128,256]{1,0:T(8,128)(2,1)S(1)} %slice.19), channel_id=1, source_target_pairs={{0,2},{2,0},{4,6},{6,4},{8,10},{10,8},{12,14},{14,12},{16,18},{18,... | collective-permute-start | bytes 196616 | tf_op jit(solution)/shard_map/ppermute | solution.py:157
  30.3 5.8 %collective-permute-start.12 = (bf16[64,256]{1,0:T(8,128)(2,1)S(1)}, bf16[64,256]{1,0:T(8,128)(2,1)S(1)}, u32[]{:S(2)}, u32[]{:S(2)}) collective-permute-start(bf16[64,256]{1,0:T(8,128)(2,1)S(1)} %get-tuple-element.17), channel_id=1, source_target_pairs={{0,24},{2,26},{4,28},{6,30},{8,16},{10,18},{12,20},{14,22},{16,8},... | collective-permute-start | bytes 98312 | tf_op jit(solution)/shard_map/ppermute | solution.py:157
  30.6 5.4 %collective-permute-start.11 = (bf16[64,256]{1,0:T(8,128)(2,1)S(1)}, bf16[64,256]{1,0:T(8,128)(2,1)S(1)}, u32[]{:S(2)}, u32[]{:S(2)}) collective-permute-start(bf16[64,256]{1,0:T(8,128)(2,1)S(1)} %get-tuple-element.18), channel_id=1, source_target_pairs={{0,16},{2,18},{4,20},{6,22},{8,24},{10,26},{12,28},{14,30},{16,0},... | collective-permute-start | bytes 98312 | tf_op jit(solution)/shard_map/ppermute | solution.py:157
  31.4 5.3 %collective-permute-start.10 = (bf16[64,256]{1,0:T(8,128)(2,1)S(1)}, bf16[64,256]{1,0:T(8,128)(2,1)S(1)}, u32[]{:S(2)}, u32[]{:S(2)}) collective-permute-start(bf16[64,256]{1,0:T(8,128)(2,1)S(1)} %get-tuple-element.19), channel_id=1, source_target_pairs={{0,8},{2,10},{4,12},{6,14},{8,0},{10,2},{12,4},{14,6},{16,24},{18,... | collective-permute-start | bytes 98312 | tf_op jit(solution)/shard_map/ppermute | solution.py:157

commit v4 on v3

--- a/solution.py
+++ b/solution.py
@@ -46,11 +46,10 @@
             place_ref[to : to + 1, :] = jnp.full((1, rows), order[h, index ^ bits] * half)
 
 
-def both_heads(ref, heads, at):
-    hd = ref.shape[1] // (2 * heads)
-    return jnp.concatenate(
-        [ref[:, (at + h) * hd : (at + h + 1) * hd] for h in range(heads)], axis=0
-    )
+def both_heads(ref, heads, which):
+    rows, hd = ref.shape[0] // 2, ref.shape[1] // heads
+    at = pl.ds(which * rows, rows)
+    return jnp.concatenate([ref[at, h * hd : (h + 1) * hd] for h in range(heads)], axis=0)
 
 
 def stats_kernel(chunks, heads, place_ref, *refs):
@@ -71,7 +70,7 @@
         bias = jnp.where(allowed, 0.0, masked_value)
         bias = jnp.concatenate([bias] * heads, axis=1)
         scores = dot(keys, both_heads(group[j], heads, 0), NT) * factor + bias
-        dprobs = dot(values, both_heads(group[j], heads, heads), NT)
+        dprobs = dot(values, both_heads(group[j], heads, 1), NT)
         top = jnp.max(scores, axis=0, keepdims=True)
         expo = jnp.exp2(scores - top)
         at = pl.ds(j * heads * rows, heads * rows)
@@ -107,7 +106,7 @@
         weights = expo_ref[:, at] * own
         weights_low = weights.astype(jnp.bfloat16)
         dscores = (weights * (dprobs_ref[:, at] - delta)).astype(jnp.bfloat16)
-        dv = dot(weights_low, both_heads(group[j], heads, heads), NN)
+        dv = dot(weights_low, both_heads(group[j], heads, 1), NN)
         dk = dot(dscores, both_heads(group[j], heads, 0), NN)
         if j == 0:
             dv_total[...] = dv
@@ -175,8 +174,11 @@
         name="place",
     )(doc_lengths, span_order.T)
 
-    packed_kv = jnp.concatenate([key_rows, value_rows], axis=1)
-    packed_qg = jnp.concatenate([queries, out_grad], axis=1)
+    packed = jnp.concatenate(
+        [jnp.concatenate([key_rows, value_rows], axis=1), queries, out_grad], axis=0
+    )
+    packed = lax.optimization_barrier(packed)
+    packed_kv, packed_qg = packed[:rows], packed[rows:]
     chunk = [packed_kv] + [swap(packed_kv, bits) for bits in chunk_bits[1:]]
     group = [packed_qg] + [swap(packed_qg, bits) for bits in group_bits[1:]]
 

time: 37.7 us -> 35.6 us (0.944)
  local copies, waits for them, and re-layouts: 4.57 us -> 1.36 us
  other arithmetic: 0.07 us -> 0.96 us
  starting transfers between devices: 16.6 us -> 17.2 us
    concatenate x2 -> x0, local copies, waits for them, and re-layouts: 1.61 us -> none  [the longest x1 0.84 us: local(): packed_qg = jnp.concatenate([queries, out_grad], axis=1)]
    unnamed x6 -> x4, local copies, waits for them, and re-layouts: 2.94 us -> 1.33 us
    concatenate x0 -> x1, other arithmetic: none -> 0.89 us  [local(): jnp.concatenate([jnp.concatenate([key_rows, value_rows], axis=1), queries...]
    ppermute x14, starting transfers between devices: 15.1 us -> 15.6 us  [swap(): return lax.ppermute(x, 'ctx', [(i, i ^ bits) for i in range(ctx_size)])]
  transfers between devices with their start and end apart: 15 -> 15, of which waited for: 8 -> 11; matrix products, arithmetic and copies ran while one was open for 5% -> 0% of each run, Pallas kernels for 2% -> 2%
where the time goes in v4:
time: 35.6 us; the launch traced here: 35.4 us
  starting transfers between devices  17.2 us (48%)
  waiting for transfers between devices  11.9 us (33%)
  Pallas kernels  3.35 us (9%)
  local copies, waits for them, and re-layouts  1.36 us (4%)
  other arithmetic  0.96 us (3%)
  between operations  0.71 us (2%)
    ppermute x14, starting transfers between devices, swap(): return lax.ppermute(x, 'ctx', [(i, i ^ bits) for i in range(ctx_size)])  15.6 us
    ppermute x14, waiting for transfers between devices, swap(): return lax.ppermute(x, 'ctx', [(i, i ^ bits) for i in range(ctx_size)])  11 us
    ppermute x1, starting transfers between devices, turn(): lax.ppermute(x, 'head', [(i, (i + by) % shards) for i in range(shards)])  1.53 us
    unnamed x4, local copies, waits for them, and re-layouts  1.33 us
    pallas_call x1, Pallas kernels, local(): pl.pallas_call(functools.partial(stats_kernel, chunks, heads), out_shape=...  1.12 us
    pallas_call x1, Pallas kernels, local(): pl.pallas_call(functools.partial(backward_kernel, chunks, heads, shards),...  0.98 us
    concatenate x1, other arithmetic, local(): jnp.concatenate([jnp.concatenate([key_rows, value_rows], axis=1), queries...  0.89 us
    ppermute x1, waiting for transfers between devices, turn(): lax.ppermute(x, 'head', [(i, (i + by) % shards) for i in range(shards)])  0.89 us
  transfers between devices with their start and end apart: 15, of which 11 were waited for; matrix products, arithmetic and copies ran while one was open for 0% of the time, Pallas kernels for 2%

profile of v4, /device:TPU:0, one launch (start us, length us, event | category | flops | bytes accessed | tf_op | source)
XLA Modules:
  0.0 35.4 jit_solution(2640308006249436206)
XLA Ops:
  0.6 0.9 %pad_maximum_fusion = bf16[384,256]{1,0:T(8,128)(2,1)S(1)} fusion(bf16[128,256]{1,0:T(8,128)(2,1)} %param.9, bf16[128,256]{1,0:T(8,128)(2,1)} %param.6, bf16[128,128]{1,0:T(8,128)(2,1)} %param.8, bf16[128,128]{1,0:T(8,128)(2,1)} %param.7), kind=kLoop, calls=%fused_computation.2 | loop fusion | flops 786432 | bytes 393216 | tf_op jit(solution)/shard_map/concatenate | solution.py:177
  1.5 5.1 %collective-permute-start.5 = (bf16[128,256]{1,0:T(8,128)(2,1)S(1)}, bf16[128,256]{1,0:T(8,128)(2,1)S(1)}, u32[]{:S(2)}, u32[]{:S(2)}) collective-permute-start(bf16[128,256]{1,0:T(8,128)(2,1)S(1)} %slice.25.refs_4_), channel_id=1, source_target_pairs={{0,24},{2,26},{4,28},{6,30},{8,16},{10,18},{12,20},{14,22},{16,8},... | collective-permute-start | bytes 196616 | tf_op jit(solution)/shard_map/ppermute | solution.py:156
  6.7 0.7 %collective-permute-start.2 = (bf16[256,256]{1,0:T(8,128)(2,1)S(1)}, bf16[256,256]{1,0:T(8,128)(2,1)S(1)}, u32[]{:S(2)}, u32[]{:S(2)}) collective-permute-start(bf16[256,256]{1,0:T(8,128)(2,1)S(1)} %slice.24.refs_0_), channel_id=1, source_target_pairs={{0,6},{2,4},{4,2},{6,0},{8,14},{10,12},{12,10},{14,8},{16,22},{18,... | collective-permute-start | bytes 393224 | tf_op jit(solution)/shard_map/ppermute | solution.py:156
  7.4 0.9 %collective-permute-start.1 = (bf16[256,256]{1,0:T(8,128)(2,1)S(1)}, bf16[256,256]{1,0:T(8,128)(2,1)S(1)}, u32[]{:S(2)}, u32[]{:S(2)}) collective-permute-start(bf16[256,256]{1,0:T(8,128)(2,1)S(1)} %slice.24.refs_0_), channel_id=1, source_target_pairs={{0,4},{2,6},{4,0},{6,2},{8,12},{10,14},{12,8},{14,10},{16,20},{18,... | collective-permute-start | bytes 393224 | tf_op jit(solution)/shard_map/ppermute | solution.py:156
  8.3 0.3 collective-permute-start
  8.6 0.0 collective-permute-start.4
  8.6 0.4 %collective-permute-done.5.refs_7_ = bf16[128,256]{1,0:T(8,128)(2,1)S(1)} collective-permute-done((bf16[128,256]{1,0:T(8,128)(2,1)S(1)}, bf16[128,256]{1,0:T(8,128)(2,1)S(1)}, u32[]{:S(2)}, u32[]{:S(2)}) %collective-permute-start.5) | collective-permute-done | bytes 65568 | tf_op jit(solution)/shard_map/ppermute | solution.py:156
  9.0 1.1 %collective-permute-start.3 = (bf16[128,256]{1,0:T(8,128)(2,1)S(1)}, bf16[128,256]{1,0:T(8,128)(2,1)S(1)}, u32[]{:S(2)}, u32[]{:S(2)}) collective-permute-start(bf16[128,256]{1,0:T(8,128)(2,1)S(1)} %slice.25.refs_4_), channel_id=1, source_target_pairs={{0,8},{2,10},{4,12},{6,14},{8,0},{10,2},{12,4},{14,6},{16,24},{18,... | collective-permute-start | bytes 196616 | tf_op jit(solution)/shard_map/ppermute | solution.py:156
  10.0 0.0 copy-start
  10.0 0.7 %copy-done = s32[16,2]{0,1:T(2,128)S(1)} copy-done((s32[16,2]{0,1:T(2,128)S(1)}, s32[16,2]{0,1:T(2,128)}, u32[]{:S(2)}) %copy-start) | copy-done | bytes 152
  10.7 0.0 copy-start.1
  10.7 0.7 %copy-done.1 = s32[8]{0:T(128)S(1)} copy-done((s32[8]{0:T(128)S(1)}, s32[8]{0:T(128)}, u32[]{:S(2)}) %copy-start.1) | copy-done | bytes 56
  11.3 0.6 %place.1.place_ref = s32[16,128]{1,0:T(8,128)S(1)} custom-call(s32[8]{0:T(128)S(1)} %copy-done.1, s32[2,16]{1,0:T(2,128)S(1)} %bitcast.1), custom_call_target="tpu_custom_call" | custom-call | tf_op jit(solution)/shard_map/place/pallas_call | solution.py:168
  11.9 2.3 %collective-permute-done.4.refs_6_ = bf16[128,256]{1,0:T(8,128)(2,1)S(1)} collective-permute-done((bf16[128,256]{1,0:T(8,128)(2,1)S(1)}, bf16[128,256]{1,0:T(8,128)(2,1)S(1)}, u32[]{:S(2)}, u32[]{:S(2)}) %collective-permute-start.4) | collective-permute-done | bytes 65568 | tf_op jit(solution)/shard_map/ppermute | solution.py:156
  14.3 0.4 collective-permute-done.3.refs_5_
  14.6 0.0 collective-permute-done.2.refs_3_
  14.6 0.7 %collective-permute-done.1.refs_2_ = bf16[256,256]{1,0:T(8,128)(2,1)S(1)} collective-permute-done((bf16[256,256]{1,0:T(8,128)(2,1)S(1)}, bf16[256,256]{1,0:T(8,128)(2,1)S(1)}, u32[]{:S(2)}, u32[]{:S(2)}) %collective-permute-start.1) | collective-permute-done | bytes 131104 | tf_op jit(solution)/shard_map/ppermute | solution.py:156
  15.3 0.0 collective-permute-done.refs_1_
  15.3 1.1 %stats.1 = (f32[4,1024]{1,0:T(4,128)S(1)}, f32[512,1024]{1,0:T(8,128)S(1)}, f32[512,1024]{1,0:T(8,128)S(1)}) custom-call(s32[16,128]{1,0:T(8,128)S(1)} %place.1.place_ref, bf16[256,256]{1,0:T(8,128)(2,1)S(1)} %slice.24.refs_0_, bf16[256,256]{1,0:T(8,128)(2,1)S(1)} %collective-permute-done.refs_1_, bf16[256,256]{1,0:T(8,128)(2,1)S(1)} %collective-permute-done.1.refs_2_, ...), custom_call_target="tpu_custom_call" | custom-call | tf_op jit(solution)/shard_map/stats/pallas_call | solution.py:186
  16.5 0.7 %collective-permute-start.8 = (f32[4,1024]{1,0:T(4,128)S(1)}, f32[4,1024]{1,0:T(4,128)S(1)}, u32[]{:S(2)}, u32[]{:S(2)}) collective-permute-start(f32[4,1024]{1,0:T(4,128)S(1)} %get-tuple-element.10.refs_8_), channel_id=1, source_target_pairs={{0,6},{2,4},{4,2},{6,0},{8,14},{10,12},{12,10},{14,8},{16,22},{18,... | collective-permute-start | bytes 49160 | tf_op jit(solution)/shard_map/ppermute | solution.py:156
  17.2 1.0 %collective-permute-start.7 = (f32[4,1024]{1,0:T(4,128)S(1)}, f32[4,1024]{1,0:T(4,128)S(1)}, u32[]{:S(2)}, u32[]{:S(2)}) collective-permute-start(f32[4,1024]{1,0:T(4,128)S(1)} %get-tuple-element.10.refs_8_), channel_id=1, source_target_pairs={{0,4},{2,6},{4,0},{6,2},{8,12},{10,14},{12,8},{14,10},{16,20},{18,... | collective-permute-start | bytes 49160 | tf_op jit(solution)/shard_map/ppermute | solution.py:156
  18.2 0.2 collective-permute-start.6
  18.4 1.3 %collective-permute-done.8.refs_11_ = f32[4,1024]{1,0:T(4,128)S(1)} collective-permute-done((f32[4,1024]{1,0:T(4,128)S(1)}, f32[4,1024]{1,0:T(4,128)S(1)}, u32[]{:S(2)}, u32[]{:S(2)}) %collective-permute-start.8) | collective-permute-done | bytes 16416 | tf_op jit(solution)/shard_map/ppermute | solution.py:156
  19.7 1.3 %collective-permute-done.7.refs_10_ = f32[4,1024]{1,0:T(4,128)S(1)} collective-permute-done((f32[4,1024]{1,0:T(4,128)S(1)}, f32[4,1024]{1,0:T(4,128)S(1)}, u32[]{:S(2)}, u32[]{:S(2)}) %collective-permute-start.7) | collective-permute-done | bytes 16416 | tf_op jit(solution)/shard_map/ppermute | solution.py:156
  20.9 0.0 collective-permute-done.6.refs_9_
  21.0 1.0 %backward.1 = (bf16[256,256]{1,0:T(8,128)(2,1)S(1)}, bf16[256,256]{1,0:T(8,128)(2,1)S(1)}, bf16[256,256]{1,0:T(8,128)(2,1)S(1)}, bf16[256,256]{1,0:T(8,128)(2,1)S(1)}) custom-call(bf16[256,256]{1,0:T(8,128)(2,1)S(1)} %slice.24.refs_0_, bf16[256,256]{1,0:T(8,128)(2,1)S(1)} %collective-permute-done.refs_1_, ...), custom_call_target="tpu_custom_call" | custom-call | tf_op jit(solution)/shard_map/backward/pallas_call | solution.py:198
  21.9 1.1 %collective-permute-start.13 = (bf16[256,256]{1,0:T(8,128)(2,1)S(1)}, bf16[256,256]{1,0:T(8,128)(2,1)S(1)}, u32[]{:S(2)}, u32[]{:S(2)}) collective-permute-start(bf16[256,256]{1,0:T(8,128)(2,1)S(1)} %get-tuple-element.16), channel_id=1, source_target_pairs={{0,4},{2,6},{4,0},{6,2},{8,12},{10,14},{12,8},{14,10},{16,20},{18,... | collective-permute-start | bytes 393224 | tf_op jit(solution)/shard_map/ppermute | solution.py:156
  23.0 1.5 %collective-permute-start.9 = (bf16[256,256]{1,0:T(8,128)(2,1)S(1)}, bf16[256,256]{1,0:T(8,128)(2,1)S(1)}, u32[]{:S(2)}, u32[]{:S(2)}) collective-permute-start(bf16[256,256]{1,0:T(8,128)(2,1)S(1)} %get-tuple-element.14), channel_id=1, source_target_pairs={{0,1},{1,0},{2,3},{3,2},{4,5},{5,4},{6,7},{7,6},{8,9},{9,8},{10,11... | collective-permute-start | bytes 393224 | tf_op jit(solution)/shard_map/ppermute | solution.py:159
  24.5 2.4 %collective-permute-done.13 = bf16[256,256]{1,0:T(8,128)(2,1)S(1)} collective-permute-done((bf16[256,256]{1,0:T(8,128)(2,1)S(1)}, bf16[256,256]{1,0:T(8,128)(2,1)S(1)}, u32[]{:S(2)}, u32[]{:S(2)}) %collective-permute-start.13) | collective-permute-done | bytes 131104 | tf_op jit(solution)/shard_map/ppermute | solution.py:156
  27.0 0.1 collective-permute-start.14
  27.1 0.9 %collective-permute-done.9 = bf16[256,256]{1,0:T(8,128)(2,1)S(1)} collective-permute-done((bf16[256,256]{1,0:T(8,128)(2,1)S(1)}, bf16[256,256]{1,0:T(8,128)(2,1)S(1)}, u32[]{:S(2)}, u32[]{:S(2)}) %collective-permute-start.9) | collective-permute-done | bytes 131104 | tf_op jit(solution)/shard_map/ppermute | solution.py:159
  28.0 1.6 %collective-permute-start.12 = (bf16[64,256]{1,0:T(8,128)(2,1)S(1)}, bf16[64,256]{1,0:T(8,128)(2,1)S(1)}, u32[]{:S(2)}, u32[]{:S(2)}) collective-permute-start(bf16[64,256]{1,0:T(8,128)(2,1)S(1)} %get-tuple-element.17), channel_id=1, source_target_pairs={{0,24},{2,26},{4,28},{6,30},{8,16},{10,18},{12,20},{14,22},{16,8},... | collective-permute-start | bytes 98312 | tf_op jit(solution)/shard_map/ppermute | solution.py:156
  29.7 0.0 collective-permute-start.11
  29.7 2.8 %collective-permute-start.10 = (bf16[64,256]{1,0:T(8,128)(2,1)S(1)}, bf16[64,256]{1,0:T(8,128)(2,1)S(1)}, u32[]{:S(2)}, u32[]{:S(2)}) collective-permute-start(bf16[64,256]{1,0:T(8,128)(2,1)S(1)} %get-tuple-element.19), channel_id=1, source_target_pairs={{0,8},{2,10},{4,12},{6,14},{8,0},{10,2},{12,4},{14,6},{16,24},{18,... | collective-permute-start | bytes 98312 | tf_op jit(solution)/shard_map/ppermute | solution.py:156
  32.5 1.3 %collective-permute-done.12.refs_2_ = bf16[64,256]{1,0:T(8,128)(2,1)S(1)} collective-permute-done((bf16[64,256]{1,0:T(8,128)(2,1)S(1)}, bf16[64,256]{1,0:T(8,128)(2,1)S(1)}, u32[]{:S(2)}, u32[]{:S(2)}) %collective-permute-start.12) | collective-permute-done | bytes 32800 | tf_op jit(solution)/shard_map/ppermute | solution.py:156
  33.8 0.8 %collective-permute-done.11.refs_1_ = bf16[64,256]{1,0:T(8,128)(2,1)S(1)} collective-permute-done((bf16[64,256]{1,0:T(8,128)(2,1)S(1)}, bf16[64,256]{1,0:T(8,128)(2,1)S(1)}, u32[]{:S(2)}, u32[]{:S(2)}) %collective-permute-start.11) | collective-permute-done | bytes 32800 | tf_op jit(solution)/shard_map/ppermute | solution.py:156
  34.6 0.1 collective-permute-done.10.refs_0_
  34.7 0.0 collective-permute-done.14.refs_4_
  34.7 0.7 %finish.1 = (bf16[128,256]{1,0:T(8,128)(2,1)}, bf16[64,128]{1,0:T(8,128)(2,1)}, bf16[64,128]{1,0:T(8,128)(2,1)}) custom-call(bf16[256,256]{1,0:T(8,128)(2,1)S(1)} %add_convert_fusion.1.owned_ref, bf16[64,256]{1,0:T(8,128)(2,1)S(1)} %collective-permute-done.10.refs_0_, bf16[64,256]{1,0:T(8,128)(2,1)S(1)} %collective-permute-done.11.refs_1_, ...), custom_call_target="tpu_custom_call" | custom-call | tf_op jit(solution)/shard_map/finish/pallas_call | solution.py:218
  (6 shorter events, 0.1 us)
Async XLA Ops:
  1.5 7.4 %collective-permute-start.5 = (bf16[128,256]{1,0:T(8,128)(2,1)S(1)}, bf16[128,256]{1,0:T(8,128)(2,1)S(1)}, u32[]{:S(2)}, u32[]{:S(2)}) collective-permute-start(bf16[128,256]{1,0:T(8,128)(2,1)S(1)} %slice.25.refs_4_), channel_id=1, source_target_pairs={{0,24},{2,26},{4,28},{6,30},{8,16},{10,18},{12,20},{14,22},{16,8},... | collective-permute-start | bytes 196616 | tf_op jit(solution)/shard_map/ppermute | solution.py:156
  6.7 7.9 %collective-permute-start.2 = (bf16[256,256]{1,0:T(8,128)(2,1)S(1)}, bf16[256,256]{1,0:T(8,128)(2,1)S(1)}, u32[]{:S(2)}, u32[]{:S(2)}) collective-permute-start(bf16[256,256]{1,0:T(8,128)(2,1)S(1)} %slice.24.refs_0_), channel_id=1, source_target_pairs={{0,6},{2,4},{4,2},{6,0},{8,14},{10,12},{12,10},{14,8},{16,22},{18,... | collective-permute-start | bytes 393224 | tf_op jit(solution)/shard_map/ppermute | solution.py:156
  7.4 8.0 %collective-permute-start.1 = (bf16[256,256]{1,0:T(8,128)(2,1)S(1)}, bf16[256,256]{1,0:T(8,128)(2,1)S(1)}, u32[]{:S(2)}, u32[]{:S(2)}) collective-permute-start(bf16[256,256]{1,0:T(8,128)(2,1)S(1)} %slice.24.refs_0_), channel_id=1, source_target_pairs={{0,4},{2,6},{4,0},{6,2},{8,12},{10,14},{12,8},{14,10},{16,20},{18,... | collective-permute-start | bytes 393224 | tf_op jit(solution)/shard_map/ppermute | solution.py:156
  8.3 7.0 %collective-permute-start = (bf16[256,256]{1,0:T(8,128)(2,1)S(1)}, bf16[256,256]{1,0:T(8,128)(2,1)S(1)}, u32[]{:S(2)}, u32[]{:S(2)}) collective-permute-start(bf16[256,256]{1,0:T(8,128)(2,1)S(1)} %slice.24.refs_0_), channel_id=1, source_target_pairs={{0,2},{2,0},{4,6},{6,4},{8,10},{10,8},{12,14},{14,12},{16,18},{18,... | collective-permute-start | bytes 393224 | tf_op jit(solution)/shard_map/ppermute | solution.py:156
  8.6 5.7 %collective-permute-start.4 = (bf16[128,256]{1,0:T(8,128)(2,1)S(1)}, bf16[128,256]{1,0:T(8,128)(2,1)S(1)}, u32[]{:S(2)}, u32[]{:S(2)}) collective-permute-start(bf16[128,256]{1,0:T(8,128)(2,1)S(1)} %slice.25.refs_4_), channel_id=1, source_target_pairs={{0,16},{2,18},{4,20},{6,22},{8,24},{10,26},{12,28},{14,30},{16,0},... | collective-permute-start | bytes 196616 | tf_op jit(solution)/shard_map/ppermute | solution.py:156
  9.0 5.7 %collective-permute-start.3 = (bf16[128,256]{1,0:T(8,128)(2,1)S(1)}, bf16[128,256]{1,0:T(8,128)(2,1)S(1)}, u32[]{:S(2)}, u32[]{:S(2)}) collective-permute-start(bf16[128,256]{1,0:T(8,128)(2,1)S(1)} %slice.25.refs_4_), channel_id=1, source_target_pairs={{0,8},{2,10},{4,12},{6,14},{8,0},{10,2},{12,4},{14,6},{16,24},{18,... | collective-permute-start | bytes 196616 | tf_op jit(solution)/shard_map/ppermute | solution.py:156
  10.0 0.7 %copy-start = (s32[16,2]{0,1:T(2,128)S(1)}, s32[16,2]{0,1:T(2,128)}, u32[]{:S(2)}) copy-start(s32[16,2]{0,1:T(2,128)} %param.11) | copy-start | bytes 388
  10.7 0.7 %copy-start.1 = (s32[8]{0:T(128)S(1)}, s32[8]{0:T(128)}, u32[]{:S(2)}) copy-start(s32[8]{0:T(128)} %lengths.1) | copy-start | bytes 100
  16.5 3.2 %collective-permute-start.8 = (f32[4,1024]{1,0:T(4,128)S(1)}, f32[4,1024]{1,0:T(4,128)S(1)}, u32[]{:S(2)}, u32[]{:S(2)}) collective-permute-start(f32[4,1024]{1,0:T(4,128)S(1)} %get-tuple-element.10.refs_8_), channel_id=1, source_target_pairs={{0,6},{2,4},{4,2},{6,0},{8,14},{10,12},{12,10},{14,8},{16,22},{18,... | collective-permute-start | bytes 49160 | tf_op jit(solution)/shard_map/ppermute | solution.py:156
  17.2 3.7 %collective-permute-start.7 = (f32[4,1024]{1,0:T(4,128)S(1)}, f32[4,1024]{1,0:T(4,128)S(1)}, u32[]{:S(2)}, u32[]{:S(2)}) collective-permute-start(f32[4,1024]{1,0:T(4,128)S(1)} %get-tuple-element.10.refs_8_), channel_id=1, source_target_pairs={{0,4},{2,6},{4,0},{6,2},{8,12},{10,14},{12,8},{14,10},{16,20},{18,... | collective-permute-start | bytes 49160 | tf_op jit(solution)/shard_map/ppermute | solution.py:156
  18.2 2.7 %collective-permute-start.6 = (f32[4,1024]{1,0:T(4,128)S(1)}, f32[4,1024]{1,0:T(4,128)S(1)}, u32[]{:S(2)}, u32[]{:S(2)}) collective-permute-start(f32[4,1024]{1,0:T(4,128)S(1)} %get-tuple-element.10.refs_8_), channel_id=1, source_target_pairs={{0,2},{2,0},{4,6},{6,4},{8,10},{10,8},{12,14},{14,12},{16,18},{18,... | collective-permute-start | bytes 49160 | tf_op jit(solution)/shard_map/ppermute | solution.py:156
  21.9 5.0 %collective-permute-start.13 = (bf16[256,256]{1,0:T(8,128)(2,1)S(1)}, bf16[256,256]{1,0:T(8,128)(2,1)S(1)}, u32[]{:S(2)}, u32[]{:S(2)}) collective-permute-start(bf16[256,256]{1,0:T(8,128)(2,1)S(1)} %get-tuple-element.16), channel_id=1, source_target_pairs={{0,4},{2,6},{4,0},{6,2},{8,12},{10,14},{12,8},{14,10},{16,20},{18,... | collective-permute-start | bytes 393224 | tf_op jit(solution)/shard_map/ppermute | solution.py:156
  23.0 5.0 %collective-permute-start.9 = (bf16[256,256]{1,0:T(8,128)(2,1)S(1)}, bf16[256,256]{1,0:T(8,128)(2,1)S(1)}, u32[]{:S(2)}, u32[]{:S(2)}) collective-permute-start(bf16[256,256]{1,0:T(8,128)(2,1)S(1)} %get-tuple-element.14), channel_id=1, source_target_pairs={{0,1},{1,0},{2,3},{3,2},{4,5},{5,4},{6,7},{7,6},{8,9},{9,8},{10,11... | collective-permute-start | bytes 393224 | tf_op jit(solution)/shard_map/ppermute | solution.py:159
  27.0 7.7 %collective-permute-start.14 = (bf16[128,256]{1,0:T(8,128)(2,1)S(1)}, bf16[128,256]{1,0:T(8,128)(2,1)S(1)}, u32[]{:S(2)}, u32[]{:S(2)}) collective-permute-start(bf16[128,256]{1,0:T(8,128)(2,1)S(1)} %slice.29), channel_id=1, source_target_pairs={{0,2},{2,0},{4,6},{6,4},{8,10},{10,8},{12,14},{14,12},{16,18},{18,... | collective-permute-start | bytes 196616 | tf_op jit(solution)/shard_map/ppermute | solution.py:156
  28.0 5.8 %collective-permute-start.12 = (bf16[64,256]{1,0:T(8,128)(2,1)S(1)}, bf16[64,256]{1,0:T(8,128)(2,1)S(1)}, u32[]{:S(2)}, u32[]{:S(2)}) collective-permute-start(bf16[64,256]{1,0:T(8,128)(2,1)S(1)} %get-tuple-element.17), channel_id=1, source_target_pairs={{0,24},{2,26},{4,28},{6,30},{8,16},{10,18},{12,20},{14,22},{16,8},... | collective-permute-start | bytes 98312 | tf_op jit(solution)/shard_map/ppermute | solution.py:156
  29.7 4.9 %collective-permute-start.11 = (bf16[64,256]{1,0:T(8,128)(2,1)S(1)}, bf16[64,256]{1,0:T(8,128)(2,1)S(1)}, u32[]{:S(2)}, u32[]{:S(2)}) collective-permute-start(bf16[64,256]{1,0:T(8,128)(2,1)S(1)} %get-tuple-element.18), channel_id=1, source_target_pairs={{0,16},{2,18},{4,20},{6,22},{8,24},{10,26},{12,28},{14,30},{16,0},... | collective-permute-start | bytes 98312 | tf_op jit(solution)/shard_map/ppermute | solution.py:156
  29.7 5.1 %collective-permute-start.10 = (bf16[64,256]{1,0:T(8,128)(2,1)S(1)}, bf16[64,256]{1,0:T(8,128)(2,1)S(1)}, u32[]{:S(2)}, u32[]{:S(2)}) collective-permute-start(bf16[64,256]{1,0:T(8,128)(2,1)S(1)} %get-tuple-element.19), channel_id=1, source_target_pairs={{0,8},{2,10},{4,12},{6,14},{8,0},{10,2},{12,4},{14,6},{16,24},{18,... | collective-permute-start | bytes 98312 | tf_op jit(solution)/shard_map/ppermute | solution.py:156

commit v5 on v4

--- a/solution.py
+++ b/solution.py
@@ -24,26 +24,28 @@
     return group, tuple(range(0, size, 4))
 
 
-def place_kernel(group, chunk, lengths, order, place_ref):
+def place_kernel(group, chunk, docs, ints, place_ref):
     rows = place_ref.shape[1]
+    count = (ints.shape[0] - docs) // 2
     index = lax.axis_index("ctx")
     half = rows // 2
     at = lax.broadcasted_iota(jnp.int32, (1, rows), 1)
     for j, bits in enumerate(group):
-        first = order[0, index ^ bits] * half
-        second = order[1, index ^ bits] * half - half
+        first = ints[docs + (index ^ bits)] * half
+        second = ints[docs + count + (index ^ bits)] * half - half
         pos = at + jnp.where(at < half, first, second)
         start = jnp.int32(0)
         opens = jnp.zeros_like(pos)
-        for d in range(lengths.shape[0]):
+        for d in range(docs):
             opens = jnp.where(pos >= start, start, opens)
-            start = start + lengths[d]
+            start = start + ints[d]
         place_ref[j : j + 1, :] = pos
         place_ref[GROUP + j : GROUP + j + 1, :] = opens
     for b, bits in enumerate(chunk):
         for h in range(2):
             to = 2 * GROUP + 2 * b + h
-            place_ref[to : to + 1, :] = jnp.full((1, rows), order[h, index ^ bits] * half)
+            base = ints[docs + h * count + (index ^ bits)] * half
+            place_ref[to : to + 1, :] = jnp.full((1, rows), base)
 
 
 def both_heads(ref, heads, which):
@@ -54,7 +56,8 @@
 
 def stats_kernel(chunks, heads, place_ref, *refs):
     group, chunk = refs[:GROUP], refs[GROUP : GROUP + chunks]
-    out_ref, expo_ref, dprobs_ref = refs[GROUP + chunks :]
+    out_ref, top_ref, expo_ref, dprobs_ref = refs[GROUP + chunks :]
+    group = (*group[:-1], group[-1].at[1 - lax.axis_index("ctx") % 2])
     rows, width = chunk[0].shape
     hd = width // 2
     factor = hd ** (-0.5) * log2_e
@@ -73,10 +76,11 @@
         dprobs = dot(values, both_heads(group[j], heads, 1), NT)
         top = jnp.max(scores, axis=0, keepdims=True)
         expo = jnp.exp2(scores - top)
+        total = jnp.sum(expo, axis=0, keepdims=True)
         at = pl.ds(j * heads * rows, heads * rows)
-        out_ref[0:1, at] = top
-        out_ref[1:2, at] = jnp.sum(expo, axis=0, keepdims=True)
-        out_ref[2:3, at] = jnp.sum(expo * dprobs, axis=0, keepdims=True)
+        out_ref[0:1, at] = top + jnp.log2(total)
+        out_ref[1:2, at] = jnp.sum(expo * dprobs, axis=0, keepdims=True) / total
+        top_ref[0:1, at] = top
         expo_ref[:, at] = expo
         dprobs_ref[:, at] = dprobs
 
@@ -84,9 +88,10 @@
 def backward_kernel(chunks, heads, shards, *refs):
     group, chunk = refs[:GROUP], refs[GROUP : GROUP + chunks]
     stats = refs[GROUP + chunks : 2 * GROUP + chunks]
-    expo_ref, dprobs_ref, near_ref, far_ref = refs[2 * GROUP + chunks : 2 * GROUP + chunks + 4]
-    outs = refs[2 * GROUP + chunks + 4 : -2]
+    top_ref, expo_ref, dprobs_ref, near_ref, far_ref = refs[2 * GROUP + chunks :][:5]
+    outs = refs[2 * GROUP + chunks + 5 : -2]
     dv_total, dk_total = refs[-2:]
+    group = (*group[:-1], group[-1].at[1 - lax.axis_index("ctx") % 2])
     rows, width = chunk[0].shape
     hd = width // 2
     shard = lax.axis_index("head")
@@ -94,15 +99,15 @@
     keys = jnp.concatenate([c[:, :hd] for c in chunk], axis=0)
     keys_across = keys.T
     for j in range(GROUP):
+        at = pl.ds(j * heads * rows, heads * rows)
         parts = [
-            s[0:3, pl.ds((j ^ t) * heads * rows, heads * rows)] for t, s in enumerate(stats)
+            s[0:2, pl.ds((j ^ t) * heads * rows, heads * rows)] for t, s in enumerate(stats)
         ]
-        top = functools.reduce(jnp.maximum, [p[0:1] for p in parts])
-        weight = [jnp.exp2(p[0:1] - top) for p in parts]
-        total = sum(w * p[1:2] for w, p in zip(weight, parts))
-        delta = sum(w * p[2:3] for w, p in zip(weight, parts)) / total
-        own = weight[0] / total
-        at = pl.ds(j * heads * rows, heads * rows)
+        largest = functools.reduce(jnp.maximum, [p[0:1] for p in parts])
+        share = [jnp.exp2(p[0:1] - largest) for p in parts]
+        total = sum(share)
+        delta = sum(w * p[1:2] for w, p in zip(share, parts)) / total
+        own = jnp.exp2(top_ref[0:1, at] - largest) / total
         weights = expo_ref[:, at] * own
         weights_low = weights.astype(jnp.bfloat16)
         dscores = (weights * (dprobs_ref[:, at] - delta)).astype(jnp.bfloat16)
@@ -116,9 +121,9 @@
             dk_total[...] += dk
         dq = ((dot(keys_across, dscores, NN) * scaling).T).astype(jnp.bfloat16)
         half = GROUP // 2
-        to = (near_ref, far_ref)[j // half]
+        to = (near_ref, far_ref)[j % half]
         for h in range(heads):
-            to[pl.ds(j % half * rows, rows), h * hd : (h + 1) * hd] = dq[h * rows : (h + 1) * rows]
+            to[pl.ds(j // half * rows, rows), h * hd : (h + 1) * hd] = dq[h * rows : (h + 1) * rows]
     part = rows // shards
     for t in range(shards):
         owner = lax.rem(shard + t, shards)
@@ -166,13 +171,13 @@
         return jax.ShapeDtypeStruct(shape, dtype)
 
     place = pl.pallas_call(
-        functools.partial(place_kernel, group_bits, chunk_bits),
+        functools.partial(place_kernel, group_bits, chunk_bits, doc_lengths.shape[0]),
         out_shape=array((2 * (GROUP + chunks), rows), jnp.int32),
-        in_specs=[pl.BlockSpec(memory_space=pltpu.SMEM)] * 2,
+        in_specs=[pl.BlockSpec(memory_space=pltpu.SMEM)],
         out_specs=vmem,
         compiler_params=small,
         name="place",
-    )(doc_lengths, span_order.T)
+    )(jnp.concatenate([doc_lengths, span_order.T.reshape(-1)]))
 
     packed = jnp.concatenate(
         [jnp.concatenate([key_rows, value_rows], axis=1), queries, out_grad], axis=0
@@ -180,14 +185,23 @@
     packed = lax.optimization_barrier(packed)
     packed_kv, packed_qg = packed[:rows], packed[rows:]
     chunk = [packed_kv] + [swap(packed_kv, bits) for bits in chunk_bits[1:]]
-    group = [packed_qg] + [swap(packed_qg, bits) for bits in group_bits[1:]]
+    across = swap(packed_qg, group_bits[2])
+    beside = swap(packed_qg, group_bits[1])
+    pairs = [[i, i + 1] for i in range(0, ctx_size, 2)]
+    both = lax.all_gather(across, "ctx", axis_index_groups=pairs)
+    group = [packed_qg, beside, across, both]
 
     square = array((chunks * rows, GROUP * heads * rows), jnp.float32)
-    stats, expo, dprobs = pl.pallas_call(
+    stats, top, expo, dprobs = pl.pallas_call(
         functools.partial(stats_kernel, chunks, heads),
-        out_shape=(array((4, GROUP * heads * rows), jnp.float32), square, square),
+        out_shape=(
+            array((2, GROUP * heads * rows), jnp.float32),
+            array((1, GROUP * heads * rows), jnp.float32),
+            square,
+            square,
+        ),
         in_specs=[vmem] * (1 + GROUP + chunks),
-        out_specs=(vmem, vmem, vmem),
+        out_specs=(vmem, vmem, vmem, vmem),
         compiler_params=params,
         name="stats",
     )(place, *group, *chunk)
@@ -198,12 +212,12 @@
     near, far, *dkv = pl.pallas_call(
         functools.partial(backward_kernel, chunks, heads, shards),
         out_shape=(half, half) + (piece,) * shards,
-        in_specs=[vmem] * (2 * GROUP + chunks + 2),
+        in_specs=[vmem] * (2 * GROUP + chunks + 3),
         out_specs=(vmem,) * (2 + shards),
         scratch_shapes=[pltpu.VMEM((chunks * rows, hd), jnp.float32)] * 2,
         compiler_params=params,
         name="backward",
-    )(*group, *chunk, *all_stats, expo, dprobs)
+    )(*group, *chunk, *all_stats, top, expo, dprobs)
 
     owned = dkv[0].astype(jnp.float32)
     for t in range(1, shards):
@@ -212,8 +226,8 @@
     came = [
         swap(owned[b * part : (b + 1) * part], chunk_bits[b]) for b in range(1, chunks)
     ]
-    pair = (near.astype(jnp.float32) + swap(far, group_bits[2]).astype(jnp.float32)).astype(jnp.bfloat16)
-    other = swap(pair[rows:], group_bits[1])
+    pair = (near.astype(jnp.float32) + swap(far, group_bits[1]).astype(jnp.float32)).astype(jnp.bfloat16)
+    other = swap(pair[rows:], group_bits[2])
     return tuple(
         pl.pallas_call(
             functools.partial(finish_kernel, chunks),

time: 35.6 us -> 34.9 us (0.980)
  waiting for transfers between devices: 11.9 us -> 9.04 us
  blocking collectives: 0 us -> 2.14 us
  other arithmetic: 0.96 us -> 1.69 us
  local copies, waits for them, and re-layouts: 1.36 us -> 0.79 us
    ppermute x14 -> x13, waiting for transfers between devices: 11 us -> 6.35 us  [swap(): return lax.ppermute(x, 'ctx', [(i, i ^ bits) for i in range(ctx_size)])]
    all_gather x0 -> x1, blocking collectives: none -> 2.14 us  [local(): both = lax.all_gather(across, 'ctx', axis_index_groups=pairs)]
    ppermute x1, waiting for transfers between devices: 0.89 us -> 2.69 us  [turn(): lax.ppermute(x, 'head', [(i, (i + by) % shards) for i in range(shards)])]
    unnamed x4 -> x0, local copies, waits for them, and re-layouts: 1.33 us -> none
    reshape x0 -> x1, local copies, waits for them, and re-layouts: none -> 0.76 us  [local(): span_order.T.reshape(-1)]
    concatenate x0 -> x1, other arithmetic: none -> 0.73 us  [local(): jnp.concatenate([doc_lengths, span_order.T.reshape(-1)])]
    ppermute x14 -> x13, starting transfers between devices: 15.6 us -> 15.4 us  [swap(): return lax.ppermute(x, 'ctx', [(i, i ^ bits) for i in range(ctx_size)])]
  transfers between devices with their start and end apart: 15 -> 14, of which waited for: 11 -> 7; matrix products, arithmetic and copies ran while one was open for 0% -> 5% of each run, Pallas kernels for 2% -> 2%
where the time goes in v5:
time: 34.9 us; the launch traced here: 34.7 us
  starting transfers between devices  17 us (49%)
  waiting for transfers between devices  9.04 us (26%)
  Pallas kernels  3.36 us (10%)
  blocking collectives  2.14 us (6%)
  other arithmetic  1.69 us (5%)
  local copies, waits for them, and re-layouts  0.79 us (2%)
  between operations  0.72 us (2%)
    ppermute x13, starting transfers between devices, swap(): return lax.ppermute(x, 'ctx', [(i, i ^ bits) for i in range(ctx_size)])  15.4 us
    ppermute x13, waiting for transfers between devices, swap(): return lax.ppermute(x, 'ctx', [(i, i ^ bits) for i in range(ctx_size)])  6.35 us
    ppermute x1, waiting for transfers between devices, turn(): lax.ppermute(x, 'head', [(i, (i + by) % shards) for i in range(shards)])  2.69 us
    all_gather x1, blocking collectives, local(): both = lax.all_gather(across, 'ctx', axis_index_groups=pairs)  2.14 us
    ppermute x1, starting transfers between devices, turn(): lax.ppermute(x, 'head', [(i, (i + by) % shards) for i in range(shards)])  1.61 us
    pallas_call x1, Pallas kernels, local(): pl.pallas_call(functools.partial(stats_kernel, chunks, heads), out_shape=...  1.14 us
    pallas_call x1, Pallas kernels, local(): pl.pallas_call(functools.partial(backward_kernel, chunks, heads, shards),...  0.99 us
    concatenate x1, other arithmetic, local(): jnp.concatenate([jnp.concatenate([key_rows, value_rows], axis=1), queries...  0.89 us
  transfers between devices with their start and end apart: 14, of which 7 were waited for; matrix products, arithmetic and copies ran while one was open for 5% of the time, Pallas kernels for 2%

profile of v5, /device:TPU:0, one launch (start us, length us, event | category | flops | bytes accessed | tf_op | source)
XLA Modules:
  0.0 34.7 jit_solution(15871194714694519581)
XLA Ops:
  0.6 0.9 %pad_maximum_fusion = bf16[384,256]{1,0:T(8,128)(2,1)S(1)} fusion(bf16[128,256]{1,0:T(8,128)(2,1)} %param.9, bf16[128,256]{1,0:T(8,128)(2,1)} %param.6, bf16[128,128]{1,0:T(8,128)(2,1)} %param.8, bf16[128,128]{1,0:T(8,128)(2,1)} %param.7), kind=kLoop, calls=%fused_computation.2 | loop fusion | flops 786432 | bytes 393216 | tf_op jit(solution)/shard_map/concatenate | solution.py:182
  1.5 3.0 %collective-permute-start.1 = (bf16[256,256]{1,0:T(8,128)(2,1)S(1)}, bf16[256,256]{1,0:T(8,128)(2,1)S(1)}, u32[]{:S(2)}, u32[]{:S(2)}) collective-permute-start(bf16[256,256]{1,0:T(8,128)(2,1)S(1)} %slice.24.refs_0_), channel_id=1, source_target_pairs={{0,4},{2,6},{4,0},{6,2},{8,12},{10,14},{12,8},{14,10},{16,20},{18,... | collective-permute-start | bytes 393224 | tf_op jit(solution)/shard_map/ppermute | solution.py:161
  4.6 3.6 %collective-permute-start.4 = (bf16[128,256]{1,0:T(8,128)(2,1)S(1)}, bf16[128,256]{1,0:T(8,128)(2,1)S(1)}, u32[]{:S(2)}, u32[]{:S(2)}) collective-permute-start(bf16[128,256]{1,0:T(8,128)(2,1)S(1)} %slice.25.refs_4_), channel_id=1, source_target_pairs={{0,24},{2,26},{4,28},{6,30},{8,16},{10,18},{12,20},{14,22},{16,8},... | collective-permute-start | bytes 196616 | tf_op jit(solution)/shard_map/ppermute | solution.py:161
  8.2 0.0 collective-permute-start.3
  8.2 0.8 %collective-permute-start.2 = (bf16[128,256]{1,0:T(8,128)(2,1)S(1)}, bf16[128,256]{1,0:T(8,128)(2,1)S(1)}, u32[]{:S(2)}, u32[]{:S(2)}) collective-permute-start(bf16[128,256]{1,0:T(8,128)(2,1)S(1)} %slice.25.refs_4_), channel_id=1, source_target_pairs={{0,8},{2,10},{4,12},{6,14},{8,0},{10,2},{12,4},{14,6},{16,24},{18,... | collective-permute-start | bytes 196616 | tf_op jit(solution)/shard_map/ppermute | solution.py:161
  8.9 0.0 collective-permute-start
  8.9 0.8 %reshape.9 = s32[32]{0:T(128)S(1)} reshape(s32[2,16]{1,0:T(2,128)} %bitcast.4) | data formatting | bytes 256 | tf_op jit(solution)/shard_map/reshape | solution.py:180
  9.7 0.7 %pad_add_fusion.ints = s32[40]{0:T(128)S(1)} fusion(s32[32]{0:T(128)S(1)} %reshape.9, s32[8]{0:T(128)} %param.10), kind=kLoop, calls=%fused_computation.3 | loop fusion | flops 40 | bytes 320 | tf_op jit(solution)/shard_map/concatenate | solution.py:180
  10.4 0.6 %place.1.place_ref = s32[16,128]{1,0:T(8,128)S(1)} custom-call(s32[40]{0:T(128)S(1)} %pad_add_fusion.ints), custom_call_target="tpu_custom_call" | custom-call | tf_op jit(solution)/shard_map/place/pallas_call | solution.py:173
  11.0 0.0 collective-permute-done.1.refs_2_
  11.0 2.1 %all-gather = bf16[512,256]{1,0:T(8,128)(2,1)S(1)} all-gather(bf16[256,256]{1,0:T(8,128)(2,1)S(1)} %collective-permute-done.1.refs_2_), channel_id=2, replica_groups={{0,2},{4,6},{8,10},{12,14},{16,18},{20,22},{24,26},{28,30},{1,3},{5,7},..., dimensions={0}, use_global_device_ids=true | all-gather | bytes 393216 | tf_op jit(solution)/shard_map/all_gather | solution.py:191
  13.2 0.0 collective-permute-done.4.refs_7_
  13.2 0.4 %collective-permute-done.3.refs_6_ = bf16[128,256]{1,0:T(8,128)(2,1)S(1)} collective-permute-done((bf16[128,256]{1,0:T(8,128)(2,1)S(1)}, bf16[128,256]{1,0:T(8,128)(2,1)S(1)}, u32[]{:S(2)}, u32[]{:S(2)}) %collective-permute-start.3) | collective-permute-done | bytes 65568 | tf_op jit(solution)/shard_map/ppermute | solution.py:161
  13.5 0.1 collective-permute-done.2.refs_5_
  13.6 0.0 collective-permute-done.refs_1_
  13.6 1.1 %stats.1 = (f32[2,1024]{1,0:T(2,128)S(1)}, f32[1,1024]{1,0:T(1,128)S(1)}, f32[512,1024]{1,0:T(8,128)S(1)}, f32[512,1024]{1,0:T(8,128)S(1)}) custom-call(s32[16,128]{1,0:T(8,128)S(1)} %place.1.place_ref, bf16[256,256]{1,0:T(8,128)(2,1)S(1)} %slice.24.refs_0_, bf16[256,256]{1,0:T(8,128)(2,1)S(1)} %collective-permute-done.refs_1_, ...), custom_call_target="tpu_custom_call" | custom-call | tf_op jit(solution)/shard_map/stats/pallas_call | solution.py:195
  14.7 0.1 collective-permute-start.7
  14.8 1.6 %collective-permute-start.6 = (f32[2,1024]{1,0:T(2,128)S(1)}, f32[2,1024]{1,0:T(2,128)S(1)}, u32[]{:S(2)}, u32[]{:S(2)}) collective-permute-start(f32[2,1024]{1,0:T(2,128)S(1)} %get-tuple-element.11.refs_8_), channel_id=1, source_target_pairs={{0,4},{2,6},{4,0},{6,2},{8,12},{10,14},{12,8},{14,10},{16,20},{18,... | collective-permute-start | bytes 24584 | tf_op jit(solution)/shard_map/ppermute | solution.py:161
  16.4 0.3 collective-permute-start.5
  16.7 1.2 %collective-permute-done.7.refs_11_ = f32[2,1024]{1,0:T(2,128)S(1)} collective-permute-done((f32[2,1024]{1,0:T(2,128)S(1)}, f32[2,1024]{1,0:T(2,128)S(1)}, u32[]{:S(2)}, u32[]{:S(2)}) %collective-permute-start.7) | collective-permute-done | bytes 8224 | tf_op jit(solution)/shard_map/ppermute | solution.py:161
  17.9 0.7 %collective-permute-done.6.refs_10_ = f32[2,1024]{1,0:T(2,128)S(1)} collective-permute-done((f32[2,1024]{1,0:T(2,128)S(1)}, f32[2,1024]{1,0:T(2,128)S(1)}, u32[]{:S(2)}, u32[]{:S(2)}) %collective-permute-start.6) | collective-permute-done | bytes 8224 | tf_op jit(solution)/shard_map/ppermute | solution.py:161
  18.5 0.0 collective-permute-done.5.refs_9_
  18.5 1.0 %backward.1 = (bf16[256,256]{1,0:T(8,128)(2,1)S(1)}, bf16[256,256]{1,0:T(8,128)(2,1)S(1)}, bf16[256,256]{1,0:T(8,128)(2,1)S(1)}, bf16[256,256]{1,0:T(8,128)(2,1)S(1)}) custom-call(bf16[256,256]{1,0:T(8,128)(2,1)S(1)} %slice.24.refs_0_, bf16[256,256]{1,0:T(8,128)(2,1)S(1)} %collective-permute-done.refs_1_, ...), custom_call_target="tpu_custom_call" | custom-call | tf_op jit(solution)/shard_map/backward/pallas_call | solution.py:212
  19.5 0.1 collective-permute-start.12
  19.6 1.6 %collective-permute-start.8 = (bf16[256,256]{1,0:T(8,128)(2,1)S(1)}, bf16[256,256]{1,0:T(8,128)(2,1)S(1)}, u32[]{:S(2)}, u32[]{:S(2)}) collective-permute-start(bf16[256,256]{1,0:T(8,128)(2,1)S(1)} %get-tuple-element.16), channel_id=1, source_target_pairs={{0,1},{1,0},{2,3},{3,2},{4,5},{5,4},{6,7},{7,6},{8,9},{9,8},{10,11... | collective-permute-start | bytes 393224 | tf_op jit(solution)/shard_map/ppermute | solution.py:164
  21.2 0.0 collective-permute-done.12
  21.3 1.6 %collective-permute-start.13 = (bf16[128,256]{1,0:T(8,128)(2,1)S(1)}, bf16[128,256]{1,0:T(8,128)(2,1)S(1)}, u32[]{:S(2)}, u32[]{:S(2)}) collective-permute-start(bf16[128,256]{1,0:T(8,128)(2,1)S(1)} %slice.29), channel_id=1, source_target_pairs={{0,4},{2,6},{4,0},{6,2},{8,12},{10,14},{12,8},{14,10},{16,20},{18,... | collective-permute-start | bytes 196616 | tf_op jit(solution)/shard_map/ppermute | solution.py:161
  22.8 2.7 %collective-permute-done.8 = bf16[256,256]{1,0:T(8,128)(2,1)S(1)} collective-permute-done((bf16[256,256]{1,0:T(8,128)(2,1)S(1)}, bf16[256,256]{1,0:T(8,128)(2,1)S(1)}, u32[]{:S(2)}, u32[]{:S(2)}) %collective-permute-start.8) | collective-permute-done | bytes 131104 | tf_op jit(solution)/shard_map/ppermute | solution.py:164
  25.6 3.7 %collective-permute-start.11 = (bf16[64,256]{1,0:T(8,128)(2,1)S(1)}, bf16[64,256]{1,0:T(8,128)(2,1)S(1)}, u32[]{:S(2)}, u32[]{:S(2)}) collective-permute-start(bf16[64,256]{1,0:T(8,128)(2,1)S(1)} %get-tuple-element.19), channel_id=1, source_target_pairs={{0,24},{2,26},{4,28},{6,30},{8,16},{10,18},{12,20},{14,22},{16,8},... | collective-permute-start | bytes 98312 | tf_op jit(solution)/shard_map/ppermute | solution.py:161
  29.3 0.0 collective-permute-start.10
  29.3 0.8 %collective-permute-start.9 = (bf16[64,256]{1,0:T(8,128)(2,1)S(1)}, bf16[64,256]{1,0:T(8,128)(2,1)S(1)}, u32[]{:S(2)}, u32[]{:S(2)}) collective-permute-start(bf16[64,256]{1,0:T(8,128)(2,1)S(1)} %get-tuple-element.21), channel_id=1, source_target_pairs={{0,8},{2,10},{4,12},{6,14},{8,0},{10,2},{12,4},{14,6},{16,24},{18,... | collective-permute-start | bytes 98312 | tf_op jit(solution)/shard_map/ppermute | solution.py:161
  30.0 1.4 %collective-permute-done.11.refs_2_ = bf16[64,256]{1,0:T(8,128)(2,1)S(1)} collective-permute-done((bf16[64,256]{1,0:T(8,128)(2,1)S(1)}, bf16[64,256]{1,0:T(8,128)(2,1)S(1)}, u32[]{:S(2)}, u32[]{:S(2)}) %collective-permute-start.11) | collective-permute-done | bytes 32800 | tf_op jit(solution)/shard_map/ppermute | solution.py:161
  31.4 2.7 %collective-permute-done.10.refs_1_ = bf16[64,256]{1,0:T(8,128)(2,1)S(1)} collective-permute-done((bf16[64,256]{1,0:T(8,128)(2,1)S(1)}, bf16[64,256]{1,0:T(8,128)(2,1)S(1)}, u32[]{:S(2)}, u32[]{:S(2)}) %collective-permute-start.10) | collective-permute-done | bytes 32800 | tf_op jit(solution)/shard_map/ppermute | solution.py:161
  34.1 0.0 collective-permute-done.9.refs_0_
  34.1 0.0 collective-permute-done.13.refs_4_
  34.1 0.7 %finish.1 = (bf16[128,256]{1,0:T(8,128)(2,1)}, bf16[64,128]{1,0:T(8,128)(2,1)}, bf16[64,128]{1,0:T(8,128)(2,1)}) custom-call(bf16[256,256]{1,0:T(8,128)(2,1)S(1)} %add_convert_fusion.1.owned_ref, bf16[64,256]{1,0:T(8,128)(2,1)S(1)} %collective-permute-done.9.refs_0_, bf16[64,256]{1,0:T(8,128)(2,1)S(1)} %collective-permute-done.10.refs_1_, ...), custom_call_target="tpu_custom_call" | custom-call | tf_op jit(solution)/shard_map/finish/pallas_call | solution.py:232
  (6 shorter events, 0.1 us)
Async XLA Ops:
  1.5 9.5 %collective-permute-start.1 = (bf16[256,256]{1,0:T(8,128)(2,1)S(1)}, bf16[256,256]{1,0:T(8,128)(2,1)S(1)}, u32[]{:S(2)}, u32[]{:S(2)}) collective-permute-start(bf16[256,256]{1,0:T(8,128)(2,1)S(1)} %slice.24.refs_0_), channel_id=1, source_target_pairs={{0,4},{2,6},{4,0},{6,2},{8,12},{10,14},{12,8},{14,10},{16,20},{18,... | collective-permute-start | bytes 393224 | tf_op jit(solution)/shard_map/ppermute | solution.py:161
  4.6 8.6 %collective-permute-start.4 = (bf16[128,256]{1,0:T(8,128)(2,1)S(1)}, bf16[128,256]{1,0:T(8,128)(2,1)S(1)}, u32[]{:S(2)}, u32[]{:S(2)}) collective-permute-start(bf16[128,256]{1,0:T(8,128)(2,1)S(1)} %slice.25.refs_4_), channel_id=1, source_target_pairs={{0,24},{2,26},{4,28},{6,30},{8,16},{10,18},{12,20},{14,22},{16,8},... | collective-permute-start | bytes 196616 | tf_op jit(solution)/shard_map/ppermute | solution.py:161
  8.2 5.4 %collective-permute-start.3 = (bf16[128,256]{1,0:T(8,128)(2,1)S(1)}, bf16[128,256]{1,0:T(8,128)(2,1)S(1)}, u32[]{:S(2)}, u32[]{:S(2)}) collective-permute-start(bf16[128,256]{1,0:T(8,128)(2,1)S(1)} %slice.25.refs_4_), channel_id=1, source_target_pairs={{0,16},{2,18},{4,20},{6,22},{8,24},{10,26},{12,28},{14,30},{16,0},... | collective-permute-start | bytes 196616 | tf_op jit(solution)/shard_map/ppermute | solution.py:161
  8.2 5.4 %collective-permute-start.2 = (bf16[128,256]{1,0:T(8,128)(2,1)S(1)}, bf16[128,256]{1,0:T(8,128)(2,1)S(1)}, u32[]{:S(2)}, u32[]{:S(2)}) collective-permute-start(bf16[128,256]{1,0:T(8,128)(2,1)S(1)} %slice.25.refs_4_), channel_id=1, source_target_pairs={{0,8},{2,10},{4,12},{6,14},{8,0},{10,2},{12,4},{14,6},{16,24},{18,... | collective-permute-start | bytes 196616 | tf_op jit(solution)/shard_map/ppermute | solution.py:161
  8.9 4.6 %collective-permute-start = (bf16[256,256]{1,0:T(8,128)(2,1)S(1)}, bf16[256,256]{1,0:T(8,128)(2,1)S(1)}, u32[]{:S(2)}, u32[]{:S(2)}) collective-permute-start(bf16[256,256]{1,0:T(8,128)(2,1)S(1)} %slice.24.refs_0_), channel_id=1, source_target_pairs={{0,2},{2,0},{4,6},{6,4},{8,10},{10,8},{12,14},{14,12},{16,18},{18,... | collective-permute-start | bytes 393224 | tf_op jit(solution)/shard_map/ppermute | solution.py:161
  14.7 3.1 %collective-permute-start.7 = (f32[2,1024]{1,0:T(2,128)S(1)}, f32[2,1024]{1,0:T(2,128)S(1)}, u32[]{:S(2)}, u32[]{:S(2)}) collective-permute-start(f32[2,1024]{1,0:T(2,128)S(1)} %get-tuple-element.11.refs_8_), channel_id=1, source_target_pairs={{0,6},{2,4},{4,2},{6,0},{8,14},{10,12},{12,10},{14,8},{16,22},{18,... | collective-permute-start | bytes 24584 | tf_op jit(solution)/shard_map/ppermute | solution.py:161
  14.8 3.7 %collective-permute-start.6 = (f32[2,1024]{1,0:T(2,128)S(1)}, f32[2,1024]{1,0:T(2,128)S(1)}, u32[]{:S(2)}, u32[]{:S(2)}) collective-permute-start(f32[2,1024]{1,0:T(2,128)S(1)} %get-tuple-element.11.refs_8_), channel_id=1, source_target_pairs={{0,4},{2,6},{4,0},{6,2},{8,12},{10,14},{12,8},{14,10},{16,20},{18,... | collective-permute-start | bytes 24584 | tf_op jit(solution)/shard_map/ppermute | solution.py:161
  16.4 2.1 %collective-permute-start.5 = (f32[2,1024]{1,0:T(2,128)S(1)}, f32[2,1024]{1,0:T(2,128)S(1)}, u32[]{:S(2)}, u32[]{:S(2)}) collective-permute-start(f32[2,1024]{1,0:T(2,128)S(1)} %get-tuple-element.11.refs_8_), channel_id=1, source_target_pairs={{0,2},{2,0},{4,6},{6,4},{8,10},{10,8},{12,14},{14,12},{16,18},{18,... | collective-permute-start | bytes 24584 | tf_op jit(solution)/shard_map/ppermute | solution.py:161
  19.5 1.7 %collective-permute-start.12 = (bf16[256,256]{1,0:T(8,128)(2,1)S(1)}, bf16[256,256]{1,0:T(8,128)(2,1)S(1)}, u32[]{:S(2)}, u32[]{:S(2)}) collective-permute-start(bf16[256,256]{1,0:T(8,128)(2,1)S(1)} %get-tuple-element.18), channel_id=1, source_target_pairs={{0,2},{2,0},{4,6},{6,4},{8,10},{10,8},{12,14},{14,12},{16,18},{18,... | collective-permute-start | bytes 393224 | tf_op jit(solution)/shard_map/ppermute | solution.py:161
  19.6 5.9 %collective-permute-start.8 = (bf16[256,256]{1,0:T(8,128)(2,1)S(1)}, bf16[256,256]{1,0:T(8,128)(2,1)S(1)}, u32[]{:S(2)}, u32[]{:S(2)}) collective-permute-start(bf16[256,256]{1,0:T(8,128)(2,1)S(1)} %get-tuple-element.16), channel_id=1, source_target_pairs={{0,1},{1,0},{2,3},{3,2},{4,5},{5,4},{6,7},{7,6},{8,9},{9,8},{10,11... | collective-permute-start | bytes 393224 | tf_op jit(solution)/shard_map/ppermute | solution.py:164
  21.3 12.8 %collective-permute-start.13 = (bf16[128,256]{1,0:T(8,128)(2,1)S(1)}, bf16[128,256]{1,0:T(8,128)(2,1)S(1)}, u32[]{:S(2)}, u32[]{:S(2)}) collective-permute-start(bf16[128,256]{1,0:T(8,128)(2,1)S(1)} %slice.29), channel_id=1, source_target_pairs={{0,4},{2,6},{4,0},{6,2},{8,12},{10,14},{12,8},{14,10},{16,20},{18,... | collective-permute-start | bytes 196616 | tf_op jit(solution)/shard_map/ppermute | solution.py:161
  25.6 5.8 %collective-permute-start.11 = (bf16[64,256]{1,0:T(8,128)(2,1)S(1)}, bf16[64,256]{1,0:T(8,128)(2,1)S(1)}, u32[]{:S(2)}, u32[]{:S(2)}) collective-permute-start(bf16[64,256]{1,0:T(8,128)(2,1)S(1)} %get-tuple-element.19), channel_id=1, source_target_pairs={{0,24},{2,26},{4,28},{6,30},{8,16},{10,18},{12,20},{14,22},{16,8},... | collective-permute-start | bytes 98312 | tf_op jit(solution)/shard_map/ppermute | solution.py:161
  29.3 4.8 %collective-permute-start.10 = (bf16[64,256]{1,0:T(8,128)(2,1)S(1)}, bf16[64,256]{1,0:T(8,128)(2,1)S(1)}, u32[]{:S(2)}, u32[]{:S(2)}) collective-permute-start(bf16[64,256]{1,0:T(8,128)(2,1)S(1)} %get-tuple-element.20), channel_id=1, source_target_pairs={{0,16},{2,18},{4,20},{6,22},{8,24},{10,26},{12,28},{14,30},{16,0},... | collective-permute-start | bytes 98312 | tf_op jit(solution)/shard_map/ppermute | solution.py:161
  29.3 4.8 %collective-permute-start.9 = (bf16[64,256]{1,0:T(8,128)(2,1)S(1)}, bf16[64,256]{1,0:T(8,128)(2,1)S(1)}, u32[]{:S(2)}, u32[]{:S(2)}) collective-permute-start(bf16[64,256]{1,0:T(8,128)(2,1)S(1)} %get-tuple-element.21), channel_id=1, source_target_pairs={{0,8},{2,10},{4,12},{6,14},{8,0},{10,2},{12,4},{14,6},{16,24},{18,... | collective-permute-start | bytes 98312 | tf_op jit(solution)/shard_map/ppermute | solution.py:161

commit v6 on v5

--- a/solution.py
+++ b/solution.py
@@ -57,7 +57,6 @@
 def stats_kernel(chunks, heads, place_ref, *refs):
     group, chunk = refs[:GROUP], refs[GROUP : GROUP + chunks]
     out_ref, top_ref, expo_ref, dprobs_ref = refs[GROUP + chunks :]
-    group = (*group[:-1], group[-1].at[1 - lax.axis_index("ctx") % 2])
     rows, width = chunk[0].shape
     hd = width // 2
     factor = hd ** (-0.5) * log2_e
@@ -91,7 +90,6 @@
     top_ref, expo_ref, dprobs_ref, near_ref, far_ref = refs[2 * GROUP + chunks :][:5]
     outs = refs[2 * GROUP + chunks + 5 : -2]
     dv_total, dk_total = refs[-2:]
-    group = (*group[:-1], group[-1].at[1 - lax.axis_index("ctx") % 2])
     rows, width = chunk[0].shape
     hd = width // 2
     shard = lax.axis_index("head")
@@ -176,6 +174,7 @@
         in_specs=[pl.BlockSpec(memory_space=pltpu.SMEM)],
         out_specs=vmem,
         compiler_params=small,
+        cost_estimate=pl.CostEstimate(flops=1000000000, bytes_accessed=0, transcendentals=0),
         name="place",
     )(jnp.concatenate([doc_lengths, span_order.T.reshape(-1)]))
 
@@ -187,9 +186,7 @@
     chunk = [packed_kv] + [swap(packed_kv, bits) for bits in chunk_bits[1:]]
     across = swap(packed_qg, group_bits[2])
     beside = swap(packed_qg, group_bits[1])
-    pairs = [[i, i + 1] for i in range(0, ctx_size, 2)]
-    both = lax.all_gather(across, "ctx", axis_index_groups=pairs)
-    group = [packed_qg, beside, across, both]
+    group = [packed_qg, beside, across, swap(across, group_bits[1])]
 
     square = array((chunks * rows, GROUP * heads * rows), jnp.float32)
     stats, top, expo, dprobs = pl.pallas_call(

time: 34.9 us -> 33.9 us (0.971)
  blocking collectives: 2.14 us -> 0 us
  waiting for transfers between devices: 9.04 us -> 10.2 us
    all_gather x1 -> x0, blocking collectives: 2.14 us -> none  [local(): both = lax.all_gather(across, 'ctx', axis_index_groups=pairs)]
    ppermute x13 -> x14, waiting for transfers between devices: 6.35 us -> 6.97 us  [swap(): return lax.ppermute(x, 'ctx', [(i, i ^ bits) for i in range(ctx_size)])]
    ppermute x1, waiting for transfers between devices: 2.69 us -> 3.19 us  [turn(): lax.ppermute(x, 'head', [(i, (i + by) % shards) for i in range(shards)])]
    ppermute x13 -> x14, starting transfers between devices: 15.4 us -> 15.4 us  [swap(): return lax.ppermute(x, 'ctx', [(i, i ^ bits) for i in range(ctx_size)])]
  transfers between devices with their start and end apart: 14 -> 15, of which waited for: 7 -> 7; matrix products, arithmetic and copies ran while one was open for 5% -> 5% of each run, Pallas kernels for 2% -> 2%
where the time goes in v6:
time: 33.9 us; the launch traced here: 33.7 us
  starting transfers between devices  17 us (50%)
  waiting for transfers between devices  10.2 us (30%)
  Pallas kernels  3.36 us (10%)
  other arithmetic  1.69 us (5%)
  local copies, waits for them, and re-layouts  0.79 us (2%)
  between operations  0.72 us (2%)
    ppermute x14, starting transfers between devices, swap(): return lax.ppermute(x, 'ctx', [(i, i ^ bits) for i in range(ctx_size)])  15.4 us
    ppermute x14, waiting for transfers between devices, swap(): return lax.ppermute(x, 'ctx', [(i, i ^ bits) for i in range(ctx_size)])  6.97 us
    ppermute x1, waiting for transfers between devices, turn(): lax.ppermute(x, 'head', [(i, (i + by) % shards) for i in range(shards)])  3.19 us
    ppermute x1, starting transfers between devices, turn(): lax.ppermute(x, 'head', [(i, (i + by) % shards) for i in range(shards)])  1.59 us
    pallas_call x1, Pallas kernels, local(): pl.pallas_call(functools.partial(stats_kernel, chunks, heads), out_shape=...  1.14 us
    pallas_call x1, Pallas kernels, local(): pl.pallas_call(functools.partial(backward_kernel, chunks, heads, shards),...  0.99 us
    concatenate x1, other arithmetic, local(): jnp.concatenate([jnp.concatenate([key_rows, value_rows], axis=1), queries...  0.89 us
    reshape x1, local copies, waits for them, and re-layouts, local(): span_order.T.reshape(-1)  0.76 us
  transfers between devices with their start and end apart: 15, of which 7 were waited for; matrix products, arithmetic and copies ran while one was open for 5% of the time, Pallas kernels for 2%

profile of v6, /device:TPU:0, one launch (start us, length us, event | category | flops | bytes accessed | tf_op | source)
XLA Modules:
  0.0 33.7 jit_solution(1262812801247619456)
XLA Ops:
  0.6 0.9 %pad_maximum_fusion = bf16[384,256]{1,0:T(8,128)(2,1)S(1)} fusion(bf16[128,256]{1,0:T(8,128)(2,1)} %param.9, bf16[128,256]{1,0:T(8,128)(2,1)} %param.6, bf16[128,128]{1,0:T(8,128)(2,1)} %param.8, bf16[128,128]{1,0:T(8,128)(2,1)} %param.7), kind=kLoop, calls=%fused_computation.2 | loop fusion | flops 786432 | bytes 393216 | tf_op jit(solution)/shard_map/concatenate | solution.py:181
  1.5 3.0 %collective-permute-start.1 = (bf16[256,256]{1,0:T(8,128)(2,1)S(1)}, bf16[256,256]{1,0:T(8,128)(2,1)S(1)}, u32[]{:S(2)}, u32[]{:S(2)}) collective-permute-start(bf16[256,256]{1,0:T(8,128)(2,1)S(1)} %slice.24.refs_0_), channel_id=1, source_target_pairs={{0,4},{2,6},{4,0},{6,2},{8,12},{10,14},{12,8},{14,10},{16,20},{18,... | collective-permute-start | bytes 393224 | tf_op jit(solution)/shard_map/ppermute | solution.py:159
  4.6 3.6 %collective-permute-start.5 = (bf16[128,256]{1,0:T(8,128)(2,1)S(1)}, bf16[128,256]{1,0:T(8,128)(2,1)S(1)}, u32[]{:S(2)}, u32[]{:S(2)}) collective-permute-start(bf16[128,256]{1,0:T(8,128)(2,1)S(1)} %slice.25.refs_4_), channel_id=1, source_target_pairs={{0,24},{2,26},{4,28},{6,30},{8,16},{10,18},{12,20},{14,22},{16,8},... | collective-permute-start | bytes 196616 | tf_op jit(solution)/shard_map/ppermute | solution.py:159
  8.2 0.0 collective-permute-start.4
  8.2 0.8 %collective-permute-start.3 = (bf16[128,256]{1,0:T(8,128)(2,1)S(1)}, bf16[128,256]{1,0:T(8,128)(2,1)S(1)}, u32[]{:S(2)}, u32[]{:S(2)}) collective-permute-start(bf16[128,256]{1,0:T(8,128)(2,1)S(1)} %slice.25.refs_4_), channel_id=1, source_target_pairs={{0,8},{2,10},{4,12},{6,14},{8,0},{10,2},{12,4},{14,6},{16,24},{18,... | collective-permute-start | bytes 196616 | tf_op jit(solution)/shard_map/ppermute | solution.py:159
  8.9 0.0 collective-permute-start
  8.9 0.8 %reshape.9 = s32[32]{0:T(128)S(1)} reshape(s32[2,16]{1,0:T(2,128)} %bitcast.1) | data formatting | bytes 256 | tf_op jit(solution)/shard_map/reshape | solution.py:179
  9.7 0.0 collective-permute-done.1.refs_2_
  9.7 0.5 %collective-permute-start.2 = (bf16[256,256]{1,0:T(8,128)(2,1)S(1)}, bf16[256,256]{1,0:T(8,128)(2,1)S(1)}, u32[]{:S(2)}, u32[]{:S(2)}) collective-permute-start(bf16[256,256]{1,0:T(8,128)(2,1)S(1)} %collective-permute-done.1.refs_2_), channel_id=1, source_target_pairs={{0,2},{2,0},{4,6},{6,4},{8,10},{10,8},{12,14},{14,12},{16,18},{18,... | collective-permute-start | bytes 393224 | tf_op jit(solution)/shard_map/ppermute | solution.py:159
  10.2 0.7 %pad_add_fusion.ints = s32[40]{0:T(128)S(1)} fusion(s32[32]{0:T(128)S(1)} %reshape.9, s32[8]{0:T(128)} %param.10), kind=kLoop, calls=%fused_computation.3 | loop fusion | flops 40 | bytes 320 | tf_op jit(solution)/shard_map/concatenate | solution.py:179
  10.9 0.6 %place.1.place_ref = s32[16,128]{1,0:T(8,128)S(1)} custom-call(s32[40]{0:T(128)S(1)} %pad_add_fusion.ints), custom_call_target="tpu_custom_call" | custom-call | flops 1000000000 | tf_op jit(solution)/shard_map/place/pallas_call | solution.py:171
  11.5 0.0 collective-permute-done.5.refs_7_
  11.5 2.0 %collective-permute-done.4.refs_6_ = bf16[128,256]{1,0:T(8,128)(2,1)S(1)} collective-permute-done((bf16[128,256]{1,0:T(8,128)(2,1)S(1)}, bf16[128,256]{1,0:T(8,128)(2,1)S(1)}, u32[]{:S(2)}, u32[]{:S(2)}) %collective-permute-start.4) | collective-permute-done | bytes 65568 | tf_op jit(solution)/shard_map/ppermute | solution.py:159
  13.5 0.1 collective-permute-done.3.refs_5_
  13.6 0.0 collective-permute-done.refs_1_
  13.6 0.0 collective-permute-done.2.refs_3_
  13.6 1.1 %stats.1 = (f32[2,1024]{1,0:T(2,128)S(1)}, f32[1,1024]{1,0:T(1,128)S(1)}, f32[512,1024]{1,0:T(8,128)S(1)}, f32[512,1024]{1,0:T(8,128)S(1)}) custom-call(s32[16,128]{1,0:T(8,128)S(1)} %place.1.place_ref, bf16[256,256]{1,0:T(8,128)(2,1)S(1)} %slice.24.refs_0_, bf16[256,256]{1,0:T(8,128)(2,1)S(1)} %collective-permute-done.refs_1_, ...), custom_call_target="tpu_custom_call" | custom-call | tf_op jit(solution)/shard_map/stats/pallas_call | solution.py:192
  14.7 0.1 collective-permute-start.8
  14.8 1.0 %collective-permute-start.7 = (f32[2,1024]{1,0:T(2,128)S(1)}, f32[2,1024]{1,0:T(2,128)S(1)}, u32[]{:S(2)}, u32[]{:S(2)}) collective-permute-start(f32[2,1024]{1,0:T(2,128)S(1)} %get-tuple-element.11.refs_8_), channel_id=1, source_target_pairs={{0,4},{2,6},{4,0},{6,2},{8,12},{10,14},{12,8},{14,10},{16,20},{18,... | collective-permute-start | bytes 24584 | tf_op jit(solution)/shard_map/ppermute | solution.py:159
  15.8 0.8 %collective-permute-start.6 = (f32[2,1024]{1,0:T(2,128)S(1)}, f32[2,1024]{1,0:T(2,128)S(1)}, u32[]{:S(2)}, u32[]{:S(2)}) collective-permute-start(f32[2,1024]{1,0:T(2,128)S(1)} %get-tuple-element.11.refs_8_), channel_id=1, source_target_pairs={{0,2},{2,0},{4,6},{6,4},{8,10},{10,8},{12,14},{14,12},{16,18},{18,... | collective-permute-start | bytes 24584 | tf_op jit(solution)/shard_map/ppermute | solution.py:159
  16.7 1.2 %collective-permute-done.8.refs_11_ = f32[2,1024]{1,0:T(2,128)S(1)} collective-permute-done((f32[2,1024]{1,0:T(2,128)S(1)}, f32[2,1024]{1,0:T(2,128)S(1)}, u32[]{:S(2)}, u32[]{:S(2)}) %collective-permute-start.8) | collective-permute-done | bytes 8224 | tf_op jit(solution)/shard_map/ppermute | solution.py:159
  17.9 0.7 %collective-permute-done.7.refs_10_ = f32[2,1024]{1,0:T(2,128)S(1)} collective-permute-done((f32[2,1024]{1,0:T(2,128)S(1)}, f32[2,1024]{1,0:T(2,128)S(1)}, u32[]{:S(2)}, u32[]{:S(2)}) %collective-permute-start.7) | collective-permute-done | bytes 8224 | tf_op jit(solution)/shard_map/ppermute | solution.py:159
  18.5 0.0 collective-permute-done.6.refs_9_
  18.5 1.0 %backward.1 = (bf16[256,256]{1,0:T(8,128)(2,1)S(1)}, bf16[256,256]{1,0:T(8,128)(2,1)S(1)}, bf16[256,256]{1,0:T(8,128)(2,1)S(1)}, bf16[256,256]{1,0:T(8,128)(2,1)S(1)}) custom-call(bf16[256,256]{1,0:T(8,128)(2,1)S(1)} %slice.24.refs_0_, bf16[256,256]{1,0:T(8,128)(2,1)S(1)} %collective-permute-done.refs_1_, ...), custom_call_target="tpu_custom_call" | custom-call | tf_op jit(solution)/shard_map/backward/pallas_call | solution.py:209
  19.5 0.1 collective-permute-start.13
  19.6 1.6 %collective-permute-start.9 = (bf16[256,256]{1,0:T(8,128)(2,1)S(1)}, bf16[256,256]{1,0:T(8,128)(2,1)S(1)}, u32[]{:S(2)}, u32[]{:S(2)}) collective-permute-start(bf16[256,256]{1,0:T(8,128)(2,1)S(1)} %get-tuple-element.16), channel_id=1, source_target_pairs={{0,1},{1,0},{2,3},{3,2},{4,5},{5,4},{6,7},{7,6},{8,9},{9,8},{10,11... | collective-permute-start | bytes 393224 | tf_op jit(solution)/shard_map/ppermute | solution.py:162
  21.2 0.0 collective-permute-done.13
  21.3 1.1 %collective-permute-start.14 = (bf16[128,256]{1,0:T(8,128)(2,1)S(1)}, bf16[128,256]{1,0:T(8,128)(2,1)S(1)}, u32[]{:S(2)}, u32[]{:S(2)}) collective-permute-start(bf16[128,256]{1,0:T(8,128)(2,1)S(1)} %slice.29), channel_id=1, source_target_pairs={{0,4},{2,6},{4,0},{6,2},{8,12},{10,14},{12,8},{14,10},{16,20},{18,... | collective-permute-start | bytes 196616 | tf_op jit(solution)/shard_map/ppermute | solution.py:159
  22.3 3.2 %collective-permute-done.9 = bf16[256,256]{1,0:T(8,128)(2,1)S(1)} collective-permute-done((bf16[256,256]{1,0:T(8,128)(2,1)S(1)}, bf16[256,256]{1,0:T(8,128)(2,1)S(1)}, u32[]{:S(2)}, u32[]{:S(2)}) %collective-permute-start.9) | collective-permute-done | bytes 131104 | tf_op jit(solution)/shard_map/ppermute | solution.py:162
  25.6 2.7 %collective-permute-start.12 = (bf16[64,256]{1,0:T(8,128)(2,1)S(1)}, bf16[64,256]{1,0:T(8,128)(2,1)S(1)}, u32[]{:S(2)}, u32[]{:S(2)}) collective-permute-start(bf16[64,256]{1,0:T(8,128)(2,1)S(1)} %get-tuple-element.19), channel_id=1, source_target_pairs={{0,24},{2,26},{4,28},{6,30},{8,16},{10,18},{12,20},{14,22},{16,8},... | collective-permute-start | bytes 98312 | tf_op jit(solution)/shard_map/ppermute | solution.py:159
  28.2 0.0 collective-permute-start.11
  28.2 1.8 %collective-permute-start.10 = (bf16[64,256]{1,0:T(8,128)(2,1)S(1)}, bf16[64,256]{1,0:T(8,128)(2,1)S(1)}, u32[]{:S(2)}, u32[]{:S(2)}) collective-permute-start(bf16[64,256]{1,0:T(8,128)(2,1)S(1)} %get-tuple-element.21), channel_id=1, source_target_pairs={{0,8},{2,10},{4,12},{6,14},{8,0},{10,2},{12,4},{14,6},{16,24},{18,... | collective-permute-start | bytes 98312 | tf_op jit(solution)/shard_map/ppermute | solution.py:159
  30.0 1.3 %collective-permute-done.12.refs_2_ = bf16[64,256]{1,0:T(8,128)(2,1)S(1)} collective-permute-done((bf16[64,256]{1,0:T(8,128)(2,1)S(1)}, bf16[64,256]{1,0:T(8,128)(2,1)S(1)}, u32[]{:S(2)}, u32[]{:S(2)}) %collective-permute-start.12) | collective-permute-done | bytes 32800 | tf_op jit(solution)/shard_map/ppermute | solution.py:159
  31.4 1.7 %collective-permute-done.11.refs_1_ = bf16[64,256]{1,0:T(8,128)(2,1)S(1)} collective-permute-done((bf16[64,256]{1,0:T(8,128)(2,1)S(1)}, bf16[64,256]{1,0:T(8,128)(2,1)S(1)}, u32[]{:S(2)}, u32[]{:S(2)}) %collective-permute-start.11) | collective-permute-done | bytes 32800 | tf_op jit(solution)/shard_map/ppermute | solution.py:159
  33.1 0.0 collective-permute-done.10.refs_0_
  33.1 0.0 collective-permute-done.14.refs_4_
  33.1 0.7 %finish.1 = (bf16[128,256]{1,0:T(8,128)(2,1)}, bf16[64,128]{1,0:T(8,128)(2,1)}, bf16[64,128]{1,0:T(8,128)(2,1)}) custom-call(bf16[256,256]{1,0:T(8,128)(2,1)S(1)} %add_convert_fusion.1.owned_ref, bf16[64,256]{1,0:T(8,128)(2,1)S(1)} %collective-permute-done.10.refs_0_, bf16[64,256]{1,0:T(8,128)(2,1)S(1)} %collective-permute-done.11.refs_1_, ...), custom_call_target="tpu_custom_call" | custom-call | tf_op jit(solution)/shard_map/finish/pallas_call | solution.py:229
  (6 shorter events, 0.1 us)
Async XLA Ops:
  1.5 8.2 %collective-permute-start.1 = (bf16[256,256]{1,0:T(8,128)(2,1)S(1)}, bf16[256,256]{1,0:T(8,128)(2,1)S(1)}, u32[]{:S(2)}, u32[]{:S(2)}) collective-permute-start(bf16[256,256]{1,0:T(8,128)(2,1)S(1)} %slice.24.refs_0_), channel_id=1, source_target_pairs={{0,4},{2,6},{4,0},{6,2},{8,12},{10,14},{12,8},{14,10},{16,20},{18,... | collective-permute-start | bytes 393224 | tf_op jit(solution)/shard_map/ppermute | solution.py:159
  4.6 7.0 %collective-permute-start.5 = (bf16[128,256]{1,0:T(8,128)(2,1)S(1)}, bf16[128,256]{1,0:T(8,128)(2,1)S(1)}, u32[]{:S(2)}, u32[]{:S(2)}) collective-permute-start(bf16[128,256]{1,0:T(8,128)(2,1)S(1)} %slice.25.refs_4_), channel_id=1, source_target_pairs={{0,24},{2,26},{4,28},{6,30},{8,16},{10,18},{12,20},{14,22},{16,8},... | collective-permute-start | bytes 196616 | tf_op jit(solution)/shard_map/ppermute | solution.py:159
  8.2 5.4 %collective-permute-start.4 = (bf16[128,256]{1,0:T(8,128)(2,1)S(1)}, bf16[128,256]{1,0:T(8,128)(2,1)S(1)}, u32[]{:S(2)}, u32[]{:S(2)}) collective-permute-start(bf16[128,256]{1,0:T(8,128)(2,1)S(1)} %slice.25.refs_4_), channel_id=1, source_target_pairs={{0,16},{2,18},{4,20},{6,22},{8,24},{10,26},{12,28},{14,30},{16,0},... | collective-permute-start | bytes 196616 | tf_op jit(solution)/shard_map/ppermute | solution.py:159
  8.2 5.4 %collective-permute-start.3 = (bf16[128,256]{1,0:T(8,128)(2,1)S(1)}, bf16[128,256]{1,0:T(8,128)(2,1)S(1)}, u32[]{:S(2)}, u32[]{:S(2)}) collective-permute-start(bf16[128,256]{1,0:T(8,128)(2,1)S(1)} %slice.25.refs_4_), channel_id=1, source_target_pairs={{0,8},{2,10},{4,12},{6,14},{8,0},{10,2},{12,4},{14,6},{16,24},{18,... | collective-permute-start | bytes 196616 | tf_op jit(solution)/shard_map/ppermute | solution.py:159
  8.9 4.6 %collective-permute-start = (bf16[256,256]{1,0:T(8,128)(2,1)S(1)}, bf16[256,256]{1,0:T(8,128)(2,1)S(1)}, u32[]{:S(2)}, u32[]{:S(2)}) collective-permute-start(bf16[256,256]{1,0:T(8,128)(2,1)S(1)} %slice.24.refs_0_), channel_id=1, source_target_pairs={{0,2},{2,0},{4,6},{6,4},{8,10},{10,8},{12,14},{14,12},{16,18},{18,... | collective-permute-start | bytes 393224 | tf_op jit(solution)/shard_map/ppermute | solution.py:159
  9.7 3.9 %collective-permute-start.2 = (bf16[256,256]{1,0:T(8,128)(2,1)S(1)}, bf16[256,256]{1,0:T(8,128)(2,1)S(1)}, u32[]{:S(2)}, u32[]{:S(2)}) collective-permute-start(bf16[256,256]{1,0:T(8,128)(2,1)S(1)} %collective-permute-done.1.refs_2_), channel_id=1, source_target_pairs={{0,2},{2,0},{4,6},{6,4},{8,10},{10,8},{12,14},{14,12},{16,18},{18,... | collective-permute-start | bytes 393224 | tf_op jit(solution)/shard_map/ppermute | solution.py:159
  14.7 3.1 %collective-permute-start.8 = (f32[2,1024]{1,0:T(2,128)S(1)}, f32[2,1024]{1,0:T(2,128)S(1)}, u32[]{:S(2)}, u32[]{:S(2)}) collective-permute-start(f32[2,1024]{1,0:T(2,128)S(1)} %get-tuple-element.11.refs_8_), channel_id=1, source_target_pairs={{0,6},{2,4},{4,2},{6,0},{8,14},{10,12},{12,10},{14,8},{16,22},{18,... | collective-permute-start | bytes 24584 | tf_op jit(solution)/shard_map/ppermute | solution.py:159
  14.8 3.7 %collective-permute-start.7 = (f32[2,1024]{1,0:T(2,128)S(1)}, f32[2,1024]{1,0:T(2,128)S(1)}, u32[]{:S(2)}, u32[]{:S(2)}) collective-permute-start(f32[2,1024]{1,0:T(2,128)S(1)} %get-tuple-element.11.refs_8_), channel_id=1, source_target_pairs={{0,4},{2,6},{4,0},{6,2},{8,12},{10,14},{12,8},{14,10},{16,20},{18,... | collective-permute-start | bytes 24584 | tf_op jit(solution)/shard_map/ppermute | solution.py:159
  15.8 2.7 %collective-permute-start.6 = (f32[2,1024]{1,0:T(2,128)S(1)}, f32[2,1024]{1,0:T(2,128)S(1)}, u32[]{:S(2)}, u32[]{:S(2)}) collective-permute-start(f32[2,1024]{1,0:T(2,128)S(1)} %get-tuple-element.11.refs_8_), channel_id=1, source_target_pairs={{0,2},{2,0},{4,6},{6,4},{8,10},{10,8},{12,14},{14,12},{16,18},{18,... | collective-permute-start | bytes 24584 | tf_op jit(solution)/shard_map/ppermute | solution.py:159
  19.5 1.7 %collective-permute-start.13 = (bf16[256,256]{1,0:T(8,128)(2,1)S(1)}, bf16[256,256]{1,0:T(8,128)(2,1)S(1)}, u32[]{:S(2)}, u32[]{:S(2)}) collective-permute-start(bf16[256,256]{1,0:T(8,128)(2,1)S(1)} %get-tuple-element.18), channel_id=1, source_target_pairs={{0,2},{2,0},{4,6},{6,4},{8,10},{10,8},{12,14},{14,12},{16,18},{18,... | collective-permute-start | bytes 393224 | tf_op jit(solution)/shard_map/ppermute | solution.py:159
  19.6 5.9 %collective-permute-start.9 = (bf16[256,256]{1,0:T(8,128)(2,1)S(1)}, bf16[256,256]{1,0:T(8,128)(2,1)S(1)}, u32[]{:S(2)}, u32[]{:S(2)}) collective-permute-start(bf16[256,256]{1,0:T(8,128)(2,1)S(1)} %get-tuple-element.16), channel_id=1, source_target_pairs={{0,1},{1,0},{2,3},{3,2},{4,5},{5,4},{6,7},{7,6},{8,9},{9,8},{10,11... | collective-permute-start | bytes 393224 | tf_op jit(solution)/shard_map/ppermute | solution.py:162
  21.3 11.8 %collective-permute-start.14 = (bf16[128,256]{1,0:T(8,128)(2,1)S(1)}, bf16[128,256]{1,0:T(8,128)(2,1)S(1)}, u32[]{:S(2)}, u32[]{:S(2)}) collective-permute-start(bf16[128,256]{1,0:T(8,128)(2,1)S(1)} %slice.29), channel_id=1, source_target_pairs={{0,4},{2,6},{4,0},{6,2},{8,12},{10,14},{12,8},{14,10},{16,20},{18,... | collective-permute-start | bytes 196616 | tf_op jit(solution)/shard_map/ppermute | solution.py:159
  25.6 5.8 %collective-permute-start.12 = (bf16[64,256]{1,0:T(8,128)(2,1)S(1)}, bf16[64,256]{1,0:T(8,128)(2,1)S(1)}, u32[]{:S(2)}, u32[]{:S(2)}) collective-permute-start(bf16[64,256]{1,0:T(8,128)(2,1)S(1)} %get-tuple-element.19), channel_id=1, source_target_pairs={{0,24},{2,26},{4,28},{6,30},{8,16},{10,18},{12,20},{14,22},{16,8},... | collective-permute-start | bytes 98312 | tf_op jit(solution)/shard_map/ppermute | solution.py:159
  28.2 4.8 %collective-permute-start.11 = (bf16[64,256]{1,0:T(8,128)(2,1)S(1)}, bf16[64,256]{1,0:T(8,128)(2,1)S(1)}, u32[]{:S(2)}, u32[]{:S(2)}) collective-permute-start(bf16[64,256]{1,0:T(8,128)(2,1)S(1)} %get-tuple-element.20), channel_id=1, source_target_pairs={{0,16},{2,18},{4,20},{6,22},{8,24},{10,26},{12,28},{14,30},{16,0},... | collective-permute-start | bytes 98312 | tf_op jit(solution)/shard_map/ppermute | solution.py:159
  28.2 4.8 %collective-permute-start.10 = (bf16[64,256]{1,0:T(8,128)(2,1)S(1)}, bf16[64,256]{1,0:T(8,128)(2,1)S(1)}, u32[]{:S(2)}, u32[]{:S(2)}) collective-permute-start(bf16[64,256]{1,0:T(8,128)(2,1)S(1)} %get-tuple-element.21), channel_id=1, source_target_pairs={{0,8},{2,10},{4,12},{6,14},{8,0},{10,2},{12,4},{14,6},{16,24},{18,... | collective-permute-start | bytes 98312 | tf_op jit(solution)/shard_map/ppermute | solution.py:159

commit v7 on v6

--- a/solution.py
+++ b/solution.py
@@ -119,29 +119,42 @@
             dk_total[...] += dk
         dq = ((dot(keys_across, dscores, NN) * scaling).T).astype(jnp.bfloat16)
         half = GROUP // 2
-        to = (near_ref, far_ref)[j % half]
+        to = (near_ref, far_ref)[j // half]
         for h in range(heads):
-            to[pl.ds(j // half * rows, rows), h * hd : (h + 1) * hd] = dq[h * rows : (h + 1) * rows]
+            to[pl.ds(j % half * rows, rows), h * hd : (h + 1) * hd] = dq[h * rows : (h + 1) * rows]
     part = rows // shards
+    half = chunks // 2
     for t in range(shards):
         owner = lax.rem(shard + t, shards)
         for b in range(chunks):
             at = pl.ds(pl.multiple_of(b * rows + owner * part, part), part)
-            to = pl.ds(b * part, part)
-            outs[t][to, :hd] = (dk_total[at, :] * scaling).astype(jnp.bfloat16)
-            outs[t][to, hd:] = dv_total[at, :].astype(jnp.bfloat16)
-
-
-def finish_kernel(chunks, owned_ref, *refs):
-    came, (pair_ref, other_ref) = refs[: chunks - 1], refs[chunks - 1 : chunks + 1]
-    query_ref, key_ref, value_ref = refs[chunks + 1 :]
+            if b < half:
+                out, to = outs[b], pl.ds(t * part, part)
+            else:
+                out, to = outs[half + t], pl.ds((b - half) * part, part)
+            out[to, :hd] = (dk_total[at, :] * scaling).astype(jnp.bfloat16)
+            out[to, hd:] = dv_total[at, :].astype(jnp.bfloat16)
+
+
+def fold_kernel(*refs):
+    total = refs[0][...].astype(jnp.float32)
+    for ref in refs[1:-1]:
+        total = total + ref[...].astype(jnp.float32)
+    refs[-1][...] = total.astype(jnp.bfloat16)
+
+
+def finish_kernel(owned_ref, *refs):
+    *came, key_ref, value_ref = refs
     part, hd = key_ref.shape
-    rows = query_ref.shape[0]
     total = owned_ref[:part].astype(jnp.float32)
     for ref in came:
         total = total + ref[...].astype(jnp.float32)
     key_ref[...] = total[:, :hd].astype(jnp.bfloat16)
     value_ref[...] = total[:, hd:].astype(jnp.bfloat16)
+
+
+def query_sum_kernel(pair_ref, other_ref, query_ref):
+    rows = query_ref.shape[0]
     query = pair_ref[:rows].astype(jnp.float32) + other_ref[...].astype(jnp.float32)
     query_ref[...] = query.astype(jnp.bfloat16)
 
@@ -204,37 +217,56 @@
     )(place, *group, *chunk)
     all_stats = [stats] + [swap(stats, bits) for bits in group_bits[1:]]
 
-    half = array((GROUP // 2 * rows, width))
-    piece = array((chunks * part, 2 * hd))
+    pair_rows = array((GROUP // 2 * rows, width))
+    half = chunks // 2
+    pieces = (array((rows, 2 * hd)),) * half + (array((half * part, 2 * hd)),) * shards
     near, far, *dkv = pl.pallas_call(
         functools.partial(backward_kernel, chunks, heads, shards),
-        out_shape=(half, half) + (piece,) * shards,
+        out_shape=(pair_rows, pair_rows) + pieces,
         in_specs=[vmem] * (2 * GROUP + chunks + 3),
-        out_specs=(vmem,) * (2 + shards),
+        out_specs=(vmem,) * (2 + len(pieces)),
         scratch_shapes=[pltpu.VMEM((chunks * rows, hd), jnp.float32)] * 2,
         compiler_params=params,
         name="backward",
     )(*group, *chunk, *all_stats, top, expo, dprobs)
 
-    owned = dkv[0].astype(jnp.float32)
-    for t in range(1, shards):
-        owned = owned + turn(dkv[t], t).astype(jnp.float32)
-    owned = owned.astype(jnp.bfloat16)
+    def fold(parts, flops):
+        return pl.pallas_call(
+            fold_kernel,
+            out_shape=jax.ShapeDtypeStruct(parts[0].shape, jnp.bfloat16),
+            in_specs=[vmem] * len(parts),
+            out_specs=vmem,
+            compiler_params=small,
+            cost_estimate=pl.CostEstimate(flops=flops, bytes_accessed=0, transcendentals=0),
+            name="fold",
+        )(*parts)
+
+    across = fold([dkv[half]] + [turn(dkv[half + t], t) for t in range(1, shards)], 0)
+    owned = fold([dkv[0]] + [swap(dkv[b], chunk_bits[b]) for b in range(1, half)], 1000000000)
     came = [
-        swap(owned[b * part : (b + 1) * part], chunk_bits[b]) for b in range(1, chunks)
-    ]
-    pair = (near.astype(jnp.float32) + swap(far, group_bits[1]).astype(jnp.float32)).astype(jnp.bfloat16)
-    other = swap(pair[rows:], group_bits[2])
-    return tuple(
-        pl.pallas_call(
-            functools.partial(finish_kernel, chunks),
-            out_shape=(array((rows, width)), array((part, hd)), array((part, hd))),
-            in_specs=[vmem] * (chunks + 2),
-            out_specs=(vmem, vmem, vmem),
-            compiler_params=small,
-            name="finish",
-        )(owned, *came, pair, other)
-    )
+        swap(across[k * part : (k + 1) * part], chunk_bits[half + k]) for k in range(half)
+    ] + [turn(owned[t * part : (t + 1) * part], t) for t in range(1, shards)]
+    pair = (near.astype(jnp.float32) + swap(far, group_bits[2]).astype(jnp.float32)).astype(jnp.bfloat16)
+    other = swap(pair[rows:], group_bits[1])
+    query_grad = pl.pallas_call(
+        query_sum_kernel,
+        out_shape=array((rows, width)),
+        in_specs=[vmem] * 2,
+        out_specs=vmem,
+        compiler_params=small,
+        cost_estimate=pl.CostEstimate(flops=1000000000, bytes_accessed=0, transcendentals=0),
+        name="query_sum",
+    )(pair, other)
+    query_grad, *came = lax.optimization_barrier((query_grad, *came))
+    key_grad, value_grad = pl.pallas_call(
+        finish_kernel,
+        out_shape=(array((part, hd)), array((part, hd))),
+        in_specs=[vmem] * (len(came) + 1),
+        out_specs=(vmem, vmem),
+        compiler_params=small,
+        name="finish",
+    )(owned, *came)
+    return query_grad, key_grad, value_grad
 
 
 def solution(mesh):

time: 33.9 us -> 32.2 us (0.950)
  waiting for transfers between devices: 10.2 us -> 8.03 us
  Pallas kernels: 3.36 us -> 4.01 us
    ppermute x1 -> x2, waiting for transfers between devices: 3.19 us -> 1.22 us  [turn(): lax.ppermute(x, 'head', [(i, (i + by) % shards) for i in range(shards)])]
    ppermute x14, starting transfers between devices: 15.4 us -> 14.1 us  [swap(): return lax.ppermute(x, 'ctx', [(i, i ^ bits) for i in range(ctx_size)])]
    ppermute x1 -> x2, starting transfers between devices: 1.59 us -> 2.7 us  [turn(): lax.ppermute(x, 'head', [(i, (i + by) % shards) for i in range(shards)])]
    pallas_call x1 -> x4, Pallas kernels: 0.67 us -> 1.31 us  [the longest x1 0.65 us: local(): pl.pallas_call(query_sum_kernel, out_shape=array((rows, width)), in_specs...]
  transfers between devices with their start and end apart: 15 -> 16, of which waited for: 7 -> 9; matrix products, arithmetic and copies ran while one was open for 5% -> 5% of each run, Pallas kernels for 2% -> 4%
where the time goes in v7:
time: 32.2 us; the launch traced here: 32 us
  starting transfers between devices  16.8 us (52%)
  waiting for transfers between devices  8.03 us (25%)
  Pallas kernels  4.01 us (12%)
  other arithmetic  1.65 us (5%)
  local copies, waits for them, and re-layouts  0.79 us (2%)
  between operations  0.74 us (2%)
    ppermute x14, starting transfers between devices, swap(): return lax.ppermute(x, 'ctx', [(i, i ^ bits) for i in range(ctx_size)])  14.1 us
    ppermute x14, waiting for transfers between devices, swap(): return lax.ppermute(x, 'ctx', [(i, i ^ bits) for i in range(ctx_size)])  6.81 us
    ppermute x2, starting transfers between devices, turn(): lax.ppermute(x, 'head', [(i, (i + by) % shards) for i in range(shards)])  2.7 us
    ppermute x2, waiting for transfers between devices, turn(): lax.ppermute(x, 'head', [(i, (i + by) % shards) for i in range(shards)])  1.22 us
    pallas_call x1, Pallas kernels, local(): pl.pallas_call(functools.partial(stats_kernel, chunks, heads), out_shape=...  1.14 us
    pallas_call x1, Pallas kernels, local(): pl.pallas_call(functools.partial(backward_kernel, chunks, heads, shards),...  0.99 us
    concatenate x1, other arithmetic, local(): jnp.concatenate([jnp.concatenate([key_rows, value_rows], axis=1), queries...  0.89 us
    reshape x1, local copies, waits for them, and re-layouts, local(): span_order.T.reshape(-1)  0.76 us
  transfers between devices with their start and end apart: 16, of which 9 were waited for; matrix products, arithmetic and copies ran while one was open for 5% of the time, Pallas kernels for 4%

profile of v7, /device:TPU:0, one launch (start us, length us, event | category | flops | bytes accessed | tf_op | source)
XLA Modules:
  0.0 32.0 jit_solution(3163873570264182265)
XLA Ops:
  0.6 0.9 %pad_maximum_fusion = bf16[384,256]{1,0:T(8,128)(2,1)S(1)} fusion(bf16[128,256]{1,0:T(8,128)(2,1)} %param.9, bf16[128,256]{1,0:T(8,128)(2,1)} %param.6, bf16[128,128]{1,0:T(8,128)(2,1)} %param.8, bf16[128,128]{1,0:T(8,128)(2,1)} %param.7), kind=kLoop, calls=%fused_computation.1 | loop fusion | flops 786432 | bytes 393216 | tf_op jit(solution)/shard_map/concatenate | solution.py:194
  1.5 3.0 %collective-permute-start.1 = (bf16[256,256]{1,0:T(8,128)(2,1)S(1)}, bf16[256,256]{1,0:T(8,128)(2,1)S(1)}, u32[]{:S(2)}, u32[]{:S(2)}) collective-permute-start(bf16[256,256]{1,0:T(8,128)(2,1)S(1)} %slice.24.refs_0_), channel_id=1, source_target_pairs={{0,4},{2,6},{4,0},{6,2},{8,12},{10,14},{12,8},{14,10},{16,20},{18,... | collective-permute-start | bytes 393224 | tf_op jit(solution)/shard_map/ppermute | solution.py:172
  4.6 3.6 %collective-permute-start.5 = (bf16[128,256]{1,0:T(8,128)(2,1)S(1)}, bf16[128,256]{1,0:T(8,128)(2,1)S(1)}, u32[]{:S(2)}, u32[]{:S(2)}) collective-permute-start(bf16[128,256]{1,0:T(8,128)(2,1)S(1)} %slice.25.refs_4_), channel_id=1, source_target_pairs={{0,24},{2,26},{4,28},{6,30},{8,16},{10,18},{12,20},{14,22},{16,8},... | collective-permute-start | bytes 196616 | tf_op jit(solution)/shard_map/ppermute | solution.py:172
  8.2 0.0 collective-permute-start.4
  8.2 0.8 %collective-permute-start.3 = (bf16[128,256]{1,0:T(8,128)(2,1)S(1)}, bf16[128,256]{1,0:T(8,128)(2,1)S(1)}, u32[]{:S(2)}, u32[]{:S(2)}) collective-permute-start(bf16[128,256]{1,0:T(8,128)(2,1)S(1)} %slice.25.refs_4_), channel_id=1, source_target_pairs={{0,8},{2,10},{4,12},{6,14},{8,0},{10,2},{12,4},{14,6},{16,24},{18,... | collective-permute-start | bytes 196616 | tf_op jit(solution)/shard_map/ppermute | solution.py:172
  8.9 0.0 collective-permute-start
  8.9 0.8 %reshape.9 = s32[32]{0:T(128)S(1)} reshape(s32[2,16]{1,0:T(2,128)} %bitcast.1) | data formatting | bytes 256 | tf_op jit(solution)/shard_map/reshape | solution.py:192
  9.7 0.0 collective-permute-done.1.refs_2_
  9.7 0.5 %collective-permute-start.2 = (bf16[256,256]{1,0:T(8,128)(2,1)S(1)}, bf16[256,256]{1,0:T(8,128)(2,1)S(1)}, u32[]{:S(2)}, u32[]{:S(2)}) collective-permute-start(bf16[256,256]{1,0:T(8,128)(2,1)S(1)} %collective-permute-done.1.refs_2_), channel_id=1, source_target_pairs={{0,2},{2,0},{4,6},{6,4},{8,10},{10,8},{12,14},{14,12},{16,18},{18,... | collective-permute-start | bytes 393224 | tf_op jit(solution)/shard_map/ppermute | solution.py:172
  10.2 0.7 %pad_add_fusion.ints = s32[40]{0:T(128)S(1)} fusion(s32[32]{0:T(128)S(1)} %reshape.9, s32[8]{0:T(128)} %param.10), kind=kLoop, calls=%fused_computation.2 | loop fusion | flops 40 | bytes 320 | tf_op jit(solution)/shard_map/concatenate | solution.py:192
  10.9 0.6 %place.1.place_ref = s32[16,128]{1,0:T(8,128)S(1)} custom-call(s32[40]{0:T(128)S(1)} %pad_add_fusion.ints), custom_call_target="tpu_custom_call" | custom-call | flops 1000000000 | tf_op jit(solution)/shard_map/place/pallas_call | solution.py:184
  11.5 0.0 collective-permute-done.5.refs_7_
  11.5 2.0 %collective-permute-done.4.refs_6_ = bf16[128,256]{1,0:T(8,128)(2,1)S(1)} collective-permute-done((bf16[128,256]{1,0:T(8,128)(2,1)S(1)}, bf16[128,256]{1,0:T(8,128)(2,1)S(1)}, u32[]{:S(2)}, u32[]{:S(2)}) %collective-permute-start.4) | collective-permute-done | bytes 65568 | tf_op jit(solution)/shard_map/ppermute | solution.py:172
  13.5 0.1 collective-permute-done.3.refs_5_
  13.6 0.0 collective-permute-done.refs_1_
  13.6 0.0 collective-permute-done.2.refs_3_
  13.6 1.1 %stats.1 = (f32[2,1024]{1,0:T(2,128)S(1)}, f32[1,1024]{1,0:T(1,128)S(1)}, f32[512,1024]{1,0:T(8,128)S(1)}, f32[512,1024]{1,0:T(8,128)S(1)}) custom-call(s32[16,128]{1,0:T(8,128)S(1)} %place.1.place_ref, bf16[256,256]{1,0:T(8,128)(2,1)S(1)} %slice.24.refs_0_, bf16[256,256]{1,0:T(8,128)(2,1)S(1)} %collective-permute-done.refs_1_, ...), custom_call_target="tpu_custom_call" | custom-call | tf_op jit(solution)/shard_map/stats/pallas_call | solution.py:205
  14.7 0.1 collective-permute-start.8
  14.8 1.0 %collective-permute-start.7 = (f32[2,1024]{1,0:T(2,128)S(1)}, f32[2,1024]{1,0:T(2,128)S(1)}, u32[]{:S(2)}, u32[]{:S(2)}) collective-permute-start(f32[2,1024]{1,0:T(2,128)S(1)} %get-tuple-element.19.refs_8_), channel_id=1, source_target_pairs={{0,4},{2,6},{4,0},{6,2},{8,12},{10,14},{12,8},{14,10},{16,20},{18,... | collective-permute-start | bytes 24584 | tf_op jit(solution)/shard_map/ppermute | solution.py:172
  15.8 0.8 %collective-permute-start.6 = (f32[2,1024]{1,0:T(2,128)S(1)}, f32[2,1024]{1,0:T(2,128)S(1)}, u32[]{:S(2)}, u32[]{:S(2)}) collective-permute-start(f32[2,1024]{1,0:T(2,128)S(1)} %get-tuple-element.19.refs_8_), channel_id=1, source_target_pairs={{0,2},{2,0},{4,6},{6,4},{8,10},{10,8},{12,14},{14,12},{16,18},{18,... | collective-permute-start | bytes 24584 | tf_op jit(solution)/shard_map/ppermute | solution.py:172
  16.7 1.2 %collective-permute-done.8.refs_11_ = f32[2,1024]{1,0:T(2,128)S(1)} collective-permute-done((f32[2,1024]{1,0:T(2,128)S(1)}, f32[2,1024]{1,0:T(2,128)S(1)}, u32[]{:S(2)}, u32[]{:S(2)}) %collective-permute-start.8) | collective-permute-done | bytes 8224 | tf_op jit(solution)/shard_map/ppermute | solution.py:172
  17.9 0.7 %collective-permute-done.7.refs_10_ = f32[2,1024]{1,0:T(2,128)S(1)} collective-permute-done((f32[2,1024]{1,0:T(2,128)S(1)}, f32[2,1024]{1,0:T(2,128)S(1)}, u32[]{:S(2)}, u32[]{:S(2)}) %collective-permute-start.7) | collective-permute-done | bytes 8224 | tf_op jit(solution)/shard_map/ppermute | solution.py:172
  18.5 0.0 collective-permute-done.6.refs_9_
  18.5 1.0 %backward.1 = (bf16[256,256]{1,0:T(8,128)(2,1)S(1)}, bf16[256,256]{1,0:T(8,128)(2,1)S(1)}, bf16[128,256]{1,0:T(8,128)(2,1)S(1)}, bf16[128,256]{1,0:T(8,128)(2,1)...) custom-call(bf16[256,256]{1,0:T(8,128)(2,1)S(1)} %slice.24.refs_0_, ...), custom_call_target="tpu_custom_call" | custom-call | tf_op jit(solution)/shard_map/backward/pallas_call | solution.py:223
  19.5 1.6 %collective-permute-start.11 = (bf16[128,256]{1,0:T(8,128)(2,1)S(1)}, bf16[128,256]{1,0:T(8,128)(2,1)S(1)}, u32[]{:S(2)}, u32[]{:S(2)}) collective-permute-start(bf16[128,256]{1,0:T(8,128)(2,1)S(1)} %get-tuple-element.26), channel_id=1, source_target_pairs={{0,1},{1,0},{2,3},{3,2},{4,5},{5,4},{6,7},{7,6},{8,9},{9,8},{10,11... | collective-permute-start | bytes 196616 | tf_op jit(solution)/shard_map/ppermute | solution.py:175
  21.1 1.0 %collective-permute-start.14 = (bf16[128,256]{1,0:T(8,128)(2,1)S(1)}, bf16[128,256]{1,0:T(8,128)(2,1)S(1)}, u32[]{:S(2)}, u32[]{:S(2)}) collective-permute-start(bf16[128,256]{1,0:T(8,128)(2,1)S(1)} %get-tuple-element.28), channel_id=1, source_target_pairs={{0,8},{2,10},{4,12},{6,14},{8,0},{10,2},{12,4},{14,6},{16,24},{18,... | collective-permute-start | bytes 196616 | tf_op jit(solution)/shard_map/ppermute | solution.py:172
  22.1 0.6 %collective-permute-start.9 = (bf16[256,256]{1,0:T(8,128)(2,1)S(1)}, bf16[256,256]{1,0:T(8,128)(2,1)S(1)}, u32[]{:S(2)}, u32[]{:S(2)}) collective-permute-start(bf16[256,256]{1,0:T(8,128)(2,1)S(1)} %get-tuple-element.24), channel_id=1, source_target_pairs={{0,4},{2,6},{4,0},{6,2},{8,12},{10,14},{12,8},{14,10},{16,20},{18,... | collective-permute-start | bytes 393224 | tf_op jit(solution)/shard_map/ppermute | solution.py:172
  22.6 1.2 %collective-permute-done.11.refs_1_ = bf16[128,256]{1,0:T(8,128)(2,1)S(1)} collective-permute-done((bf16[128,256]{1,0:T(8,128)(2,1)S(1)}, bf16[128,256]{1,0:T(8,128)(2,1)S(1)}, u32[]{:S(2)}, u32[]{:S(2)}) %collective-permute-start.11) | collective-permute-done | bytes 65568 | tf_op jit(solution)/shard_map/ppermute | solution.py:175
  23.9 2.7 %collective-permute-start.13 = (bf16[64,256]{1,0:T(8,128)(2,1)S(1)}, bf16[64,256]{1,0:T(8,128)(2,1)S(1)}, u32[]{:S(2)}, u32[]{:S(2)}) collective-permute-start(bf16[64,256]{1,0:T(8,128)(2,1)S(1)} %get-tuple-element.35), channel_id=1, source_target_pairs={{0,24},{2,26},{4,28},{6,30},{8,16},{10,18},{12,20},{14,22},{16,8},... | collective-permute-start | bytes 98312 | tf_op jit(solution)/shard_map/ppermute | solution.py:172
  26.6 0.0 collective-permute-start.12
  26.6 0.5 %collective-permute-done.9 = bf16[256,256]{1,0:T(8,128)(2,1)S(1)} collective-permute-done((bf16[256,256]{1,0:T(8,128)(2,1)S(1)}, bf16[256,256]{1,0:T(8,128)(2,1)S(1)}, u32[]{:S(2)}, u32[]{:S(2)}) %collective-permute-start.9) | collective-permute-done | bytes 131104 | tf_op jit(solution)/shard_map/ppermute | solution.py:172
  27.1 0.1 collective-permute-start.10
  27.2 0.0 collective-permute-done.14.refs_1_
  27.2 1.1 %collective-permute-start.15 = (bf16[64,256]{1,0:T(8,128)(2,1)S(1)}, bf16[64,256]{1,0:T(8,128)(2,1)S(1)}, u32[]{:S(2)}, u32[]{:S(2)}) collective-permute-start(bf16[64,256]{1,0:T(8,128)(2,1)S(1)} %slice.29), channel_id=1, source_target_pairs={{0,1},{1,0},{2,3},{3,2},{4,5},{5,4},{6,7},{7,6},{8,9},{9,8},{10,11... | collective-permute-start | bytes 98312 | tf_op jit(solution)/shard_map/ppermute | solution.py:175
  28.3 0.1 collective-permute-done.10.other_ref
  28.4 0.6 %query_sum.1 = bf16[128,256]{1,0:T(8,128)(2,1)} custom-call(bf16[256,256]{1,0:T(8,128)(2,1)S(1)} %add_convert_fusion.pair_ref, bf16[128,256]{1,0:T(8,128)(2,1)S(1)} %collective-permute-done.10.other_ref), custom_call_target="tpu_custom_call" | custom-call | flops 1000000000 | tf_op jit(solution)/shard_map/query_sum/pallas_call | solution.py:251
  29.1 0.6 %collective-permute-done.13.refs_1_ = bf16[64,256]{1,0:T(8,128)(2,1)S(1)} collective-permute-done((bf16[64,256]{1,0:T(8,128)(2,1)S(1)}, bf16[64,256]{1,0:T(8,128)(2,1)S(1)}, u32[]{:S(2)}, u32[]{:S(2)}) %collective-permute-start.13) | collective-permute-done | bytes 32800 | tf_op jit(solution)/shard_map/ppermute | solution.py:172
  29.7 1.7 %collective-permute-done.12.refs_0_ = bf16[64,256]{1,0:T(8,128)(2,1)S(1)} collective-permute-done((bf16[64,256]{1,0:T(8,128)(2,1)S(1)}, bf16[64,256]{1,0:T(8,128)(2,1)S(1)}, u32[]{:S(2)}, u32[]{:S(2)}) %collective-permute-start.12) | collective-permute-done | bytes 32800 | tf_op jit(solution)/shard_map/ppermute | solution.py:172
  31.4 0.0 collective-permute-done.15.refs_2_
  31.4 0.6 %finish.1 = (bf16[64,128]{1,0:T(8,128)(2,1)}, bf16[64,128]{1,0:T(8,128)(2,1)}) custom-call(bf16[128,256]{1,0:T(8,128)(2,1)S(1)} %fold.3.owned_ref, bf16[64,256]{1,0:T(8,128)(2,1)S(1)} %collective-permute-done.12.refs_0_, bf16[64,256]{1,0:T(8,128)(2,1)S(1)} %collective-permute-done.13.refs_1_, bf16[64,256]{1,0:T(8,128)(2,1)S(1)} %collective-permute-done.15.refs_2_), custom_call_target="tpu_custom_call" | custom-call | tf_op jit(solution)/shard_map/finish/pallas_call | solution.py:261
  (8 shorter events, 0.1 us)
Async XLA Ops:
  1.5 8.2 %collective-permute-start.1 = (bf16[256,256]{1,0:T(8,128)(2,1)S(1)}, bf16[256,256]{1,0:T(8,128)(2,1)S(1)}, u32[]{:S(2)}, u32[]{:S(2)}) collective-permute-start(bf16[256,256]{1,0:T(8,128)(2,1)S(1)} %slice.24.refs_0_), channel_id=1, source_target_pairs={{0,4},{2,6},{4,0},{6,2},{8,12},{10,14},{12,8},{14,10},{16,20},{18,... | collective-permute-start | bytes 393224 | tf_op jit(solution)/shard_map/ppermute | solution.py:172
  4.6 7.0 %collective-permute-start.5 = (bf16[128,256]{1,0:T(8,128)(2,1)S(1)}, bf16[128,256]{1,0:T(8,128)(2,1)S(1)}, u32[]{:S(2)}, u32[]{:S(2)}) collective-permute-start(bf16[128,256]{1,0:T(8,128)(2,1)S(1)} %slice.25.refs_4_), channel_id=1, source_target_pairs={{0,24},{2,26},{4,28},{6,30},{8,16},{10,18},{12,20},{14,22},{16,8},... | collective-permute-start | bytes 196616 | tf_op jit(solution)/shard_map/ppermute | solution.py:172
  8.2 5.4 %collective-permute-start.4 = (bf16[128,256]{1,0:T(8,128)(2,1)S(1)}, bf16[128,256]{1,0:T(8,128)(2,1)S(1)}, u32[]{:S(2)}, u32[]{:S(2)}) collective-permute-start(bf16[128,256]{1,0:T(8,128)(2,1)S(1)} %slice.25.refs_4_), channel_id=1, source_target_pairs={{0,16},{2,18},{4,20},{6,22},{8,24},{10,26},{12,28},{14,30},{16,0},... | collective-permute-start | bytes 196616 | tf_op jit(solution)/shard_map/ppermute | solution.py:172
  8.2 5.4 %collective-permute-start.3 = (bf16[128,256]{1,0:T(8,128)(2,1)S(1)}, bf16[128,256]{1,0:T(8,128)(2,1)S(1)}, u32[]{:S(2)}, u32[]{:S(2)}) collective-permute-start(bf16[128,256]{1,0:T(8,128)(2,1)S(1)} %slice.25.refs_4_), channel_id=1, source_target_pairs={{0,8},{2,10},{4,12},{6,14},{8,0},{10,2},{12,4},{14,6},{16,24},{18,... | collective-permute-start | bytes 196616 | tf_op jit(solution)/shard_map/ppermute | solution.py:172
  8.9 4.6 %collective-permute-start = (bf16[256,256]{1,0:T(8,128)(2,1)S(1)}, bf16[256,256]{1,0:T(8,128)(2,1)S(1)}, u32[]{:S(2)}, u32[]{:S(2)}) collective-permute-start(bf16[256,256]{1,0:T(8,128)(2,1)S(1)} %slice.24.refs_0_), channel_id=1, source_target_pairs={{0,2},{2,0},{4,6},{6,4},{8,10},{10,8},{12,14},{14,12},{16,18},{18,... | collective-permute-start | bytes 393224 | tf_op jit(solution)/shard_map/ppermute | solution.py:172
  9.7 3.9 %collective-permute-start.2 = (bf16[256,256]{1,0:T(8,128)(2,1)S(1)}, bf16[256,256]{1,0:T(8,128)(2,1)S(1)}, u32[]{:S(2)}, u32[]{:S(2)}) collective-permute-start(bf16[256,256]{1,0:T(8,128)(2,1)S(1)} %collective-permute-done.1.refs_2_), channel_id=1, source_target_pairs={{0,2},{2,0},{4,6},{6,4},{8,10},{10,8},{12,14},{14,12},{16,18},{18,... | collective-permute-start | bytes 393224 | tf_op jit(solution)/shard_map/ppermute | solution.py:172
  14.7 3.1 %collective-permute-start.8 = (f32[2,1024]{1,0:T(2,128)S(1)}, f32[2,1024]{1,0:T(2,128)S(1)}, u32[]{:S(2)}, u32[]{:S(2)}) collective-permute-start(f32[2,1024]{1,0:T(2,128)S(1)} %get-tuple-element.19.refs_8_), channel_id=1, source_target_pairs={{0,6},{2,4},{4,2},{6,0},{8,14},{10,12},{12,10},{14,8},{16,22},{18,... | collective-permute-start | bytes 24584 | tf_op jit(solution)/shard_map/ppermute | solution.py:172
  14.8 3.7 %collective-permute-start.7 = (f32[2,1024]{1,0:T(2,128)S(1)}, f32[2,1024]{1,0:T(2,128)S(1)}, u32[]{:S(2)}, u32[]{:S(2)}) collective-permute-start(f32[2,1024]{1,0:T(2,128)S(1)} %get-tuple-element.19.refs_8_), channel_id=1, source_target_pairs={{0,4},{2,6},{4,0},{6,2},{8,12},{10,14},{12,8},{14,10},{16,20},{18,... | collective-permute-start | bytes 24584 | tf_op jit(solution)/shard_map/ppermute | solution.py:172
  15.8 2.7 %collective-permute-start.6 = (f32[2,1024]{1,0:T(2,128)S(1)}, f32[2,1024]{1,0:T(2,128)S(1)}, u32[]{:S(2)}, u32[]{:S(2)}) collective-permute-start(f32[2,1024]{1,0:T(2,128)S(1)} %get-tuple-element.19.refs_8_), channel_id=1, source_target_pairs={{0,2},{2,0},{4,6},{6,4},{8,10},{10,8},{12,14},{14,12},{16,18},{18,... | collective-permute-start | bytes 24584 | tf_op jit(solution)/shard_map/ppermute | solution.py:172
  19.5 4.3 %collective-permute-start.11 = (bf16[128,256]{1,0:T(8,128)(2,1)S(1)}, bf16[128,256]{1,0:T(8,128)(2,1)S(1)}, u32[]{:S(2)}, u32[]{:S(2)}) collective-permute-start(bf16[128,256]{1,0:T(8,128)(2,1)S(1)} %get-tuple-element.26), channel_id=1, source_target_pairs={{0,1},{1,0},{2,3},{3,2},{4,5},{5,4},{6,7},{7,6},{8,9},{9,8},{10,11... | collective-permute-start | bytes 196616 | tf_op jit(solution)/shard_map/ppermute | solution.py:175
  21.1 6.1 %collective-permute-start.14 = (bf16[128,256]{1,0:T(8,128)(2,1)S(1)}, bf16[128,256]{1,0:T(8,128)(2,1)S(1)}, u32[]{:S(2)}, u32[]{:S(2)}) collective-permute-start(bf16[128,256]{1,0:T(8,128)(2,1)S(1)} %get-tuple-element.28), channel_id=1, source_target_pairs={{0,8},{2,10},{4,12},{6,14},{8,0},{10,2},{12,4},{14,6},{16,24},{18,... | collective-permute-start | bytes 196616 | tf_op jit(solution)/shard_map/ppermute | solution.py:172
  22.1 5.0 %collective-permute-start.9 = (bf16[256,256]{1,0:T(8,128)(2,1)S(1)}, bf16[256,256]{1,0:T(8,128)(2,1)S(1)}, u32[]{:S(2)}, u32[]{:S(2)}) collective-permute-start(bf16[256,256]{1,0:T(8,128)(2,1)S(1)} %get-tuple-element.24), channel_id=1, source_target_pairs={{0,4},{2,6},{4,0},{6,2},{8,12},{10,14},{12,8},{14,10},{16,20},{18,... | collective-permute-start | bytes 393224 | tf_op jit(solution)/shard_map/ppermute | solution.py:172
  23.9 5.8 %collective-permute-start.13 = (bf16[64,256]{1,0:T(8,128)(2,1)S(1)}, bf16[64,256]{1,0:T(8,128)(2,1)S(1)}, u32[]{:S(2)}, u32[]{:S(2)}) collective-permute-start(bf16[64,256]{1,0:T(8,128)(2,1)S(1)} %get-tuple-element.35), channel_id=1, source_target_pairs={{0,24},{2,26},{4,28},{6,30},{8,16},{10,18},{12,20},{14,22},{16,8},... | collective-permute-start | bytes 98312 | tf_op jit(solution)/shard_map/ppermute | solution.py:172
  26.6 4.8 %collective-permute-start.12 = (bf16[64,256]{1,0:T(8,128)(2,1)S(1)}, bf16[64,256]{1,0:T(8,128)(2,1)S(1)}, u32[]{:S(2)}, u32[]{:S(2)}) collective-permute-start(bf16[64,256]{1,0:T(8,128)(2,1)S(1)} %get-tuple-element.36), channel_id=1, source_target_pairs={{0,16},{2,18},{4,20},{6,22},{8,24},{10,26},{12,28},{14,30},{16,0},... | collective-permute-start | bytes 98312 | tf_op jit(solution)/shard_map/ppermute | solution.py:172
  27.1 1.3 %collective-permute-start.10 = (bf16[128,256]{1,0:T(8,128)(2,1)S(1)}, bf16[128,256]{1,0:T(8,128)(2,1)S(1)}, u32[]{:S(2)}, u32[]{:S(2)}) collective-permute-start(bf16[128,256]{1,0:T(8,128)(2,1)S(1)} %slice.26), channel_id=1, source_target_pairs={{0,2},{2,0},{4,6},{6,4},{8,10},{10,8},{12,14},{14,12},{16,18},{18,... | collective-permute-start | bytes 196616 | tf_op jit(solution)/shard_map/ppermute | solution.py:172
  27.2 4.1 %collective-permute-start.15 = (bf16[64,256]{1,0:T(8,128)(2,1)S(1)}, bf16[64,256]{1,0:T(8,128)(2,1)S(1)}, u32[]{:S(2)}, u32[]{:S(2)}) collective-permute-start(bf16[64,256]{1,0:T(8,128)(2,1)S(1)} %slice.29), channel_id=1, source_target_pairs={{0,1},{1,0},{2,3},{3,2},{4,5},{5,4},{6,7},{7,6},{8,9},{9,8},{10,11... | collective-permute-start | bytes 98312 | tf_op jit(solution)/shard_map/ppermute | solution.py:175

commit v8 on v7

--- a/solution.py
+++ b/solution.py
@@ -21,7 +21,7 @@
 
 def offsets(size):
     group = (0, 1, 2, 3)
-    return group, tuple(range(0, size, 4))
+    return group, tuple(range(0, size, GROUP))
 
 
 def place_kernel(group, chunk, docs, ints, place_ref):
@@ -54,18 +54,18 @@
     return jnp.concatenate([ref[at, h * hd : (h + 1) * hd] for h in range(heads)], axis=0)
 
 
-def stats_kernel(chunks, heads, place_ref, *refs):
-    group, chunk = refs[:GROUP], refs[GROUP : GROUP + chunks]
-    out_ref, top_ref, expo_ref, dprobs_ref = refs[GROUP + chunks :]
+def stats_kernel(which, heads, place_ref, *refs):
+    count = len(which)
+    group, chunk = refs[:GROUP], refs[GROUP : GROUP + count]
+    *before, out_ref, top_ref, expo_ref, dprobs_ref = refs[GROUP + count :]
     rows, width = chunk[0].shape
     hd = width // 2
     factor = hd ** (-0.5) * log2_e
     keys = jnp.concatenate([c[:, :hd] for c in chunk], axis=0)
     values = jnp.concatenate([c[:, hd:] for c in chunk], axis=0)
     at = lax.broadcasted_iota(jnp.int32, (rows // 2, rows), 0)
-    key_pos = jnp.concatenate(
-        [at + place_ref[2 * GROUP + s : 2 * GROUP + s + 1, :] for s in range(2 * chunks)], axis=0
-    )
+    spans = [2 * (GROUP + b) + h for b in which for h in range(2)]
+    key_pos = jnp.concatenate([at + place_ref[s : s + 1, :] for s in spans], axis=0)
     for j in range(GROUP):
         pos, opens = place_ref[j : j + 1, :], place_ref[GROUP + j : GROUP + j + 1, :]
         allowed = (key_pos <= pos) & (key_pos >= opens)
@@ -76,20 +76,34 @@
         top = jnp.max(scores, axis=0, keepdims=True)
         expo = jnp.exp2(scores - top)
         total = jnp.sum(expo, axis=0, keepdims=True)
-        at = pl.ds(j * heads * rows, heads * rows)
-        out_ref[0:1, at] = top + jnp.log2(total)
-        out_ref[1:2, at] = jnp.sum(expo * dprobs, axis=0, keepdims=True) / total
-        top_ref[0:1, at] = top
-        expo_ref[:, at] = expo
-        dprobs_ref[:, at] = dprobs
-
-
-def backward_kernel(chunks, heads, shards, *refs):
+        log_total = top + jnp.log2(total)
+        delta = jnp.sum(expo * dprobs, axis=0, keepdims=True) / total
+        at_j = pl.ds(j * heads * rows, heads * rows)
+        if before:
+            parts = [jnp.concatenate([log_total, delta], axis=0), before[0][:, at_j]]
+            log_total, delta = merged(parts)
+        out_ref[0:1, at_j] = log_total
+        out_ref[1:2, at_j] = delta
+        top_ref[0:1, at_j] = top
+        expo_ref[:, at_j] = expo
+        dprobs_ref[:, at_j] = dprobs
+
+
+def merged(parts):
+    largest = functools.reduce(jnp.maximum, [p[0:1] for p in parts])
+    share = [jnp.exp2(p[0:1] - largest) for p in parts]
+    total = sum(share)
+    delta = sum(w * p[1:2] for w, p in zip(share, parts)) / total
+    return largest + jnp.log2(total), delta
+
+
+def backward_kernel(order, late, heads, shards, *refs):
+    chunks = len(order)
     group, chunk = refs[:GROUP], refs[GROUP : GROUP + chunks]
-    stats = refs[GROUP + chunks : 2 * GROUP + chunks]
-    top_ref, expo_ref, dprobs_ref, near_ref, far_ref = refs[2 * GROUP + chunks :][:5]
-    outs = refs[2 * GROUP + chunks + 5 : -2]
-    dv_total, dk_total = refs[-2:]
+    chunk = chunk[late:] + chunk[:late]
+    stats, refs = refs[GROUP + chunks :][:GROUP], refs[2 * GROUP + chunks :]
+    (tops, expos, dprobs), refs = (refs[0:2], refs[2:4], refs[4:6]), refs[6:]
+    near_ref, far_ref, *outs, dv_total, dk_total = refs
     rows, width = chunk[0].shape
     hd = width // 2
     shard = lax.axis_index("head")
@@ -101,14 +115,13 @@
         parts = [
             s[0:2, pl.ds((j ^ t) * heads * rows, heads * rows)] for t, s in enumerate(stats)
         ]
-        largest = functools.reduce(jnp.maximum, [p[0:1] for p in parts])
-        share = [jnp.exp2(p[0:1] - largest) for p in parts]
-        total = sum(share)
-        delta = sum(w * p[1:2] for w, p in zip(share, parts)) / total
-        own = jnp.exp2(top_ref[0:1, at] - largest) / total
-        weights = expo_ref[:, at] * own
+        log_total, delta = merged(parts)
+        weights = jnp.concatenate(
+            [e[:, at] * jnp.exp2(t[0:1, at] - log_total) for e, t in zip(expos, tops)], axis=0
+        )
+        differences = jnp.concatenate([d[:, at] for d in dprobs], axis=0) - delta
         weights_low = weights.astype(jnp.bfloat16)
-        dscores = (weights * (dprobs_ref[:, at] - delta)).astype(jnp.bfloat16)
+        dscores = (weights * differences).astype(jnp.bfloat16)
         dv = dot(weights_low, both_heads(group[j], heads, 1), NN)
         dk = dot(dscores, both_heads(group[j], heads, 0), NN)
         if j == 0:
@@ -127,7 +140,7 @@
     for t in range(shards):
         owner = lax.rem(shard + t, shards)
         for b in range(chunks):
-            at = pl.ds(pl.multiple_of(b * rows + owner * part, part), part)
+            at = pl.ds(pl.multiple_of(order.index(b) * rows + owner * part, part), part)
             if b < half:
                 out, to = outs[b], pl.ds(t * part, part)
             else:
@@ -201,34 +214,43 @@
     beside = swap(packed_qg, group_bits[1])
     group = [packed_qg, beside, across, swap(across, group_bits[1])]
 
-    square = array((chunks * rows, GROUP * heads * rows), jnp.float32)
-    stats, top, expo, dprobs = pl.pallas_call(
-        functools.partial(stats_kernel, chunks, heads),
-        out_shape=(
-            array((2, GROUP * heads * rows), jnp.float32),
-            array((1, GROUP * heads * rows), jnp.float32),
-            square,
-            square,
-        ),
-        in_specs=[vmem] * (1 + GROUP + chunks),
-        out_specs=(vmem, vmem, vmem, vmem),
-        compiler_params=params,
-        name="stats",
-    )(place, *group, *chunk)
+    late = tuple(range(1, 3 * chunks // 4))
+    early = (0, *range(3 * chunks // 4, chunks))
+
+    def stats_of(which, before, flops):
+        wide = array((len(which) * rows, GROUP * heads * rows), jnp.float32)
+        return pl.pallas_call(
+            functools.partial(stats_kernel, which, heads),
+            out_shape=(
+                array((2, GROUP * heads * rows), jnp.float32),
+                array((1, GROUP * heads * rows), jnp.float32),
+                wide,
+                wide,
+            ),
+            in_specs=[vmem] * (1 + GROUP + len(which) + len(before)),
+            out_specs=(vmem, vmem, vmem, vmem),
+            compiler_params=params,
+            cost_estimate=pl.CostEstimate(flops=flops, bytes_accessed=0, transcendentals=0),
+            name="stats",
+        )(place, *group, *[chunk[b] for b in which], *before)
+
+    first, *kept_early = stats_of(early, (), 0)
+    stats, *kept_late = stats_of(late, (first,), 0)
+    kept = [ref for pair in zip(kept_early, kept_late) for ref in pair]
     all_stats = [stats] + [swap(stats, bits) for bits in group_bits[1:]]
 
     pair_rows = array((GROUP // 2 * rows, width))
     half = chunks // 2
     pieces = (array((rows, 2 * hd)),) * half + (array((half * part, 2 * hd)),) * shards
     near, far, *dkv = pl.pallas_call(
-        functools.partial(backward_kernel, chunks, heads, shards),
+        functools.partial(backward_kernel, early + late, len(late), heads, shards),
         out_shape=(pair_rows, pair_rows) + pieces,
-        in_specs=[vmem] * (2 * GROUP + chunks + 3),
+        in_specs=[vmem] * (2 * GROUP + chunks + len(kept)),
         out_specs=(vmem,) * (2 + len(pieces)),
         scratch_shapes=[pltpu.VMEM((chunks * rows, hd), jnp.float32)] * 2,
         compiler_params=params,
         name="backward",
-    )(*group, *chunk, *all_stats, top, expo, dprobs)
+    )(*group, *[chunk[b] for b in late + early], *all_stats, *kept)
 
     def fold(parts, flops):
         return pl.pallas_call(
@@ -244,7 +266,7 @@
     across = fold([dkv[half]] + [turn(dkv[half + t], t) for t in range(1, shards)], 0)
     owned = fold([dkv[0]] + [swap(dkv[b], chunk_bits[b]) for b in range(1, half)], 1000000000)
     came = [
-        swap(across[k * part : (k + 1) * part], chunk_bits[half + k]) for k in range(half)
+        swap(across[k * part : (k + 1) * part], chunk_bits[half + k]) for k in range(half)[::-1]
     ] + [turn(owned[t * part : (t + 1) * part], t) for t in range(1, shards)]
     pair = (near.astype(jnp.float32) + swap(far, group_bits[2]).astype(jnp.float32)).astype(jnp.bfloat16)
     other = swap(pair[rows:], group_bits[1])

time: 32.2 us -> 31.8 us (0.988)
  starting transfers between devices: 16.8 us -> 18 us
  other arithmetic: 1.65 us -> 1 us
  local copies, waits for them, and re-layouts: 0.79 us -> 0.18 us
  waiting for transfers between devices: 8.03 us -> 7.54 us
    ppermute x14, starting transfers between devices: 14.1 us -> 14.9 us  [swap(): return lax.ppermute(x, 'ctx', [(i, i ^ bits) for i in range(ctx_size)])]
    reshape x1, local copies, waits for them, and re-layouts: 0.76 us -> 0.08 us  [local(): span_order.T.reshape(-1)]
    concatenate x1, other arithmetic: 0.73 us -> 0.07 us  [local(): jnp.concatenate([doc_lengths, span_order.T.reshape(-1)])]
    ppermute x14, waiting for transfers between devices: 6.81 us -> 6.28 us  [swap(): return lax.ppermute(x, 'ctx', [(i, i ^ bits) for i in range(ctx_size)])]
    ppermute x2, starting transfers between devices: 2.7 us -> 3.18 us  [turn(): lax.ppermute(x, 'head', [(i, (i + by) % shards) for i in range(shards)])]
    pallas_call x2 -> x3, Pallas kernels: 2.13 us -> 2.24 us  [the longest x2 1.25 us: stats_of(): pl.pallas_call(functools.partial(stats_kernel, which, heads), out_shape=(...]
  transfers between devices with their start and end apart: 16 -> 16, of which waited for: 9 -> 7; matrix products, arithmetic and copies ran while one was open for 5% -> 1% of each run, Pallas kernels for 4% -> 6%
where the time goes in v8:
time: 31.8 us; the launch traced here: 31.6 us
  starting transfers between devices  18 us (57%)
  waiting for transfers between devices  7.54 us (24%)
  Pallas kernels  4.12 us (13%)
  other arithmetic  1 us (3%)
  between operations  0.75 us (2%)
    ppermute x14, starting transfers between devices, swap(): return lax.ppermute(x, 'ctx', [(i, i ^ bits) for i in range(ctx_size)])  14.9 us
    ppermute x14, waiting for transfers between devices, swap(): return lax.ppermute(x, 'ctx', [(i, i ^ bits) for i in range(ctx_size)])  6.28 us
    ppermute x2, starting transfers between devices, turn(): lax.ppermute(x, 'head', [(i, (i + by) % shards) for i in range(shards)])  3.18 us
    ppermute x2, waiting for transfers between devices, turn(): lax.ppermute(x, 'head', [(i, (i + by) % shards) for i in range(shards)])  1.25 us
    pallas_call x2, Pallas kernels, stats_of(): pl.pallas_call(functools.partial(stats_kernel, which, heads), out_shape=(...  1.25 us
    pallas_call x1, Pallas kernels, local(): pl.pallas_call(functools.partial(backward_kernel, early + late, len(late)...  0.99 us
    concatenate x1, other arithmetic, local(): jnp.concatenate([jnp.concatenate([key_rows, value_rows], axis=1), queries...  0.89 us
    pallas_call x1, Pallas kernels, local(): pl.pallas_call(query_sum_kernel, out_shape=array((rows, width)), in_specs...  0.65 us
  transfers between devices with their start and end apart: 16, of which 7 were waited for; matrix products, arithmetic and copies ran while one was open for 1% of the time, Pallas kernels for 6%

profile of v8, /device:TPU:0, one launch (start us, length us, event | category | flops | bytes accessed | tf_op | source)
XLA Modules:
  0.0 31.6 jit_solution(7516798247264768510)
XLA Ops:
  0.6 0.9 %pad_maximum_fusion = bf16[384,256]{1,0:T(8,128)(2,1)S(1)} fusion(bf16[128,256]{1,0:T(8,128)(2,1)} %param.9, bf16[128,256]{1,0:T(8,128)(2,1)} %param.6, bf16[128,128]{1,0:T(8,128)(2,1)} %param.8, bf16[128,128]{1,0:T(8,128)(2,1)} %param.7), kind=kLoop, calls=%fused_computation.1 | loop fusion | flops 786432 | bytes 393216 | tf_op jit(solution)/shard_map/concatenate | solution.py:207
  1.5 3.0 %collective-permute-start.1 = (bf16[256,256]{1,0:T(8,128)(2,1)S(1)}, bf16[256,256]{1,0:T(8,128)(2,1)S(1)}, u32[]{:S(2)}, u32[]{:S(2)}) collective-permute-start(bf16[256,256]{1,0:T(8,128)(2,1)S(1)} %slice.24.refs_0_), channel_id=1, source_target_pairs={{0,4},{2,6},{4,0},{6,2},{8,12},{10,14},{12,8},{14,10},{16,20},{18,... | collective-permute-start | bytes 393224 | tf_op jit(solution)/shard_map/ppermute | solution.py:185
  4.6 0.0 copy-start
  4.6 3.7 %collective-permute-start.5 = (bf16[128,256]{1,0:T(8,128)(2,1)S(1)}, bf16[128,256]{1,0:T(8,128)(2,1)S(1)}, u32[]{:S(2)}, u32[]{:S(2)}) collective-permute-start(bf16[128,256]{1,0:T(8,128)(2,1)S(1)} %slice.25.refs_4_.refs_6_), channel_id=1, source_target_pairs={{0,24},{2,26},{4,28},{6,30},{8,16},{10,18},{12,20},{14,22},{16,8},... | collective-permute-start | bytes 196616 | tf_op jit(solution)/shard_map/ppermute | solution.py:185
  8.2 0.0 collective-permute-start.4
  8.2 0.8 %collective-permute-start.3 = (bf16[128,256]{1,0:T(8,128)(2,1)S(1)}, bf16[128,256]{1,0:T(8,128)(2,1)S(1)}, u32[]{:S(2)}, u32[]{:S(2)}) collective-permute-start(bf16[128,256]{1,0:T(8,128)(2,1)S(1)} %slice.25.refs_4_.refs_6_), channel_id=1, source_target_pairs={{0,8},{2,10},{4,12},{6,14},{8,0},{10,2},{12,4},{14,6},{16,24},{18,... | collective-permute-start | bytes 196616 | tf_op jit(solution)/shard_map/ppermute | solution.py:185
  9.0 0.0 collective-permute-start
  9.0 0.0 copy-done
  9.0 0.0 copy-start.1
  9.0 0.1 reshape.9
  9.1 0.0 collective-permute-done.1.refs_2_
  9.1 0.5 %collective-permute-start.2 = (bf16[256,256]{1,0:T(8,128)(2,1)S(1)}, bf16[256,256]{1,0:T(8,128)(2,1)S(1)}, u32[]{:S(2)}, u32[]{:S(2)}) collective-permute-start(bf16[256,256]{1,0:T(8,128)(2,1)S(1)} %collective-permute-done.1.refs_2_), channel_id=1, source_target_pairs={{0,2},{2,0},{4,6},{6,4},{8,10},{10,8},{12,14},{14,12},{16,18},{18,... | collective-permute-start | bytes 393224 | tf_op jit(solution)/shard_map/ppermute | solution.py:185
  9.6 0.1 copy-done.1
  9.7 0.1 pad_add_fusion.ints
  9.7 0.6 %place.1.place_ref = s32[16,128]{1,0:T(8,128)S(1)} custom-call(s32[40]{0:T(128)S(1)} %pad_add_fusion.ints), custom_call_target="tpu_custom_call" | custom-call | flops 1000000000 | tf_op jit(solution)/shard_map/place/pallas_call | solution.py:197
  10.3 1.2 %collective-permute-done.5.refs_5_.refs_7_ = bf16[128,256]{1,0:T(8,128)(2,1)S(1)} collective-permute-done((bf16[128,256]{1,0:T(8,128)(2,1)S(1)}, bf16[128,256]{1,0:T(8,128)(2,1)S(1)}, u32[]{:S(2)}, u32[]{:S(2)}) %collective-permute-start.5) | collective-permute-done | bytes 65568 | tf_op jit(solution)/shard_map/ppermute | solution.py:185
  11.5 0.0 collective-permute-done.refs_1_
  11.5 0.0 collective-permute-done.2.refs_3_
  11.5 0.6 %stats.2 = (f32[2,1024]{1,0:T(2,128)S(1)}, f32[1,1024]{1,0:T(1,128)S(1)}, f32[256,1024]{1,0:T(8,128)S(1)}, f32[256,1024]{1,0:T(8,128)S(1)}) custom-call(s32[16,128]{1,0:T(8,128)S(1)} %place.1.place_ref, bf16[256,256]{1,0:T(8,128)(2,1)S(1)} %slice.24.refs_0_, bf16[256,256]{1,0:T(8,128)(2,1)S(1)} %collective-permute-done.refs_1_, ...), custom_call_target="tpu_custom_call" | custom-call | tf_op jit(solution)/shard_map/stats/pallas_call | solution.py:222
  12.1 1.5 %collective-permute-done.4.refs_5_ = bf16[128,256]{1,0:T(8,128)(2,1)S(1)} collective-permute-done((bf16[128,256]{1,0:T(8,128)(2,1)S(1)}, bf16[128,256]{1,0:T(8,128)(2,1)S(1)}, u32[]{:S(2)}, u32[]{:S(2)}) %collective-permute-start.4) | collective-permute-done | bytes 65568 | tf_op jit(solution)/shard_map/ppermute | solution.py:185
  13.6 0.1 collective-permute-done.3.refs_4_
  13.7 0.6 %stats.3 = (f32[2,1024]{1,0:T(2,128)S(1)}, f32[1,1024]{1,0:T(1,128)S(1)}, f32[256,1024]{1,0:T(8,128)S(1)}, f32[256,1024]{1,0:T(8,128)S(1)}) custom-call(s32[16,128]{1,0:T(8,128)S(1)} %place.1.place_ref, bf16[256,256]{1,0:T(8,128)(2,1)S(1)} %slice.24.refs_0_, bf16[256,256]{1,0:T(8,128)(2,1)S(1)} %collective-permute-done.refs_1_, ...), custom_call_target="tpu_custom_call" | custom-call | tf_op jit(solution)/shard_map/stats/pallas_call | solution.py:222
  14.3 0.1 collective-permute-start.8
  14.4 1.0 %collective-permute-start.7 = (f32[2,1024]{1,0:T(2,128)S(1)}, f32[2,1024]{1,0:T(2,128)S(1)}, u32[]{:S(2)}, u32[]{:S(2)}) collective-permute-start(f32[2,1024]{1,0:T(2,128)S(1)} %get-tuple-element.24.refs_8_), channel_id=1, source_target_pairs={{0,4},{2,6},{4,0},{6,2},{8,12},{10,14},{12,8},{14,10},{16,20},{18,... | collective-permute-start | bytes 24584 | tf_op jit(solution)/shard_map/ppermute | solution.py:185
  15.4 0.8 %collective-permute-start.6 = (f32[2,1024]{1,0:T(2,128)S(1)}, f32[2,1024]{1,0:T(2,128)S(1)}, u32[]{:S(2)}, u32[]{:S(2)}) collective-permute-start(f32[2,1024]{1,0:T(2,128)S(1)} %get-tuple-element.24.refs_8_), channel_id=1, source_target_pairs={{0,2},{2,0},{4,6},{6,4},{8,10},{10,8},{12,14},{14,12},{16,18},{18,... | collective-permute-start | bytes 24584 | tf_op jit(solution)/shard_map/ppermute | solution.py:185
  16.2 1.2 %collective-permute-done.8.refs_11_ = f32[2,1024]{1,0:T(2,128)S(1)} collective-permute-done((f32[2,1024]{1,0:T(2,128)S(1)}, f32[2,1024]{1,0:T(2,128)S(1)}, u32[]{:S(2)}, u32[]{:S(2)}) %collective-permute-start.8) | collective-permute-done | bytes 8224 | tf_op jit(solution)/shard_map/ppermute | solution.py:185
  17.4 0.7 %collective-permute-done.7.refs_10_ = f32[2,1024]{1,0:T(2,128)S(1)} collective-permute-done((f32[2,1024]{1,0:T(2,128)S(1)}, f32[2,1024]{1,0:T(2,128)S(1)}, u32[]{:S(2)}, u32[]{:S(2)}) %collective-permute-start.7) | collective-permute-done | bytes 8224 | tf_op jit(solution)/shard_map/ppermute | solution.py:185
  18.1 0.0 collective-permute-done.6.refs_9_
  18.1 1.0 %backward.1 = (bf16[256,256]{1,0:T(8,128)(2,1)S(1)}, bf16[256,256]{1,0:T(8,128)(2,1)S(1)}, bf16[128,256]{1,0:T(8,128)(2,1)S(1)}, bf16[128,256]{1,0:T(8,128)(2,1)...) custom-call(bf16[256,256]{1,0:T(8,128)(2,1)S(1)} %slice.24.refs_0_, ...), custom_call_target="tpu_custom_call" | custom-call | tf_op jit(solution)/shard_map/backward/pallas_call | solution.py:245
  19.1 1.6 %collective-permute-start.11 = (bf16[128,256]{1,0:T(8,128)(2,1)S(1)}, bf16[128,256]{1,0:T(8,128)(2,1)S(1)}, u32[]{:S(2)}, u32[]{:S(2)}) collective-permute-start(bf16[128,256]{1,0:T(8,128)(2,1)S(1)} %get-tuple-element.34), channel_id=1, source_target_pairs={{0,1},{1,0},{2,3},{3,2},{4,5},{5,4},{6,7},{7,6},{8,9},{9,8},{10,11... | collective-permute-start | bytes 196616 | tf_op jit(solution)/shard_map/ppermute | solution.py:188
  20.7 1.0 %collective-permute-start.14 = (bf16[128,256]{1,0:T(8,128)(2,1)S(1)}, bf16[128,256]{1,0:T(8,128)(2,1)S(1)}, u32[]{:S(2)}, u32[]{:S(2)}) collective-permute-start(bf16[128,256]{1,0:T(8,128)(2,1)S(1)} %get-tuple-element.36), channel_id=1, source_target_pairs={{0,8},{2,10},{4,12},{6,14},{8,0},{10,2},{12,4},{14,6},{16,24},{18,... | collective-permute-start | bytes 196616 | tf_op jit(solution)/shard_map/ppermute | solution.py:185
  21.6 0.6 %collective-permute-start.9 = (bf16[256,256]{1,0:T(8,128)(2,1)S(1)}, bf16[256,256]{1,0:T(8,128)(2,1)S(1)}, u32[]{:S(2)}, u32[]{:S(2)}) collective-permute-start(bf16[256,256]{1,0:T(8,128)(2,1)S(1)} %get-tuple-element.32), channel_id=1, source_target_pairs={{0,4},{2,6},{4,0},{6,2},{8,12},{10,14},{12,8},{14,10},{16,20},{18,... | collective-permute-start | bytes 393224 | tf_op jit(solution)/shard_map/ppermute | solution.py:185
  22.2 1.2 %collective-permute-done.11.refs_1_ = bf16[128,256]{1,0:T(8,128)(2,1)S(1)} collective-permute-done((bf16[128,256]{1,0:T(8,128)(2,1)S(1)}, bf16[128,256]{1,0:T(8,128)(2,1)S(1)}, u32[]{:S(2)}, u32[]{:S(2)}) %collective-permute-start.11) | collective-permute-done | bytes 65568 | tf_op jit(solution)/shard_map/ppermute | solution.py:188
  23.5 1.8 %collective-permute-start.13 = (bf16[64,256]{1,0:T(8,128)(2,1)S(1)}, bf16[64,256]{1,0:T(8,128)(2,1)S(1)}, u32[]{:S(2)}, u32[]{:S(2)}) collective-permute-start(bf16[64,256]{1,0:T(8,128)(2,1)S(1)} %get-tuple-element.43), channel_id=1, source_target_pairs={{0,16},{2,18},{4,20},{6,22},{8,24},{10,26},{12,28},{14,30},{16,0},... | collective-permute-start | bytes 98312 | tf_op jit(solution)/shard_map/ppermute | solution.py:185
  25.3 1.6 %collective-permute-start.12 = (bf16[64,256]{1,0:T(8,128)(2,1)S(1)}, bf16[64,256]{1,0:T(8,128)(2,1)S(1)}, u32[]{:S(2)}, u32[]{:S(2)}) collective-permute-start(bf16[64,256]{1,0:T(8,128)(2,1)S(1)} %get-tuple-element.44), channel_id=1, source_target_pairs={{0,24},{2,26},{4,28},{6,30},{8,16},{10,18},{12,20},{14,22},{16,8},... | collective-permute-start | bytes 98312 | tf_op jit(solution)/shard_map/ppermute | solution.py:185
  26.8 0.0 collective-permute-done.9
  26.9 0.1 collective-permute-start.10
  27.0 0.0 collective-permute-done.14.refs_1_
  27.0 1.6 %collective-permute-start.15 = (bf16[64,256]{1,0:T(8,128)(2,1)S(1)}, bf16[64,256]{1,0:T(8,128)(2,1)S(1)}, u32[]{:S(2)}, u32[]{:S(2)}) collective-permute-start(bf16[64,256]{1,0:T(8,128)(2,1)S(1)} %slice.29), channel_id=1, source_target_pairs={{0,1},{1,0},{2,3},{3,2},{4,5},{5,4},{6,7},{7,6},{8,9},{9,8},{10,11... | collective-permute-start | bytes 98312 | tf_op jit(solution)/shard_map/ppermute | solution.py:188
  28.6 0.0 collective-permute-done.10.other_ref
  28.6 0.6 %query_sum.1 = bf16[128,256]{1,0:T(8,128)(2,1)} custom-call(bf16[256,256]{1,0:T(8,128)(2,1)S(1)} %add_convert_fusion.pair_ref, bf16[128,256]{1,0:T(8,128)(2,1)S(1)} %collective-permute-done.10.other_ref), custom_call_target="tpu_custom_call" | custom-call | flops 1000000000 | tf_op jit(solution)/shard_map/query_sum/pallas_call | solution.py:273
  29.3 0.0 collective-permute-done.13.refs_1_
  29.3 1.7 %collective-permute-done.12.refs_0_ = bf16[64,256]{1,0:T(8,128)(2,1)S(1)} collective-permute-done((bf16[64,256]{1,0:T(8,128)(2,1)S(1)}, bf16[64,256]{1,0:T(8,128)(2,1)S(1)}, u32[]{:S(2)}, u32[]{:S(2)}) %collective-permute-start.12) | collective-permute-done | bytes 32800 | tf_op jit(solution)/shard_map/ppermute | solution.py:185
  31.0 0.0 collective-permute-done.15.refs_2_
  31.0 0.6 %finish.1 = (bf16[64,128]{1,0:T(8,128)(2,1)}, bf16[64,128]{1,0:T(8,128)(2,1)}) custom-call(bf16[128,256]{1,0:T(8,128)(2,1)S(1)} %fold.3.owned_ref, bf16[64,256]{1,0:T(8,128)(2,1)S(1)} %collective-permute-done.12.refs_0_, bf16[64,256]{1,0:T(8,128)(2,1)S(1)} %collective-permute-done.13.refs_1_, bf16[64,256]{1,0:T(8,128)(2,1)S(1)} %collective-permute-done.15.refs_2_), custom_call_target="tpu_custom_call" | custom-call | tf_op jit(solution)/shard_map/finish/pallas_call | solution.py:283
  (8 shorter events, 0.1 us)
Async XLA Ops:
  1.5 7.6 %collective-permute-start.1 = (bf16[256,256]{1,0:T(8,128)(2,1)S(1)}, bf16[256,256]{1,0:T(8,128)(2,1)S(1)}, u32[]{:S(2)}, u32[]{:S(2)}) collective-permute-start(bf16[256,256]{1,0:T(8,128)(2,1)S(1)} %slice.24.refs_0_), channel_id=1, source_target_pairs={{0,4},{2,6},{4,0},{6,2},{8,12},{10,14},{12,8},{14,10},{16,20},{18,... | collective-permute-start | bytes 393224 | tf_op jit(solution)/shard_map/ppermute | solution.py:185
  4.6 4.5 %copy-start = (s32[16,2]{0,1:T(2,128)S(1)}, s32[16,2]{0,1:T(2,128)}, u32[]{:S(2)}) copy-start(s32[16,2]{0,1:T(2,128)} %param.11) | copy-start | bytes 388
  4.6 6.9 %collective-permute-start.5 = (bf16[128,256]{1,0:T(8,128)(2,1)S(1)}, bf16[128,256]{1,0:T(8,128)(2,1)S(1)}, u32[]{:S(2)}, u32[]{:S(2)}) collective-permute-start(bf16[128,256]{1,0:T(8,128)(2,1)S(1)} %slice.25.refs_4_.refs_6_), channel_id=1, source_target_pairs={{0,24},{2,26},{4,28},{6,30},{8,16},{10,18},{12,20},{14,22},{16,8},... | collective-permute-start | bytes 196616 | tf_op jit(solution)/shard_map/ppermute | solution.py:185
  8.2 5.4 %collective-permute-start.4 = (bf16[128,256]{1,0:T(8,128)(2,1)S(1)}, bf16[128,256]{1,0:T(8,128)(2,1)S(1)}, u32[]{:S(2)}, u32[]{:S(2)}) collective-permute-start(bf16[128,256]{1,0:T(8,128)(2,1)S(1)} %slice.25.refs_4_.refs_6_), channel_id=1, source_target_pairs={{0,16},{2,18},{4,20},{6,22},{8,24},{10,26},{12,28},{14,30},{16,0},... | collective-permute-start | bytes 196616 | tf_op jit(solution)/shard_map/ppermute | solution.py:185
  8.2 5.4 %collective-permute-start.3 = (bf16[128,256]{1,0:T(8,128)(2,1)S(1)}, bf16[128,256]{1,0:T(8,128)(2,1)S(1)}, u32[]{:S(2)}, u32[]{:S(2)}) collective-permute-start(bf16[128,256]{1,0:T(8,128)(2,1)S(1)} %slice.25.refs_4_.refs_6_), channel_id=1, source_target_pairs={{0,8},{2,10},{4,12},{6,14},{8,0},{10,2},{12,4},{14,6},{16,24},{18,... | collective-permute-start | bytes 196616 | tf_op jit(solution)/shard_map/ppermute | solution.py:185
  9.0 2.5 %collective-permute-start = (bf16[256,256]{1,0:T(8,128)(2,1)S(1)}, bf16[256,256]{1,0:T(8,128)(2,1)S(1)}, u32[]{:S(2)}, u32[]{:S(2)}) collective-permute-start(bf16[256,256]{1,0:T(8,128)(2,1)S(1)} %slice.24.refs_0_), channel_id=1, source_target_pairs={{0,2},{2,0},{4,6},{6,4},{8,10},{10,8},{12,14},{14,12},{16,18},{18,... | collective-permute-start | bytes 393224 | tf_op jit(solution)/shard_map/ppermute | solution.py:185
  9.0 0.7 %copy-start.1 = (s32[8]{0:T(128)S(1)}, s32[8]{0:T(128)}, u32[]{:S(2)}) copy-start(s32[8]{0:T(128)} %param.10) | copy-start | bytes 100
  9.1 2.4 %collective-permute-start.2 = (bf16[256,256]{1,0:T(8,128)(2,1)S(1)}, bf16[256,256]{1,0:T(8,128)(2,1)S(1)}, u32[]{:S(2)}, u32[]{:S(2)}) collective-permute-start(bf16[256,256]{1,0:T(8,128)(2,1)S(1)} %collective-permute-done.1.refs_2_), channel_id=1, source_target_pairs={{0,2},{2,0},{4,6},{6,4},{8,10},{10,8},{12,14},{14,12},{16,18},{18,... | collective-permute-start | bytes 393224 | tf_op jit(solution)/shard_map/ppermute | solution.py:185
  14.3 3.1 %collective-permute-start.8 = (f32[2,1024]{1,0:T(2,128)S(1)}, f32[2,1024]{1,0:T(2,128)S(1)}, u32[]{:S(2)}, u32[]{:S(2)}) collective-permute-start(f32[2,1024]{1,0:T(2,128)S(1)} %get-tuple-element.24.refs_8_), channel_id=1, source_target_pairs={{0,6},{2,4},{4,2},{6,0},{8,14},{10,12},{12,10},{14,8},{16,22},{18,... | collective-permute-start | bytes 24584 | tf_op jit(solution)/shard_map/ppermute | solution.py:185
  14.4 3.7 %collective-permute-start.7 = (f32[2,1024]{1,0:T(2,128)S(1)}, f32[2,1024]{1,0:T(2,128)S(1)}, u32[]{:S(2)}, u32[]{:S(2)}) collective-permute-start(f32[2,1024]{1,0:T(2,128)S(1)} %get-tuple-element.24.refs_8_), channel_id=1, source_target_pairs={{0,4},{2,6},{4,0},{6,2},{8,12},{10,14},{12,8},{14,10},{16,20},{18,... | collective-permute-start | bytes 24584 | tf_op jit(solution)/shard_map/ppermute | solution.py:185
  15.4 2.7 %collective-permute-start.6 = (f32[2,1024]{1,0:T(2,128)S(1)}, f32[2,1024]{1,0:T(2,128)S(1)}, u32[]{:S(2)}, u32[]{:S(2)}) collective-permute-start(f32[2,1024]{1,0:T(2,128)S(1)} %get-tuple-element.24.refs_8_), channel_id=1, source_target_pairs={{0,2},{2,0},{4,6},{6,4},{8,10},{10,8},{12,14},{14,12},{16,18},{18,... | collective-permute-start | bytes 24584 | tf_op jit(solution)/shard_map/ppermute | solution.py:185
  19.1 4.3 %collective-permute-start.11 = (bf16[128,256]{1,0:T(8,128)(2,1)S(1)}, bf16[128,256]{1,0:T(8,128)(2,1)S(1)}, u32[]{:S(2)}, u32[]{:S(2)}) collective-permute-start(bf16[128,256]{1,0:T(8,128)(2,1)S(1)} %get-tuple-element.34), channel_id=1, source_target_pairs={{0,1},{1,0},{2,3},{3,2},{4,5},{5,4},{6,7},{7,6},{8,9},{9,8},{10,11... | collective-permute-start | bytes 196616 | tf_op jit(solution)/shard_map/ppermute | solution.py:188
  20.7 6.3 %collective-permute-start.14 = (bf16[128,256]{1,0:T(8,128)(2,1)S(1)}, bf16[128,256]{1,0:T(8,128)(2,1)S(1)}, u32[]{:S(2)}, u32[]{:S(2)}) collective-permute-start(bf16[128,256]{1,0:T(8,128)(2,1)S(1)} %get-tuple-element.36), channel_id=1, source_target_pairs={{0,8},{2,10},{4,12},{6,14},{8,0},{10,2},{12,4},{14,6},{16,24},{18,... | collective-permute-start | bytes 196616 | tf_op jit(solution)/shard_map/ppermute | solution.py:185
  21.6 5.2 %collective-permute-start.9 = (bf16[256,256]{1,0:T(8,128)(2,1)S(1)}, bf16[256,256]{1,0:T(8,128)(2,1)S(1)}, u32[]{:S(2)}, u32[]{:S(2)}) collective-permute-start(bf16[256,256]{1,0:T(8,128)(2,1)S(1)} %get-tuple-element.32), channel_id=1, source_target_pairs={{0,4},{2,6},{4,0},{6,2},{8,12},{10,14},{12,8},{14,10},{16,20},{18,... | collective-permute-start | bytes 393224 | tf_op jit(solution)/shard_map/ppermute | solution.py:185
  23.5 5.8 %collective-permute-start.13 = (bf16[64,256]{1,0:T(8,128)(2,1)S(1)}, bf16[64,256]{1,0:T(8,128)(2,1)S(1)}, u32[]{:S(2)}, u32[]{:S(2)}) collective-permute-start(bf16[64,256]{1,0:T(8,128)(2,1)S(1)} %get-tuple-element.43), channel_id=1, source_target_pairs={{0,16},{2,18},{4,20},{6,22},{8,24},{10,26},{12,28},{14,30},{16,0},... | collective-permute-start | bytes 98312 | tf_op jit(solution)/shard_map/ppermute | solution.py:185
  25.3 5.7 %collective-permute-start.12 = (bf16[64,256]{1,0:T(8,128)(2,1)S(1)}, bf16[64,256]{1,0:T(8,128)(2,1)S(1)}, u32[]{:S(2)}, u32[]{:S(2)}) collective-permute-start(bf16[64,256]{1,0:T(8,128)(2,1)S(1)} %get-tuple-element.44), channel_id=1, source_target_pairs={{0,24},{2,26},{4,28},{6,30},{8,16},{10,18},{12,20},{14,22},{16,8},... | collective-permute-start | bytes 98312 | tf_op jit(solution)/shard_map/ppermute | solution.py:185
  26.9 1.7 %collective-permute-start.10 = (bf16[128,256]{1,0:T(8,128)(2,1)S(1)}, bf16[128,256]{1,0:T(8,128)(2,1)S(1)}, u32[]{:S(2)}, u32[]{:S(2)}) collective-permute-start(bf16[128,256]{1,0:T(8,128)(2,1)S(1)} %slice.26), channel_id=1, source_target_pairs={{0,2},{2,0},{4,6},{6,4},{8,10},{10,8},{12,14},{14,12},{16,18},{18,... | collective-permute-start | bytes 196616 | tf_op jit(solution)/shard_map/ppermute | solution.py:185
  27.0 4.0 %collective-permute-start.15 = (bf16[64,256]{1,0:T(8,128)(2,1)S(1)}, bf16[64,256]{1,0:T(8,128)(2,1)S(1)}, u32[]{:S(2)}, u32[]{:S(2)}) collective-permute-start(bf16[64,256]{1,0:T(8,128)(2,1)S(1)} %slice.29), channel_id=1, source_target_pairs={{0,1},{1,0},{2,3},{3,2},{4,5},{5,4},{6,7},{7,6},{8,9},{9,8},{10,11... | collective-permute-start | bytes 98312 | tf_op jit(solution)/shard_map/ppermute | solution.py:188

commit v9 on v8

--- a/solution.py
+++ b/solution.py
@@ -97,32 +97,37 @@
     return largest + jnp.log2(total), delta
 
 
-def backward_kernel(order, late, heads, shards, *refs):
-    chunks = len(order)
-    group, chunk = refs[:GROUP], refs[GROUP : GROUP + chunks]
-    chunk = chunk[late:] + chunk[:late]
-    stats, refs = refs[GROUP + chunks :][:GROUP], refs[2 * GROUP + chunks :]
-    (tops, expos, dprobs), refs = (refs[0:2], refs[2:4], refs[4:6]), refs[6:]
-    near_ref, far_ref, *outs, dv_total, dk_total = refs
-    rows, width = chunk[0].shape
-    hd = width // 2
+def backward_kernel(some, kept_at, heads, shards, whole, *refs):
+    group, stats, refs = refs[:GROUP], refs[GROUP : 2 * GROUP], refs[2 * GROUP :]
+    tops, expos, dprobs, refs = refs[0:2], refs[2:4], refs[4:6], refs[6:]
+    rows, hd = group[0].shape[0] // 2, group[0].shape[1] // heads
+    if whole:
+        chunk, (other_ref, near_ref, far_ref, *outs, dv_total, dk_total) = (
+            refs[: len(kept_at)],
+            refs[len(kept_at) :],
+        )
+        keys_across = jnp.concatenate([c[:, :hd] for c in chunk], axis=0).T
+    else:
+        dscores_ref, *outs, dv_total, dk_total = refs
     shard = lax.axis_index("head")
     scaling = hd ** (-0.5)
-    keys = jnp.concatenate([c[:, :hd] for c in chunk], axis=0)
-    keys_across = keys.T
+    pair = GROUP // 2
     for j in range(GROUP):
         at = pl.ds(j * heads * rows, heads * rows)
         parts = [
             s[0:2, pl.ds((j ^ t) * heads * rows, heads * rows)] for t, s in enumerate(stats)
         ]
         log_total, delta = merged(parts)
-        weights = jnp.concatenate(
-            [e[:, at] * jnp.exp2(t[0:1, at] - log_total) for e, t in zip(expos, tops)], axis=0
-        )
-        differences = jnp.concatenate([d[:, at] for d in dprobs], axis=0) - delta
-        weights_low = weights.astype(jnp.bfloat16)
-        dscores = (weights * differences).astype(jnp.bfloat16)
-        dv = dot(weights_low, both_heads(group[j], heads, 1), NN)
+        factor = [jnp.exp2(t[0:1, at] - log_total) for t in tops]
+        weights, dscores = [], []
+        for b in some:
+            part, first = kept_at[b]
+            kept = pl.ds(first * rows, rows)
+            weights.append(expos[part][kept, at] * factor[part])
+            dscores.append(weights[-1] * (dprobs[part][kept, at] - delta))
+        weights = jnp.concatenate(weights, axis=0).astype(jnp.bfloat16)
+        dscores = jnp.concatenate(dscores, axis=0).astype(jnp.bfloat16)
+        dv = dot(weights, both_heads(group[j], heads, 1), NN)
         dk = dot(dscores, both_heads(group[j], heads, 0), NN)
         if j == 0:
             dv_total[...] = dv
@@ -130,21 +135,20 @@
         else:
             dv_total[...] += dv
             dk_total[...] += dk
+        if not whole:
+            dscores_ref[:, at] = dscores
+            continue
+        dscores = jnp.concatenate([dscores, other_ref[:, at]], axis=0)
         dq = ((dot(keys_across, dscores, NN) * scaling).T).astype(jnp.bfloat16)
-        half = GROUP // 2
-        to = (near_ref, far_ref)[j // half]
+        to = (near_ref, far_ref)[j // pair]
         for h in range(heads):
-            to[pl.ds(j % half * rows, rows), h * hd : (h + 1) * hd] = dq[h * rows : (h + 1) * rows]
-    part = rows // shards
-    half = chunks // 2
+            to[pl.ds(j % pair * rows, rows), h * hd : (h + 1) * hd] = dq[h * rows : (h + 1) * rows]
+    size = rows // shards
     for t in range(shards):
         owner = lax.rem(shard + t, shards)
-        for b in range(chunks):
-            at = pl.ds(pl.multiple_of(order.index(b) * rows + owner * part, part), part)
-            if b < half:
-                out, to = outs[b], pl.ds(t * part, part)
-            else:
-                out, to = outs[half + t], pl.ds((b - half) * part, part)
+        for k in range(len(some)):
+            at = pl.ds(pl.multiple_of(k * rows + owner * size, size), size)
+            out, to = outs[t], pl.ds(k * size, size)
             out[to, :hd] = (dk_total[at, :] * scaling).astype(jnp.bfloat16)
             out[to, hd:] = dv_total[at, :].astype(jnp.bfloat16)
 
@@ -191,6 +195,8 @@
     params = pltpu.CompilerParams(vmem_limit_bytes=40 * 1024 * 1024)
     small = pltpu.CompilerParams(vmem_limit_bytes=4 * 1024 * 1024)
 
+    order = pl.CostEstimate(flops=0, bytes_accessed=0, transcendentals=0)
+
     def array(shape, dtype=jnp.bfloat16):
         return jax.ShapeDtypeStruct(shape, dtype)
 
@@ -200,7 +206,7 @@
         in_specs=[pl.BlockSpec(memory_space=pltpu.SMEM)],
         out_specs=vmem,
         compiler_params=small,
-        cost_estimate=pl.CostEstimate(flops=1000000000, bytes_accessed=0, transcendentals=0),
+        cost_estimate=pl.CostEstimate(flops=10000000000, bytes_accessed=0, transcendentals=0),
         name="place",
     )(jnp.concatenate([doc_lengths, span_order.T.reshape(-1)]))
 
@@ -211,13 +217,13 @@
     packed_kv, packed_qg = packed[:rows], packed[rows:]
     chunk = [packed_kv] + [swap(packed_kv, bits) for bits in chunk_bits[1:]]
     across = swap(packed_qg, group_bits[2])
-    beside = swap(packed_qg, group_bits[1])
-    group = [packed_qg, beside, across, swap(across, group_bits[1])]
-
-    late = tuple(range(1, 3 * chunks // 4))
+    both = swap(jnp.concatenate([packed_qg, across], axis=0), group_bits[1])
+    group = [packed_qg, both[: 2 * rows], across, both[2 * rows :]]
+
+    late = tuple(range(1, 3 * chunks // 4))[::-1]
     early = (0, *range(3 * chunks // 4, chunks))
 
-    def stats_of(which, before, flops):
+    def stats_of(which, before):
         wide = array((len(which) * rows, GROUP * heads * rows), jnp.float32)
         return pl.pallas_call(
             functools.partial(stats_kernel, which, heads),
@@ -230,29 +236,43 @@
             in_specs=[vmem] * (1 + GROUP + len(which) + len(before)),
             out_specs=(vmem, vmem, vmem, vmem),
             compiler_params=params,
-            cost_estimate=pl.CostEstimate(flops=flops, bytes_accessed=0, transcendentals=0),
+            cost_estimate=order,
             name="stats",
         )(place, *group, *[chunk[b] for b in which], *before)
 
-    first, *kept_early = stats_of(early, (), 0)
-    stats, *kept_late = stats_of(late, (first,), 0)
-    kept = [ref for pair in zip(kept_early, kept_late) for ref in pair]
+    first, *kept_early = stats_of(early, ())
+    stats, *kept_late = stats_of(late, (first,))
+    kept = [ref for both in zip(kept_early, kept_late) for ref in both]
+    kept_at = [(0, early.index(b)) if b in early else (1, late.index(b)) for b in range(chunks)]
     all_stats = [stats] + [swap(stats, bits) for bits in group_bits[1:]]
 
+    half = chunks // 2
+    near_chunks, far_chunks = tuple(range(half)), tuple(range(half, chunks))
+
+    def backward_of(some, given, out_shape):
+        return pl.pallas_call(
+            functools.partial(backward_kernel, some, kept_at, heads, shards, len(given) > 0),
+            out_shape=out_shape,
+            in_specs=[vmem] * (2 * GROUP + len(kept) + len(given)),
+            out_specs=(vmem,) * len(out_shape),
+            scratch_shapes=[pltpu.VMEM((len(some) * rows, hd), jnp.float32)] * 2,
+            compiler_params=params,
+            cost_estimate=order,
+            name="backward",
+        )(*group, *all_stats, *kept, *given)
+
     pair_rows = array((GROUP // 2 * rows, width))
-    half = chunks // 2
-    pieces = (array((rows, 2 * hd)),) * half + (array((half * part, 2 * hd)),) * shards
-    near, far, *dkv = pl.pallas_call(
-        functools.partial(backward_kernel, early + late, len(late), heads, shards),
-        out_shape=(pair_rows, pair_rows) + pieces,
-        in_specs=[vmem] * (2 * GROUP + chunks + len(kept)),
-        out_specs=(vmem,) * (2 + len(pieces)),
-        scratch_shapes=[pltpu.VMEM((chunks * rows, hd), jnp.float32)] * 2,
-        compiler_params=params,
-        name="backward",
-    )(*group, *[chunk[b] for b in late + early], *all_stats, *kept)
-
-    def fold(parts, flops):
+    piece = (array((half * part, 2 * hd)),) * shards
+    dscores, *dkv_far = backward_of(
+        far_chunks, (), (array((half * rows, GROUP * heads * rows)),) + piece
+    )
+    near, far, *dkv_near = backward_of(
+        near_chunks,
+        (*[chunk[b] for b in near_chunks + far_chunks], dscores),
+        (pair_rows, pair_rows) + piece,
+    )
+
+    def fold(parts, flops=0):
         return pl.pallas_call(
             fold_kernel,
             out_shape=jax.ShapeDtypeStruct(parts[0].shape, jnp.bfloat16),
@@ -263,12 +283,17 @@
             name="fold",
         )(*parts)
 
-    across = fold([dkv[half]] + [turn(dkv[half + t], t) for t in range(1, shards)], 0)
-    owned = fold([dkv[0]] + [swap(dkv[b], chunk_bits[b]) for b in range(1, half)], 1000000000)
-    came = [
-        swap(across[k * part : (k + 1) * part], chunk_bits[half + k]) for k in range(half)[::-1]
-    ] + [turn(owned[t * part : (t + 1) * part], t) for t in range(1, shards)]
-    pair = (near.astype(jnp.float32) + swap(far, group_bits[2]).astype(jnp.float32)).astype(jnp.bfloat16)
+    far_sum = fold([dkv_far[0]] + [turn(dkv_far[t], t) for t in range(1, shards)])
+    near_sum = fold([dkv_near[0]] + [turn(dkv_near[t], t) for t in range(1, shards)], 1000000000)
+    sums = (near_sum, far_sum)
+
+    def arrived(b):
+        return swap(sums[b // half][b % half * part :][:part], chunk_bits[b])
+
+    owned = near_sum
+    came = [arrived(b) for b in (*range(1, half), *range(half, chunks)[::-1])]
+    pair = near.astype(jnp.float32) + swap(far, group_bits[2]).astype(jnp.float32)
+    pair = pair.astype(jnp.bfloat16)
     other = swap(pair[rows:], group_bits[1])
     query_grad = pl.pallas_call(
         query_sum_kernel,

time: 31.8 us -> 31.7 us (level)
  starting transfers between devices: 18 us -> 16.9 us
  local copies, waits for them, and re-layouts: 0.18 us -> 0.71 us
    ppermute x14 -> x13, waiting for transfers between devices: 6.28 us -> 7.68 us  [swap(): return lax.ppermute(x, 'ctx', [(i, i ^ bits) for i in range(ctx_size)])]
    ppermute x2, waiting for transfers between devices: 1.25 us -> 0.01 us  [turn(): lax.ppermute(x, 'head', [(i, (i + by) % shards) for i in range(shards)])]
    ppermute x2, starting transfers between devices: 3.18 us -> 2.16 us  [turn(): lax.ppermute(x, 'head', [(i, (i + by) % shards) for i in range(shards)])]
    unnamed x4, local copies, waits for them, and re-layouts: 0.07 us -> 0.58 us
    pallas_call x1 -> x2, Pallas kernels: 0.99 us -> 1.28 us  [backward_of(): pl.pallas_call(functools.partial(backward_kernel, some, kept_at, heads, s...]
    ppermute x14 -> x13, starting transfers between devices: 14.9 us -> 14.8 us  [swap(): return lax.ppermute(x, 'ctx', [(i, i ^ bits) for i in range(ctx_size)])]
  transfers between devices with their start and end apart: 16 -> 15, of which waited for: 7 -> 10; matrix products, arithmetic and copies ran while one was open for 1% -> 1% of each run, Pallas kernels for 6% -> 8%
where the time goes in v9:
time: 31.7 us; the launch traced here: 31.5 us
  starting transfers between devices  16.9 us (53%)
  waiting for transfers between devices  7.69 us (24%)
  Pallas kernels  4.42 us (14%)
  other arithmetic  1.02 us (3%)
  between operations  0.77 us (2%)
  local copies, waits for them, and re-layouts  0.71 us (2%)
    ppermute x13, starting transfers between devices, swap(): return lax.ppermute(x, 'ctx', [(i, i ^ bits) for i in range(ctx_size)])  14.8 us
    ppermute x13, waiting for transfers between devices, swap(): return lax.ppermute(x, 'ctx', [(i, i ^ bits) for i in range(ctx_size)])  7.68 us
    ppermute x2, starting transfers between devices, turn(): lax.ppermute(x, 'head', [(i, (i + by) % shards) for i in range(shards)])  2.16 us
    pallas_call x2, Pallas kernels, backward_of(): pl.pallas_call(functools.partial(backward_kernel, some, kept_at, heads, s...  1.28 us
    pallas_call x2, Pallas kernels, stats_of(): pl.pallas_call(functools.partial(stats_kernel, which, heads), out_shape=(...  1.25 us
    concatenate x1, other arithmetic, local(): jnp.concatenate([jnp.concatenate([key_rows, value_rows], axis=1), queries...  0.89 us
    pallas_call x1, Pallas kernels, local(): pl.pallas_call(query_sum_kernel, out_shape=array((rows, width)), in_specs...  0.65 us
  transfers between devices with their start and end apart: 15, of which 10 were waited for; matrix products, arithmetic and copies ran while one was open for 1% of the time, Pallas kernels for 8%

profile of v9, /device:TPU:0, one launch (start us, length us, event | category | flops | bytes accessed | tf_op | source)
XLA Modules:
  0.0 31.5 jit_solution(2170420343382563095)
XLA Ops:
  0.6 0.9 %pad_maximum_fusion.1 = bf16[384,256]{1,0:T(8,128)(2,1)S(1)} fusion(bf16[128,256]{1,0:T(8,128)(2,1)} %param.9, bf16[128,256]{1,0:T(8,128)(2,1)} %param.6, bf16[128,128]{1,0:T(8,128)(2,1)} %param.8, bf16[128,128]{1,0:T(8,128)(2,1)} %param.7), kind=kLoop, calls=%fused_computation.2 | loop fusion | flops 786432 | bytes 393216 | tf_op jit(solution)/shard_map/concatenate | solution.py:213
  1.5 3.0 %collective-permute-start = (bf16[256,256]{1,0:T(8,128)(2,1)S(1)}, bf16[256,256]{1,0:T(8,128)(2,1)S(1)}, u32[]{:S(2)}, u32[]{:S(2)}) collective-permute-start(bf16[256,256]{1,0:T(8,128)(2,1)S(1)} %slice.32.refs_0_), channel_id=1, source_target_pairs={{0,4},{2,6},{4,0},{6,2},{8,12},{10,14},{12,8},{14,10},{16,20},{18,... | collective-permute-start | bytes 393224 | tf_op jit(solution)/shard_map/ppermute | solution.py:189
  4.6 0.0 copy-start
  4.6 3.7 %collective-permute-start.4 = (bf16[128,256]{1,0:T(8,128)(2,1)S(1)}, bf16[128,256]{1,0:T(8,128)(2,1)S(1)}, u32[]{:S(2)}, u32[]{:S(2)}) collective-permute-start(bf16[128,256]{1,0:T(8,128)(2,1)S(1)} %slice.35.refs_4_.refs_14_), channel_id=1, source_target_pairs={{0,24},{2,26},{4,28},{6,30},{8,16},{10,18},{12,20},{14,22},{16,8},... | collective-permute-start | bytes 196616 | tf_op jit(solution)/shard_map/ppermute | solution.py:189
  8.2 0.0 collective-permute-start.2
  8.2 0.8 %collective-permute-start.3 = (bf16[128,256]{1,0:T(8,128)(2,1)S(1)}, bf16[128,256]{1,0:T(8,128)(2,1)S(1)}, u32[]{:S(2)}, u32[]{:S(2)}) collective-permute-start(bf16[128,256]{1,0:T(8,128)(2,1)S(1)} %slice.35.refs_4_.refs_14_), channel_id=1, source_target_pairs={{0,8},{2,10},{4,12},{6,14},{8,0},{10,2},{12,4},{14,6},{16,24},{18,... | collective-permute-start | bytes 196616 | tf_op jit(solution)/shard_map/ppermute | solution.py:189
  9.0 0.0 copy-done
  9.0 0.0 copy-start.1
  9.0 0.1 reshape.9
  9.1 0.6 %copy-done.1 = s32[8]{0:T(128)S(1)} copy-done((s32[8]{0:T(128)S(1)}, s32[8]{0:T(128)}, u32[]{:S(2)}) %copy-start.1) | copy-done | bytes 56
  9.7 0.1 pad_add_fusion.ints
  9.7 0.0 collective-permute-done.refs_2_
  9.8 0.1 collective-permute-start.1
  9.8 0.6 %place.1.place_ref = s32[16,128]{1,0:T(8,128)S(1)} custom-call(s32[40]{0:T(128)S(1)} %pad_add_fusion.ints), custom_call_target="tpu_custom_call" | custom-call | flops 10000000000 | tf_op jit(solution)/shard_map/place/pallas_call | solution.py:203
  10.4 0.9 %collective-permute-done.1 = bf16[512,256]{1,0:T(8,128)(2,1)S(1)} collective-permute-done((bf16[512,256]{1,0:T(8,128)(2,1)S(1)}, bf16[512,256]{1,0:T(8,128)(2,1)S(1)}, u32[]{:S(2)}, u32[]{:S(2)}) %collective-permute-start.1) | collective-permute-done | bytes 262176 | tf_op jit(solution)/shard_map/ppermute | solution.py:189
  11.4 0.1 collective-permute-done.4.refs_5_.refs_17_
  11.5 0.6 %stats.2 = (f32[2,1024]{1,0:T(2,128)S(1)}, f32[1,1024]{1,0:T(1,128)S(1)}, f32[256,1024]{1,0:T(8,128)S(1)}, f32[256,1024]{1,0:T(8,128)S(1)}) custom-call(s32[16,128]{1,0:T(8,128)S(1)} %place.1.place_ref, bf16[256,256]{1,0:T(8,128)(2,1)S(1)} %slice.32.refs_0_, bf16[256,256]{1,0:T(8,128)(2,1)S(1)} %get-tuple-element.46.refs_1_, ...), custom_call_target="tpu_custom_call" | custom-call | tf_op jit(solution)/shard_map/stats/pallas_call | solution.py:228
  12.1 1.5 %collective-permute-done.2.refs_4_.refs_16_ = bf16[128,256]{1,0:T(8,128)(2,1)S(1)} collective-permute-done((bf16[128,256]{1,0:T(8,128)(2,1)S(1)}, bf16[128,256]{1,0:T(8,128)(2,1)S(1)}, u32[]{:S(2)}, u32[]{:S(2)}) %collective-permute-start.2) | collective-permute-done | bytes 65568 | tf_op jit(solution)/shard_map/ppermute | solution.py:189
  13.6 0.1 collective-permute-done.3.refs_5_.refs_15_
  13.7 0.6 %stats.3 = (f32[2,1024]{1,0:T(2,128)S(1)}, f32[1,1024]{1,0:T(1,128)S(1)}, f32[256,1024]{1,0:T(8,128)S(1)}, f32[256,1024]{1,0:T(8,128)S(1)}) custom-call(s32[16,128]{1,0:T(8,128)S(1)} %place.1.place_ref, bf16[256,256]{1,0:T(8,128)(2,1)S(1)} %slice.32.refs_0_, bf16[256,256]{1,0:T(8,128)(2,1)S(1)} %get-tuple-element.46.refs_1_, ...), custom_call_target="tpu_custom_call" | custom-call | tf_op jit(solution)/shard_map/stats/pallas_call | solution.py:228
  14.3 0.1 collective-permute-start.5
  14.4 0.5 %collective-permute-start.6 = (f32[2,1024]{1,0:T(2,128)S(1)}, f32[2,1024]{1,0:T(2,128)S(1)}, u32[]{:S(2)}, u32[]{:S(2)}) collective-permute-start(f32[2,1024]{1,0:T(2,128)S(1)} %get-tuple-element.25.refs_4_), channel_id=1, source_target_pairs={{0,4},{2,6},{4,0},{6,2},{8,12},{10,14},{12,8},{14,10},{16,20},{18,... | collective-permute-start | bytes 24584 | tf_op jit(solution)/shard_map/ppermute | solution.py:189
  14.9 1.4 %collective-permute-start.7 = (f32[2,1024]{1,0:T(2,128)S(1)}, f32[2,1024]{1,0:T(2,128)S(1)}, u32[]{:S(2)}, u32[]{:S(2)}) collective-permute-start(f32[2,1024]{1,0:T(2,128)S(1)} %get-tuple-element.25.refs_4_), channel_id=1, source_target_pairs={{0,6},{2,4},{4,2},{6,0},{8,14},{10,12},{12,10},{14,8},{16,22},{18,... | collective-permute-start | bytes 24584 | tf_op jit(solution)/shard_map/ppermute | solution.py:189
  16.2 0.0 collective-permute-done.5.refs_5_
  16.2 1.9 %collective-permute-done.6.refs_6_ = f32[2,1024]{1,0:T(2,128)S(1)} collective-permute-done((f32[2,1024]{1,0:T(2,128)S(1)}, f32[2,1024]{1,0:T(2,128)S(1)}, u32[]{:S(2)}, u32[]{:S(2)}) %collective-permute-start.6) | collective-permute-done | bytes 8224 | tf_op jit(solution)/shard_map/ppermute | solution.py:189
  18.1 0.0 collective-permute-done.7.refs_7_
  18.1 0.6 %backward.2 = (bf16[256,1024]{1,0:T(8,128)(2,1)S(1)}, bf16[128,256]{1,0:T(8,128)(2,1)S(1)}, bf16[128,256]{1,0:T(8,128)(2,1)S(1)}) custom-call(bf16[256,256]{1,0:T(8,128)(2,1)S(1)} %slice.32.refs_0_, bf16[256,256]{1,0:T(8,128)(2,1)S(1)} %get-tuple-element.46.refs_1_, bf16[256,256]{1,0:T(8,128)(2,1)S(1)} %collective-permute-done.refs_2_, ...), custom_call_target="tpu_custom_call" | custom-call | tf_op jit(solution)/shard_map/backward/pallas_call | solution.py:253
  18.7 1.6 %collective-permute-start.12 = (bf16[128,256]{1,0:T(8,128)(2,1)S(1)}, bf16[128,256]{1,0:T(8,128)(2,1)S(1)}, u32[]{:S(2)}, u32[]{:S(2)}) collective-permute-start(bf16[128,256]{1,0:T(8,128)(2,1)S(1)} %get-tuple-element.38), channel_id=1, source_target_pairs={{0,1},{1,0},{2,3},{3,2},{4,5},{5,4},{6,7},{7,6},{8,9},{9,8},{10,11... | collective-permute-start | bytes 196616 | tf_op jit(solution)/shard_map/ppermute | solution.py:192
  20.3 0.7 %backward.3 = (bf16[256,256]{1,0:T(8,128)(2,1)S(1)}, bf16[256,256]{1,0:T(8,128)(2,1)S(1)}, bf16[128,256]{1,0:T(8,128)(2,1)S(1)}, bf16[128,256]{1,0:T(8,128)(2,1)S(1)}) custom-call(bf16[256,256]{1,0:T(8,128)(2,1)S(1)} %slice.32.refs_0_, bf16[256,256]{1,0:T(8,128)(2,1)S(1)} %get-tuple-element.46.refs_1_, bf16[256,256]{1,0:T(8,128)(2,1)S(1)} %collective-permute-done.refs_2_, ...), custom_call_target="tpu_custom_call" | custom-call | tf_op jit(solution)/shard_map/backward/pallas_call | solution.py:253
  21.0 0.5 %collective-permute-start.10 = (bf16[128,256]{1,0:T(8,128)(2,1)S(1)}, bf16[128,256]{1,0:T(8,128)(2,1)S(1)}, u32[]{:S(2)}, u32[]{:S(2)}) collective-permute-start(bf16[128,256]{1,0:T(8,128)(2,1)S(1)} %get-tuple-element.36), channel_id=1, source_target_pairs={{0,1},{1,0},{2,3},{3,2},{4,5},{5,4},{6,7},{7,6},{8,9},{9,8},{10,11... | collective-permute-start | bytes 196616 | tf_op jit(solution)/shard_map/ppermute | solution.py:192
  21.5 1.4 %collective-permute-start.8 = (bf16[256,256]{1,0:T(8,128)(2,1)S(1)}, bf16[256,256]{1,0:T(8,128)(2,1)S(1)}, u32[]{:S(2)}, u32[]{:S(2)}) collective-permute-start(bf16[256,256]{1,0:T(8,128)(2,1)S(1)} %get-tuple-element.34), channel_id=1, source_target_pairs={{0,4},{2,6},{4,0},{6,2},{8,12},{10,14},{12,8},{14,10},{16,20},{18,... | collective-permute-start | bytes 393224 | tf_op jit(solution)/shard_map/ppermute | solution.py:189
  23.0 0.0 collective-permute-done.12.refs_1_
  23.0 2.7 %collective-permute-start.13 = (bf16[64,256]{1,0:T(8,128)(2,1)S(1)}, bf16[64,256]{1,0:T(8,128)(2,1)S(1)}, u32[]{:S(2)}, u32[]{:S(2)}) collective-permute-start(bf16[64,256]{1,0:T(8,128)(2,1)S(1)} %get-tuple-element.48), channel_id=1, source_target_pairs={{0,24},{2,26},{4,28},{6,30},{8,16},{10,18},{12,20},{14,22},{16,8},... | collective-permute-start | bytes 98312 | tf_op jit(solution)/shard_map/ppermute | solution.py:189
  25.7 0.0 collective-permute-start.14
  25.7 0.8 %collective-permute-done.8 = bf16[256,256]{1,0:T(8,128)(2,1)S(1)} collective-permute-done((bf16[256,256]{1,0:T(8,128)(2,1)S(1)}, bf16[256,256]{1,0:T(8,128)(2,1)S(1)}, u32[]{:S(2)}, u32[]{:S(2)}) %collective-permute-start.8) | collective-permute-done | bytes 131104 | tf_op jit(solution)/shard_map/ppermute | solution.py:189
  26.6 0.1 collective-permute-start.9
  26.6 0.0 collective-permute-done.10.refs_1_
  26.7 1.1 %collective-permute-start.11 = (bf16[64,256]{1,0:T(8,128)(2,1)S(1)}, bf16[64,256]{1,0:T(8,128)(2,1)S(1)}, u32[]{:S(2)}, u32[]{:S(2)}) collective-permute-start(bf16[64,256]{1,0:T(8,128)(2,1)S(1)} %slice.37), channel_id=1, source_target_pairs={{0,8},{2,10},{4,12},{6,14},{8,0},{10,2},{12,4},{14,6},{16,24},{18,... | collective-permute-start | bytes 98312 | tf_op jit(solution)/shard_map/ppermute | solution.py:189
  27.8 0.1 collective-permute-done.9.other_ref
  27.9 0.6 %query_sum.1 = bf16[128,256]{1,0:T(8,128)(2,1)} custom-call(bf16[256,256]{1,0:T(8,128)(2,1)S(1)} %add_convert_fusion.pair_ref, bf16[128,256]{1,0:T(8,128)(2,1)S(1)} %collective-permute-done.9.other_ref), custom_call_target="tpu_custom_call" | custom-call | flops 1000000000 | tf_op jit(solution)/shard_map/query_sum/pallas_call | solution.py:298
  28.5 0.4 %collective-permute-done.13.refs_1_ = bf16[64,256]{1,0:T(8,128)(2,1)S(1)} collective-permute-done((bf16[64,256]{1,0:T(8,128)(2,1)S(1)}, bf16[64,256]{1,0:T(8,128)(2,1)S(1)}, u32[]{:S(2)}, u32[]{:S(2)}) %collective-permute-start.13) | collective-permute-done | bytes 32800 | tf_op jit(solution)/shard_map/ppermute | solution.py:189
  28.9 1.7 %collective-permute-done.14.refs_2_ = bf16[64,256]{1,0:T(8,128)(2,1)S(1)} collective-permute-done((bf16[64,256]{1,0:T(8,128)(2,1)S(1)}, bf16[64,256]{1,0:T(8,128)(2,1)S(1)}, u32[]{:S(2)}, u32[]{:S(2)}) %collective-permute-start.14) | collective-permute-done | bytes 32800 | tf_op jit(solution)/shard_map/ppermute | solution.py:189
  30.6 0.3 %collective-permute-done.11.refs_0_ = bf16[64,256]{1,0:T(8,128)(2,1)S(1)} collective-permute-done((bf16[64,256]{1,0:T(8,128)(2,1)S(1)}, bf16[64,256]{1,0:T(8,128)(2,1)S(1)}, u32[]{:S(2)}, u32[]{:S(2)}) %collective-permute-start.11) | collective-permute-done | bytes 32800 | tf_op jit(solution)/shard_map/ppermute | solution.py:189
  30.9 0.6 %finish.1 = (bf16[64,128]{1,0:T(8,128)(2,1)}, bf16[64,128]{1,0:T(8,128)(2,1)}) custom-call(bf16[128,256]{1,0:T(8,128)(2,1)S(1)} %fold.2.owned_ref, bf16[64,256]{1,0:T(8,128)(2,1)S(1)} %collective-permute-done.11.refs_0_, bf16[64,256]{1,0:T(8,128)(2,1)S(1)} %collective-permute-done.13.refs_1_, bf16[64,256]{1,0:T(8,128)(2,1)S(1)} %collective-permute-done.14.refs_2_), custom_call_target="tpu_custom_call" | custom-call | tf_op jit(solution)/shard_map/finish/pallas_call | solution.py:308
  (10 shorter events, 0.1 us)
Async XLA Ops:
  1.5 8.2 %collective-permute-start = (bf16[256,256]{1,0:T(8,128)(2,1)S(1)}, bf16[256,256]{1,0:T(8,128)(2,1)S(1)}, u32[]{:S(2)}, u32[]{:S(2)}) collective-permute-start(bf16[256,256]{1,0:T(8,128)(2,1)S(1)} %slice.32.refs_0_), channel_id=1, source_target_pairs={{0,4},{2,6},{4,0},{6,2},{8,12},{10,14},{12,8},{14,10},{16,20},{18,... | collective-permute-start | bytes 393224 | tf_op jit(solution)/shard_map/ppermute | solution.py:189
  4.6 4.5 %copy-start = (s32[16,2]{0,1:T(2,128)S(1)}, s32[16,2]{0,1:T(2,128)}, u32[]{:S(2)}) copy-start(s32[16,2]{0,1:T(2,128)} %param.11) | copy-start | bytes 388
  4.6 6.9 %collective-permute-start.4 = (bf16[128,256]{1,0:T(8,128)(2,1)S(1)}, bf16[128,256]{1,0:T(8,128)(2,1)S(1)}, u32[]{:S(2)}, u32[]{:S(2)}) collective-permute-start(bf16[128,256]{1,0:T(8,128)(2,1)S(1)} %slice.35.refs_4_.refs_14_), channel_id=1, source_target_pairs={{0,24},{2,26},{4,28},{6,30},{8,16},{10,18},{12,20},{14,22},{16,8},... | collective-permute-start | bytes 196616 | tf_op jit(solution)/shard_map/ppermute | solution.py:189
  8.2 5.4 %collective-permute-start.2 = (bf16[128,256]{1,0:T(8,128)(2,1)S(1)}, bf16[128,256]{1,0:T(8,128)(2,1)S(1)}, u32[]{:S(2)}, u32[]{:S(2)}) collective-permute-start(bf16[128,256]{1,0:T(8,128)(2,1)S(1)} %slice.35.refs_4_.refs_14_), channel_id=1, source_target_pairs={{0,16},{2,18},{4,20},{6,22},{8,24},{10,26},{12,28},{14,30},{16,0},... | collective-permute-start | bytes 196616 | tf_op jit(solution)/shard_map/ppermute | solution.py:189
  8.2 5.4 %collective-permute-start.3 = (bf16[128,256]{1,0:T(8,128)(2,1)S(1)}, bf16[128,256]{1,0:T(8,128)(2,1)S(1)}, u32[]{:S(2)}, u32[]{:S(2)}) collective-permute-start(bf16[128,256]{1,0:T(8,128)(2,1)S(1)} %slice.35.refs_4_.refs_14_), channel_id=1, source_target_pairs={{0,8},{2,10},{4,12},{6,14},{8,0},{10,2},{12,4},{14,6},{16,24},{18,... | collective-permute-start | bytes 196616 | tf_op jit(solution)/shard_map/ppermute | solution.py:189
  9.0 0.7 %copy-start.1 = (s32[8]{0:T(128)S(1)}, s32[8]{0:T(128)}, u32[]{:S(2)}) copy-start(s32[8]{0:T(128)} %param.10) | copy-start | bytes 100
  9.8 1.6 %collective-permute-start.1 = (bf16[512,256]{1,0:T(8,128)(2,1)S(1)}, bf16[512,256]{1,0:T(8,128)(2,1)S(1)}, u32[]{:S(2)}, u32[]{:S(2)}) collective-permute-start(bf16[512,256]{1,0:T(8,128)(2,1)S(1)} %pad_maximum_fusion), channel_id=1, source_target_pairs={{0,2},{2,0},{4,6},{6,4},{8,10},{10,8},{12,14},{14,12},{16,18},{18,... | collective-permute-start | bytes 786440 | tf_op jit(solution)/shard_map/ppermute | solution.py:189
  14.3 1.9 %collective-permute-start.5 = (f32[2,1024]{1,0:T(2,128)S(1)}, f32[2,1024]{1,0:T(2,128)S(1)}, u32[]{:S(2)}, u32[]{:S(2)}) collective-permute-start(f32[2,1024]{1,0:T(2,128)S(1)} %get-tuple-element.25.refs_4_), channel_id=1, source_target_pairs={{0,2},{2,0},{4,6},{6,4},{8,10},{10,8},{12,14},{14,12},{16,18},{18,... | collective-permute-start | bytes 24584 | tf_op jit(solution)/shard_map/ppermute | solution.py:189
  14.4 3.7 %collective-permute-start.6 = (f32[2,1024]{1,0:T(2,128)S(1)}, f32[2,1024]{1,0:T(2,128)S(1)}, u32[]{:S(2)}, u32[]{:S(2)}) collective-permute-start(f32[2,1024]{1,0:T(2,128)S(1)} %get-tuple-element.25.refs_4_), channel_id=1, source_target_pairs={{0,4},{2,6},{4,0},{6,2},{8,12},{10,14},{12,8},{14,10},{16,20},{18,... | collective-permute-start | bytes 24584 | tf_op jit(solution)/shard_map/ppermute | solution.py:189
  14.9 3.2 %collective-permute-start.7 = (f32[2,1024]{1,0:T(2,128)S(1)}, f32[2,1024]{1,0:T(2,128)S(1)}, u32[]{:S(2)}, u32[]{:S(2)}) collective-permute-start(f32[2,1024]{1,0:T(2,128)S(1)} %get-tuple-element.25.refs_4_), channel_id=1, source_target_pairs={{0,6},{2,4},{4,2},{6,0},{8,14},{10,12},{12,10},{14,8},{16,22},{18,... | collective-permute-start | bytes 24584 | tf_op jit(solution)/shard_map/ppermute | solution.py:189
  18.7 4.3 %collective-permute-start.12 = (bf16[128,256]{1,0:T(8,128)(2,1)S(1)}, bf16[128,256]{1,0:T(8,128)(2,1)S(1)}, u32[]{:S(2)}, u32[]{:S(2)}) collective-permute-start(bf16[128,256]{1,0:T(8,128)(2,1)S(1)} %get-tuple-element.38), channel_id=1, source_target_pairs={{0,1},{1,0},{2,3},{3,2},{4,5},{5,4},{6,7},{7,6},{8,9},{9,8},{10,11... | collective-permute-start | bytes 196616 | tf_op jit(solution)/shard_map/ppermute | solution.py:192
  21.0 5.6 %collective-permute-start.10 = (bf16[128,256]{1,0:T(8,128)(2,1)S(1)}, bf16[128,256]{1,0:T(8,128)(2,1)S(1)}, u32[]{:S(2)}, u32[]{:S(2)}) collective-permute-start(bf16[128,256]{1,0:T(8,128)(2,1)S(1)} %get-tuple-element.36), channel_id=1, source_target_pairs={{0,1},{1,0},{2,3},{3,2},{4,5},{5,4},{6,7},{7,6},{8,9},{9,8},{10,11... | collective-permute-start | bytes 196616 | tf_op jit(solution)/shard_map/ppermute | solution.py:192
  21.5 5.0 %collective-permute-start.8 = (bf16[256,256]{1,0:T(8,128)(2,1)S(1)}, bf16[256,256]{1,0:T(8,128)(2,1)S(1)}, u32[]{:S(2)}, u32[]{:S(2)}) collective-permute-start(bf16[256,256]{1,0:T(8,128)(2,1)S(1)} %get-tuple-element.34), channel_id=1, source_target_pairs={{0,4},{2,6},{4,0},{6,2},{8,12},{10,14},{12,8},{14,10},{16,20},{18,... | collective-permute-start | bytes 393224 | tf_op jit(solution)/shard_map/ppermute | solution.py:189
  23.0 5.9 %collective-permute-start.13 = (bf16[64,256]{1,0:T(8,128)(2,1)S(1)}, bf16[64,256]{1,0:T(8,128)(2,1)S(1)}, u32[]{:S(2)}, u32[]{:S(2)}) collective-permute-start(bf16[64,256]{1,0:T(8,128)(2,1)S(1)} %get-tuple-element.48), channel_id=1, source_target_pairs={{0,24},{2,26},{4,28},{6,30},{8,16},{10,18},{12,20},{14,22},{16,8},... | collective-permute-start | bytes 98312 | tf_op jit(solution)/shard_map/ppermute | solution.py:189
  25.7 4.8 %collective-permute-start.14 = (bf16[64,256]{1,0:T(8,128)(2,1)S(1)}, bf16[64,256]{1,0:T(8,128)(2,1)S(1)}, u32[]{:S(2)}, u32[]{:S(2)}) collective-permute-start(bf16[64,256]{1,0:T(8,128)(2,1)S(1)} %get-tuple-element.47), channel_id=1, source_target_pairs={{0,16},{2,18},{4,20},{6,22},{8,24},{10,26},{12,28},{14,30},{16,0},... | collective-permute-start | bytes 98312 | tf_op jit(solution)/shard_map/ppermute | solution.py:189
  26.6 1.3 %collective-permute-start.9 = (bf16[128,256]{1,0:T(8,128)(2,1)S(1)}, bf16[128,256]{1,0:T(8,128)(2,1)S(1)}, u32[]{:S(2)}, u32[]{:S(2)}) collective-permute-start(bf16[128,256]{1,0:T(8,128)(2,1)S(1)} %slice.36), channel_id=1, source_target_pairs={{0,2},{2,0},{4,6},{6,4},{8,10},{10,8},{12,14},{14,12},{16,18},{18,... | collective-permute-start | bytes 196616 | tf_op jit(solution)/shard_map/ppermute | solution.py:189
  26.7 4.2 %collective-permute-start.11 = (bf16[64,256]{1,0:T(8,128)(2,1)S(1)}, bf16[64,256]{1,0:T(8,128)(2,1)S(1)}, u32[]{:S(2)}, u32[]{:S(2)}) collective-permute-start(bf16[64,256]{1,0:T(8,128)(2,1)S(1)} %slice.37), channel_id=1, source_target_pairs={{0,8},{2,10},{4,12},{6,14},{8,0},{10,2},{12,4},{14,6},{16,24},{18,... | collective-permute-start | bytes 98312 | tf_op jit(solution)/shard_map/ppermute | solution.py:189

commit v10 on v8

--- a/solution.py
+++ b/solution.py
@@ -44,7 +44,8 @@
     for b, bits in enumerate(chunk):
         for h in range(2):
             to = 2 * GROUP + 2 * b + h
-            base = ints[docs + h * count + (index ^ bits)] * half
+            origin = lax.rem(index + bits, count)
+            base = ints[docs + h * count + origin] * half
             place_ref[to : to + 1, :] = jnp.full((1, rows), base)
 
 
@@ -107,6 +108,7 @@
     rows, width = chunk[0].shape
     hd = width // 2
     shard = lax.axis_index("head")
+    plane = lax.axis_index("ctx") // GROUP
     scaling = hd ** (-0.5)
     keys = jnp.concatenate([c[:, :hd] for c in chunk], axis=0)
     keys_across = keys.T
@@ -140,7 +142,9 @@
     for t in range(shards):
         owner = lax.rem(shard + t, shards)
         for b in range(chunks):
-            at = pl.ds(pl.multiple_of(order.index(b) * rows + owner * part, part), part)
+            came = lax.rem((plane ^ b) - plane + chunks, chunks)
+            at = sum(jnp.where(came == k, order.index(k), 0) for k in range(chunks))
+            at = pl.ds(pl.multiple_of(at * rows + owner * part, part), part)
             if b < half:
                 out, to = outs[b], pl.ds(t * part, part)
             else:
@@ -184,6 +188,9 @@
     def swap(x, bits):
         return lax.ppermute(x, "ctx", [(i, i ^ bits) for i in range(ctx_size)])
 
+    def shift(x, by):
+        return lax.ppermute(x, "ctx", [(i, (i - by) % ctx_size) for i in range(ctx_size)])
+
     def turn(x, by):
         return lax.ppermute(x, "head", [(i, (i + by) % shards) for i in range(shards)])
 
@@ -200,7 +207,7 @@
         in_specs=[pl.BlockSpec(memory_space=pltpu.SMEM)],
         out_specs=vmem,
         compiler_params=small,
-        cost_estimate=pl.CostEstimate(flops=1000000000, bytes_accessed=0, transcendentals=0),
+        cost_estimate=pl.CostEstimate(flops=10000000000, bytes_accessed=0, transcendentals=0),
         name="place",
     )(jnp.concatenate([doc_lengths, span_order.T.reshape(-1)]))
 
@@ -209,10 +216,10 @@
     )
     packed = lax.optimization_barrier(packed)
     packed_kv, packed_qg = packed[:rows], packed[rows:]
-    chunk = [packed_kv] + [swap(packed_kv, bits) for bits in chunk_bits[1:]]
+    chunk = [packed_kv] + [shift(packed_kv, bits) for bits in chunk_bits[1:]]
     across = swap(packed_qg, group_bits[2])
-    beside = swap(packed_qg, group_bits[1])
-    group = [packed_qg, beside, across, swap(across, group_bits[1])]
+    both = swap(jnp.concatenate([packed_qg, across], axis=0), group_bits[1])
+    group = [packed_qg, both[: 2 * rows], across, both[2 * rows :]]
 
     late = tuple(range(1, 3 * chunks // 4))
     early = (0, *range(3 * chunks // 4, chunks))
@@ -266,7 +273,7 @@
     across = fold([dkv[half]] + [turn(dkv[half + t], t) for t in range(1, shards)], 0)
     owned = fold([dkv[0]] + [swap(dkv[b], chunk_bits[b]) for b in range(1, half)], 1000000000)
     came = [
-        swap(across[k * part : (k + 1) * part], chunk_bits[half + k]) for k in range(half)[::-1]
+        swap(across[k * part : (k + 1) * part], chunk_bits[half + k]) for k in range(half)
     ] + [turn(owned[t * part : (t + 1) * part], t) for t in range(1, shards)]
     pair = (near.astype(jnp.float32) + swap(far, group_bits[2]).astype(jnp.float32)).astype(jnp.bfloat16)
     other = swap(pair[rows:], group_bits[1])

time: 31.8 us -> 31.7 us (level)
  waiting for transfers between devices: 7.54 us -> 6.99 us
  local copies, waits for them, and re-layouts: 0.18 us -> 0.71 us
    ppermute x0 -> x3, starting transfers between devices: none -> 5.56 us  [shift(): lax.ppermute(x, 'ctx', [(i, (i - by) % ctx_size) for i in range(ctx_size)])]
    ppermute x14 -> x10, starting transfers between devices: 14.9 us -> 9.86 us  [swap(): return lax.ppermute(x, 'ctx', [(i, i ^ bits) for i in range(ctx_size)])]
    ppermute x2, starting transfers between devices: 3.18 us -> 2.52 us  [turn(): lax.ppermute(x, 'head', [(i, (i + by) % shards) for i in range(shards)])]
    unnamed x4, local copies, waits for them, and re-layouts: 0.07 us -> 0.58 us
    ppermute x2, waiting for transfers between devices: 1.25 us -> 0.75 us  [turn(): lax.ppermute(x, 'head', [(i, (i + by) % shards) for i in range(shards)])]
    ppermute x14 -> x10, waiting for transfers between devices: 6.28 us -> 5.86 us  [swap(): return lax.ppermute(x, 'ctx', [(i, i ^ bits) for i in range(ctx_size)])]
    ppermute x0 -> x3, waiting for transfers between devices: none -> 0.39 us  [shift(): lax.ppermute(x, 'ctx', [(i, (i - by) % ctx_size) for i in range(ctx_size)])]
  transfers between devices with their start and end apart: 16 -> 15, of which waited for: 7 -> 9; matrix products, arithmetic and copies ran while one was open for 1% -> 1% of each run, Pallas kernels for 6% -> 6%
where the time goes in v10:
time: 31.7 us; the launch traced here: 31.5 us
  starting transfers between devices  17.9 us (56%)
  waiting for transfers between devices  6.99 us (22%)
  Pallas kernels  4.11 us (13%)
  other arithmetic  1.02 us (3%)
  between operations  0.77 us (2%)
  local copies, waits for them, and re-layouts  0.71 us (2%)
    ppermute x10, starting transfers between devices, swap(): return lax.ppermute(x, 'ctx', [(i, i ^ bits) for i in range(ctx_size)])  9.86 us
    ppermute x10, waiting for transfers between devices, swap(): return lax.ppermute(x, 'ctx', [(i, i ^ bits) for i in range(ctx_size)])  5.86 us
    ppermute x3, starting transfers between devices, shift(): lax.ppermute(x, 'ctx', [(i, (i - by) % ctx_size) for i in range(ctx_size)])  5.56 us
    ppermute x2, starting transfers between devices, turn(): lax.ppermute(x, 'head', [(i, (i + by) % shards) for i in range(shards)])  2.52 us
    pallas_call x2, Pallas kernels, stats_of(): pl.pallas_call(functools.partial(stats_kernel, which, heads), out_shape=(...  1.26 us
    pallas_call x1, Pallas kernels, local(): pl.pallas_call(functools.partial(backward_kernel, early + late, len(late)...  0.96 us
    concatenate x1, other arithmetic, local(): jnp.concatenate([jnp.concatenate([key_rows, value_rows], axis=1), queries...  0.89 us
    ppermute x2, waiting for transfers between devices, turn(): lax.ppermute(x, 'head', [(i, (i + by) % shards) for i in range(shards)])  0.75 us
  transfers between devices with their start and end apart: 15, of which 9 were waited for; matrix products, arithmetic and copies ran while one was open for 1% of the time, Pallas kernels for 6%

profile of v10, /device:TPU:0, one launch (start us, length us, event | category | flops | bytes accessed | tf_op | source)
XLA Modules:
  0.0 31.5 jit_solution(6805517751389217750)
XLA Ops:
  0.6 0.9 %pad_maximum_fusion.1 = bf16[384,256]{1,0:T(8,128)(2,1)S(1)} fusion(bf16[128,256]{1,0:T(8,128)(2,1)} %param.9, bf16[128,256]{1,0:T(8,128)(2,1)} %param.6, bf16[128,128]{1,0:T(8,128)(2,1)} %param.8, bf16[128,128]{1,0:T(8,128)(2,1)} %param.7), kind=kLoop, calls=%fused_computation.2 | loop fusion | flops 786432 | bytes 393216 | tf_op jit(solution)/shard_map/concatenate | solution.py:214
  1.5 3.0 %collective-permute-start = (bf16[256,256]{1,0:T(8,128)(2,1)S(1)}, bf16[256,256]{1,0:T(8,128)(2,1)S(1)}, u32[]{:S(2)}, u32[]{:S(2)}) collective-permute-start(bf16[256,256]{1,0:T(8,128)(2,1)S(1)} %slice.32.refs_0_), channel_id=1, source_target_pairs={{0,4},{2,6},{4,0},{6,2},{8,12},{10,14},{12,8},{14,10},{16,20},{18,... | collective-permute-start | bytes 393224 | tf_op jit(solution)/shard_map/ppermute | solution.py:189
  4.6 0.0 copy-start
  4.6 1.6 %collective-permute-start.4 = (bf16[128,256]{1,0:T(8,128)(2,1)S(1)}, bf16[128,256]{1,0:T(8,128)(2,1)S(1)}, u32[]{:S(2)}, u32[]{:S(2)}) collective-permute-start(bf16[128,256]{1,0:T(8,128)(2,1)S(1)} %slice.35.refs_4_.refs_6_), channel_id=1, source_target_pairs={{0,8},{2,10},{4,12},{6,14},{8,16},{10,18},{12,20},{14,22},{16,24},... | collective-permute-start | bytes 196616 | tf_op jit(solution)/shard_map/ppermute | solution.py:192
  6.2 2.6 %collective-permute-start.3 = (bf16[128,256]{1,0:T(8,128)(2,1)S(1)}, bf16[128,256]{1,0:T(8,128)(2,1)S(1)}, u32[]{:S(2)}, u32[]{:S(2)}) collective-permute-start(bf16[128,256]{1,0:T(8,128)(2,1)S(1)} %slice.35.refs_4_.refs_6_), channel_id=1, source_target_pairs={{0,16},{2,18},{4,20},{6,22},{8,24},{10,26},{12,28},{14,30},{16,0},... | collective-permute-start | bytes 196616 | tf_op jit(solution)/shard_map/ppermute | solution.py:192
  8.8 1.3 %collective-permute-start.2 = (bf16[128,256]{1,0:T(8,128)(2,1)S(1)}, bf16[128,256]{1,0:T(8,128)(2,1)S(1)}, u32[]{:S(2)}, u32[]{:S(2)}) collective-permute-start(bf16[128,256]{1,0:T(8,128)(2,1)S(1)} %slice.35.refs_4_.refs_6_), channel_id=1, source_target_pairs={{0,24},{2,26},{4,28},{6,30},{8,0},{10,2},{12,4},{14,6},{16,8},{18,... | collective-permute-start | bytes 196616 | tf_op jit(solution)/shard_map/ppermute | solution.py:192
  10.1 0.0 copy-done
  10.1 0.0 copy-start.1
  10.1 0.1 reshape.9
  10.2 0.6 %copy-done.1 = s32[8]{0:T(128)S(1)} copy-done((s32[8]{0:T(128)S(1)}, s32[8]{0:T(128)}, u32[]{:S(2)}) %copy-start.1) | copy-done | bytes 56
  10.8 0.1 pad_add_fusion.ints
  10.9 0.0 collective-permute-done.refs_2_
  10.9 0.1 collective-permute-start.1
  11.0 0.6 %place.1.place_ref = s32[16,128]{1,0:T(8,128)S(1)} custom-call(s32[40]{0:T(128)S(1)} %pad_add_fusion.ints), custom_call_target="tpu_custom_call" | custom-call | flops 10000000000 | tf_op jit(solution)/shard_map/place/pallas_call | solution.py:204
  11.5 0.9 %collective-permute-done.1 = bf16[512,256]{1,0:T(8,128)(2,1)S(1)} collective-permute-done((bf16[512,256]{1,0:T(8,128)(2,1)S(1)}, bf16[512,256]{1,0:T(8,128)(2,1)S(1)}, u32[]{:S(2)}, u32[]{:S(2)}) %collective-permute-start.1) | collective-permute-done | bytes 262176 | tf_op jit(solution)/shard_map/ppermute | solution.py:189
  12.5 0.0 collective-permute-done.4.refs_5_.refs_7_
  12.5 0.6 %stats.2 = (f32[2,1024]{1,0:T(2,128)S(1)}, f32[1,1024]{1,0:T(1,128)S(1)}, f32[256,1024]{1,0:T(8,128)S(1)}, f32[256,1024]{1,0:T(8,128)S(1)}) custom-call(s32[16,128]{1,0:T(8,128)S(1)} %place.1.place_ref, bf16[256,256]{1,0:T(8,128)(2,1)S(1)} %slice.32.refs_0_, bf16[256,256]{1,0:T(8,128)(2,1)S(1)} %get-tuple-element.44.refs_1_, ...), custom_call_target="tpu_custom_call" | custom-call | tf_op jit(solution)/shard_map/stats/pallas_call | solution.py:229
  13.1 0.4 %collective-permute-done.3.refs_5_ = bf16[128,256]{1,0:T(8,128)(2,1)S(1)} collective-permute-done((bf16[128,256]{1,0:T(8,128)(2,1)S(1)}, bf16[128,256]{1,0:T(8,128)(2,1)S(1)}, u32[]{:S(2)}, u32[]{:S(2)}) %collective-permute-start.3) | collective-permute-done | bytes 65568 | tf_op jit(solution)/shard_map/ppermute | solution.py:192
  13.5 0.0 collective-permute-done.2.refs_4_
  13.5 0.6 %stats.3 = (f32[2,1024]{1,0:T(2,128)S(1)}, f32[1,1024]{1,0:T(1,128)S(1)}, f32[256,1024]{1,0:T(8,128)S(1)}, f32[256,1024]{1,0:T(8,128)S(1)}) custom-call(s32[16,128]{1,0:T(8,128)S(1)} %place.1.place_ref, bf16[256,256]{1,0:T(8,128)(2,1)S(1)} %slice.32.refs_0_, bf16[256,256]{1,0:T(8,128)(2,1)S(1)} %get-tuple-element.44.refs_1_, ...), custom_call_target="tpu_custom_call" | custom-call | tf_op jit(solution)/shard_map/stats/pallas_call | solution.py:229
  14.2 0.1 collective-permute-start.7
  14.3 1.4 %collective-permute-start.6 = (f32[2,1024]{1,0:T(2,128)S(1)}, f32[2,1024]{1,0:T(2,128)S(1)}, u32[]{:S(2)}, u32[]{:S(2)}) collective-permute-start(f32[2,1024]{1,0:T(2,128)S(1)} %get-tuple-element.24.refs_8_), channel_id=1, source_target_pairs={{0,4},{2,6},{4,0},{6,2},{8,12},{10,14},{12,8},{14,10},{16,20},{18,... | collective-permute-start | bytes 24584 | tf_op jit(solution)/shard_map/ppermute | solution.py:189
  15.6 0.5 %collective-permute-start.5 = (f32[2,1024]{1,0:T(2,128)S(1)}, f32[2,1024]{1,0:T(2,128)S(1)}, u32[]{:S(2)}, u32[]{:S(2)}) collective-permute-start(f32[2,1024]{1,0:T(2,128)S(1)} %get-tuple-element.24.refs_8_), channel_id=1, source_target_pairs={{0,2},{2,0},{4,6},{6,4},{8,10},{10,8},{12,14},{14,12},{16,18},{18,... | collective-permute-start | bytes 24584 | tf_op jit(solution)/shard_map/ppermute | solution.py:189
  16.1 1.3 %collective-permute-done.7.refs_11_ = f32[2,1024]{1,0:T(2,128)S(1)} collective-permute-done((f32[2,1024]{1,0:T(2,128)S(1)}, f32[2,1024]{1,0:T(2,128)S(1)}, u32[]{:S(2)}, u32[]{:S(2)}) %collective-permute-start.7) | collective-permute-done | bytes 8224 | tf_op jit(solution)/shard_map/ppermute | solution.py:189
  17.4 0.6 %collective-permute-done.6.refs_10_ = f32[2,1024]{1,0:T(2,128)S(1)} collective-permute-done((f32[2,1024]{1,0:T(2,128)S(1)}, f32[2,1024]{1,0:T(2,128)S(1)}, u32[]{:S(2)}, u32[]{:S(2)}) %collective-permute-start.6) | collective-permute-done | bytes 8224 | tf_op jit(solution)/shard_map/ppermute | solution.py:189
  18.0 0.0 collective-permute-done.5.refs_9_
  18.0 1.0 %backward.1 = (bf16[256,256]{1,0:T(8,128)(2,1)S(1)}, bf16[256,256]{1,0:T(8,128)(2,1)S(1)}, bf16[128,256]{1,0:T(8,128)(2,1)S(1)}, bf16[128,256]{1,0:T(8,128)(2,1)...) custom-call(bf16[256,256]{1,0:T(8,128)(2,1)S(1)} %slice.32.refs_0_, ...), custom_call_target="tpu_custom_call" | custom-call | tf_op jit(solution)/shard_map/backward/pallas_call | solution.py:252
  18.9 1.6 %collective-permute-start.10 = (bf16[128,256]{1,0:T(8,128)(2,1)S(1)}, bf16[128,256]{1,0:T(8,128)(2,1)S(1)}, u32[]{:S(2)}, u32[]{:S(2)}) collective-permute-start(bf16[128,256]{1,0:T(8,128)(2,1)S(1)} %get-tuple-element.34), channel_id=1, source_target_pairs={{0,1},{1,0},{2,3},{3,2},{4,5},{5,4},{6,7},{7,6},{8,9},{9,8},{10,11... | collective-permute-start | bytes 196616 | tf_op jit(solution)/shard_map/ppermute | solution.py:195
  20.5 1.3 %collective-permute-start.13 = (bf16[128,256]{1,0:T(8,128)(2,1)S(1)}, bf16[128,256]{1,0:T(8,128)(2,1)S(1)}, u32[]{:S(2)}, u32[]{:S(2)}) collective-permute-start(bf16[128,256]{1,0:T(8,128)(2,1)S(1)} %get-tuple-element.36), channel_id=1, source_target_pairs={{0,8},{2,10},{4,12},{6,14},{8,0},{10,2},{12,4},{14,6},{16,24},{18,... | collective-permute-start | bytes 196616 | tf_op jit(solution)/shard_map/ppermute | solution.py:189
  21.8 0.7 %collective-permute-start.8 = (bf16[256,256]{1,0:T(8,128)(2,1)S(1)}, bf16[256,256]{1,0:T(8,128)(2,1)S(1)}, u32[]{:S(2)}, u32[]{:S(2)}) collective-permute-start(bf16[256,256]{1,0:T(8,128)(2,1)S(1)} %get-tuple-element.32), channel_id=1, source_target_pairs={{0,4},{2,6},{4,0},{6,2},{8,12},{10,14},{12,8},{14,10},{16,20},{18,... | collective-permute-start | bytes 393224 | tf_op jit(solution)/shard_map/ppermute | solution.py:189
  22.5 0.7 %collective-permute-done.10.refs_1_ = bf16[128,256]{1,0:T(8,128)(2,1)S(1)} collective-permute-done((bf16[128,256]{1,0:T(8,128)(2,1)S(1)}, bf16[128,256]{1,0:T(8,128)(2,1)S(1)}, u32[]{:S(2)}, u32[]{:S(2)}) %collective-permute-start.10) | collective-permute-done | bytes 65568 | tf_op jit(solution)/shard_map/ppermute | solution.py:195
  23.3 2.8 %collective-permute-start.12 = (bf16[64,256]{1,0:T(8,128)(2,1)S(1)}, bf16[64,256]{1,0:T(8,128)(2,1)S(1)}, u32[]{:S(2)}, u32[]{:S(2)}) collective-permute-start(bf16[64,256]{1,0:T(8,128)(2,1)S(1)} %get-tuple-element.45), channel_id=1, source_target_pairs={{0,24},{2,26},{4,28},{6,30},{8,16},{10,18},{12,20},{14,22},{16,8},... | collective-permute-start | bytes 98312 | tf_op jit(solution)/shard_map/ppermute | solution.py:189
  26.1 0.0 collective-permute-start.11
  26.1 0.7 %collective-permute-done.8 = bf16[256,256]{1,0:T(8,128)(2,1)S(1)} collective-permute-done((bf16[256,256]{1,0:T(8,128)(2,1)S(1)}, bf16[256,256]{1,0:T(8,128)(2,1)S(1)}, u32[]{:S(2)}, u32[]{:S(2)}) %collective-permute-start.8) | collective-permute-done | bytes 131104 | tf_op jit(solution)/shard_map/ppermute | solution.py:189
  26.8 0.1 collective-permute-start.9
  26.9 0.0 collective-permute-done.13.refs_1_
  26.9 0.9 %collective-permute-start.14 = (bf16[64,256]{1,0:T(8,128)(2,1)S(1)}, bf16[64,256]{1,0:T(8,128)(2,1)S(1)}, u32[]{:S(2)}, u32[]{:S(2)}) collective-permute-start(bf16[64,256]{1,0:T(8,128)(2,1)S(1)} %slice.39), channel_id=1, source_target_pairs={{0,1},{1,0},{2,3},{3,2},{4,5},{5,4},{6,7},{7,6},{8,9},{9,8},{10,11... | collective-permute-start | bytes 98312 | tf_op jit(solution)/shard_map/ppermute | solution.py:195
  27.9 0.3 collective-permute-done.9.other_ref
  28.1 0.6 %query_sum.1 = bf16[128,256]{1,0:T(8,128)(2,1)} custom-call(bf16[256,256]{1,0:T(8,128)(2,1)S(1)} %add_convert_fusion.pair_ref, bf16[128,256]{1,0:T(8,128)(2,1)S(1)} %collective-permute-done.9.other_ref), custom_call_target="tpu_custom_call" | custom-call | flops 1000000000 | tf_op jit(solution)/shard_map/query_sum/pallas_call | solution.py:280
  28.8 0.3 collective-permute-done.12.refs_1_
  29.1 1.8 %collective-permute-done.11.refs_0_ = bf16[64,256]{1,0:T(8,128)(2,1)S(1)} collective-permute-done((bf16[64,256]{1,0:T(8,128)(2,1)S(1)}, bf16[64,256]{1,0:T(8,128)(2,1)S(1)}, u32[]{:S(2)}, u32[]{:S(2)}) %collective-permute-start.11) | collective-permute-done | bytes 32800 | tf_op jit(solution)/shard_map/ppermute | solution.py:189
  30.9 0.0 collective-permute-done.14.refs_2_
  30.9 0.6 %finish.1 = (bf16[64,128]{1,0:T(8,128)(2,1)}, bf16[64,128]{1,0:T(8,128)(2,1)}) custom-call(bf16[128,256]{1,0:T(8,128)(2,1)S(1)} %fold.3.owned_ref, bf16[64,256]{1,0:T(8,128)(2,1)S(1)} %collective-permute-done.11.refs_0_, bf16[64,256]{1,0:T(8,128)(2,1)S(1)} %collective-permute-done.12.refs_1_, bf16[64,256]{1,0:T(8,128)(2,1)S(1)} %collective-permute-done.14.refs_2_), custom_call_target="tpu_custom_call" | custom-call | tf_op jit(solution)/shard_map/finish/pallas_call | solution.py:290
  (10 shorter events, 0.1 us)
Async XLA Ops:
  1.5 9.3 %collective-permute-start = (bf16[256,256]{1,0:T(8,128)(2,1)S(1)}, bf16[256,256]{1,0:T(8,128)(2,1)S(1)}, u32[]{:S(2)}, u32[]{:S(2)}) collective-permute-start(bf16[256,256]{1,0:T(8,128)(2,1)S(1)} %slice.32.refs_0_), channel_id=1, source_target_pairs={{0,4},{2,6},{4,0},{6,2},{8,12},{10,14},{12,8},{14,10},{16,20},{18,... | collective-permute-start | bytes 393224 | tf_op jit(solution)/shard_map/ppermute | solution.py:189
  4.6 5.6 %copy-start = (s32[16,2]{0,1:T(2,128)S(1)}, s32[16,2]{0,1:T(2,128)}, u32[]{:S(2)}) copy-start(s32[16,2]{0,1:T(2,128)} %param.11) | copy-start | bytes 388
  4.6 7.9 %collective-permute-start.4 = (bf16[128,256]{1,0:T(8,128)(2,1)S(1)}, bf16[128,256]{1,0:T(8,128)(2,1)S(1)}, u32[]{:S(2)}, u32[]{:S(2)}) collective-permute-start(bf16[128,256]{1,0:T(8,128)(2,1)S(1)} %slice.35.refs_4_.refs_6_), channel_id=1, source_target_pairs={{0,8},{2,10},{4,12},{6,14},{8,16},{10,18},{12,20},{14,22},{16,24},... | collective-permute-start | bytes 196616 | tf_op jit(solution)/shard_map/ppermute | solution.py:192
  6.2 7.3 %collective-permute-start.3 = (bf16[128,256]{1,0:T(8,128)(2,1)S(1)}, bf16[128,256]{1,0:T(8,128)(2,1)S(1)}, u32[]{:S(2)}, u32[]{:S(2)}) collective-permute-start(bf16[128,256]{1,0:T(8,128)(2,1)S(1)} %slice.35.refs_4_.refs_6_), channel_id=1, source_target_pairs={{0,16},{2,18},{4,20},{6,22},{8,24},{10,26},{12,28},{14,30},{16,0},... | collective-permute-start | bytes 196616 | tf_op jit(solution)/shard_map/ppermute | solution.py:192
  8.8 4.8 %collective-permute-start.2 = (bf16[128,256]{1,0:T(8,128)(2,1)S(1)}, bf16[128,256]{1,0:T(8,128)(2,1)S(1)}, u32[]{:S(2)}, u32[]{:S(2)}) collective-permute-start(bf16[128,256]{1,0:T(8,128)(2,1)S(1)} %slice.35.refs_4_.refs_6_), channel_id=1, source_target_pairs={{0,24},{2,26},{4,28},{6,30},{8,0},{10,2},{12,4},{14,6},{16,8},{18,... | collective-permute-start | bytes 196616 | tf_op jit(solution)/shard_map/ppermute | solution.py:192
  10.1 0.7 %copy-start.1 = (s32[8]{0:T(128)S(1)}, s32[8]{0:T(128)}, u32[]{:S(2)}) copy-start(s32[8]{0:T(128)} %param.10) | copy-start | bytes 100
  10.9 1.6 %collective-permute-start.1 = (bf16[512,256]{1,0:T(8,128)(2,1)S(1)}, bf16[512,256]{1,0:T(8,128)(2,1)S(1)}, u32[]{:S(2)}, u32[]{:S(2)}) collective-permute-start(bf16[512,256]{1,0:T(8,128)(2,1)S(1)} %pad_maximum_fusion), channel_id=1, source_target_pairs={{0,2},{2,0},{4,6},{6,4},{8,10},{10,8},{12,14},{14,12},{16,18},{18,... | collective-permute-start | bytes 786440 | tf_op jit(solution)/shard_map/ppermute | solution.py:189
  14.2 3.2 %collective-permute-start.7 = (f32[2,1024]{1,0:T(2,128)S(1)}, f32[2,1024]{1,0:T(2,128)S(1)}, u32[]{:S(2)}, u32[]{:S(2)}) collective-permute-start(f32[2,1024]{1,0:T(2,128)S(1)} %get-tuple-element.24.refs_8_), channel_id=1, source_target_pairs={{0,6},{2,4},{4,2},{6,0},{8,14},{10,12},{12,10},{14,8},{16,22},{18,... | collective-permute-start | bytes 24584 | tf_op jit(solution)/shard_map/ppermute | solution.py:189
  14.3 3.7 %collective-permute-start.6 = (f32[2,1024]{1,0:T(2,128)S(1)}, f32[2,1024]{1,0:T(2,128)S(1)}, u32[]{:S(2)}, u32[]{:S(2)}) collective-permute-start(f32[2,1024]{1,0:T(2,128)S(1)} %get-tuple-element.24.refs_8_), channel_id=1, source_target_pairs={{0,4},{2,6},{4,0},{6,2},{8,12},{10,14},{12,8},{14,10},{16,20},{18,... | collective-permute-start | bytes 24584 | tf_op jit(solution)/shard_map/ppermute | solution.py:189
  15.6 2.3 %collective-permute-start.5 = (f32[2,1024]{1,0:T(2,128)S(1)}, f32[2,1024]{1,0:T(2,128)S(1)}, u32[]{:S(2)}, u32[]{:S(2)}) collective-permute-start(f32[2,1024]{1,0:T(2,128)S(1)} %get-tuple-element.24.refs_8_), channel_id=1, source_target_pairs={{0,2},{2,0},{4,6},{6,4},{8,10},{10,8},{12,14},{14,12},{16,18},{18,... | collective-permute-start | bytes 24584 | tf_op jit(solution)/shard_map/ppermute | solution.py:189
  18.9 4.3 %collective-permute-start.10 = (bf16[128,256]{1,0:T(8,128)(2,1)S(1)}, bf16[128,256]{1,0:T(8,128)(2,1)S(1)}, u32[]{:S(2)}, u32[]{:S(2)}) collective-permute-start(bf16[128,256]{1,0:T(8,128)(2,1)S(1)} %get-tuple-element.34), channel_id=1, source_target_pairs={{0,1},{1,0},{2,3},{3,2},{4,5},{5,4},{6,7},{7,6},{8,9},{9,8},{10,11... | collective-permute-start | bytes 196616 | tf_op jit(solution)/shard_map/ppermute | solution.py:195
  20.5 6.4 %collective-permute-start.13 = (bf16[128,256]{1,0:T(8,128)(2,1)S(1)}, bf16[128,256]{1,0:T(8,128)(2,1)S(1)}, u32[]{:S(2)}, u32[]{:S(2)}) collective-permute-start(bf16[128,256]{1,0:T(8,128)(2,1)S(1)} %get-tuple-element.36), channel_id=1, source_target_pairs={{0,8},{2,10},{4,12},{6,14},{8,0},{10,2},{12,4},{14,6},{16,24},{18,... | collective-permute-start | bytes 196616 | tf_op jit(solution)/shard_map/ppermute | solution.py:189
  21.8 5.0 %collective-permute-start.8 = (bf16[256,256]{1,0:T(8,128)(2,1)S(1)}, bf16[256,256]{1,0:T(8,128)(2,1)S(1)}, u32[]{:S(2)}, u32[]{:S(2)}) collective-permute-start(bf16[256,256]{1,0:T(8,128)(2,1)S(1)} %get-tuple-element.32), channel_id=1, source_target_pairs={{0,4},{2,6},{4,0},{6,2},{8,12},{10,14},{12,8},{14,10},{16,20},{18,... | collective-permute-start | bytes 393224 | tf_op jit(solution)/shard_map/ppermute | solution.py:189
  23.3 5.8 %collective-permute-start.12 = (bf16[64,256]{1,0:T(8,128)(2,1)S(1)}, bf16[64,256]{1,0:T(8,128)(2,1)S(1)}, u32[]{:S(2)}, u32[]{:S(2)}) collective-permute-start(bf16[64,256]{1,0:T(8,128)(2,1)S(1)} %get-tuple-element.45), channel_id=1, source_target_pairs={{0,24},{2,26},{4,28},{6,30},{8,16},{10,18},{12,20},{14,22},{16,8},... | collective-permute-start | bytes 98312 | tf_op jit(solution)/shard_map/ppermute | solution.py:189
  26.1 4.8 %collective-permute-start.11 = (bf16[64,256]{1,0:T(8,128)(2,1)S(1)}, bf16[64,256]{1,0:T(8,128)(2,1)S(1)}, u32[]{:S(2)}, u32[]{:S(2)}) collective-permute-start(bf16[64,256]{1,0:T(8,128)(2,1)S(1)} %get-tuple-element.46), channel_id=1, source_target_pairs={{0,16},{2,18},{4,20},{6,22},{8,24},{10,26},{12,28},{14,30},{16,0},... | collective-permute-start | bytes 98312 | tf_op jit(solution)/shard_map/ppermute | solution.py:189
  26.8 1.3 %collective-permute-start.9 = (bf16[128,256]{1,0:T(8,128)(2,1)S(1)}, bf16[128,256]{1,0:T(8,128)(2,1)S(1)}, u32[]{:S(2)}, u32[]{:S(2)}) collective-permute-start(bf16[128,256]{1,0:T(8,128)(2,1)S(1)} %slice.36), channel_id=1, source_target_pairs={{0,2},{2,0},{4,6},{6,4},{8,10},{10,8},{12,14},{14,12},{16,18},{18,... | collective-permute-start | bytes 196616 | tf_op jit(solution)/shard_map/ppermute | solution.py:189
  26.9 4.0 %collective-permute-start.14 = (bf16[64,256]{1,0:T(8,128)(2,1)S(1)}, bf16[64,256]{1,0:T(8,128)(2,1)S(1)}, u32[]{:S(2)}, u32[]{:S(2)}) collective-permute-start(bf16[64,256]{1,0:T(8,128)(2,1)S(1)} %slice.39), channel_id=1, source_target_pairs={{0,1},{1,0},{2,3},{3,2},{4,5},{5,4},{6,7},{7,6},{8,9},{9,8},{10,11... | collective-permute-start | bytes 98312 | tf_op jit(solution)/shard_map/ppermute | solution.py:195

commit v11 on v10

--- a/solution.py
+++ b/solution.py
@@ -101,9 +101,9 @@
 def backward_kernel(order, late, heads, shards, *refs):
     chunks = len(order)
     group, chunk = refs[:GROUP], refs[GROUP : GROUP + chunks]
-    chunk = chunk[late:] + chunk[:late]
+    chunk = chunk[late[1] :] + chunk[late[0] : late[1]] + chunk[: late[0]]
     stats, refs = refs[GROUP + chunks :][:GROUP], refs[2 * GROUP + chunks :]
-    (tops, expos, dprobs), refs = (refs[0:2], refs[2:4], refs[4:6]), refs[6:]
+    (tops, expos, dprobs), refs = (refs[0:3], refs[3:6], refs[6:9]), refs[9:]
     near_ref, far_ref, *outs, dv_total, dk_total = refs
     rows, width = chunk[0].shape
     hd = width // 2
@@ -221,7 +221,9 @@
     both = swap(jnp.concatenate([packed_qg, across], axis=0), group_bits[1])
     group = [packed_qg, both[: 2 * rows], across, both[2 * rows :]]
 
-    late = tuple(range(1, 3 * chunks // 4))
+    last = tuple(range(1, chunks // 2))
+    middle = tuple(range(chunks // 2, 3 * chunks // 4))
+    late = middle + last
     early = (0, *range(3 * chunks // 4, chunks))
 
     def stats_of(which, before, flops):
@@ -242,22 +244,23 @@
         )(place, *group, *[chunk[b] for b in which], *before)
 
     first, *kept_early = stats_of(early, (), 0)
-    stats, *kept_late = stats_of(late, (first,), 0)
-    kept = [ref for pair in zip(kept_early, kept_late) for ref in pair]
+    second, *kept_middle = stats_of(middle, (first,), 0)
+    stats, *kept_last = stats_of(last, (second,), 0)
+    kept = [ref for three in zip(kept_early, kept_middle, kept_last) for ref in three]
     all_stats = [stats] + [swap(stats, bits) for bits in group_bits[1:]]
 
     pair_rows = array((GROUP // 2 * rows, width))
     half = chunks // 2
     pieces = (array((rows, 2 * hd)),) * half + (array((half * part, 2 * hd)),) * shards
     near, far, *dkv = pl.pallas_call(
-        functools.partial(backward_kernel, early + late, len(late), heads, shards),
+        functools.partial(backward_kernel, early + late, (len(last), len(late)), heads, shards),
         out_shape=(pair_rows, pair_rows) + pieces,
         in_specs=[vmem] * (2 * GROUP + chunks + len(kept)),
         out_specs=(vmem,) * (2 + len(pieces)),
         scratch_shapes=[pltpu.VMEM((chunks * rows, hd), jnp.float32)] * 2,
         compiler_params=params,
         name="backward",
-    )(*group, *[chunk[b] for b in late + early], *all_stats, *kept)
+    )(*group, *[chunk[b] for b in last + middle + early], *all_stats, *kept)
 
     def fold(parts, flops):
         return pl.pallas_call(

time: 31.7 us -> 31.5 us (level)
  starting transfers between devices: 17.9 us -> 17.5 us
    ppermute x10, starting transfers between devices: 9.86 us -> 9.4 us  [swap(): return lax.ppermute(x, 'ctx', [(i, i ^ bits) for i in range(ctx_size)])]
    pallas_call x2 -> x3, Pallas kernels: 1.26 us -> 1.47 us  [stats_of(): pl.pallas_call(functools.partial(stats_kernel, which, heads), out_shape=(...]
  transfers between devices with their start and end apart: 15 -> 15, of which waited for: 9 -> 9; matrix products, arithmetic and copies ran while one was open for 1% -> 1% of each run, Pallas kernels for 6% -> 7%
where the time goes in v11:
time: 31.5 us; the launch traced here: 31.4 us
  starting transfers between devices  17.5 us (56%)
  waiting for transfers between devices  7.04 us (22%)
  Pallas kernels  4.34 us (14%)
  other arithmetic  1.02 us (3%)
  between operations  0.78 us (2%)
  local copies, waits for them, and re-layouts  0.71 us (2%)
    ppermute x10, starting transfers between devices, swap(): return lax.ppermute(x, 'ctx', [(i, i ^ bits) for i in range(ctx_size)])  9.4 us
    ppermute x10, waiting for transfers between devices, swap(): return lax.ppermute(x, 'ctx', [(i, i ^ bits) for i in range(ctx_size)])  5.87 us
    ppermute x3, starting transfers between devices, shift(): lax.ppermute(x, 'ctx', [(i, (i - by) % ctx_size) for i in range(ctx_size)])  5.56 us
    ppermute x2, starting transfers between devices, turn(): lax.ppermute(x, 'head', [(i, (i + by) % shards) for i in range(shards)])  2.5 us
    pallas_call x3, Pallas kernels, stats_of(): pl.pallas_call(functools.partial(stats_kernel, which, heads), out_shape=(...  1.47 us
    pallas_call x1, Pallas kernels, local(): pl.pallas_call(functools.partial(backward_kernel, early + late, (len(last...  0.98 us
    concatenate x1, other arithmetic, local(): jnp.concatenate([jnp.concatenate([key_rows, value_rows], axis=1), queries...  0.89 us
    ppermute x2, waiting for transfers between devices, turn(): lax.ppermute(x, 'head', [(i, (i + by) % shards) for i in range(shards)])  0.77 us
  transfers between devices with their start and end apart: 15, of which 9 were waited for; matrix products, arithmetic and copies ran while one was open for 1% of the time, Pallas kernels for 7%

profile of v11, /device:TPU:0, one launch (start us, length us, event | category | flops | bytes accessed | tf_op | source)
XLA Modules:
  0.0 31.4 jit_solution(9962445523152896114)
XLA Ops:
  0.6 0.9 %pad_maximum_fusion.1 = bf16[384,256]{1,0:T(8,128)(2,1)S(1)} fusion(bf16[128,256]{1,0:T(8,128)(2,1)} %param.9, bf16[128,256]{1,0:T(8,128)(2,1)} %param.6, bf16[128,128]{1,0:T(8,128)(2,1)} %param.8, bf16[128,128]{1,0:T(8,128)(2,1)} %param.7), kind=kLoop, calls=%fused_computation.2 | loop fusion | flops 786432 | bytes 393216 | tf_op jit(solution)/shard_map/concatenate | solution.py:214
  1.5 3.0 %collective-permute-start = (bf16[256,256]{1,0:T(8,128)(2,1)S(1)}, bf16[256,256]{1,0:T(8,128)(2,1)S(1)}, u32[]{:S(2)}, u32[]{:S(2)}) collective-permute-start(bf16[256,256]{1,0:T(8,128)(2,1)S(1)} %slice.32.refs_0_), channel_id=1, source_target_pairs={{0,4},{2,6},{4,0},{6,2},{8,12},{10,14},{12,8},{14,10},{16,20},{18,... | collective-permute-start | bytes 393224 | tf_op jit(solution)/shard_map/ppermute | solution.py:189
  4.6 0.0 copy-start
  4.6 1.6 %collective-permute-start.4 = (bf16[128,256]{1,0:T(8,128)(2,1)S(1)}, bf16[128,256]{1,0:T(8,128)(2,1)S(1)}, u32[]{:S(2)}, u32[]{:S(2)}) collective-permute-start(bf16[128,256]{1,0:T(8,128)(2,1)S(1)} %slice.35.refs_4_.refs_6_), channel_id=1, source_target_pairs={{0,8},{2,10},{4,12},{6,14},{8,16},{10,18},{12,20},{14,22},{16,24},... | collective-permute-start | bytes 196616 | tf_op jit(solution)/shard_map/ppermute | solution.py:192
  6.2 2.6 %collective-permute-start.3 = (bf16[128,256]{1,0:T(8,128)(2,1)S(1)}, bf16[128,256]{1,0:T(8,128)(2,1)S(1)}, u32[]{:S(2)}, u32[]{:S(2)}) collective-permute-start(bf16[128,256]{1,0:T(8,128)(2,1)S(1)} %slice.35.refs_4_.refs_6_), channel_id=1, source_target_pairs={{0,16},{2,18},{4,20},{6,22},{8,24},{10,26},{12,28},{14,30},{16,0},... | collective-permute-start | bytes 196616 | tf_op jit(solution)/shard_map/ppermute | solution.py:192
  8.8 1.3 %collective-permute-start.2 = (bf16[128,256]{1,0:T(8,128)(2,1)S(1)}, bf16[128,256]{1,0:T(8,128)(2,1)S(1)}, u32[]{:S(2)}, u32[]{:S(2)}) collective-permute-start(bf16[128,256]{1,0:T(8,128)(2,1)S(1)} %slice.35.refs_4_.refs_6_), channel_id=1, source_target_pairs={{0,24},{2,26},{4,28},{6,30},{8,0},{10,2},{12,4},{14,6},{16,8},{18,... | collective-permute-start | bytes 196616 | tf_op jit(solution)/shard_map/ppermute | solution.py:192
  10.1 0.0 copy-done
  10.1 0.0 copy-start.1
  10.1 0.1 reshape.9
  10.2 0.6 %copy-done.1 = s32[8]{0:T(128)S(1)} copy-done((s32[8]{0:T(128)S(1)}, s32[8]{0:T(128)}, u32[]{:S(2)}) %copy-start.1) | copy-done | bytes 56
  10.8 0.1 pad_add_fusion.ints
  10.9 0.0 collective-permute-done.refs_2_
  10.9 0.1 collective-permute-start.1
  11.0 0.6 %place.1.place_ref = s32[16,128]{1,0:T(8,128)S(1)} custom-call(s32[40]{0:T(128)S(1)} %pad_add_fusion.ints), custom_call_target="tpu_custom_call" | custom-call | flops 10000000000 | tf_op jit(solution)/shard_map/place/pallas_call | solution.py:204
  11.5 0.9 %collective-permute-done.1 = bf16[512,256]{1,0:T(8,128)(2,1)S(1)} collective-permute-done((bf16[512,256]{1,0:T(8,128)(2,1)S(1)}, bf16[512,256]{1,0:T(8,128)(2,1)S(1)}, u32[]{:S(2)}, u32[]{:S(2)}) %collective-permute-start.1) | collective-permute-done | bytes 262176 | tf_op jit(solution)/shard_map/ppermute | solution.py:189
  12.5 0.0 collective-permute-done.4.refs_5_.refs_7_
  12.5 0.6 %stats.3 = (f32[2,1024]{1,0:T(2,128)S(1)}, f32[1,1024]{1,0:T(1,128)S(1)}, f32[256,1024]{1,0:T(8,128)S(1)}, f32[256,1024]{1,0:T(8,128)S(1)}) custom-call(s32[16,128]{1,0:T(8,128)S(1)} %place.1.place_ref, bf16[256,256]{1,0:T(8,128)(2,1)S(1)} %slice.32.refs_0_, bf16[256,256]{1,0:T(8,128)(2,1)S(1)} %get-tuple-element.52.refs_1_, ...), custom_call_target="tpu_custom_call" | custom-call | tf_op jit(solution)/shard_map/stats/pallas_call | solution.py:231
  13.1 0.4 %collective-permute-done.3.refs_4_.refs_5_ = bf16[128,256]{1,0:T(8,128)(2,1)S(1)} collective-permute-done((bf16[128,256]{1,0:T(8,128)(2,1)S(1)}, bf16[128,256]{1,0:T(8,128)(2,1)S(1)}, u32[]{:S(2)}, u32[]{:S(2)}) %collective-permute-start.3) | collective-permute-done | bytes 65568 | tf_op jit(solution)/shard_map/ppermute | solution.py:192
  13.5 0.4 %stats.4 = (f32[2,1024]{1,0:T(2,128)S(1)}, f32[1,1024]{1,0:T(1,128)S(1)}, f32[128,1024]{1,0:T(8,128)S(1)}, f32[128,1024]{1,0:T(8,128)S(1)}) custom-call(s32[16,128]{1,0:T(8,128)S(1)} %place.1.place_ref, bf16[256,256]{1,0:T(8,128)(2,1)S(1)} %slice.32.refs_0_, bf16[256,256]{1,0:T(8,128)(2,1)S(1)} %get-tuple-element.52.refs_1_, ...), custom_call_target="tpu_custom_call" | custom-call | tf_op jit(solution)/shard_map/stats/pallas_call | solution.py:231
  14.0 0.0 collective-permute-done.2.refs_4_
  14.0 0.4 %stats.5 = (f32[2,1024]{1,0:T(2,128)S(1)}, f32[1,1024]{1,0:T(1,128)S(1)}, f32[128,1024]{1,0:T(8,128)S(1)}, f32[128,1024]{1,0:T(8,128)S(1)}) custom-call(s32[16,128]{1,0:T(8,128)S(1)} %place.1.place_ref, bf16[256,256]{1,0:T(8,128)(2,1)S(1)} %slice.32.refs_0_, bf16[256,256]{1,0:T(8,128)(2,1)S(1)} %get-tuple-element.52.refs_1_, ...), custom_call_target="tpu_custom_call" | custom-call | tf_op jit(solution)/shard_map/stats/pallas_call | solution.py:231
  14.4 0.1 collective-permute-start.7
  14.5 1.4 %collective-permute-start.6 = (f32[2,1024]{1,0:T(2,128)S(1)}, f32[2,1024]{1,0:T(2,128)S(1)}, u32[]{:S(2)}, u32[]{:S(2)}) collective-permute-start(f32[2,1024]{1,0:T(2,128)S(1)} %get-tuple-element.29.refs_8_), channel_id=1, source_target_pairs={{0,4},{2,6},{4,0},{6,2},{8,12},{10,14},{12,8},{14,10},{16,20},{18,... | collective-permute-start | bytes 24584 | tf_op jit(solution)/shard_map/ppermute | solution.py:189
  15.9 0.5 %collective-permute-start.5 = (f32[2,1024]{1,0:T(2,128)S(1)}, f32[2,1024]{1,0:T(2,128)S(1)}, u32[]{:S(2)}, u32[]{:S(2)}) collective-permute-start(f32[2,1024]{1,0:T(2,128)S(1)} %get-tuple-element.29.refs_8_), channel_id=1, source_target_pairs={{0,2},{2,0},{4,6},{6,4},{8,10},{10,8},{12,14},{14,12},{16,18},{18,... | collective-permute-start | bytes 24584 | tf_op jit(solution)/shard_map/ppermute | solution.py:189
  16.3 1.2 %collective-permute-done.7.refs_11_ = f32[2,1024]{1,0:T(2,128)S(1)} collective-permute-done((f32[2,1024]{1,0:T(2,128)S(1)}, f32[2,1024]{1,0:T(2,128)S(1)}, u32[]{:S(2)}, u32[]{:S(2)}) %collective-permute-start.7) | collective-permute-done | bytes 8224 | tf_op jit(solution)/shard_map/ppermute | solution.py:189
  17.6 0.6 %collective-permute-done.6.refs_10_ = f32[2,1024]{1,0:T(2,128)S(1)} collective-permute-done((f32[2,1024]{1,0:T(2,128)S(1)}, f32[2,1024]{1,0:T(2,128)S(1)}, u32[]{:S(2)}, u32[]{:S(2)}) %collective-permute-start.6) | collective-permute-done | bytes 8224 | tf_op jit(solution)/shard_map/ppermute | solution.py:189
  18.2 0.0 collective-permute-done.5.refs_9_
  18.2 1.0 %backward.1 = (bf16[256,256]{1,0:T(8,128)(2,1)S(1)}, bf16[256,256]{1,0:T(8,128)(2,1)S(1)}, bf16[128,256]{1,0:T(8,128)(2,1)S(1)}, bf16[128,256]{1,0:T(8,128)(2,1)...) custom-call(bf16[256,256]{1,0:T(8,128)(2,1)S(1)} %slice.32.refs_0_, ...), custom_call_target="tpu_custom_call" | custom-call | tf_op jit(solution)/shard_map/backward/pallas_call | solution.py:255
  19.2 1.6 %collective-permute-start.10 = (bf16[128,256]{1,0:T(8,128)(2,1)S(1)}, bf16[128,256]{1,0:T(8,128)(2,1)S(1)}, u32[]{:S(2)}, u32[]{:S(2)}) collective-permute-start(bf16[128,256]{1,0:T(8,128)(2,1)S(1)} %get-tuple-element.42), channel_id=1, source_target_pairs={{0,1},{1,0},{2,3},{3,2},{4,5},{5,4},{6,7},{7,6},{8,9},{9,8},{10,11... | collective-permute-start | bytes 196616 | tf_op jit(solution)/shard_map/ppermute | solution.py:195
  20.8 0.8 %collective-permute-start.13 = (bf16[128,256]{1,0:T(8,128)(2,1)S(1)}, bf16[128,256]{1,0:T(8,128)(2,1)S(1)}, u32[]{:S(2)}, u32[]{:S(2)}) collective-permute-start(bf16[128,256]{1,0:T(8,128)(2,1)S(1)} %get-tuple-element.44), channel_id=1, source_target_pairs={{0,8},{2,10},{4,12},{6,14},{8,0},{10,2},{12,4},{14,6},{16,24},{18,... | collective-permute-start | bytes 196616 | tf_op jit(solution)/shard_map/ppermute | solution.py:189
  21.6 1.2 %collective-permute-start.8 = (bf16[256,256]{1,0:T(8,128)(2,1)S(1)}, bf16[256,256]{1,0:T(8,128)(2,1)S(1)}, u32[]{:S(2)}, u32[]{:S(2)}) collective-permute-start(bf16[256,256]{1,0:T(8,128)(2,1)S(1)} %get-tuple-element.40), channel_id=1, source_target_pairs={{0,4},{2,6},{4,0},{6,2},{8,12},{10,14},{12,8},{14,10},{16,20},{18,... | collective-permute-start | bytes 393224 | tf_op jit(solution)/shard_map/ppermute | solution.py:189
  22.8 0.8 %collective-permute-done.10.refs_1_ = bf16[128,256]{1,0:T(8,128)(2,1)S(1)} collective-permute-done((bf16[128,256]{1,0:T(8,128)(2,1)S(1)}, bf16[128,256]{1,0:T(8,128)(2,1)S(1)}, u32[]{:S(2)}, u32[]{:S(2)}) %collective-permute-start.10) | collective-permute-done | bytes 65568 | tf_op jit(solution)/shard_map/ppermute | solution.py:195
  23.6 2.3 %collective-permute-start.12 = (bf16[64,256]{1,0:T(8,128)(2,1)S(1)}, bf16[64,256]{1,0:T(8,128)(2,1)S(1)}, u32[]{:S(2)}, u32[]{:S(2)}) collective-permute-start(bf16[64,256]{1,0:T(8,128)(2,1)S(1)} %get-tuple-element.53), channel_id=1, source_target_pairs={{0,24},{2,26},{4,28},{6,30},{8,16},{10,18},{12,20},{14,22},{16,8},... | collective-permute-start | bytes 98312 | tf_op jit(solution)/shard_map/ppermute | solution.py:189
  25.9 0.0 collective-permute-start.11
  25.9 0.7 %collective-permute-done.8 = bf16[256,256]{1,0:T(8,128)(2,1)S(1)} collective-permute-done((bf16[256,256]{1,0:T(8,128)(2,1)S(1)}, bf16[256,256]{1,0:T(8,128)(2,1)S(1)}, u32[]{:S(2)}, u32[]{:S(2)}) %collective-permute-start.8) | collective-permute-done | bytes 131104 | tf_op jit(solution)/shard_map/ppermute | solution.py:189
  26.6 0.1 collective-permute-start.9
  26.7 0.0 collective-permute-done.13.refs_1_
  26.7 0.9 %collective-permute-start.14 = (bf16[64,256]{1,0:T(8,128)(2,1)S(1)}, bf16[64,256]{1,0:T(8,128)(2,1)S(1)}, u32[]{:S(2)}, u32[]{:S(2)}) collective-permute-start(bf16[64,256]{1,0:T(8,128)(2,1)S(1)} %slice.39), channel_id=1, source_target_pairs={{0,1},{1,0},{2,3},{3,2},{4,5},{5,4},{6,7},{7,6},{8,9},{9,8},{10,11... | collective-permute-start | bytes 98312 | tf_op jit(solution)/shard_map/ppermute | solution.py:195
  27.7 0.3 collective-permute-done.9.other_ref
  27.9 0.6 %query_sum.1 = bf16[128,256]{1,0:T(8,128)(2,1)} custom-call(bf16[256,256]{1,0:T(8,128)(2,1)S(1)} %add_convert_fusion.pair_ref, bf16[128,256]{1,0:T(8,128)(2,1)S(1)} %collective-permute-done.9.other_ref), custom_call_target="tpu_custom_call" | custom-call | flops 1000000000 | tf_op jit(solution)/shard_map/query_sum/pallas_call | solution.py:283
  28.6 0.8 %collective-permute-done.12.refs_1_ = bf16[64,256]{1,0:T(8,128)(2,1)S(1)} collective-permute-done((bf16[64,256]{1,0:T(8,128)(2,1)S(1)}, bf16[64,256]{1,0:T(8,128)(2,1)S(1)}, u32[]{:S(2)}, u32[]{:S(2)}) %collective-permute-start.12) | collective-permute-done | bytes 32800 | tf_op jit(solution)/shard_map/ppermute | solution.py:189
  29.4 1.4 %collective-permute-done.11.refs_0_ = bf16[64,256]{1,0:T(8,128)(2,1)S(1)} collective-permute-done((bf16[64,256]{1,0:T(8,128)(2,1)S(1)}, bf16[64,256]{1,0:T(8,128)(2,1)S(1)}, u32[]{:S(2)}, u32[]{:S(2)}) %collective-permute-start.11) | collective-permute-done | bytes 32800 | tf_op jit(solution)/shard_map/ppermute | solution.py:189
  30.7 0.0 collective-permute-done.14.refs_2_
  30.7 0.6 %finish.1 = (bf16[64,128]{1,0:T(8,128)(2,1)}, bf16[64,128]{1,0:T(8,128)(2,1)}) custom-call(bf16[128,256]{1,0:T(8,128)(2,1)S(1)} %fold.3.owned_ref, bf16[64,256]{1,0:T(8,128)(2,1)S(1)} %collective-permute-done.11.refs_0_, bf16[64,256]{1,0:T(8,128)(2,1)S(1)} %collective-permute-done.12.refs_1_, bf16[64,256]{1,0:T(8,128)(2,1)S(1)} %collective-permute-done.14.refs_2_), custom_call_target="tpu_custom_call" | custom-call | tf_op jit(solution)/shard_map/finish/pallas_call | solution.py:293
  (10 shorter events, 0.1 us)
Async XLA Ops:
  1.5 9.3 %collective-permute-start = (bf16[256,256]{1,0:T(8,128)(2,1)S(1)}, bf16[256,256]{1,0:T(8,128)(2,1)S(1)}, u32[]{:S(2)}, u32[]{:S(2)}) collective-permute-start(bf16[256,256]{1,0:T(8,128)(2,1)S(1)} %slice.32.refs_0_), channel_id=1, source_target_pairs={{0,4},{2,6},{4,0},{6,2},{8,12},{10,14},{12,8},{14,10},{16,20},{18,... | collective-permute-start | bytes 393224 | tf_op jit(solution)/shard_map/ppermute | solution.py:189
  4.6 5.6 %copy-start = (s32[16,2]{0,1:T(2,128)S(1)}, s32[16,2]{0,1:T(2,128)}, u32[]{:S(2)}) copy-start(s32[16,2]{0,1:T(2,128)} %param.11) | copy-start | bytes 388
  4.6 7.9 %collective-permute-start.4 = (bf16[128,256]{1,0:T(8,128)(2,1)S(1)}, bf16[128,256]{1,0:T(8,128)(2,1)S(1)}, u32[]{:S(2)}, u32[]{:S(2)}) collective-permute-start(bf16[128,256]{1,0:T(8,128)(2,1)S(1)} %slice.35.refs_4_.refs_6_), channel_id=1, source_target_pairs={{0,8},{2,10},{4,12},{6,14},{8,16},{10,18},{12,20},{14,22},{16,24},... | collective-permute-start | bytes 196616 | tf_op jit(solution)/shard_map/ppermute | solution.py:192
  6.2 7.3 %collective-permute-start.3 = (bf16[128,256]{1,0:T(8,128)(2,1)S(1)}, bf16[128,256]{1,0:T(8,128)(2,1)S(1)}, u32[]{:S(2)}, u32[]{:S(2)}) collective-permute-start(bf16[128,256]{1,0:T(8,128)(2,1)S(1)} %slice.35.refs_4_.refs_6_), channel_id=1, source_target_pairs={{0,16},{2,18},{4,20},{6,22},{8,24},{10,26},{12,28},{14,30},{16,0},... | collective-permute-start | bytes 196616 | tf_op jit(solution)/shard_map/ppermute | solution.py:192
  8.8 5.2 %collective-permute-start.2 = (bf16[128,256]{1,0:T(8,128)(2,1)S(1)}, bf16[128,256]{1,0:T(8,128)(2,1)S(1)}, u32[]{:S(2)}, u32[]{:S(2)}) collective-permute-start(bf16[128,256]{1,0:T(8,128)(2,1)S(1)} %slice.35.refs_4_.refs_6_), channel_id=1, source_target_pairs={{0,24},{2,26},{4,28},{6,30},{8,0},{10,2},{12,4},{14,6},{16,8},{18,... | collective-permute-start | bytes 196616 | tf_op jit(solution)/shard_map/ppermute | solution.py:192
  10.1 0.7 %copy-start.1 = (s32[8]{0:T(128)S(1)}, s32[8]{0:T(128)}, u32[]{:S(2)}) copy-start(s32[8]{0:T(128)} %param.10) | copy-start | bytes 100
  10.9 1.6 %collective-permute-start.1 = (bf16[512,256]{1,0:T(8,128)(2,1)S(1)}, bf16[512,256]{1,0:T(8,128)(2,1)S(1)}, u32[]{:S(2)}, u32[]{:S(2)}) collective-permute-start(bf16[512,256]{1,0:T(8,128)(2,1)S(1)} %pad_maximum_fusion), channel_id=1, source_target_pairs={{0,2},{2,0},{4,6},{6,4},{8,10},{10,8},{12,14},{14,12},{16,18},{18,... | collective-permute-start | bytes 786440 | tf_op jit(solution)/shard_map/ppermute | solution.py:189
  14.4 3.2 %collective-permute-start.7 = (f32[2,1024]{1,0:T(2,128)S(1)}, f32[2,1024]{1,0:T(2,128)S(1)}, u32[]{:S(2)}, u32[]{:S(2)}) collective-permute-start(f32[2,1024]{1,0:T(2,128)S(1)} %get-tuple-element.29.refs_8_), channel_id=1, source_target_pairs={{0,6},{2,4},{4,2},{6,0},{8,14},{10,12},{12,10},{14,8},{16,22},{18,... | collective-permute-start | bytes 24584 | tf_op jit(solution)/shard_map/ppermute | solution.py:189
  14.5 3.7 %collective-permute-start.6 = (f32[2,1024]{1,0:T(2,128)S(1)}, f32[2,1024]{1,0:T(2,128)S(1)}, u32[]{:S(2)}, u32[]{:S(2)}) collective-permute-start(f32[2,1024]{1,0:T(2,128)S(1)} %get-tuple-element.29.refs_8_), channel_id=1, source_target_pairs={{0,4},{2,6},{4,0},{6,2},{8,12},{10,14},{12,8},{14,10},{16,20},{18,... | collective-permute-start | bytes 24584 | tf_op jit(solution)/shard_map/ppermute | solution.py:189
  15.9 2.4 %collective-permute-start.5 = (f32[2,1024]{1,0:T(2,128)S(1)}, f32[2,1024]{1,0:T(2,128)S(1)}, u32[]{:S(2)}, u32[]{:S(2)}) collective-permute-start(f32[2,1024]{1,0:T(2,128)S(1)} %get-tuple-element.29.refs_8_), channel_id=1, source_target_pairs={{0,2},{2,0},{4,6},{6,4},{8,10},{10,8},{12,14},{14,12},{16,18},{18,... | collective-permute-start | bytes 24584 | tf_op jit(solution)/shard_map/ppermute | solution.py:189
  19.2 4.3 %collective-permute-start.10 = (bf16[128,256]{1,0:T(8,128)(2,1)S(1)}, bf16[128,256]{1,0:T(8,128)(2,1)S(1)}, u32[]{:S(2)}, u32[]{:S(2)}) collective-permute-start(bf16[128,256]{1,0:T(8,128)(2,1)S(1)} %get-tuple-element.42), channel_id=1, source_target_pairs={{0,1},{1,0},{2,3},{3,2},{4,5},{5,4},{6,7},{7,6},{8,9},{9,8},{10,11... | collective-permute-start | bytes 196616 | tf_op jit(solution)/shard_map/ppermute | solution.py:195
  20.8 5.9 %collective-permute-start.13 = (bf16[128,256]{1,0:T(8,128)(2,1)S(1)}, bf16[128,256]{1,0:T(8,128)(2,1)S(1)}, u32[]{:S(2)}, u32[]{:S(2)}) collective-permute-start(bf16[128,256]{1,0:T(8,128)(2,1)S(1)} %get-tuple-element.44), channel_id=1, source_target_pairs={{0,8},{2,10},{4,12},{6,14},{8,0},{10,2},{12,4},{14,6},{16,24},{18,... | collective-permute-start | bytes 196616 | tf_op jit(solution)/shard_map/ppermute | solution.py:189
  21.6 5.0 %collective-permute-start.8 = (bf16[256,256]{1,0:T(8,128)(2,1)S(1)}, bf16[256,256]{1,0:T(8,128)(2,1)S(1)}, u32[]{:S(2)}, u32[]{:S(2)}) collective-permute-start(bf16[256,256]{1,0:T(8,128)(2,1)S(1)} %get-tuple-element.40), channel_id=1, source_target_pairs={{0,4},{2,6},{4,0},{6,2},{8,12},{10,14},{12,8},{14,10},{16,20},{18,... | collective-permute-start | bytes 393224 | tf_op jit(solution)/shard_map/ppermute | solution.py:189
  23.6 5.8 %collective-permute-start.12 = (bf16[64,256]{1,0:T(8,128)(2,1)S(1)}, bf16[64,256]{1,0:T(8,128)(2,1)S(1)}, u32[]{:S(2)}, u32[]{:S(2)}) collective-permute-start(bf16[64,256]{1,0:T(8,128)(2,1)S(1)} %get-tuple-element.53), channel_id=1, source_target_pairs={{0,24},{2,26},{4,28},{6,30},{8,16},{10,18},{12,20},{14,22},{16,8},... | collective-permute-start | bytes 98312 | tf_op jit(solution)/shard_map/ppermute | solution.py:189
  25.9 4.8 %collective-permute-start.11 = (bf16[64,256]{1,0:T(8,128)(2,1)S(1)}, bf16[64,256]{1,0:T(8,128)(2,1)S(1)}, u32[]{:S(2)}, u32[]{:S(2)}) collective-permute-start(bf16[64,256]{1,0:T(8,128)(2,1)S(1)} %get-tuple-element.54), channel_id=1, source_target_pairs={{0,16},{2,18},{4,20},{6,22},{8,24},{10,26},{12,28},{14,30},{16,0},... | collective-permute-start | bytes 98312 | tf_op jit(solution)/shard_map/ppermute | solution.py:189
  26.6 1.3 %collective-permute-start.9 = (bf16[128,256]{1,0:T(8,128)(2,1)S(1)}, bf16[128,256]{1,0:T(8,128)(2,1)S(1)}, u32[]{:S(2)}, u32[]{:S(2)}) collective-permute-start(bf16[128,256]{1,0:T(8,128)(2,1)S(1)} %slice.36), channel_id=1, source_target_pairs={{0,2},{2,0},{4,6},{6,4},{8,10},{10,8},{12,14},{14,12},{16,18},{18,... | collective-permute-start | bytes 196616 | tf_op jit(solution)/shard_map/ppermute | solution.py:189
  26.7 4.0 %collective-permute-start.14 = (bf16[64,256]{1,0:T(8,128)(2,1)S(1)}, bf16[64,256]{1,0:T(8,128)(2,1)S(1)}, u32[]{:S(2)}, u32[]{:S(2)}) collective-permute-start(bf16[64,256]{1,0:T(8,128)(2,1)S(1)} %slice.39), channel_id=1, source_target_pairs={{0,1},{1,0},{2,3},{3,2},{4,5},{5,4},{6,7},{7,6},{8,9},{9,8},{10,11... | collective-permute-start | bytes 98312 | tf_op jit(solution)/shard_map/ppermute | solution.py:195

commit v12 on v11

--- a/solution.py
+++ b/solution.py
@@ -103,7 +103,7 @@
     group, chunk = refs[:GROUP], refs[GROUP : GROUP + chunks]
     chunk = chunk[late[1] :] + chunk[late[0] : late[1]] + chunk[: late[0]]
     stats, refs = refs[GROUP + chunks :][:GROUP], refs[2 * GROUP + chunks :]
-    (tops, expos, dprobs), refs = (refs[0:3], refs[3:6], refs[6:9]), refs[9:]
+    (tops, expos, dprobs), refs = (refs[0:4], refs[4:8], refs[8:12]), refs[12:]
     near_ref, far_ref, *outs, dv_total, dk_total = refs
     rows, width = chunk[0].shape
     hd = width // 2
@@ -243,10 +243,11 @@
             name="stats",
         )(place, *group, *[chunk[b] for b in which], *before)
 
-    first, *kept_early = stats_of(early, (), 0)
+    own, *kept_own = stats_of(early[:1], (), 0)
+    first, *kept_early = stats_of(early[1:], (own,), 0)
     second, *kept_middle = stats_of(middle, (first,), 0)
     stats, *kept_last = stats_of(last, (second,), 0)
-    kept = [ref for three in zip(kept_early, kept_middle, kept_last) for ref in three]
+    kept = [ref for four in zip(kept_own, kept_early, kept_middle, kept_last) for ref in four]
     all_stats = [stats] + [swap(stats, bits) for bits in group_bits[1:]]
 
     pair_rows = array((GROUP // 2 * rows, width))

time: 31.5 us -> 31.5 us (level)
  waiting for transfers between devices: 7.04 us -> 6.7 us
    pallas_call x3 -> x4, Pallas kernels: 1.47 us -> 1.67 us  [stats_of(): pl.pallas_call(functools.partial(stats_kernel, which, heads), out_shape=(...]
  transfers between devices with their start and end apart: 15 -> 15, of which waited for: 9 -> 9; matrix products, arithmetic and copies ran while one was open for 1% -> 1% of each run, Pallas kernels for 7% -> 8%
where the time goes in v12:
time: 31.5 us; the launch traced here: 31.3 us
  starting transfers between devices  17.6 us (56%)
  waiting for transfers between devices  6.7 us (21%)
  Pallas kernels  4.54 us (14%)
  other arithmetic  1.02 us (3%)
  between operations  0.78 us (2%)
  local copies, waits for them, and re-layouts  0.71 us (2%)
    ppermute x10, starting transfers between devices, swap(): return lax.ppermute(x, 'ctx', [(i, i ^ bits) for i in range(ctx_size)])  9.54 us
    ppermute x10, waiting for transfers between devices, swap(): return lax.ppermute(x, 'ctx', [(i, i ^ bits) for i in range(ctx_size)])  5.9 us
    ppermute x3, starting transfers between devices, shift(): lax.ppermute(x, 'ctx', [(i, (i - by) % ctx_size) for i in range(ctx_size)])  5.56 us
    ppermute x2, starting transfers between devices, turn(): lax.ppermute(x, 'head', [(i, (i + by) % shards) for i in range(shards)])  2.5 us
    pallas_call x4, Pallas kernels, stats_of(): pl.pallas_call(functools.partial(stats_kernel, which, heads), out_shape=(...  1.67 us
    pallas_call x1, Pallas kernels, local(): pl.pallas_call(functools.partial(backward_kernel, early + late, (len(last...  0.97 us
    concatenate x1, other arithmetic, local(): jnp.concatenate([jnp.concatenate([key_rows, value_rows], axis=1), queries...  0.89 us
    pallas_call x1, Pallas kernels, local(): pl.pallas_call(query_sum_kernel, out_shape=array((rows, width)), in_specs...  0.65 us
  transfers between devices with their start and end apart: 15, of which 9 were waited for; matrix products, arithmetic and copies ran while one was open for 1% of the time, Pallas kernels for 8%

profile of v12, /device:TPU:0, one launch (start us, length us, event | category | flops | bytes accessed | tf_op | source)
XLA Modules:
  0.0 31.3 jit_solution(14037369958180374141)
XLA Ops:
  0.6 0.9 %pad_maximum_fusion.1 = bf16[384,256]{1,0:T(8,128)(2,1)S(1)} fusion(bf16[128,256]{1,0:T(8,128)(2,1)} %param.9, bf16[128,256]{1,0:T(8,128)(2,1)} %param.6, bf16[128,128]{1,0:T(8,128)(2,1)} %param.8, bf16[128,128]{1,0:T(8,128)(2,1)} %param.7), kind=kLoop, calls=%fused_computation.2 | loop fusion | flops 786432 | bytes 393216 | tf_op jit(solution)/shard_map/concatenate | solution.py:214
  1.5 3.0 %collective-permute-start = (bf16[256,256]{1,0:T(8,128)(2,1)S(1)}, bf16[256,256]{1,0:T(8,128)(2,1)S(1)}, u32[]{:S(2)}, u32[]{:S(2)}) collective-permute-start(bf16[256,256]{1,0:T(8,128)(2,1)S(1)} %slice.32.refs_0_), channel_id=1, source_target_pairs={{0,4},{2,6},{4,0},{6,2},{8,12},{10,14},{12,8},{14,10},{16,20},{18,... | collective-permute-start | bytes 393224 | tf_op jit(solution)/shard_map/ppermute | solution.py:189
  4.6 0.0 copy-start
  4.6 1.6 %collective-permute-start.4 = (bf16[128,256]{1,0:T(8,128)(2,1)S(1)}, bf16[128,256]{1,0:T(8,128)(2,1)S(1)}, u32[]{:S(2)}, u32[]{:S(2)}) collective-permute-start(bf16[128,256]{1,0:T(8,128)(2,1)S(1)} %slice.35.refs_4_.refs_6_), channel_id=1, source_target_pairs={{0,8},{2,10},{4,12},{6,14},{8,16},{10,18},{12,20},{14,22},{16,24},... | collective-permute-start | bytes 196616 | tf_op jit(solution)/shard_map/ppermute | solution.py:192
  6.2 2.6 %collective-permute-start.3 = (bf16[128,256]{1,0:T(8,128)(2,1)S(1)}, bf16[128,256]{1,0:T(8,128)(2,1)S(1)}, u32[]{:S(2)}, u32[]{:S(2)}) collective-permute-start(bf16[128,256]{1,0:T(8,128)(2,1)S(1)} %slice.35.refs_4_.refs_6_), channel_id=1, source_target_pairs={{0,16},{2,18},{4,20},{6,22},{8,24},{10,26},{12,28},{14,30},{16,0},... | collective-permute-start | bytes 196616 | tf_op jit(solution)/shard_map/ppermute | solution.py:192
  8.8 1.3 %collective-permute-start.2 = (bf16[128,256]{1,0:T(8,128)(2,1)S(1)}, bf16[128,256]{1,0:T(8,128)(2,1)S(1)}, u32[]{:S(2)}, u32[]{:S(2)}) collective-permute-start(bf16[128,256]{1,0:T(8,128)(2,1)S(1)} %slice.35.refs_4_.refs_6_), channel_id=1, source_target_pairs={{0,24},{2,26},{4,28},{6,30},{8,0},{10,2},{12,4},{14,6},{16,8},{18,... | collective-permute-start | bytes 196616 | tf_op jit(solution)/shard_map/ppermute | solution.py:192
  10.1 0.0 copy-done
  10.1 0.0 copy-start.1
  10.1 0.1 reshape.9
  10.2 0.6 %copy-done.1 = s32[8]{0:T(128)S(1)} copy-done((s32[8]{0:T(128)S(1)}, s32[8]{0:T(128)}, u32[]{:S(2)}) %copy-start.1) | copy-done | bytes 56
  10.8 0.1 pad_add_fusion.ints
  10.9 0.0 collective-permute-done.refs_2_
  10.9 0.1 collective-permute-start.1
  11.0 0.6 %place.1.place_ref = s32[16,128]{1,0:T(8,128)S(1)} custom-call(s32[40]{0:T(128)S(1)} %pad_add_fusion.ints), custom_call_target="tpu_custom_call" | custom-call | flops 10000000000 | tf_op jit(solution)/shard_map/place/pallas_call | solution.py:204
  11.5 0.9 %collective-permute-done.1 = bf16[512,256]{1,0:T(8,128)(2,1)S(1)} collective-permute-done((bf16[512,256]{1,0:T(8,128)(2,1)S(1)}, bf16[512,256]{1,0:T(8,128)(2,1)S(1)}, u32[]{:S(2)}, u32[]{:S(2)}) %collective-permute-start.1) | collective-permute-done | bytes 262176 | tf_op jit(solution)/shard_map/ppermute | solution.py:189
  12.5 0.4 %stats.4 = (f32[2,1024]{1,0:T(2,128)S(1)}, f32[1,1024]{1,0:T(1,128)S(1)}, f32[128,1024]{1,0:T(8,128)S(1)}, f32[128,1024]{1,0:T(8,128)S(1)}) custom-call(s32[16,128]{1,0:T(8,128)S(1)} %place.1.place_ref, bf16[256,256]{1,0:T(8,128)(2,1)S(1)} %slice.32.refs_0_, bf16[256,256]{1,0:T(8,128)(2,1)S(1)} %get-tuple-element.60.refs_1_, ...), custom_call_target="tpu_custom_call" | custom-call | tf_op jit(solution)/shard_map/stats/pallas_call | solution.py:231
  12.9 0.0 collective-permute-done.4.refs_4_.refs_7_
  12.9 0.4 %stats.5 = (f32[2,1024]{1,0:T(2,128)S(1)}, f32[1,1024]{1,0:T(1,128)S(1)}, f32[128,1024]{1,0:T(8,128)S(1)}, f32[128,1024]{1,0:T(8,128)S(1)}) custom-call(s32[16,128]{1,0:T(8,128)S(1)} %place.1.place_ref, bf16[256,256]{1,0:T(8,128)(2,1)S(1)} %slice.32.refs_0_, bf16[256,256]{1,0:T(8,128)(2,1)S(1)} %get-tuple-element.60.refs_1_, ...), custom_call_target="tpu_custom_call" | custom-call | tf_op jit(solution)/shard_map/stats/pallas_call | solution.py:231
  13.3 0.2 collective-permute-done.3.refs_4_.refs_5_
  13.5 0.4 %stats.6 = (f32[2,1024]{1,0:T(2,128)S(1)}, f32[1,1024]{1,0:T(1,128)S(1)}, f32[128,1024]{1,0:T(8,128)S(1)}, f32[128,1024]{1,0:T(8,128)S(1)}) custom-call(s32[16,128]{1,0:T(8,128)S(1)} %place.1.place_ref, bf16[256,256]{1,0:T(8,128)(2,1)S(1)} %slice.32.refs_0_, bf16[256,256]{1,0:T(8,128)(2,1)S(1)} %get-tuple-element.60.refs_1_, ...), custom_call_target="tpu_custom_call" | custom-call | tf_op jit(solution)/shard_map/stats/pallas_call | solution.py:231
  14.0 0.0 collective-permute-done.2.refs_4_
  14.0 0.4 %stats.7 = (f32[2,1024]{1,0:T(2,128)S(1)}, f32[1,1024]{1,0:T(1,128)S(1)}, f32[128,1024]{1,0:T(8,128)S(1)}, f32[128,1024]{1,0:T(8,128)S(1)}) custom-call(s32[16,128]{1,0:T(8,128)S(1)} %place.1.place_ref, bf16[256,256]{1,0:T(8,128)(2,1)S(1)} %slice.32.refs_0_, bf16[256,256]{1,0:T(8,128)(2,1)S(1)} %get-tuple-element.60.refs_1_, ...), custom_call_target="tpu_custom_call" | custom-call | tf_op jit(solution)/shard_map/stats/pallas_call | solution.py:231
  14.4 0.2 collective-permute-start.7
  14.6 1.5 %collective-permute-start.6 = (f32[2,1024]{1,0:T(2,128)S(1)}, f32[2,1024]{1,0:T(2,128)S(1)}, u32[]{:S(2)}, u32[]{:S(2)}) collective-permute-start(f32[2,1024]{1,0:T(2,128)S(1)} %get-tuple-element.34.refs_8_), channel_id=1, source_target_pairs={{0,4},{2,6},{4,0},{6,2},{8,12},{10,14},{12,8},{14,10},{16,20},{18,... | collective-permute-start | bytes 24584 | tf_op jit(solution)/shard_map/ppermute | solution.py:189
  16.1 0.3 collective-permute-start.5
  16.3 1.2 %collective-permute-done.7.refs_11_ = f32[2,1024]{1,0:T(2,128)S(1)} collective-permute-done((f32[2,1024]{1,0:T(2,128)S(1)}, f32[2,1024]{1,0:T(2,128)S(1)}, u32[]{:S(2)}, u32[]{:S(2)}) %collective-permute-start.7) | collective-permute-done | bytes 8224 | tf_op jit(solution)/shard_map/ppermute | solution.py:189
  17.5 0.7 %collective-permute-done.6.refs_10_ = f32[2,1024]{1,0:T(2,128)S(1)} collective-permute-done((f32[2,1024]{1,0:T(2,128)S(1)}, f32[2,1024]{1,0:T(2,128)S(1)}, u32[]{:S(2)}, u32[]{:S(2)}) %collective-permute-start.6) | collective-permute-done | bytes 8224 | tf_op jit(solution)/shard_map/ppermute | solution.py:189
  18.2 0.0 collective-permute-done.5.refs_9_
  18.3 1.0 %backward.1 = (bf16[256,256]{1,0:T(8,128)(2,1)S(1)}, bf16[256,256]{1,0:T(8,128)(2,1)S(1)}, bf16[128,256]{1,0:T(8,128)(2,1)S(1)}, bf16[128,256]{1,0:T(8,128)(2,1)...) custom-call(bf16[256,256]{1,0:T(8,128)(2,1)S(1)} %slice.32.refs_0_, ...), custom_call_target="tpu_custom_call" | custom-call | tf_op jit(solution)/shard_map/backward/pallas_call | solution.py:256
  19.2 1.6 %collective-permute-start.10 = (bf16[128,256]{1,0:T(8,128)(2,1)S(1)}, bf16[128,256]{1,0:T(8,128)(2,1)S(1)}, u32[]{:S(2)}, u32[]{:S(2)}) collective-permute-start(bf16[128,256]{1,0:T(8,128)(2,1)S(1)} %get-tuple-element.50), channel_id=1, source_target_pairs={{0,1},{1,0},{2,3},{3,2},{4,5},{5,4},{6,7},{7,6},{8,9},{9,8},{10,11... | collective-permute-start | bytes 196616 | tf_op jit(solution)/shard_map/ppermute | solution.py:195
  20.8 0.8 %collective-permute-start.13 = (bf16[128,256]{1,0:T(8,128)(2,1)S(1)}, bf16[128,256]{1,0:T(8,128)(2,1)S(1)}, u32[]{:S(2)}, u32[]{:S(2)}) collective-permute-start(bf16[128,256]{1,0:T(8,128)(2,1)S(1)} %get-tuple-element.52), channel_id=1, source_target_pairs={{0,8},{2,10},{4,12},{6,14},{8,0},{10,2},{12,4},{14,6},{16,24},{18,... | collective-permute-start | bytes 196616 | tf_op jit(solution)/shard_map/ppermute | solution.py:189
  21.6 1.4 %collective-permute-start.8 = (bf16[256,256]{1,0:T(8,128)(2,1)S(1)}, bf16[256,256]{1,0:T(8,128)(2,1)S(1)}, u32[]{:S(2)}, u32[]{:S(2)}) collective-permute-start(bf16[256,256]{1,0:T(8,128)(2,1)S(1)} %get-tuple-element.48), channel_id=1, source_target_pairs={{0,4},{2,6},{4,0},{6,2},{8,12},{10,14},{12,8},{14,10},{16,20},{18,... | collective-permute-start | bytes 393224 | tf_op jit(solution)/shard_map/ppermute | solution.py:189
  23.0 0.6 %collective-permute-done.10.refs_1_ = bf16[128,256]{1,0:T(8,128)(2,1)S(1)} collective-permute-done((bf16[128,256]{1,0:T(8,128)(2,1)S(1)}, bf16[128,256]{1,0:T(8,128)(2,1)S(1)}, u32[]{:S(2)}, u32[]{:S(2)}) %collective-permute-start.10) | collective-permute-done | bytes 65568 | tf_op jit(solution)/shard_map/ppermute | solution.py:195
  23.6 2.3 %collective-permute-start.12 = (bf16[64,256]{1,0:T(8,128)(2,1)S(1)}, bf16[64,256]{1,0:T(8,128)(2,1)S(1)}, u32[]{:S(2)}, u32[]{:S(2)}) collective-permute-start(bf16[64,256]{1,0:T(8,128)(2,1)S(1)} %get-tuple-element.61), channel_id=1, source_target_pairs={{0,24},{2,26},{4,28},{6,30},{8,16},{10,18},{12,20},{14,22},{16,8},... | collective-permute-start | bytes 98312 | tf_op jit(solution)/shard_map/ppermute | solution.py:189
  25.9 0.0 collective-permute-start.11
  25.9 0.7 %collective-permute-done.8 = bf16[256,256]{1,0:T(8,128)(2,1)S(1)} collective-permute-done((bf16[256,256]{1,0:T(8,128)(2,1)S(1)}, bf16[256,256]{1,0:T(8,128)(2,1)S(1)}, u32[]{:S(2)}, u32[]{:S(2)}) %collective-permute-start.8) | collective-permute-done | bytes 131104 | tf_op jit(solution)/shard_map/ppermute | solution.py:189
  26.6 0.1 collective-permute-start.9
  26.7 0.0 collective-permute-done.13.refs_1_
  26.7 0.9 %collective-permute-start.14 = (bf16[64,256]{1,0:T(8,128)(2,1)S(1)}, bf16[64,256]{1,0:T(8,128)(2,1)S(1)}, u32[]{:S(2)}, u32[]{:S(2)}) collective-permute-start(bf16[64,256]{1,0:T(8,128)(2,1)S(1)} %slice.39), channel_id=1, source_target_pairs={{0,1},{1,0},{2,3},{3,2},{4,5},{5,4},{6,7},{7,6},{8,9},{9,8},{10,11... | collective-permute-start | bytes 98312 | tf_op jit(solution)/shard_map/ppermute | solution.py:195
  27.7 0.3 collective-permute-done.9.other_ref
  27.9 0.6 %query_sum.1 = bf16[128,256]{1,0:T(8,128)(2,1)} custom-call(bf16[256,256]{1,0:T(8,128)(2,1)S(1)} %add_convert_fusion.pair_ref, bf16[128,256]{1,0:T(8,128)(2,1)S(1)} %collective-permute-done.9.other_ref), custom_call_target="tpu_custom_call" | custom-call | flops 1000000000 | tf_op jit(solution)/shard_map/query_sum/pallas_call | solution.py:284
  28.6 0.8 %collective-permute-done.12.refs_1_ = bf16[64,256]{1,0:T(8,128)(2,1)S(1)} collective-permute-done((bf16[64,256]{1,0:T(8,128)(2,1)S(1)}, bf16[64,256]{1,0:T(8,128)(2,1)S(1)}, u32[]{:S(2)}, u32[]{:S(2)}) %collective-permute-start.12) | collective-permute-done | bytes 32800 | tf_op jit(solution)/shard_map/ppermute | solution.py:189
  29.4 1.3 %collective-permute-done.11.refs_0_ = bf16[64,256]{1,0:T(8,128)(2,1)S(1)} collective-permute-done((bf16[64,256]{1,0:T(8,128)(2,1)S(1)}, bf16[64,256]{1,0:T(8,128)(2,1)S(1)}, u32[]{:S(2)}, u32[]{:S(2)}) %collective-permute-start.11) | collective-permute-done | bytes 32800 | tf_op jit(solution)/shard_map/ppermute | solution.py:189
  30.7 0.0 collective-permute-done.14.refs_2_
  30.7 0.6 %finish.1 = (bf16[64,128]{1,0:T(8,128)(2,1)}, bf16[64,128]{1,0:T(8,128)(2,1)}) custom-call(bf16[128,256]{1,0:T(8,128)(2,1)S(1)} %fold.3.owned_ref, bf16[64,256]{1,0:T(8,128)(2,1)S(1)} %collective-permute-done.11.refs_0_, bf16[64,256]{1,0:T(8,128)(2,1)S(1)} %collective-permute-done.12.refs_1_, bf16[64,256]{1,0:T(8,128)(2,1)S(1)} %collective-permute-done.14.refs_2_), custom_call_target="tpu_custom_call" | custom-call | tf_op jit(solution)/shard_map/finish/pallas_call | solution.py:294
  (10 shorter events, 0.1 us)
Async XLA Ops:
  1.5 9.3 %collective-permute-start = (bf16[256,256]{1,0:T(8,128)(2,1)S(1)}, bf16[256,256]{1,0:T(8,128)(2,1)S(1)}, u32[]{:S(2)}, u32[]{:S(2)}) collective-permute-start(bf16[256,256]{1,0:T(8,128)(2,1)S(1)} %slice.32.refs_0_), channel_id=1, source_target_pairs={{0,4},{2,6},{4,0},{6,2},{8,12},{10,14},{12,8},{14,10},{16,20},{18,... | collective-permute-start | bytes 393224 | tf_op jit(solution)/shard_map/ppermute | solution.py:189
  4.6 5.6 %copy-start = (s32[16,2]{0,1:T(2,128)S(1)}, s32[16,2]{0,1:T(2,128)}, u32[]{:S(2)}) copy-start(s32[16,2]{0,1:T(2,128)} %param.11) | copy-start | bytes 388
  4.6 8.3 %collective-permute-start.4 = (bf16[128,256]{1,0:T(8,128)(2,1)S(1)}, bf16[128,256]{1,0:T(8,128)(2,1)S(1)}, u32[]{:S(2)}, u32[]{:S(2)}) collective-permute-start(bf16[128,256]{1,0:T(8,128)(2,1)S(1)} %slice.35.refs_4_.refs_6_), channel_id=1, source_target_pairs={{0,8},{2,10},{4,12},{6,14},{8,16},{10,18},{12,20},{14,22},{16,24},... | collective-permute-start | bytes 196616 | tf_op jit(solution)/shard_map/ppermute | solution.py:192
  6.2 7.3 %collective-permute-start.3 = (bf16[128,256]{1,0:T(8,128)(2,1)S(1)}, bf16[128,256]{1,0:T(8,128)(2,1)S(1)}, u32[]{:S(2)}, u32[]{:S(2)}) collective-permute-start(bf16[128,256]{1,0:T(8,128)(2,1)S(1)} %slice.35.refs_4_.refs_6_), channel_id=1, source_target_pairs={{0,16},{2,18},{4,20},{6,22},{8,24},{10,26},{12,28},{14,30},{16,0},... | collective-permute-start | bytes 196616 | tf_op jit(solution)/shard_map/ppermute | solution.py:192
  8.8 5.2 %collective-permute-start.2 = (bf16[128,256]{1,0:T(8,128)(2,1)S(1)}, bf16[128,256]{1,0:T(8,128)(2,1)S(1)}, u32[]{:S(2)}, u32[]{:S(2)}) collective-permute-start(bf16[128,256]{1,0:T(8,128)(2,1)S(1)} %slice.35.refs_4_.refs_6_), channel_id=1, source_target_pairs={{0,24},{2,26},{4,28},{6,30},{8,0},{10,2},{12,4},{14,6},{16,8},{18,... | collective-permute-start | bytes 196616 | tf_op jit(solution)/shard_map/ppermute | solution.py:192
  10.1 0.7 %copy-start.1 = (s32[8]{0:T(128)S(1)}, s32[8]{0:T(128)}, u32[]{:S(2)}) copy-start(s32[8]{0:T(128)} %param.10) | copy-start | bytes 100
  10.9 1.6 %collective-permute-start.1 = (bf16[512,256]{1,0:T(8,128)(2,1)S(1)}, bf16[512,256]{1,0:T(8,128)(2,1)S(1)}, u32[]{:S(2)}, u32[]{:S(2)}) collective-permute-start(bf16[512,256]{1,0:T(8,128)(2,1)S(1)} %pad_maximum_fusion), channel_id=1, source_target_pairs={{0,2},{2,0},{4,6},{6,4},{8,10},{10,8},{12,14},{14,12},{16,18},{18,... | collective-permute-start | bytes 786440 | tf_op jit(solution)/shard_map/ppermute | solution.py:189
  14.4 3.1 %collective-permute-start.7 = (f32[2,1024]{1,0:T(2,128)S(1)}, f32[2,1024]{1,0:T(2,128)S(1)}, u32[]{:S(2)}, u32[]{:S(2)}) collective-permute-start(f32[2,1024]{1,0:T(2,128)S(1)} %get-tuple-element.34.refs_8_), channel_id=1, source_target_pairs={{0,6},{2,4},{4,2},{6,0},{8,14},{10,12},{12,10},{14,8},{16,22},{18,... | collective-permute-start | bytes 24584 | tf_op jit(solution)/shard_map/ppermute | solution.py:189
  14.6 3.7 %collective-permute-start.6 = (f32[2,1024]{1,0:T(2,128)S(1)}, f32[2,1024]{1,0:T(2,128)S(1)}, u32[]{:S(2)}, u32[]{:S(2)}) collective-permute-start(f32[2,1024]{1,0:T(2,128)S(1)} %get-tuple-element.34.refs_8_), channel_id=1, source_target_pairs={{0,4},{2,6},{4,0},{6,2},{8,12},{10,14},{12,8},{14,10},{16,20},{18,... | collective-permute-start | bytes 24584 | tf_op jit(solution)/shard_map/ppermute | solution.py:189
  16.1 2.2 %collective-permute-start.5 = (f32[2,1024]{1,0:T(2,128)S(1)}, f32[2,1024]{1,0:T(2,128)S(1)}, u32[]{:S(2)}, u32[]{:S(2)}) collective-permute-start(f32[2,1024]{1,0:T(2,128)S(1)} %get-tuple-element.34.refs_8_), channel_id=1, source_target_pairs={{0,2},{2,0},{4,6},{6,4},{8,10},{10,8},{12,14},{14,12},{16,18},{18,... | collective-permute-start | bytes 24584 | tf_op jit(solution)/shard_map/ppermute | solution.py:189
  19.2 4.3 %collective-permute-start.10 = (bf16[128,256]{1,0:T(8,128)(2,1)S(1)}, bf16[128,256]{1,0:T(8,128)(2,1)S(1)}, u32[]{:S(2)}, u32[]{:S(2)}) collective-permute-start(bf16[128,256]{1,0:T(8,128)(2,1)S(1)} %get-tuple-element.50), channel_id=1, source_target_pairs={{0,1},{1,0},{2,3},{3,2},{4,5},{5,4},{6,7},{7,6},{8,9},{9,8},{10,11... | collective-permute-start | bytes 196616 | tf_op jit(solution)/shard_map/ppermute | solution.py:195
  20.8 5.9 %collective-permute-start.13 = (bf16[128,256]{1,0:T(8,128)(2,1)S(1)}, bf16[128,256]{1,0:T(8,128)(2,1)S(1)}, u32[]{:S(2)}, u32[]{:S(2)}) collective-permute-start(bf16[128,256]{1,0:T(8,128)(2,1)S(1)} %get-tuple-element.52), channel_id=1, source_target_pairs={{0,8},{2,10},{4,12},{6,14},{8,0},{10,2},{12,4},{14,6},{16,24},{18,... | collective-permute-start | bytes 196616 | tf_op jit(solution)/shard_map/ppermute | solution.py:189
  21.6 5.0 %collective-permute-start.8 = (bf16[256,256]{1,0:T(8,128)(2,1)S(1)}, bf16[256,256]{1,0:T(8,128)(2,1)S(1)}, u32[]{:S(2)}, u32[]{:S(2)}) collective-permute-start(bf16[256,256]{1,0:T(8,128)(2,1)S(1)} %get-tuple-element.48), channel_id=1, source_target_pairs={{0,4},{2,6},{4,0},{6,2},{8,12},{10,14},{12,8},{14,10},{16,20},{18,... | collective-permute-start | bytes 393224 | tf_op jit(solution)/shard_map/ppermute | solution.py:189
  23.6 5.8 %collective-permute-start.12 = (bf16[64,256]{1,0:T(8,128)(2,1)S(1)}, bf16[64,256]{1,0:T(8,128)(2,1)S(1)}, u32[]{:S(2)}, u32[]{:S(2)}) collective-permute-start(bf16[64,256]{1,0:T(8,128)(2,1)S(1)} %get-tuple-element.61), channel_id=1, source_target_pairs={{0,24},{2,26},{4,28},{6,30},{8,16},{10,18},{12,20},{14,22},{16,8},... | collective-permute-start | bytes 98312 | tf_op jit(solution)/shard_map/ppermute | solution.py:189
  25.9 4.8 %collective-permute-start.11 = (bf16[64,256]{1,0:T(8,128)(2,1)S(1)}, bf16[64,256]{1,0:T(8,128)(2,1)S(1)}, u32[]{:S(2)}, u32[]{:S(2)}) collective-permute-start(bf16[64,256]{1,0:T(8,128)(2,1)S(1)} %get-tuple-element.62), channel_id=1, source_target_pairs={{0,16},{2,18},{4,20},{6,22},{8,24},{10,26},{12,28},{14,30},{16,0},... | collective-permute-start | bytes 98312 | tf_op jit(solution)/shard_map/ppermute | solution.py:189
  26.6 1.3 %collective-permute-start.9 = (bf16[128,256]{1,0:T(8,128)(2,1)S(1)}, bf16[128,256]{1,0:T(8,128)(2,1)S(1)}, u32[]{:S(2)}, u32[]{:S(2)}) collective-permute-start(bf16[128,256]{1,0:T(8,128)(2,1)S(1)} %slice.36), channel_id=1, source_target_pairs={{0,2},{2,0},{4,6},{6,4},{8,10},{10,8},{12,14},{14,12},{16,18},{18,... | collective-permute-start | bytes 196616 | tf_op jit(solution)/shard_map/ppermute | solution.py:189
  26.7 4.0 %collective-permute-start.14 = (bf16[64,256]{1,0:T(8,128)(2,1)S(1)}, bf16[64,256]{1,0:T(8,128)(2,1)S(1)}, u32[]{:S(2)}, u32[]{:S(2)}) collective-permute-start(bf16[64,256]{1,0:T(8,128)(2,1)S(1)} %slice.39), channel_id=1, source_target_pairs={{0,1},{1,0},{2,3},{3,2},{4,5},{5,4},{6,7},{7,6},{8,9},{9,8},{10,11... | collective-permute-start | bytes 98312 | tf_op jit(solution)/shard_map/ppermute | solution.py:195
